TPU v7x, 32 devices: a whole 2x2x4 slice. The times are simulated.
32 devices in a mesh: gy: 4 (over y, x), gx: 8 (over z, core).
Axes of the slice: x: 2, y: 2, z: 4, core: 2. Of those that a mesh axis runs over, the one named last changes fastest.
Arguments:
- tokens: bfloat16 [8192, 1152], P(('gy', 'gx')), may hold values from -6 to 6
- text_states: bfloat16 [512, 4096], P(('gy', 'gx')), may hold values from -6 to 6
- pooled_text: float32 [4, 1152], replicated, may hold values from -5 to 5
- timesteps: int32 [4], replicated, may hold values from 0 to 999
- frame_counts: int32 [4], replicated, may hold values from 1 to 3, as said below
- still_clips: int32 [4], replicated, may hold values from 0 to 1, as said below
- text_lengths: int32 [4], replicated, may hold values from 16 to 128, as said below
- w_ada: bfloat16 [1152, 10368], P('gy', 'gx'), may hold values from -0.1875 to 0.1875
- w_sqkv: bfloat16 [1152, 3456], P('gy', 'gx'), may hold values from -0.1875 to 0.1875
- w_sout: bfloat16 [1152, 1152], P('gy', 'gx'), may hold values from -1.5 to 1.5
- w_cq: bfloat16 [1152, 1152], P('gy', 'gx'), may hold values from -0.1875 to 0.1875
- w_ckv: bfloat16 [4096, 2304], P('gy', 'gx'), may hold values from -0.09375 to 0.09375
- w_cout: bfloat16 [1152, 1152], P('gy', 'gx'), may hold values from -0.75 to 0.75
- w_up: bfloat16 [1152, 4608], P('gy', 'gx'), may hold values from -0.1875 to 0.1875
- w_down: bfloat16 [4608, 1152], P('gy', 'gx'), may hold values from -0.09375 to 0.09375
- w_tqkv: bfloat16 [1152, 3456], P('gy', 'gx'), may hold values from -0.1875 to 0.1875
- w_tout: bfloat16 [1152, 1152], P('gy', 'gx'), may hold values from -0.375 to 0.375
- grad_out: bfloat16 [8192, 1152], P(('gy', 'gx')), may hold values from -6 to 6
Outputs:
- mixed: bfloat16 [8192, 1152], P(('gy', 'gx'))
- grad_tokens: bfloat16 [8192, 1152], P(('gy', 'gx'))
- grad_ada: float32 [1152, 10368], P('gy', 'gx')
- grad_sqkv: float32 [1152, 3456], P('gy', 'gx')
- grad_sout: float32 [1152, 1152], P('gy', 'gx')
- grad_cq: float32 [1152, 1152], P('gy', 'gx')
- grad_ckv: float32 [4096, 2304], P('gy', 'gx')
- grad_cout: float32 [1152, 1152], P('gy', 'gx')
- grad_up: float32 [1152, 4608], P('gy', 'gx')
- grad_down: float32 [4608, 1152], P('gy', 'gx')
- grad_tqkv: float32 [1152, 3456], P('gy', 'gx')
- grad_tout: float32 [1152, 1152], P('gy', 'gx')
Inputs may be any that keep to these rules, and one draw needn't show every extreme that they name: `frame_counts`: they sum to 8; at least one clip, drawn from the seed, has 3 frames. `still_clips`: exactly two of the 4 clips are marked. `text_lengths`: some clip has all 128 slots live.
All inputs are finite; a program needn't handle non-finite values.
Results may differ from a plain program's by a relative error of at most 0.025.
Values may be sent and summed in bfloat16 or wider, within the bound.
No kernel may reach another device: no remote copies, remote signals or barrier semaphores. Data moves between devices by JAX's collectives and lax.ppermute only.
A program may use at most 384 MiB of HBM per device.

v0:
```python
import math

import jax
import jax.numpy as jnp
from jax import lax
from jax.sharding import PartitionSpec as P

D = 1152
HEADS = 16
HEAD_DIM = 72
FRAME = 1024
CLIPS = 4


norm_eps = 1e-06
masked_score = -1e30
highest = lax.Precision.HIGHEST


def for_sending(x):

    def short(part):
        return part.astype(jnp.bfloat16) if part.dtype == jnp.float32 else part

    return jax.tree.map(short, x)


def shifted(x, axis, by):
    devices = lax.axis_size(axis)
    pairs = [(i, i + by) for i in range(devices) if 0 <= i + by < devices]
    return lax.ppermute(x, axis, pairs)


def layer_stats(values):
    centred = values - jnp.mean(values, axis=-1, keepdims=True)
    inv_std = lax.rsqrt(jnp.mean(centred * centred, axis=-1, keepdims=True) + norm_eps)
    return (centred * inv_std, inv_std)


def layer_back(grad_norm, normed, inv_std):
    return inv_std * (
        grad_norm
        - jnp.mean(grad_norm, axis=-1, keepdims=True)
        - normed * jnp.mean(grad_norm * normed, axis=-1, keepdims=True)
    )


def condition(timesteps, pooled_text):
    half_width = D // 2
    frequency = jnp.exp(
        -math.log(10000.0) * jnp.arange(half_width).astype(jnp.float32) / half_width
    )
    angles = timesteps.astype(jnp.float32)[:, None] * frequency[None, :]
    embedded = jnp.concatenate([jnp.cos(angles), jnp.sin(angles)], axis=1)
    return jax.nn.silu(embedded + pooled_text)


def split_heads(values):
    return values.reshape(values.shape[:-1] + (HEADS, HEAD_DIM))


def attn_probs(queries, keys, key_ok):
    scores = jnp.einsum(
        "qbhd,kbhd->bhqk",
        split_heads(queries),
        split_heads(keys),
        preferred_element_type=jnp.float32,
    )
    scores = jnp.where(key_ok, scores * HEAD_DIM ** (-0.5), masked_score)
    return jax.nn.softmax(scores, axis=-1)


def attn_forward(queries, keys, values, key_ok):
    probs = attn_probs(queries, keys, key_ok)
    output = jnp.einsum(
        "bhqk,kbhd->qbhd",
        probs.astype(jnp.bfloat16),
        split_heads(values),
        preferred_element_type=jnp.float32,
    )
    return output.reshape(queries.shape).astype(jnp.bfloat16)


def attn_backward(queries, keys, values, key_ok, grad_output):
    probs = attn_probs(queries, keys, key_ok)
    grad_probs = jnp.einsum(
        "qbhd,kbhd->bhqk",
        split_heads(grad_output),
        split_heads(values),
        preferred_element_type=jnp.float32,
    )
    grad_scores = (
        probs * (grad_probs - jnp.sum(probs * grad_probs, axis=-1, keepdims=True))
    ).astype(jnp.bfloat16)
    score_scale = HEAD_DIM ** (-0.5)
    grad_queries = (
        jnp.einsum(
            "bhqk,kbhd->qbhd", grad_scores, split_heads(keys), preferred_element_type=jnp.float32
        )
        * score_scale
    )
    grad_keys = (
        jnp.einsum(
            "bhqk,qbhd->kbhd", grad_scores, split_heads(queries), preferred_element_type=jnp.float32
        )
        * score_scale
    )
    grad_values = jnp.einsum(
        "bhqk,qbhd->kbhd",
        probs.astype(jnp.bfloat16),
        split_heads(grad_output),
        preferred_element_type=jnp.float32,
    )
    return (
        grad_queries.reshape(queries.shape),
        grad_keys.reshape(keys.shape),
        grad_values.reshape(values.shape),
    )


def fetch(weights):
    columns = jax.tree.map(
        lambda part, own: part.astype(own.dtype),
        lax.all_gather(for_sending(weights), "gx", axis=1, tiled=True),
        weights,
    )
    return jax.tree.map(
        lambda part, own: part.astype(own.dtype),
        lax.all_gather(for_sending(columns), "gy", axis=0, tiled=True),
        columns,
    )


def reduce_grads(grads):
    columns = jax.tree.map(
        lambda part: part.astype(jnp.float32),
        lax.psum_scatter(for_sending(grads), "gx", scatter_dimension=1, tiled=True),
    )
    return jax.tree.map(
        lambda part: part.astype(jnp.float32),
        lax.psum_scatter(for_sending(columns), "gy", scatter_dimension=0, tiled=True),
    )


def reorder(values):
    devices = lax.axis_size(("gy", "gx"))
    per_device = values.shape[0] // devices
    moved = lax.all_to_all(
        values.reshape(devices, per_device, values.shape[1]),
        ("gy", "gx"),
        split_axis=0,
        concat_axis=0,
        tiled=True,
    )
    return moved.reshape(values.shape)


def left_product(left, right):
    return jnp.einsum("rd,re->de", left, right, preferred_element_type=jnp.float32)


def right_product(grad, weight):
    return jnp.einsum("re,de->rd", grad, weight, preferred_element_type=jnp.float32)


def local(
    tokens,
    text_states,
    pooled_text,
    timesteps,
    frame_counts,
    still_clips,
    text_lengths,
    w_ada,
    w_sqkv,
    w_sout,
    w_cq,
    w_ckv,
    w_cout,
    w_up,
    w_down,
    w_tqkv,
    w_tout,
    grad_out,
):
    devices = lax.axis_size(("gy", "gx"))
    device = lax.axis_index(("gy", "gx"))
    column = lax.axis_index("gx")
    tok_rows = tokens.shape[0]
    frame_devs = FRAME // tok_rows
    frames_all = tok_rows * devices // FRAME
    frame_here = device // frame_devs
    clip_ends = jnp.cumsum(frame_counts)
    clip_here = jnp.sum((clip_ends <= frame_here).astype(jnp.int32))
    clip_mark = jnp.arange(CLIPS) == clip_here
    clip_pick = clip_mark.astype(jnp.float32)
    cond_all = condition(timesteps, pooled_text)
    cond_here = jnp.dot(clip_pick, cond_all, precision=highest)
    keep_here = 1.0 - jnp.sum(clip_pick * still_clips.astype(jnp.float32))
    length_here = jnp.sum(jnp.where(clip_mark, text_lengths, 0))
    full = fetch((w_ada, w_sqkv, w_sout, w_cq, w_ckv, w_cout, w_up, w_down, w_tqkv, w_tout))
    (
        full_ada,
        full_sqkv,
        full_sout,
        full_cq,
        full_ckv,
        full_cout,
        full_up,
        full_down,
        full_tqkv,
        full_tout,
    ) = full
    modulation = jnp.dot(
        cond_here, full_ada, precision=highest, preferred_element_type=jnp.float32
    ).reshape(9, D)
    inputs = tokens.astype(jnp.float32)
    normed_a, inv_a = layer_stats(inputs)
    hidden_a = (normed_a * (1.0 + modulation[1]) + modulation[0]).astype(jnp.bfloat16)
    qkv_a = jnp.dot(hidden_a, full_sqkv, preferred_element_type=jnp.float32).astype(jnp.bfloat16)
    query_a = qkv_a[:, :D]
    pair_a = qkv_a[:, D:]
    offsets = []
    for distance in range(1, frame_devs):
        offsets = offsets + [distance, -distance]
    window = [pair_a]
    window_ok = [jnp.ones((tok_rows,), dtype=bool)]
    for offset in offsets:
        window.append(shifted(pair_a, "gx", offset))
        same_frame = (column - offset) // frame_devs == column // frame_devs
        window_ok.append(jnp.broadcast_to(same_frame, (tok_rows,)))
    window_pairs = jnp.concatenate(window, axis=0)
    key_ok_a = jnp.concatenate(window_ok)[None, None, None, :]
    out_a = attn_forward(
        query_a[:, None], window_pairs[:, None, :D], window_pairs[:, None, D:], key_ok_a
    )[:, 0]
    branch_a = jnp.dot(out_a, full_sout, preferred_element_type=jnp.float32)
    after_a = inputs + modulation[2] * branch_a
    normed_b, inv_b = layer_stats(after_a)
    hidden_b = normed_b.astype(jnp.bfloat16)
    query_b = jnp.dot(hidden_b, full_cq, preferred_element_type=jnp.float32).astype(jnp.bfloat16)
    own_text = jnp.dot(text_states, full_ckv, preferred_element_type=jnp.float32).astype(
        jnp.bfloat16
    )
    text_pairs = lax.all_gather(own_text, ("gy", "gx"), axis=0, tiled=True)
    text_index = jnp.arange(text_pairs.shape[0])
    text_ok = ((text_index % CLIPS == clip_here) & (text_index // CLIPS < length_here))[
        None, None, None, :
    ]
    out_b = attn_forward(
        query_b[:, None], text_pairs[:, None, :D], text_pairs[:, None, D:], text_ok
    )[:, 0]
    after_b = after_a + jnp.dot(out_b, full_cout, preferred_element_type=jnp.float32)
    normed_c, inv_c = layer_stats(after_b)
    hidden_c = (normed_c * (1.0 + modulation[4]) + modulation[3]).astype(jnp.bfloat16)
    pre_act = jnp.dot(hidden_c, full_up, preferred_element_type=jnp.float32)
    activated = jax.nn.gelu(pre_act).astype(jnp.bfloat16)
    branch_c = jnp.dot(activated, full_down, preferred_element_type=jnp.float32)
    after_c = after_b + modulation[5] * branch_c
    normed_d, inv_d = layer_stats(after_c)
    hidden_d = (normed_d * (1.0 + modulation[7]) + modulation[6]).astype(jnp.bfloat16)
    moved_d = reorder(hidden_d)
    qkv_d = (
        jnp.dot(moved_d, full_tqkv, preferred_element_type=jnp.float32)
        .astype(jnp.bfloat16)
        .reshape(frames_all, -1, 3 * D)
    )
    frame_clip = jnp.sum(
        (clip_ends[None, :] <= jnp.arange(frames_all)[:, None]).astype(jnp.int32), axis=1
    )
    time_ok = (frame_clip[:, None] == frame_clip[None, :])[None, None]
    out_d = attn_forward(
        qkv_d[..., :D], qkv_d[..., D : 2 * D], qkv_d[..., 2 * D :], time_ok
    ).reshape(tok_rows, D)
    branch_moved = jnp.dot(out_d, full_tout, preferred_element_type=jnp.float32).astype(
        jnp.bfloat16
    )
    branch_d = reorder(branch_moved).astype(jnp.float32)
    mixed = (after_c + keep_here * modulation[8] * branch_d).astype(jnp.bfloat16)
    grad_res = grad_out.astype(jnp.float32)
    back_tqkv, back_tout, back_up, back_down = fetch((w_tqkv, w_tout, w_up, w_down))
    grad_branch_d = (keep_here * modulation[8] * grad_res).astype(jnp.bfloat16)
    grad_moved = reorder(grad_branch_d)
    d_tout = left_product(out_d, grad_moved)
    grad_out_d = (
        right_product(grad_moved, back_tout).astype(jnp.bfloat16).reshape(frames_all, -1, D)
    )
    grad_tq, grad_tk, grad_tv = attn_backward(
        qkv_d[..., :D], qkv_d[..., D : 2 * D], qkv_d[..., 2 * D :], time_ok, grad_out_d
    )
    grad_qkv_d = (
        jnp.concatenate([grad_tq, grad_tk, grad_tv], axis=-1)
        .reshape(tok_rows, 3 * D)
        .astype(jnp.bfloat16)
    )
    d_tqkv = left_product(moved_d, grad_qkv_d)
    grad_hidden_d = reorder(right_product(grad_qkv_d, back_tqkv).astype(jnp.bfloat16)).astype(
        jnp.float32
    )
    d_gate3 = jnp.sum(keep_here * grad_res * branch_d, axis=0)
    d_shift3 = jnp.sum(grad_hidden_d, axis=0)
    d_scale3 = jnp.sum(grad_hidden_d * normed_d, axis=0)
    grad_res = grad_res + layer_back(grad_hidden_d * (1.0 + modulation[7]), normed_d, inv_d)
    grad_branch_c = (modulation[5] * grad_res).astype(jnp.bfloat16)
    d_down = left_product(activated, grad_branch_c)
    grad_act = right_product(grad_branch_c, back_down)
    unused_value, gelu_back = jax.vjp(jax.nn.gelu, pre_act)
    grad_pre = gelu_back(grad_act)[0].astype(jnp.bfloat16)
    d_up = left_product(hidden_c, grad_pre)
    grad_hidden_c = right_product(grad_pre, back_up)
    d_gate2 = jnp.sum(grad_res * branch_c, axis=0)
    d_shift2 = jnp.sum(grad_hidden_c, axis=0)
    d_scale2 = jnp.sum(grad_hidden_c * normed_c, axis=0)
    grad_res = grad_res + layer_back(grad_hidden_c * (1.0 + modulation[4]), normed_c, inv_c)
    late_grads = reduce_grads((d_tqkv, d_tout, d_up, d_down))
    back_sqkv, back_sout, back_cq, back_cout = fetch((w_sqkv, w_sout, w_cq, w_cout))
    grad_branch_b = grad_res.astype(jnp.bfloat16)
    d_cout = left_product(out_b, grad_branch_b)
    grad_out_b = right_product(grad_branch_b, back_cout).astype(jnp.bfloat16)
    grad_cq_rows, grad_ck, grad_cv = attn_backward(
        query_b[:, None],
        text_pairs[:, None, :D],
        text_pairs[:, None, D:],
        text_ok,
        grad_out_b[:, None],
    )
    grad_query_b = grad_cq_rows[:, 0].astype(jnp.bfloat16)
    d_cq = left_product(hidden_b, grad_query_b)
    grad_hidden_b = right_product(grad_query_b, back_cq)
    text_terms = jnp.concatenate([grad_ck[:, 0], grad_cv[:, 0]], axis=-1)
    text_grad = lax.psum_scatter(text_terms, ("gy", "gx"), scatter_dimension=0, tiled=True).astype(
        jnp.bfloat16
    )
    d_ckv = left_product(text_states, text_grad)
    grad_res = grad_res + layer_back(grad_hidden_b, normed_b, inv_b)
    grad_branch_a = (modulation[2] * grad_res).astype(jnp.bfloat16)
    d_gate1 = jnp.sum(grad_res * branch_a, axis=0)
    d_sout = left_product(out_a, grad_branch_a)
    grad_out_a = right_product(grad_branch_a, back_sout).astype(jnp.bfloat16)
    grad_sq, grad_sk, grad_sv = attn_backward(
        query_a[:, None],
        window_pairs[:, None, :D],
        window_pairs[:, None, D:],
        key_ok_a,
        grad_out_a[:, None],
    )
    grad_pairs = jnp.concatenate([grad_sk[:, 0], grad_sv[:, 0]], axis=-1)
    own_grads = grad_pairs[:tok_rows]
    for position_slot, offset in enumerate(offsets):
        grad_piece = grad_pairs[(position_slot + 1) * tok_rows : (position_slot + 2) * tok_rows]
        own_grads = own_grads + shifted(grad_piece.astype(jnp.bfloat16), "gx", -offset).astype(
            grad_piece.dtype
        )
    grad_qkv_a = jnp.concatenate([grad_sq[:, 0], own_grads], axis=-1).astype(jnp.bfloat16)
    d_sqkv = left_product(hidden_a, grad_qkv_a)
    grad_hidden_a = right_product(grad_qkv_a, back_sqkv)
    d_shift1 = jnp.sum(grad_hidden_a, axis=0)
    d_scale1 = jnp.sum(grad_hidden_a * normed_a, axis=0)
    grad_res = grad_res + layer_back(grad_hidden_a * (1.0 + modulation[1]), normed_a, inv_a)
    grad_mod = jnp.stack(
        [d_shift1, d_scale1, d_gate1, d_shift2, d_scale2, d_gate2, d_shift3, d_scale3, d_gate3]
    ).reshape(-1)
    d_ada = cond_here[:, None] * grad_mod[None, :]
    early_grads = reduce_grads((d_ada, d_sqkv, d_sout, d_cq, d_ckv, d_cout))
    grad_ada_out = early_grads[0]
    rest = early_grads[1:]
    return (
        mixed,
        grad_res.astype(jnp.bfloat16),
        grad_ada_out,
        rest[0],
        rest[1],
        rest[2],
        rest[3],
        rest[4],
        late_grads[2],
        late_grads[3],
        late_grads[0],
        late_grads[1],
    )


def solution(mesh):
    return jax.shard_map(
        local,
        mesh=mesh,
        in_specs=(
            P(("gy", "gx"), None),
            P(("gy", "gx"), None),
            P(),
            P(),
            P(),
            P(),
            P(),
            P("gy", "gx"),
            P("gy", "gx"),
            P("gy", "gx"),
            P("gy", "gx"),
            P("gy", "gx"),
            P("gy", "gx"),
            P("gy", "gx"),
            P("gy", "gx"),
            P("gy", "gx"),
            P("gy", "gx"),
            P(("gy", "gx"), None),
        ),
        out_specs=(
            P(("gy", "gx"), None),
            P(("gy", "gx"), None),
            P("gy", "gx"),
            P("gy", "gx"),
            P("gy", "gx"),
            P("gy", "gx"),
            P("gy", "gx"),
            P("gy", "gx"),
            P("gy", "gx"),
            P("gy", "gx"),
            P("gy", "gx"),
            P("gy", "gx"),
        ),
        check_vma=False,
    )
```

profile of v0, /device:TPU:0, one launch (start us, length us, event | category | flops | bytes accessed | tf_op | source)
XLA Modules:
  0.0 3170.7 jit_solution(5998881756319538283)
XLA Ops:
  9.5 54.7 %all-gather.28.cloned.1.call-done = bf16[1024,2304]{0,1:T(8,128)(2,1)} async-done(((bf16[1024,288]{0,1:T(8,128)(2,1)}), bf16[1024,2304]{0,1:T(8,128)(2,1)}) %all-gather.28.cloned.1.call-update) | async-done | bytes 4718608 | tf_op jit(solution)/shard_map/all_gather | solution.py:124
  65.3 65.6 %all-gather.48.cloned.1.call-done = bf16[8,1296,288]{1,2,0:T(8,128)(2,1)} async-done(((bf16[1,1296,288]{1,2,0:T(8,128)(2,1)}), bf16[8,1296,288]{1,2,0:T(8,128)(2,1)}) %all-gather.48.cloned.1.call-update) | async-done | bytes 5971984 | tf_op jit(solution)/shard_map/all_gather | solution.py:124
  131.0 7.7 copy.148
  138.7 10.7 reshape.469
  149.5 13.4 all-gather.50.cloned.1.call-done
  170.7 169.0 %all-gather.30.cloned.1.call-done = bf16[4096,2304]{0,1:T(8,128)(2,1)} async-done(((bf16[1024,2304]{0,1:T(8,128)(2,1)}), bf16[4096,2304]{0,1:T(8,128)(2,1)}) %all-gather.30.cloned.1.call-update) | async-done | bytes 18874384 | tf_op jit(solution)/shard_map/all_gather | solution.py:129
  339.7 12.0 convolution_convert_fusion.11
  351.8 21.6 all_gather.83
  374.6 18.8 all_gather.88
  394.6 20.1 all_gather.90
  422.0 7.4 all-gather.40.cloned.1.call-done
  429.5 16.2 all_gather.98
  455.0 192.9 %all-gather.22.cloned.1.call-done = bf16[1152,10368]{1,0:T(8,128)(2,1)} async-done(((bf16[288,10368]{1,0:T(8,128)(2,1)}), bf16[1152,10368]{1,0:T(8,128)(2,1)}) %all-gather.22.cloned.1.call-update) | async-done | bytes 23887888 | tf_op jit(solution)/shard_map/all_gather | solution.py:129
  647.8 14.5 convolution_reduce_fusion
  662.4 71.4 %all-gather.24.cloned.1.call-done = bf16[1152,3456]{1,0:T(8,128)(2,1)} async-done(((bf16[288,3456]{1,0:T(8,128)(2,1)}), bf16[1152,3456]{1,0:T(8,128)(2,1)}) %all-gather.24.cloned.1.call-update) | async-done | bytes 7962640 | tf_op jit(solution)/shard_map/all_gather | solution.py:129
  746.8 23.7 all-gather.54.cloned.1.call-done
  781.9 52.0 %all-gather.32.cloned.1.call-done = bf16[512,2304]{1,0:T(8,128)(2,1)} async-done(((bf16[16,2304]{1,0:T(8,128)(2,1)}), bf16[512,2304]{1,0:T(8,128)(2,1)}) %all-gather.32.cloned.1.call-update) | async-done | bytes 2359312 | tf_op jit(solution)/shard_map/all_gather | solution.py:245
  861.0 7.8 collective-permute-done.2
  877.6 16.5 collective-permute-done.4
  904.8 6.5 copy.152
  911.3 6.4 copy.150
  917.7 16.3 fusion.148
  934.0 13.8 fusion.60
  971.0 99.4 %all-gather.38.cloned.1.call-done = bf16[1152,4608]{1,0:T(8,128)(2,1)} async-done(((bf16[288,4608]{1,0:T(8,128)(2,1)}), bf16[1152,4608]{1,0:T(8,128)(2,1)}) %all-gather.38.cloned.1.call-update) | async-done | bytes 10616848 | tf_op jit(solution)/shard_map/all_gather | solution.py:129
  1070.4 9.0 fusion.138
  1079.4 98.8 %all-gather.42.cloned.1.call-done = bf16[4608,1152]{0,1:T(8,128)(2,1)} async-done(((bf16[1152,1152]{0,1:T(8,128)(2,1)}), bf16[4608,1152]{0,1:T(8,128)(2,1)}) %all-gather.42.cloned.1.call-update) | async-done | bytes 10616848 | tf_op jit(solution)/shard_map/all_gather | solution.py:129
  1178.3 10.6 fusion.141
  1196.7 25.6 all-gather.46.cloned.1.call-done
  1229.8 77.5 %all-gather.44.cloned.1.call-done = bf16[1152,3456]{1,0:T(8,128)(2,1)} async-done(((bf16[288,3456]{1,0:T(8,128)(2,1)}), bf16[1152,3456]{1,0:T(8,128)(2,1)}) %all-gather.44.cloned.1.call-update) | async-done | bytes 7962640 | tf_op jit(solution)/shard_map/all_gather | solution.py:129
  1356.2 6.7 fusion.26
  1378.3 7.0 all-to-all-done.3
  1391.9 14.4 all-to-all-done.1
  1410.7 11.3 fusion.20
  1479.1 7.1 convolution_convert_fusion.4
  1489.4 21.1 multiply_reduce_fusion
  1510.6 24.9 multiply_convert_fusion.1
  1535.5 14.5 fusion.9
  1550.0 8.1 convolution_multiply_fusion
  1583.7 43.6 %collective-permute-done.10 = bf16[256,2304]{0,1:T(8,128)(2,1)} collective-permute-done((bf16[256,2304]{0,1:T(8,128)(2,1)S(1)}, bf16[256,2304]{0,1:T(8,128)(2,1)}, u32[]{:S(2)}, u32[]{:S(2)}) %collective-permute-start.10) | collective-permute-done | bytes 1179680 | tf_op jit(solution)/shard_map/ppermute | solution.py:31
  1627.4 9.9 collective-permute-start.9
  1637.4 11.0 fusion.56
  1648.5 31.0 collective-permute-done.8
  1690.6 7.0 fusion.70
  1697.7 8.3 multiply_convert_fusion
  1713.7 9.1 convolution_convert_fusion.2
  1724.1 9.4 convolution_convert_fusion.1
  1734.8 9.0 fusion.4
  1750.3 18.3 reduce-scatter.44.cloned.1.call-done
  1770.7 85.3 %reduce-scatter.58.cloned.1.call-done = bf16[1152,432]{0,1:T(8,128)(2,1)} async-done(((bf16[1152,3456]{0,1:T(8,128)(2,1)}), bf16[1152,432]{0,1:T(8,128)(2,1)}) %reduce-scatter.58.cloned.1.call-update) | async-done | bytes 995344 | tf_op jit(solution)/shard_map/reduce_scatter | solution.py:137
  1859.9 464.5 %all-reduce.3.cloned.1.call-done = bf16[1152,10368]{1,0:T(8,128)(2,1)} async-done(((bf16[1152,10368]{1,0:T(8,128)(2,1)}), bf16[1152,10368]{1,0:T(8,128)(2,1)}) %all-reduce.3.cloned.1.call-update) | async-done | bytes 23887888
  2329.8 82.7 %reduce-scatter.42.cloned.1.call-done = bf16[1152,432]{0,1:T(8,128)(2,1)} async-done(((bf16[1152,3456]{0,1:T(8,128)(2,1)}), bf16[1152,432]{0,1:T(8,128)(2,1)}) %reduce-scatter.42.cloned.1.call-update) | async-done | bytes 995344 | tf_op jit(solution)/shard_map/reduce_scatter | solution.py:137
  2415.0 108.7 %reduce-scatter.54.cloned.1.call-done = bf16[1152,576]{0,1:T(8,128)(2,1)} async-done(((bf16[1152,4608]{0,1:T(8,128)(2,1)}), bf16[1152,576]{0,1:T(8,128)(2,1)}) %reduce-scatter.54.cloned.1.call-update) | async-done | bytes 1327120 | tf_op jit(solution)/shard_map/reduce_scatter | solution.py:137
  2526.4 108.6 %reduce-scatter.56.cloned.1.call-done = bf16[4608,144]{0,1:T(8,128)(2,1)} async-done(((bf16[4608,1152]{0,1:T(8,128)(2,1)}), bf16[4608,144]{0,1:T(8,128)(2,1)}) %reduce-scatter.56.cloned.1.call-update) | async-done | bytes 1327120 | tf_op jit(solution)/shard_map/reduce_scatter | solution.py:137
  2638.8 184.9 %reduce-scatter.48.cloned.1.call-done = bf16[4096,288]{0,1:T(8,128)(2,1)} async-done(((bf16[4096,2304]{0,1:T(8,128)(2,1)}), bf16[4096,288]{0,1:T(8,128)(2,1)}) %reduce-scatter.48.cloned.1.call-update) | async-done | bytes 2359312 | tf_op jit(solution)/shard_map/reduce_scatter | solution.py:137
  2825.0 25.6 reduce-scatter.78.cloned.1.call-done
  2852.4 26.9 reduce-scatter.70.cloned.1.call-done
  2881.0 26.8 reduce-scatter.66.cloned.1.call-done
  2909.5 27.0 reduce-scatter.64.cloned.1.call-done
  2938.3 29.6 reduce-scatter.76.cloned.1.call-done
  2970.1 45.7 %reduce-scatter.40.cloned.1.call-done = bf16[288,1296]{1,0:T(8,128)(2,1)} async-done(((bf16[1152,1296]{1,0:T(8,128)(2,1)}), bf16[288,1296]{1,0:T(8,128)(2,1)}) %reduce-scatter.40.cloned.1.call-update) | async-done | bytes 746512 | tf_op jit(solution)/shard_map/reduce_scatter | solution.py:141
  3018.1 29.1 reduce-scatter.62.cloned.1.call-done
  3049.4 31.0 reduce-scatter.72.cloned.1.call-done
  3082.7 38.3 %reduce-scatter.74.cloned.1.call-done = bf16[1152,144]{1,0:T(8,128)(2,1)} async-done(((bf16[4608,144]{1,0:T(8,128)(2,1)}), bf16[1152,144]{1,0:T(8,128)(2,1)}) %reduce-scatter.74.cloned.1.call-update) | async-done | bytes 331792
  3123.2 38.5 %reduce-scatter.50.cloned.1.call-done = bf16[1024,288]{0,1:T(8,128)(2,1)} async-done(((bf16[4096,288]{0,1:T(8,128)(2,1)}), bf16[1024,288]{0,1:T(8,128)(2,1)}) %reduce-scatter.50.cloned.1.call-update) | async-done | bytes 589840 | tf_op jit(solution)/shard_map/reduce_scatter | solution.py:141
  (486 shorter events, 368.4 us)
Async XLA Ops:
  7.2 332.5 %copy-start = (bf16[16,4096]{1,0:T(8,128)(2,1)S(1)}, bf16[16,4096]{1,0:T(8,128)(2,1)}, u32[]{:S(2)}) copy-start(bf16[16,4096]{1,0:T(8,128)(2,1)} %param.19) | copy-start | bytes 393220
  7.2 56.9 %all-gather.28.cloned.1.call-start = ((), (), s32[]{:S(2)}) async-start(), calls=%async_computation.27 | async-start | bytes 5308416 | tf_op jit(solution)/shard_map/all_gather | solution.py:124
  7.9 123.0 %all-gather.48.cloned.1.call-start = ((), (), s32[]{:S(2)}) async-start(), calls=%async_computation.48 | async-start | bytes 7299072 | tf_op jit(solution)/shard_map/all_gather | solution.py:124
  8.7 154.2 %all-gather.50.cloned.1.call-start = ((), (), s32[]{:S(2)}) async-start(), calls=%async_computation.49 | async-start | bytes 2654208 | tf_op jit(solution)/shard_map/all_gather | solution.py:124
  9.4 330.3 %all-gather.30.cloned.1.call-start = ((), (), s32[]{:S(2)}) async-start(), calls=%async_computation.28 | async-start | bytes 23592960 | tf_op jit(solution)/shard_map/all_gather | solution.py:129
  64.1 351.8 %all-gather.52.cloned.1.call-start = ((), (), s32[]{:S(2)}) async-start(), calls=%async_computation.50 | async-start | bytes 3317760 | tf_op jit(solution)/shard_map/all_gather | solution.py:124
  64.7 364.7 %all-gather.40.cloned.1.call-start = ((), (), s32[]{:S(2)}) async-start(), calls=%async_computation.33 | async-start | bytes 2985984 | tf_op jit(solution)/shard_map/all_gather | solution.py:124
  65.3 582.5 %all-gather.22.cloned.1.call-start = ((), (), s32[]{:S(2)}) async-start(), calls=%async_computation.24 | async-start | bytes 29859840 | tf_op jit(solution)/shard_map/all_gather | solution.py:129
  149.4 584.3 %all-gather.24.cloned.1.call-start = ((), (), s32[]{:S(2)}) async-start(), calls=%async_computation.25 | async-start | bytes 9953280 | tf_op jit(solution)/shard_map/all_gather | solution.py:129
  169.9 600.6 %all-gather.54.cloned.1.call-start = ((), (), s32[]{:S(2)}) async-start(), calls=%async_computation.51 | async-start | bytes 2654208 | tf_op jit(solution)/shard_map/all_gather | solution.py:124
  170.6 663.2 %all-gather.32.cloned.1.call-start = ((), (), s32[]{:S(2)}) async-start(), calls=%async_computation.29 | async-start | bytes 2433024 | tf_op jit(solution)/shard_map/all_gather | solution.py:245
  351.7 596.1 %all-gather.26.cloned.1.call-start = ((), (), s32[]{:S(2)}) async-start(), calls=%async_computation.26 | async-start | bytes 3317760 | tf_op jit(solution)/shard_map/all_gather | solution.py:129
  374.5 577.6 %all-gather.34.cloned.1.call-start = ((), (), s32[]{:S(2)}) async-start(), calls=%async_computation.30 | async-start | bytes 3317760 | tf_op jit(solution)/shard_map/all_gather | solution.py:129
  394.6 573.0 %all-gather.36.cloned.1.call-start = ((), (), s32[]{:S(2)}) async-start(), calls=%async_computation.31 | async-start | bytes 3317760 | tf_op jit(solution)/shard_map/all_gather | solution.py:129
  415.8 654.6 %all-gather.38.cloned.1.call-start = ((), (), s32[]{:S(2)}) async-start(), calls=%async_computation.32 | async-start | bytes 13271040 | tf_op jit(solution)/shard_map/all_gather | solution.py:129
  422.0 756.3 %all-gather.42.cloned.1.call-start = ((), (), s32[]{:S(2)}) async-start(), calls=%async_computation.34 | async-start | bytes 13271040 | tf_op jit(solution)/shard_map/all_gather | solution.py:129
  429.5 792.8 %all-gather.46.cloned.1.call-start = ((), (), s32[]{:S(2)}) async-start(), calls=%async_computation.36 | async-start | bytes 3317760 | tf_op jit(solution)/shard_map/all_gather | solution.py:129
  446.9 860.4 %all-gather.44.cloned.1.call-start = ((), (), s32[]{:S(2)}) async-start(), calls=%async_computation.35 | async-start | bytes 9953280 | tf_op jit(solution)/shard_map/all_gather | solution.py:129
  447.3 286.4 %copy-start.74 = (f32[256]{0:T(256)}, f32[256]{0:T(256)S(1)}, u32[]{:S(2)}) copy-start(f32[256]{0:T(256)S(1)} %broadcast_multiply_fusion.11) | copy-start | bytes 3076
  453.0 481.0 %copy-start.91 = (pred[1792]{0:T(1024)(128)(4,1)}, pred[1792]{0:T(1024)(128)(4,1)S(1)}, u32[]{:S(2)}) copy-start(pred[1792]{0:T(1024)(128)(4,1)S(1)} %dynamic-update-slice.9) | copy-start | bytes 5380
  453.3 280.5 %copy-start.82 = (f32[256]{0:T(256)}, f32[256]{0:T(256)S(1)}, u32[]{:S(2)}) copy-start(f32[256]{0:T(256)S(1)} %add_rsqrt_fusion.3) | copy-start | bytes 3076
  662.4 187.1 %copy-start.54 = (f32[1152]{0:T(1024)}, f32[1152]{0:T(1024)S(1)}, u32[]{:S(2)}) copy-start(f32[1152]{0:T(1024)S(1)} %get-tuple-element.111) | copy-start | bytes 13828
  662.4 285.5 %copy-start.52 = (f32[1152]{0:T(1024)}, f32[1152]{0:T(1024)S(1)}, u32[]{:S(2)}) copy-start(f32[1152]{0:T(1024)S(1)} %get-tuple-element.119) | copy-start | bytes 13828
  662.4 408.0 %copy-start.44 = (f32[1152]{0:T(1024)}, f32[1152]{0:T(1024)S(1)}, u32[]{:S(2)}) copy-start(f32[1152]{0:T(1024)S(1)} %get-tuple-element.114) | copy-start | bytes 13828
  662.4 515.9 %copy-start.85 = (f32[1152]{0:T(1024)}, f32[1152]{0:T(1024)S(1)}, u32[]{:S(2)}) copy-start(f32[1152]{0:T(1024)S(1)} %get-tuple-element.116) | copy-start | bytes 13828
  662.4 763.6 %copy-start.42 = (f32[1152]{0:T(1024)}, f32[1152]{0:T(1024)S(1)}, u32[]{:S(2)}) copy-start(f32[1152]{0:T(1024)S(1)} %get-tuple-element.115) | copy-start | bytes 13828
  742.6 112.4 %collective-permute-start = (bf16[256,2304]{1,0:T(8,128)(2,1)}, bf16[256,2304]{1,0:T(8,128)(2,1)}, u32[]{:S(2)}, u32[]{:S(2)}) collective-permute-start(bf16[256,2304]{1,0:T(8,128)(2,1)} %get-tuple-element.107), channel_id=1, source_target_pairs={{0,1},{1,2},{2,3},{3,4},{4,5},{5,6},{6,7},{8,9},{9,10},{10,11},{11... | collective-permute-start | bytes 3538952 | tf_op jit(solution)/shard_map/ppermute | solution.py:31
  780.6 78.1 %collective-permute-start.1 = (bf16[256,2304]{1,0:T(8,128)(2,1)}, bf16[256,2304]{1,0:T(8,128)(2,1)}, u32[]{:S(2)}, u32[]{:S(2)}) collective-permute-start(bf16[256,2304]{1,0:T(8,128)(2,1)} %get-tuple-element.107), channel_id=1, source_target_pairs={{1,0},{2,1},{3,2},{4,3},{5,4},{6,5},{7,6},{9,8},{10,9},{11,10},{12... | collective-permute-start | bytes 3538952 | tf_op jit(solution)/shard_map/ppermute | solution.py:31
  839.7 29.1 collective-permute-start.2
  843.2 32.0 %collective-permute-start.3 = (bf16[256,2304]{1,0:T(8,128)(2,1)}, bf16[256,2304]{1,0:T(8,128)(2,1)}, u32[]{:S(2)}, u32[]{:S(2)}) collective-permute-start(bf16[256,2304]{1,0:T(8,128)(2,1)} %get-tuple-element.107), channel_id=1, source_target_pairs={{2,0},{3,1},{4,2},{5,3},{6,4},{7,5},{10,8},{11,9},{12,10},{13,11},... | collective-permute-start | bytes 3538952 | tf_op jit(solution)/shard_map/ppermute | solution.py:31
  844.5 49.6 %collective-permute-start.4 = (bf16[256,2304]{1,0:T(8,128)(2,1)}, bf16[256,2304]{1,0:T(8,128)(2,1)}, u32[]{:S(2)}, u32[]{:S(2)}) collective-permute-start(bf16[256,2304]{1,0:T(8,128)(2,1)} %get-tuple-element.107), channel_id=1, source_target_pairs={{0,3},{1,4},{2,5},{3,6},{4,7},{8,11},{9,12},{10,13},{11,14},{12,15... | collective-permute-start | bytes 3538952 | tf_op jit(solution)/shard_map/ppermute | solution.py:31
  851.7 339.3 %all-to-all-start.2 = ((bf16[32,8,1152]{2,1,0:T(8,128)(2,1)}), bf16[32,8,1152]{2,1,0:T(8,128)(2,1)}, u32[]{:S(2)}, u32[]{:S(2)}) async-start(bf16[32,8,1152]{2,1,0:T(8,128)(2,1)} %fusion.99), calls=%async_computation.2 | async-start | bytes 1179648 | tf_op jit(solution)/shard_map/all_to_all | solution.py:148
  855.0 42.8 %collective-permute-start.5 = (bf16[256,2304]{1,0:T(8,128)(2,1)}, bf16[256,2304]{1,0:T(8,128)(2,1)S(1)}, u32[]{:S(2)}, u32[]{:S(2)}) collective-permute-start(bf16[256,2304]{1,0:T(8,128)(2,1)} %get-tuple-element.107), channel_id=1, source_target_pairs={{3,0},{4,1},{5,2},{6,3},{7,4},{11,8},{12,9},{13,10},{14,11},{15,12... | collective-permute-start | bytes 3538952 | tf_op jit(solution)/shard_map/ppermute | solution.py:31
  970.7 455.3 %copy-start.4 = (f32[256,1152]{1,0:T(8,128)}, f32[256,1152]{1,0:T(8,128)S(1)}, u32[]{:S(2)}) copy-start(f32[256,1152]{1,0:T(8,128)S(1)} %get-tuple-element.128) | copy-start | bytes 3538948
  1191.0 116.3 %all-to-all-start = ((bf16[32,8,1152]{2,1,0:T(8,128)(2,1)}), bf16[32,8,1152]{2,1,0:T(8,128)(2,1)S(1)}, u32[]{:S(2)}, u32[]{:S(2)}) async-start(bf16[32,8,1152]{2,1,0:T(8,128)(2,1)} %fusion.98), calls=%async_computation | async-start | bytes 1179648 | tf_op jit(solution)/shard_map/all_to_all | solution.py:148
  1362.9 22.4 all-to-all-start.3
  1385.3 21.1 all-to-all-start.1
  1388.6 345.0 %reduce-scatter.68.cloned.1.call-start = ((), (), s32[]{:S(2)}) async-start(), calls=%async_computation.55 | async-start | bytes 4866048
  1455.1 288.8 %reduce-scatter.60.cloned.1.call-start = ((), (), s32[]{:S(2)}) async-start(), calls=%async_computation.47 | async-start | bytes 2985984 | tf_op jit(solution)/shard_map/reduce_scatter | solution.py:137
  1459.7 286.4 %reduce-scatter.52.cloned.1.call-start = ((), (), s32[]{:S(2)}) async-start(), calls=%async_computation.43 | async-start | bytes 2985984 | tf_op jit(solution)/shard_map/reduce_scatter | solution.py:137
  1463.6 284.6 %reduce-scatter.46.cloned.1.call-start = ((), (), s32[]{:S(2)}) async-start(), calls=%async_computation.40 | async-start | bytes 2985984 | tf_op jit(solution)/shard_map/reduce_scatter | solution.py:137
  1471.2 297.5 %reduce-scatter.44.cloned.1.call-start = ((), (), s32[]{:S(2)}) async-start(), calls=%async_computation.39 | async-start | bytes 2985984 | tf_op jit(solution)/shard_map/reduce_scatter | solution.py:137
  1478.0 378.0 %reduce-scatter.58.cloned.1.call-start = ((), (), s32[]{:S(2)}) async-start(), calls=%async_computation.46 | async-start | bytes 8957952 | tf_op jit(solution)/shard_map/reduce_scatter | solution.py:137
  1486.2 838.2 %all-reduce.3.cloned.1.call-start = ((), (), s32[]{:S(2)}) async-start(), calls=%async_computation.61 | async-start | bytes 47775744
  1570.0 57.4 %collective-permute-start.10 = (bf16[256,2304]{0,1:T(8,128)(2,1)S(1)}, bf16[256,2304]{0,1:T(8,128)(2,1)}, u32[]{:S(2)}, u32[]{:S(2)}) collective-permute-start(bf16[256,2304]{0,1:T(8,128)(2,1)S(1)} %get-tuple-element.96), channel_id=1, source_target_pairs={{3,0},{4,1},{5,2},{6,3},{7,4},{11,8},{12,9},{13,10},{14,11},{15,12... | collective-permute-start | bytes 3538952 | tf_op jit(solution)/shard_map/ppermute | solution.py:31
  1571.3 77.2 %collective-permute-start.11 = (bf16[256,2304]{0,1:T(8,128)(2,1)}, bf16[256,2304]{0,1:T(8,128)(2,1)}, u32[]{:S(2)}, u32[]{:S(2)}) collective-permute-start(bf16[256,2304]{0,1:T(8,128)(2,1)} %get-tuple-element.95), channel_id=1, source_target_pairs={{0,3},{1,4},{2,5},{3,6},{4,7},{8,11},{9,12},{10,13},{11,14},{12,15... | collective-permute-start | bytes 3538952 | tf_op jit(solution)/shard_map/ppermute | solution.py:31
  1576.6 71.9 %collective-permute-start.6 = (bf16[256,2304]{0,1:T(8,128)(2,1)}, bf16[256,2304]{0,1:T(8,128)(2,1)}, u32[]{:S(2)}, u32[]{:S(2)}) collective-permute-start(bf16[256,2304]{0,1:T(8,128)(2,1)} %get-tuple-element.94), channel_id=1, source_target_pairs={{1,0},{2,1},{3,2},{4,3},{5,4},{6,5},{7,6},{9,8},{10,9},{11,10},{12... | collective-permute-start | bytes 3538952 | tf_op jit(solution)/shard_map/ppermute | solution.py:31
  1577.9 70.6 %collective-permute-start.7 = (bf16[256,2304]{0,1:T(8,128)(2,1)}, bf16[256,2304]{0,1:T(8,128)(2,1)}, u32[]{:S(2)}, u32[]{:S(2)}) collective-permute-start(bf16[256,2304]{0,1:T(8,128)(2,1)} %get-tuple-element.99), channel_id=1, source_target_pairs={{0,1},{1,2},{2,3},{3,4},{4,5},{5,6},{6,7},{8,9},{9,10},{10,11},{11... | collective-permute-start | bytes 3538952 | tf_op jit(solution)/shard_map/ppermute | solution.py:31
  1582.4 97.0 %collective-permute-start.8 = (bf16[256,2304]{0,1:T(8,128)(2,1)}, bf16[256,2304]{0,1:T(8,128)(2,1)}, u32[]{:S(2)}, u32[]{:S(2)}) collective-permute-start(bf16[256,2304]{0,1:T(8,128)(2,1)} %get-tuple-element.98), channel_id=1, source_target_pairs={{2,0},{3,1},{4,2},{5,3},{6,4},{7,5},{10,8},{11,9},{12,10},{13,11},... | collective-permute-start | bytes 3538952 | tf_op jit(solution)/shard_map/ppermute | solution.py:31
  1627.4 58.4 %collective-permute-start.9 = (bf16[256,2304]{0,1:T(8,128)(2,1)S(1)}, bf16[256,2304]{0,1:T(8,128)(2,1)}, u32[]{:S(2)}, u32[]{:S(2)}) collective-permute-start(bf16[256,2304]{0,1:T(8,128)(2,1)S(1)} %get-tuple-element.97), channel_id=1, source_target_pairs={{0,2},{1,3},{2,4},{3,5},{4,6},{5,7},{8,10},{9,11},{10,12},{11,13},... | collective-permute-start | bytes 3538952 | tf_op jit(solution)/shard_map/ppermute | solution.py:31
  1706.0 706.4 %reduce-scatter.42.cloned.1.call-start = ((), (), s32[]{:S(2)}) async-start(), calls=%async_computation.38 | async-start | bytes 8957952 | tf_op jit(solution)/shard_map/reduce_scatter | solution.py:137
  1712.5 811.2 %reduce-scatter.54.cloned.1.call-start = ((), (), s32[]{:S(2)}) async-start(), calls=%async_computation.44 | async-start | bytes 11943936 | tf_op jit(solution)/shard_map/reduce_scatter | solution.py:137
  1722.8 912.2 %reduce-scatter.56.cloned.1.call-start = ((), (), s32[]{:S(2)}) async-start(), calls=%async_computation.45 | async-start | bytes 11943936 | tf_op jit(solution)/shard_map/reduce_scatter | solution.py:137
  1733.5 1090.2 %reduce-scatter.48.cloned.1.call-start = ((), (), s32[]{:S(2)}) async-start(), calls=%async_computation.41 | async-start | bytes 21233664 | tf_op jit(solution)/shard_map/reduce_scatter | solution.py:137
  1743.9 1106.7 %reduce-scatter.78.cloned.1.call-start = ((), (), s32[]{:S(2)}) async-start(), calls=%async_computation.60 | async-start | bytes 737280
  1746.0 1133.2 %reduce-scatter.70.cloned.1.call-start = ((), (), s32[]{:S(2)}) async-start(), calls=%async_computation.56 | async-start | bytes 737280
  1748.2 1159.6 %reduce-scatter.66.cloned.1.call-start = ((), (), s32[]{:S(2)}) async-start(), calls=%async_computation.54 | async-start | bytes 737280
  1750.3 1186.3 %reduce-scatter.64.cloned.1.call-start = ((), (), s32[]{:S(2)}) async-start(), calls=%async_computation.53 | async-start | bytes 737280
  1770.7 1197.2 %reduce-scatter.76.cloned.1.call-start = ((), (), s32[]{:S(2)}) async-start(), calls=%async_computation.59 | async-start | bytes 1474560
  1858.4 1157.3 %reduce-scatter.40.cloned.1.call-start = ((), (), s32[]{:S(2)}) async-start(), calls=%async_computation.37 | async-start | bytes 4055040 | tf_op jit(solution)/shard_map/reduce_scatter | solution.py:141
  2329.7 717.5 %reduce-scatter.62.cloned.1.call-start = ((), (), s32[]{:S(2)}) async-start(), calls=%async_computation.52 | async-start | bytes 1474560
  2415.0 665.4 %reduce-scatter.72.cloned.1.call-start = ((), (), s32[]{:S(2)}) async-start(), calls=%async_computation.57 | async-start | bytes 1843200
  2526.3 594.7 %reduce-scatter.74.cloned.1.call-start = ((), (), s32[]{:S(2)}) async-start(), calls=%async_computation.58 | async-start | bytes 2949120
  2638.8 523.0 %reduce-scatter.50.cloned.1.call-start = ((), (), s32[]{:S(2)}) async-start(), calls=%async_computation.42 | async-start | bytes 2949120 | tf_op jit(solution)/shard_map/reduce_scatter | solution.py:141
  (92 other events, 2430.1 us)
Sparse Core Ops, SparseCore 0:
  9.7 54.3 all-gather.27
  65.7 65.1 all-gather.47
  132.6 30.2 all-gather.49
  164.6 175.0 all-gather.29
  341.2 47.3 all-gather.51
  390.1 39.2 all-gather.39
  431.3 216.5 all-gather.21
  649.7 84.0 all-gather.23
  735.4 35.0 all-gather.53
  774.0 59.8 all-gather.31
  836.3 39.3 all-gather.25
  878.0 41.0 all-gather.33
  921.0 41.4 all-gather.35
  964.2 106.1 all-gather.37
  1072.1 106.1 all-gather.41
  1180.0 42.2 all-gather.45
  1224.0 83.2 all-gather.43
  1455.3 104.4 reduce-scatter.67
  1562.2 56.3 reduce-scatter.59
  1620.9 66.4 reduce-scatter.51
  1689.7 39.7 reduce-scatter.45
  1731.9 36.6 reduce-scatter.43
  1771.1 84.8 reduce-scatter.57
  1858.4 466.0 all-reduce.2
  2326.9 85.5 reduce-scatter.41
  2414.7 108.9 reduce-scatter.53
  2525.9 108.9 reduce-scatter.55
  2637.3 186.3 reduce-scatter.47
  2827.1 23.4 reduce-scatter.77
  2854.2 25.0 reduce-scatter.69
  2882.7 25.0 reduce-scatter.65
  2911.5 25.0 reduce-scatter.63
  2939.3 28.5 reduce-scatter.75
  2970.9 44.7 reduce-scatter.39
  3018.6 28.5 reduce-scatter.61
  3050.0 30.3 reduce-scatter.71
  3083.6 37.3 reduce-scatter.73
  3124.3 37.3 reduce-scatter.49
where the time goes:
time: 3180 us; the launch traced here: 3170 us
  waiting for transfers between devices  2460 us (77%)
  matrix products  290 us (9%)
  local copies, waits for them, and re-layouts  190 us (6%)
  other arithmetic  79.6 us (3%)
  blocking collectives  76.6 us (2%)
  starting transfers between devices  57.2 us (2%)
    all_gather x10, waiting for transfers between devices, fetch(): lax.all_gather(for_sending(columns), 'gy', axis=0, tiled=True)  735 us
    unnamed x48, waiting for transfers between devices  703 us
    reduce_scatter x9, waiting for transfers between devices, reduce_grads(): lax.psum_scatter(for_sending(grads), 'gx', scatter_dimension=1, tiled=True)  588 us
    all_gather x6, waiting for transfers between devices, fetch(): lax.all_gather(for_sending(weights), 'gx', axis=1, tiled=True)  165 us
    ppermute x12, waiting for transfers between devices, shifted(): return lax.ppermute(x, axis, pairs)  111 us
    unnamed x242, local copies, waits for them, and re-layouts  101 us
    reduce_scatter x2, waiting for transfers between devices, reduce_grads(): lax.psum_scatter(for_sending(columns), 'gy', scatter_dimension=0, tiled=T...  84.2 us
    all_gather x4, blocking collectives, fetch(): lax.all_gather(for_sending(weights), 'gx', axis=1, tiled=True)  76.6 us
  transfers between devices with their start and end apart: 54, of which 39 were waited for; matrix products, arithmetic and copies ran while one was open for 14% of the time, Pallas kernels for 0%

commit v1 on v0

v1 whole, which is shorter than its diff:
```python
import functools
import math

import jax
import jax.numpy as jnp
from jax import lax
from jax.experimental import pallas as pl
from jax.experimental.pallas import tpu as pltpu
from jax.sharding import PartitionSpec as P

D = 1152
HEADS = 16
HEAD_DIM = 72
FRAME = 1024
CLIPS = 4

norm_eps = 1e-06
masked_score = -1e30
highest = lax.Precision.HIGHEST
f32 = jnp.float32
bf16 = jnp.bfloat16
score_scale = HEAD_DIM ** (-0.5)
log2_scale = score_scale * math.log2(math.e)
row_axes = ("gy", "gx")
col_axes = ("gx", "gy")
nt = (((1,), (1,)), ((), ()))


def vmem():
    return pl.BlockSpec(memory_space=pltpu.VMEM)


def smem():
    return pl.BlockSpec(memory_space=pltpu.SMEM)


def hbm():
    return pl.BlockSpec(memory_space=pl.ANY)


def shape(*size, dtype=f32):
    return jax.ShapeDtypeStruct(size, dtype)


def run(kernel, outs, specs, scratch, args, flops, moved):
    return pl.pallas_call(
        kernel,
        out_shape=outs,
        in_specs=specs,
        out_specs=[vmem() for _ in outs],
        scratch_shapes=scratch,
        compiler_params=pltpu.CompilerParams(vmem_limit_bytes=56 << 20),
        cost_estimate=pl.CostEstimate(flops=flops, bytes_accessed=moved, transcendentals=0),
    )(*args)


class Window:
    def __init__(self, lo, hi):
        self.lo, self.hi = lo, hi
        self.start = lo // 128 * 128
        self.stop = -(-hi // 128) * 128
        self.off = lo - self.start
        self.n = hi - lo
        self.width = self.stop - self.start

    def inside(self, outer):
        return Window(self.lo - outer.start, self.hi - outer.start)


def padded(lanes):
    return -(-lanes // 128) * 128


def block_copies(source, window, buffer, sems, count):
    return [
        pltpu.make_async_copy(
            source.at[i, :, window.start : window.stop], buffer.at[i], sems.at[i]
        )
        for i in range(count)
    ]


def stats(values):
    centred = values - jnp.mean(values, axis=-1, keepdims=True)
    inv_std = lax.rsqrt(jnp.mean(centred * centred, axis=-1, keepdims=True) + norm_eps)
    return centred * inv_std, inv_std


def stats_back(grad_norm, normed, inv_std):
    return inv_std * (
        grad_norm
        - jnp.mean(grad_norm, axis=-1, keepdims=True)
        - normed * jnp.mean(grad_norm * normed, axis=-1, keepdims=True)
    )


def mm(left, right):
    return jnp.dot(left, right, preferred_element_type=f32)


def mm_nt(left, right):
    return lax.dot_general(left, right, nt, preferred_element_type=f32)


def put(dests, start, value):
    base, width = 0, value.shape[1]
    for ref in dests:
        size = ref.shape[1]
        lo, hi = max(start, base), min(start + width, base + size)
        if lo < hi:
            ref[:, lo - base : hi - base] = value[:, lo - start : hi - start].astype(ref.dtype)
        base += size


def take(pad, off, sources, start, width):
    base = 0
    for ref in sources:
        size = ref.shape[1]
        lo, hi = max(start, base), min(start + width, base + size)
        if lo < hi:
            pad[:, off + lo - start : off + hi - start] = ref[:, lo - base : hi - base]
        base += size


def head(h):
    return slice(h * HEAD_DIM, (h + 1) * HEAD_DIM)


def gelu_parts(u):
    c = math.sqrt(2.0 / math.pi)
    square = u * u
    return jnp.tanh(c * u * (1.0 + 0.044715 * square)), square, c


def qkv_kernel(win, nx, x_ref, mod_ref, w_ref, h_ref, q_ref, kv_ref, buf, sems):
    copies = block_copies(w_ref, win, buf, sems, nx)
    for copy in copies:
        copy.start()
    normed, _ = stats(x_ref[...].astype(f32))
    hidden = (normed * (1.0 + mod_ref[1:2, :]) + mod_ref[0:1, :]).astype(bf16)
    h_ref[...] = hidden
    for x in range(nx):
        copies[x].wait()
        block = mm(hidden, buf[x])[:, win.off : win.off + win.n]
        put([q_ref, kv_ref], x * win.n, block)


def stage_heads(dest, row, source, start):
    rows = source.shape[0]
    for h in range(HEADS):
        dest[h, row : row + rows, :HEAD_DIM] = source[
            :, start + h * HEAD_DIM : start + (h + 1) * HEAD_DIM
        ]


def spatial_kernel(pieces, *refs):
    q_ref = refs[0]
    kv_refs = refs[1 : 1 + pieces]
    o_ref, lse_ref, q_t, v_t, k_heads, o_t = refs[1 + pieces :]
    rows = q_ref.shape[0]
    q_t[...] = q_ref[...].astype(f32).T
    for i, kv in enumerate(kv_refs):
        v_t[:, i * rows : (i + 1) * rows] = kv[:, D:].astype(f32).T
        stage_heads(k_heads, i * rows, kv, 0)

    def one_head(h, carry):
        span = pl.ds(pl.multiple_of(h * HEAD_DIM, 8), HEAD_DIM)
        scores = mm(k_heads[h, :, :HEAD_DIM], q_t[span, :].astype(bf16)) * log2_scale
        top = jnp.max(scores, axis=0, keepdims=True)
        weights = jnp.exp2(scores - top)
        total = jnp.sum(weights, axis=0, keepdims=True)
        o_t[span, :] = mm(v_t[span, :].astype(bf16), weights.astype(bf16)) / total
        lse_ref[pl.ds(h, 1), :] = top + jnp.log2(total)
        return carry

    lax.fori_loop(0, HEADS, one_head, 0)
    o_ref[...] = o_t[...].T.astype(bf16)


def text_probs(text_ref, q_t, h, length):
    scores = mm(text_ref[:, head(h)], q_t[head(h), :].astype(bf16)) * score_scale
    slot = lax.broadcasted_iota(jnp.int32, scores.shape, 0)
    scores = jnp.where(slot < length, scores, masked_score)
    weights = jnp.exp(scores - jnp.max(scores, axis=0, keepdims=True))
    return weights / jnp.sum(weights, axis=0, keepdims=True)


def text_kernel(
    outer, w_out, w_cq, w_cout, nx, x_ref, o_ref, mod_ref, w_ref, text_ref, length_ref,
    a1_ref, x1_ref, hc_ref, qc_ref, oc_ref, x2_ref, h3_ref,
    buf, sems, acc, q_t, v_t,
):
    copies = block_copies(w_ref, outer, buf, sems, nx)
    for copy in copies:
        copy.start()

    def product(left, win, dest, wait=False):
        for x in range(nx):
            if wait:
                copies[x].wait()
            block = mm(left, buf[x, :, win.start : win.stop])[:, win.off : win.off + win.n]
            put([dest], x * win.n, block)

    product(o_ref[...], w_out, a1_ref, wait=True)
    after_a = x_ref[...].astype(f32) + mod_ref[2:3, :] * a1_ref[...]
    x1_ref[...] = after_a
    hidden = stats(after_a)[0].astype(bf16)
    hc_ref[...] = hidden
    product(hidden, w_cq, qc_ref)
    q_t[...] = qc_ref[...].astype(f32).T
    v_t[...] = text_ref[:, D:].astype(f32).T
    length = length_ref[0]
    for h in range(HEADS):
        probs = text_probs(text_ref, q_t, h, length).astype(bf16)
        acc[head(h), :] = mm(v_t[head(h), :].astype(bf16), probs)
    oc_ref[...] = acc[...].T.astype(bf16)
    product(oc_ref[...], w_cout, x2_ref)
    after_b = x1_ref[...] + x2_ref[...]
    x2_ref[...] = after_b
    h3_ref[...] = (
        stats(after_b)[0] * (1.0 + mod_ref[4:5, :]) + mod_ref[3:4, :]
    ).astype(bf16)


def ff_kernel(
    win, nx, ny, h_ref, x2_ref, mod_ref, up_ref, down_ref,
    u_ref, g_ref, m_ref, x3_ref, h4_ref, up_buf, down_buf, up_sems, down_sems,
):
    ups = block_copies(up_ref, win, up_buf, up_sems, nx)
    width = down_ref.shape[2]
    downs = block_copies(down_ref, Window(0, width), down_buf, down_sems, ny)
    for copy in ups + downs:
        copy.start()
    hidden = h_ref[...]
    for x in range(nx):
        ups[x].wait()
        u = mm(hidden, up_buf[x])[:, win.off : win.off + win.n]
        put([u_ref], x * win.n, u)
        put([g_ref], x * win.n, 0.5 * u * (1.0 + gelu_parts(u)[0]))
    total = jnp.zeros(m_ref.shape, f32)
    for i in range(ny):
        downs[i].wait()
        total = total + mm_nt(g_ref[:, i * width : (i + 1) * width], down_buf[i])
    m_ref[...] = total
    after_c = x2_ref[...] + mod_ref[5:6, :] * total
    x3_ref[...] = after_c
    h4_ref[...] = (
        stats(after_c)[0] * (1.0 + mod_ref[7:8, :]) + mod_ref[6:7, :]
    ).astype(bf16)


def early_kernel(win, nx, g_ref, mod_ref, keep_ref, w_ref, da_ref, do_ref, buf, pad, sems):
    copies = block_copies(w_ref, win, buf, sems, nx)
    for copy in copies:
        copy.start()
    da_ref[...] = (keep_ref[0] * mod_ref[8:9, :] * g_ref[...].astype(f32)).astype(bf16)
    pad[...] = jnp.zeros(pad.shape, bf16)
    total = jnp.zeros(g_ref.shape, f32)
    for x in range(nx):
        copies[x].wait()
        take(pad, win.off, [da_ref], x * win.n, win.n)
        total = total + mm_nt(pad[...], buf[x])
    do_ref[...] = total.astype(bf16)


def temporal_kernel(
    win, nx, frames, h_ref, do_in, w_ref, row_clip, frame_clip,
    o_ref, dqkv_ref, dh_ref, buf, sems, pad, q_s, k_s, v_s, do_s, o_s, dq_s, dk_s, dv_s, qkv_s,
):
    copies = block_copies(w_ref, win, buf, sems, nx)
    for copy in copies:
        copy.start()
    rows = h_ref.shape[0]
    spots = rows // frames
    hidden = h_ref[...]
    for x in range(nx):
        copies[x].wait()
        block = mm(hidden, buf[x])[:, win.off : win.off + win.n]
        put([qkv_s], x * win.n, block)
    q_s[...] = qkv_s[:, :D].astype(f32)
    k_s[...] = qkv_s[:, D : 2 * D].astype(f32)
    v_s[...] = qkv_s[:, 2 * D :].astype(f32)
    do_s[...] = do_in[...].astype(f32)
    dk_s[...] = jnp.zeros(dk_s.shape, f32)
    dv_s[...] = jnp.zeros(dv_s.shape, f32)

    def one_hot(size, feature, slot):
        first = lax.broadcasted_iota(jnp.int32, size, slot) * HEAD_DIM
        place = lax.broadcasted_iota(jnp.int32, size, feature)
        return jnp.where((place >= first) & (place < first + HEAD_DIM), 1.0, 0.0).astype(bf16)

    gather = one_hot((D, 128), 0, 1)
    spread = one_hot((128, D), 1, 0)

    def per_head(values):
        high = values.astype(bf16)
        low = (values - high.astype(f32)).astype(bf16)
        return mm(high, gather) + mm(low, gather)

    def every_frame(values):
        return jnp.broadcast_to(values[None], (frames, spots, D)).reshape(rows, D)

    def over_frames(values):
        return jnp.sum(values.reshape(frames, spots, values.shape[-1]), axis=0)

    def one_frame(f, carry):
        span = pl.ds(pl.multiple_of(f * spots, 8), spots)
        queries = every_frame(q_s[span, :])
        grads = every_frame(do_s[span, :])
        scores = per_head(queries * k_s[...]) * score_scale
        scores = jnp.where(row_clip[...] == frame_clip[f], scores, masked_score)
        scores = scores.reshape(frames, spots, 128)
        weights = jnp.exp(scores - jnp.max(scores, axis=0, keepdims=True))
        probs = weights / jnp.sum(weights, axis=0, keepdims=True)
        grad_probs = per_head(grads * v_s[...]).reshape(frames, spots, 128)
        inner = jnp.sum(probs * grad_probs, axis=0, keepdims=True)
        grad_scores = (probs * (grad_probs - inner)).reshape(rows, 128).astype(bf16)
        probs_wide = mm(probs.reshape(rows, 128).astype(bf16), spread)
        grads_wide = mm(grad_scores, spread)
        o_s[span, :] = over_frames(probs_wide * v_s[...])
        dq_s[span, :] = over_frames(grads_wide * k_s[...]) * score_scale
        dk_s[...] += grads_wide * queries
        dv_s[...] += probs_wide * grads
        return carry

    lax.fori_loop(0, frames, one_frame, 0)
    o_ref[...] = o_s[...].astype(bf16)
    dqkv_ref[:, :D] = dq_s[...].astype(bf16)
    dqkv_ref[:, D : 2 * D] = (dk_s[...] * score_scale).astype(bf16)
    dqkv_ref[:, 2 * D :] = dv_s[...].astype(bf16)
    pad[...] = jnp.zeros(pad.shape, bf16)
    total = jnp.zeros(dh_ref.shape, f32)
    for x in range(nx):
        take(pad, win.off, [dqkv_ref], x * win.n, win.n)
        total = total + mm_nt(pad[...], buf[x])
    dh_ref[...] = total.astype(bf16)


def mixed_kernel(
    win, nx, o_ref, x3_ref, g_ref, mod_ref, keep_ref, w_ref, y_ref, gate_ref, buf, sems, acc
):
    copies = block_copies(w_ref, win, buf, sems, nx)
    for copy in copies:
        copy.start()
    for x in range(nx):
        copies[x].wait()
        put([acc], x * win.n, mm(o_ref[...], buf[x])[:, win.off : win.off + win.n])
    branch = acc[...].astype(bf16).astype(f32)
    keep = keep_ref[0]
    y_ref[...] = (x3_ref[...] + keep * mod_ref[8:9, :] * branch).astype(bf16)
    gate_ref[...] = jnp.sum(keep * g_ref[...].astype(f32) * branch, axis=0, keepdims=True)


def column_sum(values):
    return jnp.sum(values, axis=0, keepdims=True)


def ff_back_kernel(
    win, nx, ny, g_ref, dh4_ref, x3_ref, x2_ref, u_ref, m_ref, mod_ref, up_ref, down_ref,
    dm_ref, du_ref, dx2_ref, sum_ref, up_buf, down_buf, up_sems, down_sems, du_s, pad,
):
    width = down_ref.shape[2]
    downs = block_copies(down_ref, Window(0, width), down_buf, down_sems, ny)
    ups = block_copies(up_ref, win, up_buf, up_sems, nx)
    for copy in downs + ups:
        copy.start()
    dh4 = dh4_ref[...].astype(f32)
    normed, inv_std = stats(x3_ref[...])
    dx3 = g_ref[...].astype(f32) + stats_back(dh4 * (1.0 + mod_ref[7:8, :]), normed, inv_std)
    sum_ref[0:1, :] = column_sum(dh4)
    sum_ref[1:2, :] = column_sum(dh4 * normed)
    sum_ref[2:3, :] = column_sum(dx3 * m_ref[...])
    dm = (mod_ref[5:6, :] * dx3).astype(bf16)
    dm_ref[...] = dm
    for i in range(ny):
        downs[i].wait()
        grad = mm(dm, down_buf[i])
        u = u_ref[:, i * width : (i + 1) * width]
        tanh, square, c = gelu_parts(u)
        slope = 0.5 * (1.0 + tanh) + 0.5 * u * (1.0 - tanh * tanh) * (
            c * (1.0 + 3.0 * 0.044715 * square)
        )
        du_s[:, i * width : (i + 1) * width] = (grad * slope).astype(bf16)
    pad[...] = jnp.zeros(pad.shape, bf16)
    total = jnp.zeros(dx2_ref.shape, f32)
    for x in range(nx):
        ups[x].wait()
        take(pad, win.off, [du_s], x * win.n, win.n)
        du_ref[x] = pad[:, win.off : win.off + win.n]
        total = total + mm_nt(pad[...], up_buf[x])
    normed, inv_std = stats(x2_ref[...])
    sum_ref[3:4, :] = column_sum(total)
    sum_ref[4:5, :] = column_sum(total * normed)
    sum_ref[5:8, :] = jnp.zeros((3, D), f32)
    dx2_ref[...] = dx3 + stats_back(total * (1.0 + mod_ref[4:5, :]), normed, inv_std)


def text_back_kernel(
    outer, w_out, w_cq, w_cout, nx, dx2_ref, x1_ref, a1_ref, mod_ref, w_ref, qc_ref, text_ref,
    length_ref, dac_ref, dqc_ref, dx1_ref, da1_ref, do1_ref, dtext_ref, gate_ref,
    buf, sems, pad, acc, q_t, do_t, k_t, do_s, dtext_s,
):
    copies = block_copies(w_ref, outer, buf, sems, nx)
    for copy in copies:
        copy.start()

    def product(source, win, wait=False):
        pad[...] = jnp.zeros(pad.shape, bf16)
        total = jnp.zeros(dx2_ref.shape, f32)
        for x in range(nx):
            if wait:
                copies[x].wait()
            take(pad, win.off, [source], x * win.n, win.n)
            total = total + mm_nt(pad[:, : win.width], buf[x, :, win.start : win.stop])
        return total

    dx2 = dx2_ref[...]
    dac_ref[...] = dx2.astype(bf16)
    grad_o = product(dac_ref, w_cout, wait=True).astype(bf16)
    do_s[...] = grad_o
    do_t[...] = grad_o.astype(f32).T
    q_t[...] = qc_ref[...].astype(f32).T
    k_t[...] = text_ref[:, :D].astype(f32).T
    length = length_ref[0]
    for h in range(HEADS):
        probs = text_probs(text_ref, q_t, h, length)
        values = text_ref[:, D + h * HEAD_DIM : D + (h + 1) * HEAD_DIM]
        grad_probs = mm(values, do_t[head(h), :].astype(bf16))
        inner = jnp.sum(probs * grad_probs, axis=0, keepdims=True)
        grad_scores = (probs * (grad_probs - inner)).astype(bf16)
        dtext_s[:, head(h)] = mm(grad_scores, qc_ref[:, head(h)]) * score_scale
        dtext_s[:, D + h * HEAD_DIM : D + (h + 1) * HEAD_DIM] = mm(
            probs.astype(bf16), do_s[:, head(h)]
        )
        acc[head(h), :] = mm(k_t[head(h), :].astype(bf16), grad_scores) * score_scale
    width = dtext_ref.shape[2]
    for x in range(nx):
        dtext_ref[x] = dtext_s[:, x * width : (x + 1) * width].astype(bf16)
    dqc_ref[...] = acc[...].T.astype(bf16)
    normed, inv_std = stats(x1_ref[...])
    dx1 = dx2 + stats_back(product(dqc_ref, w_cq), normed, inv_std)
    dx1_ref[...] = dx1
    gate_ref[...] = column_sum(dx1 * a1_ref[...])
    da1_ref[...] = (mod_ref[2:3, :] * dx1).astype(bf16)
    do1_ref[...] = product(da1_ref, w_out).astype(bf16)


def spatial_back_kernel(pieces, *refs):
    q_ref, do_ref, o_ref, lse_ref = refs[:4]
    kv_refs = refs[4 : 4 + pieces]
    (
        dq_ref, dkv_ref,
        q_t, do_t, o_t, k_t, dq_t, q_heads, do_heads, k_heads, v_heads, dk_heads, dv_heads,
    ) = refs[4 + pieces :]
    rows = q_ref.shape[0]
    q_t[...] = q_ref[...].astype(f32).T
    do_t[...] = do_ref[...].astype(f32).T
    o_t[...] = o_ref[...].astype(f32).T
    stage_heads(q_heads, 0, q_ref, 0)
    stage_heads(do_heads, 0, do_ref, 0)
    for i, kv in enumerate(kv_refs):
        k_t[:, i * rows : (i + 1) * rows] = kv[:, :D].astype(f32).T
        stage_heads(k_heads, i * rows, kv, 0)
        stage_heads(v_heads, i * rows, kv, D)

    def one_head(h, carry):
        span = pl.ds(pl.multiple_of(h * HEAD_DIM, 8), HEAD_DIM)
        grad_o = do_t[span, :]
        inner = jnp.sum(grad_o * o_t[span, :], axis=0, keepdims=True)
        scores = mm(k_heads[h, :, :HEAD_DIM], q_t[span, :].astype(bf16)) * log2_scale
        probs = jnp.exp2(scores - lse_ref[pl.ds(h, 1), :])
        grad_probs = mm(v_heads[h, :, :HEAD_DIM], grad_o.astype(bf16))
        grad_scores = (probs * (grad_probs - inner)).astype(bf16)
        dv_heads[h, :, :HEAD_DIM] = mm(probs.astype(bf16), do_heads[h, :, :HEAD_DIM]).astype(bf16)
        dk_heads[h, :, :HEAD_DIM] = (
            mm(grad_scores, q_heads[h, :, :HEAD_DIM]) * score_scale
        ).astype(bf16)
        dq_t[span, :] = mm(k_t[span, :].astype(bf16), grad_scores) * score_scale
        return carry

    lax.fori_loop(0, HEADS, one_head, 0)
    dq_ref[...] = dq_t[...].T.astype(bf16)
    for i in range(pieces):
        span = slice(i * rows, (i + 1) * rows)
        for h in range(HEADS):
            dkv_ref[i, :, head(h)] = dk_heads[h, span, :HEAD_DIM]
            dkv_ref[i, :, D + h * HEAD_DIM : D + (h + 1) * HEAD_DIM] = dv_heads[
                h, span, :HEAD_DIM
            ]


def qkv_back_kernel(
    win, nx, dq_ref, own_ref, come_ref, x_ref, mod_ref, dx1_ref, w_ref,
    dkv_ref, gx_ref, sum_ref, buf, sems, pad,
):
    copies = block_copies(w_ref, win, buf, sems, nx)
    for copy in copies:
        copy.start()
    dkv_ref[...] = (own_ref[...].astype(f32) + come_ref[...].astype(f32)).astype(bf16)
    pad[...] = jnp.zeros(pad.shape, bf16)
    total = jnp.zeros(dx1_ref.shape, f32)
    for x in range(nx):
        copies[x].wait()
        take(pad, win.off, [dq_ref, dkv_ref], x * win.n, win.n)
        total = total + mm_nt(pad[...], buf[x])
    normed, inv_std = stats(x_ref[...].astype(f32))
    sum_ref[0:1, :] = column_sum(total)
    sum_ref[1:2, :] = column_sum(total * normed)
    gx_ref[...] = (
        dx1_ref[...] + stats_back(total * (1.0 + mod_ref[1:2, :]), normed, inv_std)
    ).astype(bf16)


def weight_kernel(nx, lanes, counts, *refs):
    lefts, k = [], 0
    for count in counts:
        lefts.append((refs[k], refs[k + 1 : k + 1 + count]))
        k += 1 + count
    out_ref, pads, turned = refs[k], refs[k + 1 :: 2], refs[k + 2 :: 2]
    x = pl.program_id(0)

    @pl.when(x == 0)
    def _():
        for (left, _), turn in zip(lefts, turned):
            turn[...] = left[...].astype(f32).T.astype(bf16)

    at = 0
    for (_, rights), pad, turn in zip(lefts, pads, turned):
        n = pad.shape[1]
        for i in range(nx):

            @pl.when(x == i)
            def _():
                take(pad, 0, rights, i * n, n)

        out_ref[0, :, at : at + n] = mm(turn[...], pad[...]).astype(bf16)
        at += n
    if at < lanes:
        out_ref[0, :, at:] = jnp.zeros((out_ref.shape[1], lanes - at), bf16)


def weight_grads(nx, pairs):
    widths = [sum(r.shape[1] for r in rights) // nx for _, rights in pairs]
    lanes = padded(sum(widths))
    rows = pairs[0][0].shape[0]
    args, specs, scratch = [], [], []
    for (left, rights), width in zip(pairs, widths):
        args += [left, *rights]
        specs += [vmem() for _ in range(1 + len(rights))]
        scratch += [pltpu.VMEM((rows, width), bf16), pltpu.VMEM((D, rows), bf16)]
    return pl.pallas_call(
        functools.partial(weight_kernel, nx, lanes, [len(r) for _, r in pairs]),
        out_shape=shape(nx, D, lanes, dtype=bf16),
        grid=(nx,),
        in_specs=specs,
        out_specs=pl.BlockSpec((1, D, lanes), lambda x: (x, 0, 0)),
        scratch_shapes=scratch,
        compiler_params=pltpu.CompilerParams(vmem_limit_bytes=56 << 20),
        cost_estimate=pl.CostEstimate(
            flops=4 * rows * D * nx * lanes, bytes_accessed=2 * nx * D * lanes, transcendentals=0
        ),
    )(*args)


def ff_grads(h3, du, dm, g):
    nx, rows, n = du.shape
    lanes = padded(n)

    def up_kernel(h_ref, du_ref, out_ref, turn):
        @pl.when(pl.program_id(0) == 0)
        def _():
            turn[...] = h_ref[...].astype(f32).T.astype(bf16)

        out_ref[0, :, :n] = mm(turn[...], du_ref[0]).astype(bf16)
        if n < lanes:
            out_ref[0, :, n:] = jnp.zeros((D, lanes - n), bf16)

    d_up = pl.pallas_call(
        up_kernel,
        out_shape=shape(nx, D, lanes, dtype=bf16),
        grid=(nx,),
        in_specs=[vmem(), pl.BlockSpec((1, rows, n), lambda x: (x, 0, 0))],
        out_specs=pl.BlockSpec((1, D, lanes), lambda x: (x, 0, 0)),
        scratch_shapes=[pltpu.VMEM((D, rows), bf16)],
        compiler_params=pltpu.CompilerParams(vmem_limit_bytes=56 << 20),
        cost_estimate=pl.CostEstimate(
            flops=4 * rows * D * nx * n, bytes_accessed=2 * nx * D * n, transcendentals=0
        ),
    )(h3, du)
    ny = lax.axis_size("gy")
    width = g.shape[1] // ny

    def down_kernel(dm_ref, g_ref, out_ref, turn):
        @pl.when(pl.program_id(0) == 0)
        def _():
            turn[...] = dm_ref[...].astype(f32).T.astype(bf16)

        out_ref[0] = mm(turn[...], g_ref[...]).astype(bf16)

    d_down = pl.pallas_call(
        down_kernel,
        out_shape=shape(ny, D, width, dtype=bf16),
        grid=(ny,),
        in_specs=[vmem(), pl.BlockSpec((rows, width), lambda i: (0, i))],
        out_specs=pl.BlockSpec((1, D, width), lambda i: (i, 0, 0)),
        scratch_shapes=[pltpu.VMEM((D, rows), bf16)],
        compiler_params=pltpu.CompilerParams(vmem_limit_bytes=56 << 20),
        cost_estimate=pl.CostEstimate(
            flops=4 * rows * D * ny * width, bytes_accessed=2 * ny * D * width, transcendentals=0
        ),
    )(dm, g)
    return d_up, d_down


def gather_columns(shard):
    nx = lax.axis_size("gx")
    whole = lax.all_gather(shard, col_axes, axis=0, tiled=True)
    return whole.reshape(nx, -1, shard.shape[1])


def gather_rows(shard):
    ny = lax.axis_size("gy")
    whole = lax.all_gather(shard, row_axes, axis=0, tiled=True)
    return whole.reshape(ny, -1, shard.shape[1])


def scatter(blocks, axes):
    flat = blocks.reshape(-1, blocks.shape[-1])
    return lax.psum_scatter(flat, axes, scatter_dimension=0, tiled=True).astype(f32)


def swap(values, axis, mask):
    return lax.ppermute(values, axis, [(i, i ^ mask) for i in range(lax.axis_size(axis))])


def reorder(values):
    devices = lax.axis_size(row_axes)
    return lax.all_to_all(
        values.reshape(devices, values.shape[0] // devices, values.shape[1]),
        row_axes,
        split_axis=0,
        concat_axis=0,
        tiled=True,
    ).reshape(values.shape)


def pad_lanes(values):
    return jnp.pad(values, ((0, 0), (0, padded(values.shape[1]) - values.shape[1])))


def condition(timesteps, pooled_text):
    half_width = D // 2
    frequency = jnp.exp(
        -math.log(10000.0) * jnp.arange(half_width).astype(jnp.float32) / half_width
    )
    angles = timesteps.astype(jnp.float32)[:, None] * frequency[None, :]
    embedded = jnp.concatenate([jnp.cos(angles), jnp.sin(angles)], axis=1)
    return jax.nn.silu(embedded + pooled_text)


def local(
    tokens,
    text_states,
    pooled_text,
    timesteps,
    frame_counts,
    still_clips,
    text_lengths,
    w_ada,
    w_sqkv,
    w_sout,
    w_cq,
    w_ckv,
    w_cout,
    w_up,
    w_down,
    w_tqkv,
    w_tout,
    grad_out,
):
    nx, ny = lax.axis_size("gx"), lax.axis_size("gy")
    gx, gy = lax.axis_index("gx"), lax.axis_index("gy")
    devices = nx * ny
    device = gy * nx + gx
    rows = tokens.shape[0]
    frame_devs = FRAME // rows
    frames = rows * devices // FRAME
    k_rows = w_ada.shape[0]
    clip_ends = jnp.cumsum(frame_counts)
    clip_here = jnp.sum((clip_ends <= device // frame_devs).astype(jnp.int32))
    clip_mark = jnp.arange(CLIPS) == clip_here
    clip_pick = clip_mark.astype(f32)
    keep_here = (1.0 - jnp.sum(clip_pick * still_clips.astype(f32))).reshape(1)
    length_here = jnp.sum(jnp.where(clip_mark, text_lengths, 0)).reshape(1)
    frame_clip = jnp.sum(
        (clip_ends[None, :] <= jnp.arange(frames)[:, None]).astype(jnp.int32), axis=1
    ).astype(f32)
    row_clip = jnp.repeat(frame_clip, rows // frames)[:, None]

    n_sqkv, n_one, n_up = w_sqkv.shape[1], w_sout.shape[1], w_up.shape[1]
    full_a = gather_columns(pad_lanes(jnp.concatenate([w_sqkv, w_sout, w_cq, w_cout], axis=1)))
    full_b = gather_columns(pad_lanes(jnp.concatenate([w_up, w_tqkv, w_tout], axis=1)))
    full_down = gather_rows(w_down.T)
    ff_width = full_down.shape[2]
    ff = ff_width * ny
    win_sqkv = Window(0, n_sqkv)
    at = n_sqkv
    win_rest = Window(at, at + 3 * n_one)
    win_sout, win_cq, win_cout = [
        Window(at + i * n_one, at + (i + 1) * n_one).inside(win_rest) for i in range(3)
    ]
    win_up = Window(0, n_up)
    win_tqkv = Window(n_up, n_up + n_sqkv)
    win_tout = Window(n_up + n_sqkv, n_up + n_sqkv + n_one)

    cond_all = condition(timesteps, pooled_text)
    cond_rows = lax.dynamic_slice_in_dim(cond_all, gy * k_rows, k_rows, axis=1)
    mod_part = jnp.dot(cond_rows, w_ada.astype(f32), precision=highest)
    mod_all = lax.all_gather(lax.psum(mod_part, "gy"), "gx", axis=1, tiled=True)
    mod = jnp.dot(clip_pick, mod_all, precision=highest).reshape(9, D)

    own = text_states.shape[0]
    depth = w_ckv.shape[0]
    pieces = text_states.reshape(own // CLIPS, CLIPS, ny, depth).transpose(2, 1, 0, 3)
    pieces = lax.all_to_all(
        pieces.reshape(ny, own, depth), "gy", split_axis=0, concat_axis=0, tiled=True
    )
    text_block = lax.all_gather(pieces, "gx", axis=0)
    text_block = (
        text_block.reshape(nx, ny, CLIPS, own // CLIPS, depth)
        .transpose(2, 1, 0, 3, 4)
        .reshape(own * devices, depth)
    )
    text_part = jnp.dot(text_block, w_ckv, preferred_element_type=f32)
    text_sum = lax.psum_scatter(text_part, "gy", scatter_dimension=0, tiled=True).astype(bf16)
    text_all = lax.all_gather(text_sum, row_axes, axis=0)
    slots = own * devices // CLIPS
    text_all = text_all.reshape(ny, nx, -1, w_ckv.shape[1]).transpose(0, 2, 1, 3)
    text_all = text_all.reshape(CLIPS, slots, 2 * D)
    text_pairs = lax.dynamic_index_in_dim(text_all, clip_here, axis=0, keepdims=False)

    win = win_sqkv
    hidden_a, query_a, pair_a = run(
        functools.partial(qkv_kernel, win, nx),
        [
            shape(rows, D, dtype=bf16),
            shape(rows, D, dtype=bf16),
            shape(rows, 2 * D, dtype=bf16),
        ],
        [vmem(), vmem(), hbm()],
        [pltpu.VMEM((nx, D, win.width), bf16), pltpu.SemaphoreType.DMA((nx,))],
        (tokens, mod, full_a),
        4 * rows * D * 3 * D,
        2 * D * 3 * D,
    )
    pairs = [pair_a]
    bit = frame_devs // 2
    while bit:
        pairs = pairs + [swap(p, "gx", bit) for p in pairs]
        bit //= 2
    count = len(pairs)
    keys = count * rows
    out_a, lse_a = run(
        functools.partial(spatial_kernel, count),
        [shape(rows, D, dtype=bf16), shape(HEADS, rows)],
        [vmem() for _ in range(1 + count)],
        [
            pltpu.VMEM((D, rows), f32),
            pltpu.VMEM((D, keys), f32),
            pltpu.VMEM((HEADS, keys, 128), bf16),
            pltpu.VMEM((D, rows), f32),
        ],
        (query_a, *pairs),
        16 * rows * keys * HEADS * 128,
        4 * keys * D,
    )

    branch_a, after_a, hidden_b, query_b, out_b, after_b, hidden_c = run(
        functools.partial(text_kernel, win_rest, win_sout, win_cq, win_cout, nx),
        [
            shape(rows, D),
            shape(rows, D),
            shape(rows, D, dtype=bf16),
            shape(rows, D, dtype=bf16),
            shape(rows, D, dtype=bf16),
            shape(rows, D),
            shape(rows, D, dtype=bf16),
        ],
        [vmem(), vmem(), vmem(), hbm(), vmem(), smem()],
        [
            pltpu.VMEM((nx, D, win_rest.width), bf16),
            pltpu.SemaphoreType.DMA((nx,)),
            pltpu.VMEM((D, rows), f32),
            pltpu.VMEM((D, rows), f32),
            pltpu.VMEM((D, slots), f32),
        ],
        (tokens, out_a, mod, full_a, text_pairs, length_here),
        8 * rows * D * 3 * D,
        2 * D * 4 * D,
    )

    pre_act, activated, branch_c, after_c, hidden_d = run(
        functools.partial(ff_kernel, win_up, nx, ny),
        [
            shape(rows, ff),
            shape(rows, ff, dtype=bf16),
            shape(rows, D),
            shape(rows, D),
            shape(rows, D, dtype=bf16),
        ],
        [vmem(), vmem(), vmem(), hbm(), hbm()],
        [
            pltpu.VMEM((nx, D, win_up.width), bf16),
            pltpu.VMEM((ny, D, ff_width), bf16),
            pltpu.SemaphoreType.DMA((nx,)),
            pltpu.SemaphoreType.DMA((ny,)),
        ],
        (hidden_c, after_b, mod, full_b, full_down),
        8 * rows * D * ff,
        4 * D * ff,
    )

    win = win_tout
    grad_branch_d, grad_out_d = run(
        functools.partial(early_kernel, win, nx),
        [shape(rows, D, dtype=bf16), shape(rows, D, dtype=bf16)],
        [vmem(), vmem(), smem(), hbm()],
        [
            pltpu.VMEM((nx, D, win.width), bf16),
            pltpu.VMEM((rows, win.width), bf16),
            pltpu.SemaphoreType.DMA((nx,)),
        ],
        (grad_out, mod, keep_here, full_b),
        4 * rows * D * D,
        2 * D * D,
    )
    grad_out_moved = reorder(grad_out_d)
    moved_d = reorder(hidden_d)
    win = win_tqkv
    out_moved, grad_qkv_d, grad_hidden_moved = run(
        functools.partial(temporal_kernel, win, nx, frames),
        [
            shape(rows, D, dtype=bf16),
            shape(rows, 3 * D, dtype=bf16),
            shape(rows, D, dtype=bf16),
        ],
        [vmem(), vmem(), hbm(), vmem(), smem()],
        [
            pltpu.VMEM((nx, D, win.width), bf16),
            pltpu.SemaphoreType.DMA((nx,)),
            pltpu.VMEM((rows, win.width), bf16),
        ]
        + [pltpu.VMEM((rows, D), f32)] * 8
        + [pltpu.VMEM((rows, 3 * D), bf16)],
        (moved_d, grad_out_moved, full_b, row_clip, frame_clip),
        16 * rows * D * 3 * D,
        2 * D * 3 * D,
    )
    grad_hidden_d = reorder(grad_hidden_moved)
    out_d = reorder(out_moved)
    win = win_tout
    mixed, d_gate3 = run(
        functools.partial(mixed_kernel, win, nx),
        [shape(rows, D, dtype=bf16), shape(1, D)],
        [vmem(), vmem(), vmem(), vmem(), smem(), hbm()],
        [
            pltpu.VMEM((nx, D, win.width), bf16),
            pltpu.SemaphoreType.DMA((nx,)),
            pltpu.VMEM((rows, D), f32),
        ],
        (out_d, after_c, grad_out, mod, keep_here, full_b),
        4 * rows * D * D,
        2 * D * D,
    )
    late = scatter(
        weight_grads(nx, [(moved_d, [grad_qkv_d]), (out_d, [grad_branch_d])]), col_axes
    )
    d_tqkv, d_tout = late[:, :n_sqkv], late[:, n_sqkv : n_sqkv + n_one]

    grad_branch_c, grad_pre, grad_b, sums_c = run(
        functools.partial(ff_back_kernel, win_up, nx, ny),
        [
            shape(rows, D, dtype=bf16),
            shape(nx, rows, n_up, dtype=bf16),
            shape(rows, D),
            shape(8, D),
        ],
        [vmem()] * 7 + [hbm(), hbm()],
        [
            pltpu.VMEM((nx, D, win_up.width), bf16),
            pltpu.VMEM((ny, D, ff_width), bf16),
            pltpu.SemaphoreType.DMA((nx,)),
            pltpu.SemaphoreType.DMA((ny,)),
            pltpu.VMEM((rows, ff), bf16),
            pltpu.VMEM((rows, win_up.width), bf16),
        ],
        (grad_out, grad_hidden_d, after_c, after_b, pre_act, branch_c, mod, full_b, full_down),
        8 * rows * D * ff,
        4 * D * ff,
    )
    up_terms, down_terms = ff_grads(hidden_c, grad_pre, grad_branch_c, activated)
    d_up = scatter(up_terms, col_axes)[:, :n_up]
    d_down = scatter(down_terms, row_axes).T

    kv_width = w_ckv.shape[1]
    grad_cout_rows, grad_query_b, grad_a, grad_branch_a, grad_out_a, text_terms, d_gate1 = run(
        functools.partial(text_back_kernel, win_rest, win_sout, win_cq, win_cout, nx),
        [
            shape(rows, D, dtype=bf16),
            shape(rows, D, dtype=bf16),
            shape(rows, D),
            shape(rows, D, dtype=bf16),
            shape(rows, D, dtype=bf16),
            shape(nx, slots, kv_width, dtype=bf16),
            shape(1, D),
        ],
        [vmem()] * 4 + [hbm(), vmem(), vmem(), smem()],
        [
            pltpu.VMEM((nx, D, win_rest.width), bf16),
            pltpu.SemaphoreType.DMA((nx,)),
            pltpu.VMEM((rows, max(w.width for w in (win_sout, win_cq, win_cout))), bf16),
            pltpu.VMEM((D, rows), f32),
            pltpu.VMEM((D, rows), f32),
            pltpu.VMEM((D, rows), f32),
            pltpu.VMEM((D, slots), f32),
            pltpu.VMEM((rows, D), bf16),
            pltpu.VMEM((slots, 2 * D), f32),
        ],
        (grad_b, after_a, branch_a, mod, full_a, query_b, text_pairs, length_here),
        8 * rows * D * 3 * D,
        2 * D * 4 * D,
    )
    text_terms = jnp.where(clip_mark[None, :, None, None], text_terms[:, None], 0)
    text_terms = lax.psum_scatter(
        text_terms.reshape(nx, -1, kv_width), "gx", scatter_dimension=0, tiled=True
    )
    text_grad = lax.psum(text_terms[0].astype(f32), "gy").astype(bf16)
    d_ckv = jnp.einsum("rd,re->de", text_block, text_grad, preferred_element_type=f32)

    grad_query_a, grad_pairs = run(
        functools.partial(spatial_back_kernel, count),
        [shape(rows, D, dtype=bf16), shape(count, rows, 2 * D, dtype=bf16)],
        [vmem() for _ in range(4 + count)],
        [pltpu.VMEM((D, rows), f32)] * 3
        + [pltpu.VMEM((D, keys), f32), pltpu.VMEM((D, rows), f32)]
        + [pltpu.VMEM((HEADS, rows, 128), bf16)] * 2
        + [pltpu.VMEM((HEADS, keys, 128), bf16)] * 4,
        (query_a, grad_out_a, out_a, lse_a, *pairs),
        40 * rows * keys * HEADS * 128,
        8 * keys * D,
    )
    bit = 1
    while bit < frame_devs // 2:
        half = grad_pairs.shape[0] // 2
        come = swap(grad_pairs[half:], "gx", bit)
        grad_pairs = (grad_pairs[:half].astype(f32) + come.astype(f32)).astype(bf16)
        bit *= 2
    come = swap(grad_pairs[1], "gx", bit)
    win = win_sqkv
    grad_pair_a, grad_tokens, sums_a = run(
        functools.partial(qkv_back_kernel, win, nx),
        [shape(rows, 2 * D, dtype=bf16), shape(rows, D, dtype=bf16), shape(2, D)],
        [vmem()] * 6 + [hbm()],
        [
            pltpu.VMEM((nx, D, win.width), bf16),
            pltpu.SemaphoreType.DMA((nx,)),
            pltpu.VMEM((rows, win.width), bf16),
        ],
        (grad_query_a, grad_pairs[0], come, tokens, mod, grad_a, full_a),
        4 * rows * D * 3 * D,
        2 * D * 3 * D,
    )
    early = scatter(
        weight_grads(
            nx,
            [
                (hidden_a, [grad_query_a, grad_pair_a]),
                (out_a, [grad_branch_a]),
                (hidden_b, [grad_query_b]),
                (out_b, [grad_cout_rows]),
            ],
        ),
        col_axes,
    )
    d_sqkv = early[:, :n_sqkv]
    d_sout, d_cq, d_cout = [
        early[:, n_sqkv + i * n_one : n_sqkv + (i + 1) * n_one] for i in range(3)
    ]

    grad_mod = jnp.concatenate(
        [sums_a, d_gate1, sums_c[3:5], sums_c[2:3], sums_c[0:2], d_gate3]
    ).reshape(-1)
    grad_mod = jnp.where(clip_mark[:, None], grad_mod[None, :], 0.0)
    grad_mod = lax.psum_scatter(grad_mod, "gx", scatter_dimension=1, tiled=True)
    grad_mod = lax.psum(grad_mod, "gy")
    d_ada = lax.dot_general(
        cond_rows, grad_mod, (((0,), (0,)), ((), ())), precision=highest
    )
    return (
        mixed,
        grad_tokens,
        d_ada,
        d_sqkv,
        d_sout,
        d_cq,
        d_ckv,
        d_cout,
        d_up,
        d_down,
        d_tqkv,
        d_tout,
    )


def solution(mesh):
    rows = P(("gy", "gx"), None)
    both = P("gy", "gx")
    return jax.shard_map(
        local,
        mesh=mesh,
        in_specs=(rows, rows, P(), P(), P(), P(), P()) + (both,) * 10 + (rows,),
        out_specs=(rows, rows) + (both,) * 10,
        check_vma=False,
    )
```

time: 3180 us -> 1430 us (0.45)
  waiting for transfers between devices: 2460 us -> 1010 us
  matrix products: 290 us -> 8.76 us
  Pallas kernels: 0 us -> 232 us
  local copies, waits for them, and re-layouts: 190 us -> 33.9 us
  other arithmetic: 79.6 us -> 17.5 us
  starting transfers between devices: 57.2 us -> 10.4 us
    all_gather x17 -> x5, waiting for transfers between devices: 951 us -> 273 us  [the longest x2 171 us: gather_columns(): whole = lax.all_gather(shard, col_axes, axis=0, tiled=True)]
    unnamed x48 -> x15, waiting for transfers between devices: 703 us -> 348 us
    reduce_scatter x11 -> x4, waiting for transfers between devices: 673 us -> 317 us  [the longest x2 259 us: scatter(): lax.psum_scatter(flat, axes, scatter_dimension=0, tiled=True).astype(f32)]
    dot_general x43 -> x5, matrix products: 263 us -> 8.76 us  [the longest x1 3.64 us: local(): lax.dot_general(cond_rows, grad_mod, (((0,), (0,)), ((), ())), precision=...]
    pallas_call x0 -> x15, Pallas kernels: none -> 232 us  [the longest x11 174 us: run(): pl.pallas_call(kernel, out_shape=outs, in_specs=specs, out_specs=[vmem()...]
    unnamed x242 -> x69, local copies, waits for them, and re-layouts: 101 us -> 17.7 us
    ppermute x12 -> x5, waiting for transfers between devices: 111 us -> 45.7 us  [swap(): lax.ppermute(values, axis, [(i, i ^ mask) for i in range(lax.axis_size(ax...]
    all_gather x4 -> x1, blocking collectives: 76.6 us -> 14.8 us  [local(): mod_all = lax.all_gather(lax.psum(mod_part, 'gy'), 'gx', axis=1, tiled=True)]
  transfers between devices with their start and end apart: 54 -> 20, of which waited for: 39 -> 16; matrix products, arithmetic and copies ran while one was open for 14% -> 3% of each run, Pallas kernels for 0% -> 9%
where the time goes in v1:
time: 1430 us
  waiting for transfers between devices  1010 us (71%)
  Pallas kernels  232 us (16%)
  blocking collectives  93.9 us (7%)
  local copies, waits for them, and re-layouts  33.9 us (2%)
  between operations  19.3 us (1%)
  other arithmetic  17.5 us (1%)
    unnamed x15, waiting for transfers between devices  348 us
    reduce_scatter x2, waiting for transfers between devices, scatter(): lax.psum_scatter(flat, axes, scatter_dimension=0, tiled=True).astype(f32)  259 us
    pallas_call x11, Pallas kernels, run(): pl.pallas_call(kernel, out_shape=outs, in_specs=specs, out_specs=[vmem()...  174 us
    all_gather x2, waiting for transfers between devices, gather_columns(): whole = lax.all_gather(shard, col_axes, axis=0, tiled=True)  171 us
    all_gather x1, waiting for transfers between devices, gather_rows(): whole = lax.all_gather(shard, row_axes, axis=0, tiled=True)  68.3 us
    ppermute x5, waiting for transfers between devices, swap(): lax.ppermute(values, axis, [(i, i ^ mask) for i in range(lax.axis_size(ax...  45.7 us
    pallas_call x2, Pallas kernels, weight_grads(): pl.pallas_call(functools.partial(weight_kernel, nx, lanes, [len(r) for _,...  41.1 us
    reduce_scatter x1, waiting for transfers between devices, local(): lax.psum_scatter(text_terms.reshape(nx, -1, kv_width), 'gx', scatter_dime...  37.3 us
  transfers between devices with their start and end apart: 20, of which 16 were waited for; matrix products, arithmetic and copies ran while one was open for 3% of the time, Pallas kernels for 9%

profile of v1, /device:TPU:0, one launch (start us, length us, event | category | flops | bytes accessed | tf_op | source)
XLA Modules:
  0.0 1428.7 jit_solution(18074139276006645476)
XLA Ops:
  8.1 1.0 reshape.145
  9.2 10.1 all_to_all.25
  19.4 21.9 %all-gather.15.cloned.1.call-done = bf16[32,16,1024]{2,1,0:T(8,128)(2,1)} async-done(((bf16[4,16,1024]{2,1,0:T(8,128)(2,1)}), bf16[32,16,1024]{2,1,0:T(8,128)(2,1)}) %all-gather.15.cloned.1.call-update) | async-done | bytes 1048592 | tf_op jit(solution)/shard_map/all_gather | solution.py:728
  41.3 1.5 reshape.147
  43.9 1.3 fusion.17
  46.6 2.0 fusion.6
  48.7 21.4 %reduce-scatter.14.cloned.1.call-done = f32[128,288]{0,1:T(8,128)} async-done(((f32[512,288]{0,1:T(8,128)}), f32[128,288]{0,1:T(8,128)}) %reduce-scatter.14.cloned.1.call-update) | async-done | bytes 147472 | tf_op jit(solution)/shard_map/reduce_scatter | solution.py:735
  70.1 1.6 convert_element_type.60
  71.8 1.2 concatenate.14
  74.8 1.3 fusion.13
  76.0 16.1 %psum.21 = f32[4,1296]{1,0:T(4,128)S(1)} all-reduce(f32[4,1296]{1,0:T(4,128)S(1)} %fusion.13), channel_id=1, replica_groups=mesh['gy'=4,'gx'=8] {'gy'}, use_global_device_ids=true, to_apply=%region_2.3 | all-reduce | flops 5184 | bytes 41472 | tf_op jit(solution)/shard_map/psum | solution.py:719
  92.1 14.8 %all-gather.2 = f32[8,1296,4]{1,2,0:T(4,128)S(1)} all-gather(f32[1,1296,4]{1,2,0:T(4,128)S(1)} %bitcast.107), channel_id=1, replica_groups=mesh['gy'=4,'gx'=8] {'gx'}, dimensions={0}, use_global_device_ids=true | all-gather | bytes 186624 | tf_op jit(solution)/shard_map/all_gather | solution.py:719
  109.5 55.0 %all-gather.9.cloned.1.call-done = bf16[9216,896]{1,0:T(8,128)(2,1)} async-done(((bf16[288,896]{1,0:T(8,128)(2,1)}), bf16[9216,896]{1,0:T(8,128)(2,1)}) %all-gather.9.cloned.1.call-update) | async-done | bytes 16515088 | tf_op jit(solution)/shard_map/all_gather | solution.py:617
  164.5 8.0 shard_map.265
  173.2 32.6 %collective-permute-done.refs_2_.refs_5_ = bf16[256,2304]{1,0:T(8,128)(2,1)S(1)} collective-permute-done((bf16[256,2304]{1,0:T(8,128)(2,1)}, bf16[256,2304]{1,0:T(8,128)(2,1)S(1)}, u32[]{:S(2)}, u32[]{:S(2)}) %collective-permute-start) | collective-permute-done | bytes 1179680 | tf_op jit(solution)/shard_map/ppermute | solution.py:633
  207.2 1.3 select_reduce_fusion
  209.8 1.3 select_reduce_fusion.1
  211.2 12.5 all-gather.17.cloned.1.call-done
  223.7 2.2 copy.89
  226.8 1.1 copy.76
  227.9 18.0 %shard_map.266 = (bf16[256,1152]{1,0:T(8,128)(2,1)}, f32[16,256]{1,0:T(8,128)}) custom-call(bf16[256,1152]{1,0:T(8,128)(2,1)} %get-tuple-element.52.refs_0_, bf16[256,2304]{1,0:T(8,128)(2,1)} %get-tuple-element.53.refs_1_.refs_4_, bf16[256,2304]{1,0:T(8,128)(2,1)} %copy-done.23, bf16[256,2304]{1,0:T(8,128)(2,1)} %collective-permute-done.1.refs_3_.refs_6_, ...), custom_call_target="tpu_custom_call" | custom-call | flops 8589934592 | bytes 4718592 | tf_op jit(solution)/shard_map/pallas_call | solution.py:46
  245.9 115.7 %all-gather.11.cloned.1.call-done = bf16[9216,1152]{1,0:T(8,128)(2,1)} async-done(((bf16[288,1152]{1,0:T(8,128)(2,1)}), bf16[9216,1152]{1,0:T(8,128)(2,1)}) %all-gather.11.cloned.1.call-update) | async-done | bytes 21233680 | tf_op jit(solution)/shard_map/all_gather | solution.py:617
  361.6 5.8 shard_map.269
  367.4 3.0 all-to-all-start.2
  370.4 17.3 %shard_map.267 = (f32[256,1152]{1,0:T(8,128)}, f32[256,1152]{1,0:T(8,128)}, bf16[256,1152]{1,0:T(8,128)(2,1)}, bf16[256,1152]{1,0:T(8,128)(2,1)}, bf16[256,1152]...) custom-call(bf16[256,1152]{1,0:T(8,128)(2,1)} %x_ref.5, ...), custom_call_target="tpu_custom_call" | custom-call | flops 8153726976 | bytes 10616832 | tf_op jit(solution)/shard_map/pallas_call | solution.py:46
  387.7 68.3 %all-gather.13.cloned.1.call-done = bf16[4608,1152]{1,0:T(8,128)(2,1)} async-done(((bf16[144,1152]{1,0:T(8,128)(2,1)}), bf16[4608,1152]{1,0:T(8,128)(2,1)}) %all-gather.13.cloned.1.call-update) | async-done | bytes 10616848 | tf_op jit(solution)/shard_map/all_gather | solution.py:623
  456.0 17.1 %shard_map.268 = (f32[256,4608]{1,0:T(8,128)}, bf16[256,4608]{1,0:T(8,128)(2,1)}, f32[256,1152]{1,0:T(8,128)}, f32[256,1152]{1,0:T(8,128)}, bf16[256,1152]{1,0:T(8,128)(2,1)}) custom-call(bf16[256,1152]{1,0:T(8,128)(2,1)} %get-tuple-element.55.h_ref, f32[256,1152]{1,0:T(8,128)} %get-tuple-element.56.x2_ref, f32[9,1152]{1,0:T(8,128)} %reshape.143.mod_ref, ...), custom_call_target="tpu_custom_call" | custom-call | flops 10871635968 | bytes 21233664 | tf_op jit(solution)/shard_map/pallas_call | solution.py:46
  473.2 3.2 all-to-all-start.1
  477.3 16.8 %all-to-all-done.1 = bf16[32,8,1152]{2,1,0:T(8,128)(2,1)S(1)} async-done(((bf16[32,8,1152]{2,1,0:T(8,128)(2,1)}), bf16[32,8,1152]{2,1,0:T(8,128)(2,1)S(1)}, u32[]{:S(2)}, u32[]{:S(2)}) %all-to-all-start.1) | async-done | bytes 589856 | tf_op jit(solution)/shard_map/all_to_all | solution.py:638
  495.0 22.7 %shard_map.270 = (bf16[256,1152]{1,0:T(8,128)(2,1)}, bf16[256,3456]{1,0:T(8,128)(2,1)}, bf16[256,1152]{1,0:T(8,128)(2,1)}) custom-call(bf16[256,1152]{1,0:T(8,128)(2,1)} %bitcast.96, bf16[256,1152]{1,0:T(8,128)(2,1)} %bitcast.101, bf16[8,1152,1152]{2,1,0:T(8,128)(2,1)} %bitcast.74, f32[256,1]{1,0:T(8,128)} %broadcast_in_dim_reshape.5.row_clip, f32[8]{0:T(128)} %copy-done.22), custom_call_target="tpu_custom_call" | custom-call | flops 16307453952 | bytes 7962624 | tf_op jit(solution)/shard_map/pallas_call | solution.py:46
  517.6 21.1 %all_to_all.26 = bf16[32,8,1152]{2,1,0:T(8,128)(2,1)} all-to-all(bf16[32,8,1152]{2,1,0:T(8,128)(2,1)} %bitcast.104), channel_id=1, replica_groups=mesh['gy'=4,'gx'=8] {'gy','gx'}, dimensions={0} | all-to-all | bytes 1179648 | tf_op jit(solution)/shard_map/all_to_all | solution.py:638
  538.7 20.0 %shard_map.272 = (bf16[256,1152]{1,0:T(8,128)(2,1)}, bf16[8,256,576]{2,1,0:T(8,128)(2,1)}, f32[256,1152]{1,0:T(8,128)}, f32[8,1152]{1,0:T(8,128)}) custom-call(bf16[256,1152]{1,0:T(8,128)(2,1)} %g_ref.5, bf16[256,1152]{1,0:T(8,128)(2,1)} %bitcast.94, f32[256,1152]{1,0:T(8,128)} %get-tuple-element.60.x3_ref, f32[256,1152]{1,0:T(8,128)} %get-tuple-element.56.x2_ref, ...), custom_call_target="tpu_custom_call" | custom-call | flops 10871635968 | bytes 21233664 | tf_op jit(solution)/shard_map/pallas_call | solution.py:46
  558.7 18.6 %shard_map.273 = (bf16[256,1152]{1,0:T(8,128)(2,1)}, bf16[256,1152]{1,0:T(8,128)(2,1)}, f32[256,1152]{1,0:T(8,128)}, bf16[256,1152]{1,0:T(8,128)(2,1)}, bf16[256...) custom-call(f32[256,1152]{1,0:T(8,128)} %get-tuple-element.65.dx2_ref, ...), custom_call_target="tpu_custom_call" | custom-call | flops 8153726976 | bytes 10616832 | tf_op jit(solution)/shard_map/pallas_call | solution.py:46
  577.4 28.3 %shard_map.274 = (bf16[256,1152]{1,0:T(8,128)(2,1)}, bf16[4,256,2304]{2,1,0:T(8,128)(2,1)}) custom-call(bf16[256,1152]{1,0:T(8,128)(2,1)} %get-tuple-element.52.refs_0_, bf16[256,1152]{1,0:T(8,128)(2,1)} %get-tuple-element.69.refs_1_, bf16[256,1152]{1,0:T(8,128)(2,1)} %get-tuple-element.54.o_ref.refs_2_.refs_3_, f32[16,256]{1,0:T(8,128)} %get-tuple-element.70.refs_3_, ...), custom_call_target="tpu_custom_call" | custom-call | flops 21474836480 | bytes 9437184 | tf_op jit(solution)/shard_map/pallas_call | solution.py:46
  605.7 3.2 slice.46
  608.9 2.6 all-to-all-start.3
  611.7 1.9 collective-permute-done.3
  613.6 2.4 add_convert_fusion
  616.0 1.2 slice_bitcast_fusion
  617.9 11.4 all-to-all-done.3
  630.1 8.1 shard_map.271
  638.2 11.2 collective-permute-done.4.come_ref
  650.4 9.6 shard_map.275
  660.9 3.4 copy.83
  665.5 2.1 bitcast_select_fusion
  667.7 7.9 shard_map.278
  675.6 14.9 %shard_map.279 = bf16[8,1152,640]{2,1,0:T(8,128)(2,1)} custom-call(bf16[256,1152]{1,0:T(8,128)(2,1)} %bitcast.97, bf16[256,3456]{1,0:T(8,128)(2,1)} %get-tuple-element.90.refs_1_, bf16[256,1152]{1,0:T(8,128)(2,1)} %bitcast.92, bf16[256,1152]{1,0:T(8,128)(2,1)} %get-tuple-element.91.refs_3_), custom_call_target="tpu_custom_call" | custom-call | flops 6039797760 | bytes 11796480 | tf_op jit(solution)/shard_map/pallas_call | solution.py:551
  690.8 9.9 shard_map.277
  700.8 26.2 %shard_map.276 = bf16[8,1152,896]{2,1,0:T(8,128)(2,1)} custom-call(bf16[256,1152]{1,0:T(8,128)(2,1)} %get-tuple-element.79.refs_0_, bf16[256,1152]{1,0:T(8,128)(2,1)} %get-tuple-element.71.dq_ref.refs_1_, bf16[256,2304]{1,0:T(8,128)(2,1)} %get-tuple-element.80.refs_2_, bf16[256,1152]{1,0:T(8,128)(2,1)} %get-tuple-element.54.o_ref.refs_2_.refs_3_, ...), custom_call_target="tpu_custom_call" | custom-call | flops 8455716864 | bytes 16515072 | tf_op jit(solution)/shard_map/pallas_call | solution.py:551
  727.1 1.4 copy.84
  728.5 37.3 %reduce-scatter.16.cloned.1.call-done = bf16[1,512,288]{2,1,0:T(8,128)(2,1)} async-done(((bf16[8,512,288]{2,1,0:T(8,128)(2,1)}), bf16[1,512,288]{2,1,0:T(8,128)(2,1)}) %reduce-scatter.16.cloned.1.call-update) | async-done | bytes 294928 | tf_op jit(solution)/shard_map/reduce_scatter | solution.py:934
  765.8 1.0 bitcast_convert_fusion
  766.9 31.8 %all-reduce.3 = (f32[4,1296]{1,0:T(4,128)S(1)}, bf16[512,288]{1,0:T(8,128)(2,1)S(1)}) all-reduce(f32[4,1296]{1,0:T(4,128)S(1)} %copy.84, f32[512,288]{1,0:T(8,128)S(1)} %bitcast_convert_fusion), channel_id=1, replica_groups=mesh['gy'=4,'gx'=8] {'gy'}, use_global_device_ids=true, to_apply=%region_8.9 | all-reduce | flops 152640 | bytes 926208 | tf_op jit(solution)/shard_map/psum | solution.py:995
  798.7 3.6 fusion.14
  802.3 1.5 convolution_bitcast_fusion
  803.8 110.0 %reduce-scatter.20.cloned.1.call-done = bf16[144,1152]{1,0:T(8,128)(2,1)} async-done(((bf16[4608,1152]{1,0:T(8,128)(2,1)}), bf16[144,1152]{1,0:T(8,128)(2,1)}) %reduce-scatter.20.cloned.1.call-update) | async-done | bytes 331792 | tf_op jit(solution)/shard_map/reduce_scatter | solution.py:629
  913.8 1.9 convert_bitcast_fusion
  915.6 151.8 %reduce-scatter.26.cloned.1.call-done = bf16[288,640]{1,0:T(8,128)(2,1)} async-done(((bf16[9216,640]{1,0:T(8,128)(2,1)}), bf16[288,640]{1,0:T(8,128)(2,1)}) %reduce-scatter.26.cloned.1.call-update) | async-done | bytes 368656
  1070.5 1.1 copy.82
  1071.6 148.9 %reduce-scatter.18.cloned.1.call-done = bf16[288,640]{1,0:T(8,128)(2,1)} async-done(((bf16[9216,640]{1,0:T(8,128)(2,1)}), bf16[288,640]{1,0:T(8,128)(2,1)}) %reduce-scatter.18.cloned.1.call-update) | async-done | bytes 368656 | tf_op jit(solution)/shard_map/reduce_scatter | solution.py:629
  1220.5 2.0 slice_convert_fusion
  1222.4 195.1 %reduce-scatter.24.cloned.1.call-done = bf16[288,896]{1,0:T(8,128)(2,1)} async-done(((bf16[9216,896]{1,0:T(8,128)(2,1)}), bf16[288,896]{1,0:T(8,128)(2,1)}) %reduce-scatter.24.cloned.1.call-update) | async-done | bytes 516112
  1417.5 1.4 copy.86
  1419.8 1.1 copy.81
  (125 shorter events, 19.7 us)
Async XLA Ops:
  8.0 66.8 %copy-start = (bf16[288,1296]{1,0:T(8,128)(2,1)S(1)}, bf16[288,1296]{1,0:T(8,128)(2,1)}, u32[]{:S(2)}) copy-start(bf16[288,1296]{1,0:T(8,128)(2,1)} %param.25) | copy-start | bytes 2239492
  8.0 33.3 %all-gather.15.cloned.1.call-start = ((), (), s32[]{:S(2)}) async-start(), calls=%async_computation.19 | async-start | bytes 1179648 | tf_op jit(solution)/shard_map/all_gather | solution.py:728
  19.3 50.7 %reduce-scatter.14.cloned.1.call-start = ((), (), s32[]{:S(2)}) async-start(), calls=%async_computation.13 | async-start | bytes 737280 | tf_op jit(solution)/shard_map/reduce_scatter | solution.py:735
  42.8 1.1 copy-start.9
  43.9 4.7 copy-start.2
  43.9 1.4 copy-start.12
  43.9 1.5 copy-start.13
  45.2 26.5 %copy-start.14 = (bf16[288,144]{0,1:T(8,128)(2,1)S(1)}, bf16[288,144]{0,1:T(8,128)(2,1)}, u32[]{:S(2)}) copy-start(bf16[288,144]{0,1:T(8,128)(2,1)} %param.34) | copy-start | bytes 248836
  45.2 26.6 %copy-start.10 = (bf16[288,576]{1,0:T(8,128)(2,1)S(1)}, bf16[288,576]{1,0:T(8,128)(2,1)}, u32[]{:S(2)}) copy-start(bf16[288,576]{1,0:T(8,128)(2,1)} %param.31) | copy-start | bytes 995332
  45.2 26.7 %copy-start.11 = (bf16[288,432]{1,0:T(8,128)(2,1)S(1)}, bf16[288,432]{1,0:T(8,128)(2,1)}, u32[]{:S(2)}) copy-start(bf16[288,432]{1,0:T(8,128)(2,1)} %param.33) | copy-start | bytes 746500
  45.2 119.3 %all-gather.9.cloned.1.call-start = ((), (), s32[]{:S(2)}) async-start(), calls=%async_computation.12 | async-start | bytes 17031168 | tf_op jit(solution)/shard_map/all_gather | solution.py:617
  46.5 27.2 %copy-start.24 = (s32[4]{0:T(128)S(1)}, s32[4]{0:T(128)}, u32[]{:S(2)}) copy-start(s32[4]{0:T(128)} %param.22) | copy-start | bytes 52
  46.6 27.4 %copy-start.25 = (s32[4]{0:T(128)S(1)}, s32[4]{0:T(128)}, u32[]{:S(2)}) copy-start(s32[4]{0:T(128)} %param.21) | copy-start | bytes 52
  48.6 175.1 %all-gather.17.cloned.1.call-start = ((), (), s32[]{:S(2)}) async-start(), calls=%async_computation.20 | async-start | bytes 2433024 | tf_op jit(solution)/shard_map/all_gather | solution.py:736
  71.6 289.9 %all-gather.11.cloned.1.call-start = ((), (), s32[]{:S(2)}) async-start(), calls=%async_computation.14 | async-start | bytes 21897216 | tf_op jit(solution)/shard_map/all_gather | solution.py:617
  73.0 383.0 %all-gather.13.cloned.1.call-start = ((), (), s32[]{:S(2)}) async-start(), calls=%async_computation.15 | async-start | bytes 10948608 | tf_op jit(solution)/shard_map/all_gather | solution.py:623
  74.2 0.6 copy-start.15
  74.2 0.6 copy-start.17
  164.5 42.6 %copy-start.26 = (s32[4]{0:T(128)S(1)}, s32[4]{0:T(128)}, u32[]{:S(2)}) copy-start(s32[4]{0:T(128)} %param.23) | copy-start | bytes 52
  164.5 45.3 %copy-start.27 = (s32[4]{0:T(128)S(1)}, s32[4]{0:T(128)}, u32[]{:S(2)}) copy-start(s32[4]{0:T(128)} %param.24) | copy-start | bytes 52
  172.6 33.2 %collective-permute-start = (bf16[256,2304]{1,0:T(8,128)(2,1)}, bf16[256,2304]{1,0:T(8,128)(2,1)S(1)}, u32[]{:S(2)}, u32[]{:S(2)}) collective-permute-start(bf16[256,2304]{1,0:T(8,128)(2,1)} %get-tuple-element.53.refs_1_.refs_4_), channel_id=1, source_target_pairs={{0,2},{1,3},{2,0},{3,1},{4,6},{5,7},{6,4},{7,5},{8,10},{9,11},{10,... | collective-permute-start | bytes 3538952 | tf_op jit(solution)/shard_map/ppermute | solution.py:633
  173.2 54.7 %collective-permute-start.1 = (bf16[256,2304]{1,0:T(8,128)(2,1)}, bf16[256,2304]{1,0:T(8,128)(2,1)}, u32[]{:S(2)}, u32[]{:S(2)}) collective-permute-start(bf16[256,2304]{1,0:T(8,128)(2,1)} %get-tuple-element.53.refs_1_.refs_4_), channel_id=1, source_target_pairs={{0,1},{1,0},{2,3},{3,2},{4,5},{5,4},{6,7},{7,6},{8,9},{9,8},{10,11... | collective-permute-start | bytes 3538952 | tf_op jit(solution)/shard_map/ppermute | solution.py:633
  205.8 20.1 %copy-start.23 = (bf16[256,2304]{1,0:T(8,128)(2,1)}, bf16[256,2304]{1,0:T(8,128)(2,1)S(1)}, u32[]{:S(2)}) copy-start(bf16[256,2304]{1,0:T(8,128)(2,1)S(1)} %collective-permute-done.refs_2_.refs_5_) | copy-start | bytes 3538948
  205.8 22.1 %collective-permute-start.2 = (bf16[256,2304]{1,0:T(8,128)(2,1)S(1)}, bf16[256,2304]{1,0:T(8,128)(2,1)}, u32[]{:S(2)}, u32[]{:S(2)}) collective-permute-start(bf16[256,2304]{1,0:T(8,128)(2,1)S(1)} %collective-permute-done.refs_2_.refs_5_), channel_id=1, source_target_pairs={{0,1},{1,0},{2,3},{3,2},{4,5},{5,4},{6,7},{7,6},{8,9},{9,8},{10,11... | collective-permute-start | bytes 3538952 | tf_op jit(solution)/shard_map/ppermute | solution.py:633
  367.4 105.8 %all-to-all-start.2 = ((bf16[32,8,1152]{2,1,0:T(8,128)(2,1)}), bf16[32,8,1152]{2,1,0:T(8,128)(2,1)S(1)}, u32[]{:S(2)}, u32[]{:S(2)}) async-start(bf16[32,8,1152]{2,1,0:T(8,128)(2,1)} %bitcast.102), calls=%async_computation.3 | async-start | bytes 1179648 | tf_op jit(solution)/shard_map/all_to_all | solution.py:638
  473.1 21.0 %copy-start.8 = (bf16[32,8,1152]{2,1,0:T(8,128)(2,1)}, bf16[32,8,1152]{2,1,0:T(8,128)(2,1)S(1)}, u32[]{:S(2)}) copy-start(bf16[32,8,1152]{2,1,0:T(8,128)(2,1)S(1)} %all-to-all-done.2) | copy-start | bytes 1769476
  473.2 21.0 %all-to-all-start.1 = ((bf16[32,8,1152]{2,1,0:T(8,128)(2,1)}), bf16[32,8,1152]{2,1,0:T(8,128)(2,1)S(1)}, u32[]{:S(2)}, u32[]{:S(2)}) async-start(bf16[32,8,1152]{2,1,0:T(8,128)(2,1)} %bitcast.103), calls=%async_computation.2 | async-start | bytes 1179648 | tf_op jit(solution)/shard_map/all_to_all | solution.py:638
  476.5 17.7 %copy-start.22 = (f32[8]{0:T(128)}, f32[8]{0:T(128)S(1)}, u32[]{:S(2)}) copy-start(f32[8]{0:T(128)S(1)} %convert_element_type.63.frame_clip) | copy-start | bytes 100
  494.1 0.8 copy-start.7
  608.9 4.7 collective-permute-start.3
  608.9 20.4 %all-to-all-start.3 = ((bf16[32,8,1152]{2,1,0:T(8,128)(2,1)}), bf16[32,8,1152]{2,1,0:T(8,128)(2,1)S(1)}, u32[]{:S(2)}, u32[]{:S(2)}) async-start(bf16[32,8,1152]{2,1,0:T(8,128)(2,1)} %bitcast.100), calls=%async_computation.4 | async-start | bytes 1179648 | tf_op jit(solution)/shard_map/all_to_all | solution.py:638
  611.5 115.6 %reduce-scatter.22.cloned.1.call-start = ((), (), s32[]{:S(2)}) async-start(), calls=%async_computation.21 | async-start | bytes 5971968
  616.0 1.9 copy-start.19
  617.1 32.3 %collective-permute-start.4 = (bf16[256,2304]{1,0:T(8,128)(2,1)S(1)}, bf16[256,2304]{1,0:T(8,128)(2,1)S(1)}, u32[]{:S(2)}, u32[]{:S(2)}) collective-permute-start(bf16[256,2304]{1,0:T(8,128)(2,1)S(1)} %get-tuple-element.142), channel_id=1, source_target_pairs={{0,2},{1,3},{2,0},{3,1},{4,6},{5,7},{6,4},{7,5},{8,10},{9,11},{10,... | collective-permute-start | bytes 3538952 | tf_op jit(solution)/shard_map/ppermute | solution.py:633
  629.2 0.8 copy-start.4
  649.4 1.0 copy-start.5
  650.4 9.6 copy-start.20
  650.4 9.6 copy-start.21
  664.3 1.1 copy-start.6
  664.4 101.5 %reduce-scatter.16.cloned.1.call-start = ((), (), s32[]{:S(2)}) async-start(), calls=%async_computation.16 | async-start | bytes 3538944 | tf_op jit(solution)/shard_map/reduce_scatter | solution.py:934
  667.6 246.2 %reduce-scatter.20.cloned.1.call-start = ((), (), s32[]{:S(2)}) async-start(), calls=%async_computation.18 | async-start | bytes 10948608 | tf_op jit(solution)/shard_map/reduce_scatter | solution.py:629
  675.5 391.9 %reduce-scatter.26.cloned.1.call-start = ((), (), s32[]{:S(2)}) async-start(), calls=%async_computation.23 | async-start | bytes 12165120
  690.5 529.9 %reduce-scatter.18.cloned.1.call-start = ((), (), s32[]{:S(2)}) async-start(), calls=%async_computation.17 | async-start | bytes 12165120 | tf_op jit(solution)/shard_map/reduce_scatter | solution.py:629
  700.8 716.8 %reduce-scatter.24.cloned.1.call-start = ((), (), s32[]{:S(2)}) async-start(), calls=%async_computation.22 | async-start | bytes 17031168
  727.1 71.6 %copy-start.16 = (f32[4,576]{1,0:T(4,128)S(1)}, f32[4,576]{1,0:T(4,128)}, u32[]{:S(2)}) copy-start(f32[4,576]{1,0:T(4,128)} %copy-done.15) | copy-start | bytes 27652
  727.1 71.6 %copy-start.18 = (f32[4,576]{1,0:T(4,128)S(1)}, f32[4,576]{1,0:T(4,128)}, u32[]{:S(2)}) copy-start(f32[4,576]{1,0:T(4,128)} %copy-done.17) | copy-start | bytes 27652
  727.1 75.2 %copy-start.3 = (bf16[512,1024]{1,0:T(8,128)(2,1)S(1)}, bf16[512,1024]{1,0:T(8,128)(2,1)}, u32[]{:S(2)}) copy-start(bf16[512,1024]{1,0:T(8,128)(2,1)} %copy-done.2) | copy-start | bytes 3145732
  1220.5 200.4 %copy-start.1 = (bf16[288,1296]{1,0:T(8,128)(2,1)S(1)}, bf16[288,1296]{1,0:T(8,128)(2,1)}, u32[]{:S(2)}) copy-start(bf16[288,1296]{1,0:T(8,128)(2,1)} %param.25) | copy-start | bytes 2239492
Sparse Core Ops, SparseCore 0:
  19.5 21.8 all-gather.14
  45.3 24.6 reduce-scatter.13
  664.5 60.2 reduce-scatter.21
  727.0 38.7 reduce-scatter.15
  772.8 140.9 reduce-scatter.19
  920.8 146.5 reduce-scatter.25
  1073.5 146.9 reduce-scatter.17
  1227.9 189.5 reduce-scatter.23
Sparse Core Ops, SparseCore 1:
  49.2 115.3 all-gather.8
  168.3 55.3 all-gather.16
  227.4 134.1 all-gather.10
  365.1 90.9 all-gather.12

commit v2 on v1

--- a/solution.py
+++ b/solution.py
@@ -22,7 +22,6 @@
 score_scale = HEAD_DIM ** (-0.5)
 log2_scale = score_scale * math.log2(math.e)
 row_axes = ("gy", "gx")
-col_axes = ("gx", "gy")
 nt = (((1,), (1,)), ((), ()))
 
 
@@ -42,16 +41,28 @@
     return jax.ShapeDtypeStruct(size, dtype)
 
 
-def run(kernel, outs, specs, scratch, args, flops, moved):
+def cost(micros):
+    return pl.CostEstimate(flops=micros * 20000000, bytes_accessed=0, transcendentals=0)
+
+
+def run(kernel, outs, specs, scratch, args, micros):
+    flat, tree = jax.tree.flatten(tuple(args))
+    flat_specs = []
+    for arg, spec in zip(args, specs):
+        flat_specs += [spec] * len(jax.tree.leaves(arg))
+
+    def grouped(*refs):
+        kernel(*jax.tree.unflatten(tree, refs[: len(flat)]), *refs[len(flat) :])
+
     return pl.pallas_call(
-        kernel,
+        grouped,
         out_shape=outs,
-        in_specs=specs,
+        in_specs=flat_specs,
         out_specs=[vmem() for _ in outs],
         scratch_shapes=scratch,
         compiler_params=pltpu.CompilerParams(vmem_limit_bytes=56 << 20),
-        cost_estimate=pl.CostEstimate(flops=flops, bytes_accessed=moved, transcendentals=0),
-    )(*args)
+        cost_estimate=cost(micros),
+    )(*flat)
 
 
 class Window:
@@ -71,13 +82,74 @@
     return -(-lanes // 128) * 128
 
 
-def block_copies(source, window, buffer, sems, count):
-    return [
-        pltpu.make_async_copy(
-            source.at[i, :, window.start : window.stop], buffer.at[i], sems.at[i]
-        )
-        for i in range(count)
-    ]
+def piece_places(nx):
+    half = nx // 4
+    for core in range(2):
+        for k, (first, last, low) in enumerate(((1, 0, 0), (1, 2, 0), (2, 0, half), (2, 1, half))):
+            for i in range(2):
+                for j in range(half):
+                    yield core * 4 + k, i, j, (2 * (low + j)) ^ core, (first * i) ^ last
+
+
+class Pieces:
+    def __init__(self, sources, me, window, buffer, sems, nx):
+        rows = sources[0].shape[2]
+        columns = slice(window.start, window.stop)
+        for k, i, j, far_x, far_y in piece_places(nx):
+            x, y = me[0] ^ far_x, me[1] ^ far_y
+            pltpu.make_async_copy(
+                sources[k].at[i, j, :, columns],
+                buffer.at[x, pl.ds(pl.multiple_of(y * rows, 16), rows), :],
+                sems.at[x],
+            ).start()
+        self.buffer, self.sems = buffer, sems
+
+    def wait(self, x):
+        pltpu.make_async_copy(self.buffer.at[x], self.buffer.at[x], self.sems.at[x]).wait()
+
+
+class Blocks:
+    def __init__(self, source, buffer, sems):
+        self.copies = [
+            pltpu.make_async_copy(source.at[i], buffer.at[i], sems.at[i])
+            for i in range(source.shape[0])
+        ]
+        for copy in self.copies:
+            copy.start()
+
+    def wait(self, i):
+        self.copies[i].wait()
+
+
+class Folded:
+    def __init__(self, sources, me, start, buffer, sems, nx):
+        rows = sources[0].shape[2] // 2
+        width = buffer.shape[2]
+        fold = fold_width(width)
+        for k, i, j, far_x, far_y in piece_places(nx):
+            x, y = me[0] ^ far_x, me[1] ^ far_y
+            place = pl.ds(pl.multiple_of(x * rows, 16), rows)
+            for top, columns in ((0, slice(0, fold)), (rows, slice(fold, width))):
+                lanes = slice(start, start + columns.stop - columns.start)
+                pltpu.make_async_copy(
+                    sources[k].at[i, j, top : top + rows, lanes],
+                    buffer.at[y, place, columns],
+                    sems.at[y],
+                ).start()
+        self.buffer, self.sems = buffer, sems
+
+    def wait(self, y):
+        pltpu.make_async_copy(self.buffer.at[y], self.buffer.at[y], self.sems.at[y]).wait()
+
+
+def fold_width(width):
+    return padded(width // 2)
+
+
+def down_blocks(up_refs, down_ref, me_ref, start, buf, sems, nx):
+    if down_ref is None:
+        return Folded(up_refs, me_ref, start, buf, sems, nx)
+    return Blocks(down_ref, buf, sems)
 
 
 def stats(values):
@@ -132,15 +204,13 @@
     return jnp.tanh(c * u * (1.0 + 0.044715 * square)), square, c
 
 
-def qkv_kernel(win, nx, x_ref, mod_ref, w_ref, h_ref, q_ref, kv_ref, buf, sems):
-    copies = block_copies(w_ref, win, buf, sems, nx)
-    for copy in copies:
-        copy.start()
+def qkv_kernel(win, nx, me_ref, x_ref, mod_ref, w_refs, h_ref, q_ref, kv_ref, buf, sems):
+    pieces = Pieces(w_refs, me_ref, win, buf, sems, nx)
     normed, _ = stats(x_ref[...].astype(f32))
     hidden = (normed * (1.0 + mod_ref[1:2, :]) + mod_ref[0:1, :]).astype(bf16)
     h_ref[...] = hidden
     for x in range(nx):
-        copies[x].wait()
+        pieces.wait(x)
         block = mm(hidden, buf[x])[:, win.off : win.off + win.n]
         put([q_ref, kv_ref], x * win.n, block)
 
@@ -186,18 +256,16 @@
 
 
 def text_kernel(
-    outer, w_out, w_cq, w_cout, nx, x_ref, o_ref, mod_ref, w_ref, text_ref, length_ref,
+    outer, w_out, w_cq, w_cout, nx, me_ref, x_ref, o_ref, mod_ref, w_refs, text_ref, length_ref,
     a1_ref, x1_ref, hc_ref, qc_ref, oc_ref, x2_ref, h3_ref,
     buf, sems, acc, q_t, v_t,
 ):
-    copies = block_copies(w_ref, outer, buf, sems, nx)
-    for copy in copies:
-        copy.start()
+    pieces = Pieces(w_refs, me_ref, outer, buf, sems, nx)
 
     def product(left, win, dest, wait=False):
         for x in range(nx):
             if wait:
-                copies[x].wait()
+                pieces.wait(x)
             block = mm(left, buf[x, :, win.start : win.stop])[:, win.off : win.off + win.n]
             put([dest], x * win.n, block)
 
@@ -223,23 +291,21 @@
 
 
 def ff_kernel(
-    win, nx, ny, h_ref, x2_ref, mod_ref, up_ref, down_ref,
+    win, nx, ny, me_ref, h_ref, x2_ref, mod_ref, up_refs, down_ref,
     u_ref, g_ref, m_ref, x3_ref, h4_ref, up_buf, down_buf, up_sems, down_sems,
 ):
-    ups = block_copies(up_ref, win, up_buf, up_sems, nx)
-    width = down_ref.shape[2]
-    downs = block_copies(down_ref, Window(0, width), down_buf, down_sems, ny)
-    for copy in ups + downs:
-        copy.start()
+    ups = Pieces(up_refs, me_ref, win, up_buf, up_sems, nx)
+    width = down_buf.shape[2]
+    downs = down_blocks(up_refs, down_ref, me_ref, win.stop, down_buf, down_sems, nx)
     hidden = h_ref[...]
     for x in range(nx):
-        ups[x].wait()
+        ups.wait(x)
         u = mm(hidden, up_buf[x])[:, win.off : win.off + win.n]
         put([u_ref], x * win.n, u)
         put([g_ref], x * win.n, 0.5 * u * (1.0 + gelu_parts(u)[0]))
     total = jnp.zeros(m_ref.shape, f32)
     for i in range(ny):
-        downs[i].wait()
+        downs.wait(i)
         total = total + mm_nt(g_ref[:, i * width : (i + 1) * width], down_buf[i])
     m_ref[...] = total
     after_c = x2_ref[...] + mod_ref[5:6, :] * total
@@ -249,38 +315,27 @@
     ).astype(bf16)
 
 
-def early_kernel(win, nx, g_ref, mod_ref, keep_ref, w_ref, da_ref, do_ref, buf, pad, sems):
-    copies = block_copies(w_ref, win, buf, sems, nx)
-    for copy in copies:
-        copy.start()
-    da_ref[...] = (keep_ref[0] * mod_ref[8:9, :] * g_ref[...].astype(f32)).astype(bf16)
-    pad[...] = jnp.zeros(pad.shape, bf16)
-    total = jnp.zeros(g_ref.shape, f32)
-    for x in range(nx):
-        copies[x].wait()
-        take(pad, win.off, [da_ref], x * win.n, win.n)
-        total = total + mm_nt(pad[...], buf[x])
-    do_ref[...] = total.astype(bf16)
-
-
 def temporal_kernel(
-    win, nx, frames, h_ref, do_in, w_ref, row_clip, frame_clip,
-    o_ref, dqkv_ref, dh_ref, buf, sems, pad, q_s, k_s, v_s, do_s, o_s, dq_s, dk_s, dv_s, qkv_s,
+    win_all, win, w_out, nx, frames, me_ref, h_ref, da_ref, w_refs, row_clip, frame_clip,
+    o_ref, at_ref, dqkv_ref, dh_ref, buf, sems, pad, q_s, k_s, v_s, do_s, o_s, dq_s, dk_s, dv_s, qkv_s,
 ):
-    copies = block_copies(w_ref, win, buf, sems, nx)
-    for copy in copies:
-        copy.start()
+    pieces = Pieces(w_refs, me_ref, win_all, buf, sems, nx)
     rows = h_ref.shape[0]
     spots = rows // frames
     hidden = h_ref[...]
+    out_cols = slice(w_out.start, w_out.stop)
+    pad[...] = jnp.zeros(pad.shape, bf16)
+    total = jnp.zeros(h_ref.shape, f32)
     for x in range(nx):
-        copies[x].wait()
-        block = mm(hidden, buf[x])[:, win.off : win.off + win.n]
+        pieces.wait(x)
+        block = mm(hidden, buf[x, :, win.start : win.stop])[:, win.off : win.off + win.n]
         put([qkv_s], x * win.n, block)
+        take(pad, w_out.off, [da_ref], x * w_out.n, w_out.n)
+        total = total + mm_nt(pad[:, : w_out.width], buf[x, :, out_cols])
+    do_s[...] = total.astype(bf16).astype(f32)
     q_s[...] = qkv_s[:, :D].astype(f32)
     k_s[...] = qkv_s[:, D : 2 * D].astype(f32)
     v_s[...] = qkv_s[:, 2 * D :].astype(f32)
-    do_s[...] = do_in[...].astype(f32)
     dk_s[...] = jnp.zeros(dk_s.shape, f32)
     dv_s[...] = jnp.zeros(dv_s.shape, f32)
 
@@ -325,6 +380,9 @@
 
     lax.fori_loop(0, frames, one_frame, 0)
     o_ref[...] = o_s[...].astype(bf16)
+    for x in range(nx):
+        block = mm(o_ref[...], buf[x, :, out_cols])[:, w_out.off : w_out.off + w_out.n]
+        put([at_ref], x * w_out.n, block)
     dqkv_ref[:, :D] = dq_s[...].astype(bf16)
     dqkv_ref[:, D : 2 * D] = (dk_s[...] * score_scale).astype(bf16)
     dqkv_ref[:, 2 * D :] = dv_s[...].astype(bf16)
@@ -332,20 +390,12 @@
     total = jnp.zeros(dh_ref.shape, f32)
     for x in range(nx):
         take(pad, win.off, [dqkv_ref], x * win.n, win.n)
-        total = total + mm_nt(pad[...], buf[x])
+        total = total + mm_nt(pad[:, : win.width], buf[x, :, win.start : win.stop])
     dh_ref[...] = total.astype(bf16)
 
 
-def mixed_kernel(
-    win, nx, o_ref, x3_ref, g_ref, mod_ref, keep_ref, w_ref, y_ref, gate_ref, buf, sems, acc
-):
-    copies = block_copies(w_ref, win, buf, sems, nx)
-    for copy in copies:
-        copy.start()
-    for x in range(nx):
-        copies[x].wait()
-        put([acc], x * win.n, mm(o_ref[...], buf[x])[:, win.off : win.off + win.n])
-    branch = acc[...].astype(bf16).astype(f32)
+def mixed_kernel(at_ref, x3_ref, g_ref, mod_ref, keep_ref, y_ref, gate_ref):
+    branch = at_ref[...].astype(f32)
     keep = keep_ref[0]
     y_ref[...] = (x3_ref[...] + keep * mod_ref[8:9, :] * branch).astype(bf16)
     gate_ref[...] = jnp.sum(keep * g_ref[...].astype(f32) * branch, axis=0, keepdims=True)
@@ -356,14 +406,12 @@
 
 
 def ff_back_kernel(
-    win, nx, ny, g_ref, dh4_ref, x3_ref, x2_ref, u_ref, m_ref, mod_ref, up_ref, down_ref,
+    win, nx, ny, me_ref, g_ref, dh4_ref, x3_ref, x2_ref, u_ref, m_ref, mod_ref, up_refs, down_ref,
     dm_ref, du_ref, dx2_ref, sum_ref, up_buf, down_buf, up_sems, down_sems, du_s, pad,
 ):
-    width = down_ref.shape[2]
-    downs = block_copies(down_ref, Window(0, width), down_buf, down_sems, ny)
-    ups = block_copies(up_ref, win, up_buf, up_sems, nx)
-    for copy in downs + ups:
-        copy.start()
+    width = down_buf.shape[2]
+    downs = down_blocks(up_refs, down_ref, me_ref, win.stop, down_buf, down_sems, nx)
+    ups = Pieces(up_refs, me_ref, win, up_buf, up_sems, nx)
     dh4 = dh4_ref[...].astype(f32)
     normed, inv_std = stats(x3_ref[...])
     dx3 = g_ref[...].astype(f32) + stats_back(dh4 * (1.0 + mod_ref[7:8, :]), normed, inv_std)
@@ -373,7 +421,7 @@
     dm = (mod_ref[5:6, :] * dx3).astype(bf16)
     dm_ref[...] = dm
     for i in range(ny):
-        downs[i].wait()
+        downs.wait(i)
         grad = mm(dm, down_buf[i])
         u = u_ref[:, i * width : (i + 1) * width]
         tanh, square, c = gelu_parts(u)
@@ -384,7 +432,7 @@
     pad[...] = jnp.zeros(pad.shape, bf16)
     total = jnp.zeros(dx2_ref.shape, f32)
     for x in range(nx):
-        ups[x].wait()
+        ups.wait(x)
         take(pad, win.off, [du_s], x * win.n, win.n)
         du_ref[x] = pad[:, win.off : win.off + win.n]
         total = total + mm_nt(pad[...], up_buf[x])
@@ -396,20 +444,18 @@
 
 
 def text_back_kernel(
-    outer, w_out, w_cq, w_cout, nx, dx2_ref, x1_ref, a1_ref, mod_ref, w_ref, qc_ref, text_ref,
+    outer, w_out, w_cq, w_cout, nx, me_ref, dx2_ref, x1_ref, a1_ref, mod_ref, w_refs, qc_ref, text_ref,
     length_ref, dac_ref, dqc_ref, dx1_ref, da1_ref, do1_ref, dtext_ref, gate_ref,
     buf, sems, pad, acc, q_t, do_t, k_t, do_s, dtext_s,
 ):
-    copies = block_copies(w_ref, outer, buf, sems, nx)
-    for copy in copies:
-        copy.start()
+    pieces = Pieces(w_refs, me_ref, outer, buf, sems, nx)
 
     def product(source, win, wait=False):
         pad[...] = jnp.zeros(pad.shape, bf16)
         total = jnp.zeros(dx2_ref.shape, f32)
         for x in range(nx):
             if wait:
-                copies[x].wait()
+                pieces.wait(x)
             take(pad, win.off, [source], x * win.n, win.n)
             total = total + mm_nt(pad[:, : win.width], buf[x, :, win.start : win.stop])
         return total
@@ -490,17 +536,15 @@
 
 
 def qkv_back_kernel(
-    win, nx, dq_ref, own_ref, come_ref, x_ref, mod_ref, dx1_ref, w_ref,
+    win, nx, me_ref, dq_ref, own_ref, come_ref, x_ref, mod_ref, dx1_ref, w_refs,
     dkv_ref, gx_ref, sum_ref, buf, sems, pad,
 ):
-    copies = block_copies(w_ref, win, buf, sems, nx)
-    for copy in copies:
-        copy.start()
+    pieces = Pieces(w_refs, me_ref, win, buf, sems, nx)
     dkv_ref[...] = (own_ref[...].astype(f32) + come_ref[...].astype(f32)).astype(bf16)
     pad[...] = jnp.zeros(pad.shape, bf16)
     total = jnp.zeros(dx1_ref.shape, f32)
     for x in range(nx):
-        copies[x].wait()
+        pieces.wait(x)
         take(pad, win.off, [dq_ref, dkv_ref], x * win.n, win.n)
         total = total + mm_nt(pad[...], buf[x])
     normed, inv_std = stats(x_ref[...].astype(f32))
@@ -511,21 +555,36 @@
     ).astype(bf16)
 
 
-def weight_kernel(nx, lanes, counts, *refs):
+def step_block(step, me_x, nx):
+    half = nx // 2
+    return me_x ^ (2 * lax.rem(step, half) + (1 - step // half))
+
+
+def turn_rows(turn, value, me_y, ny):
+    rows = turn.shape[0] // ny
+    flipped = value.astype(f32).T.astype(bf16)
+    for y in range(ny):
+        turn[pl.ds(pl.multiple_of((y ^ me_y) * rows, 16), rows), :] = flipped[
+            y * rows : (y + 1) * rows
+        ]
+
+
+def weight_kernel(nx, ny, lanes, counts, me_ref, *refs):
     lefts, k = [], 0
     for count in counts:
         lefts.append((refs[k], refs[k + 1 : k + 1 + count]))
         k += 1 + count
-    out_ref, pads, turned = refs[k], refs[k + 1 :: 2], refs[k + 2 :: 2]
-    x = pl.program_id(0)
-
-    @pl.when(x == 0)
+    send_ref, keep_ref = refs[k : k + 2]
+    pads, turned = refs[k + 2 :: 2], refs[k + 3 :: 2]
+    step = pl.program_id(0)
+    x = step_block(step, me_ref[0], nx)
+
+    @pl.when(step == 0)
     def _():
         for (left, _), turn in zip(lefts, turned):
-            turn[...] = left[...].astype(f32).T.astype(bf16)
-
-    at = 0
-    for (_, rights), pad, turn in zip(lefts, pads, turned):
+            turn_rows(turn, left[...], me_ref[1], ny)
+
+    for (_, rights), pad in zip(lefts, pads):
         n = pad.shape[1]
         for i in range(nx):
 
@@ -533,95 +592,234 @@
             def _():
                 take(pad, 0, rights, i * n, n)
 
-        out_ref[0, :, at : at + n] = mm(turn[...], pad[...]).astype(bf16)
-        at += n
-    if at < lanes:
-        out_ref[0, :, at:] = jnp.zeros((out_ref.shape[1], lanes - at), bf16)
-
-
-def weight_grads(nx, pairs):
+    def fill(out_ref):
+        at = 0
+        for pad, turn in zip(pads, turned):
+            n = pad.shape[1]
+            out_ref[0, :, at : at + n] = mm(turn[...], pad[...]).astype(bf16)
+            at += n
+        if at < lanes:
+            out_ref[0, :, at:] = jnp.zeros((out_ref.shape[1], lanes - at), bf16)
+
+    @pl.when(step < nx // 2)
+    def _():
+        fill(send_ref)
+
+    @pl.when(step >= nx // 2)
+    def _():
+        fill(keep_ref)
+
+
+def weight_grads(nx, me, pairs):
     widths = [sum(r.shape[1] for r in rights) // nx for _, rights in pairs]
     lanes = padded(sum(widths))
     rows = pairs[0][0].shape[0]
+    half = nx // 2
     args, specs, scratch = [], [], []
     for (left, rights), width in zip(pairs, widths):
         args += [left, *rights]
         specs += [vmem() for _ in range(1 + len(rights))]
         scratch += [pltpu.VMEM((rows, width), bf16), pltpu.VMEM((D, rows), bf16)]
-    return pl.pallas_call(
-        functools.partial(weight_kernel, nx, lanes, [len(r) for _, r in pairs]),
-        out_shape=shape(nx, D, lanes, dtype=bf16),
-        grid=(nx,),
-        in_specs=specs,
-        out_specs=pl.BlockSpec((1, D, lanes), lambda x: (x, 0, 0)),
-        scratch_shapes=scratch,
+    send, keep = pl.pallas_call(
+        functools.partial(
+            weight_kernel, nx, lax.axis_size("gy"), lanes, [len(r) for _, r in pairs]
+        ),
+        out_shape=[shape(half, D, lanes, dtype=bf16)] * 2,
+        grid_spec=pltpu.PrefetchScalarGridSpec(
+            num_scalar_prefetch=1,
+            grid=(nx,),
+            in_specs=specs,
+            out_specs=[
+                pl.BlockSpec((1, D, lanes), lambda t, me: (jnp.minimum(t, half - 1), 0, 0)),
+                pl.BlockSpec((1, D, lanes), lambda t, me: (jnp.maximum(t - half, 0), 0, 0)),
+            ],
+            scratch_shapes=scratch,
+        ),
         compiler_params=pltpu.CompilerParams(vmem_limit_bytes=56 << 20),
-        cost_estimate=pl.CostEstimate(
-            flops=4 * rows * D * nx * lanes, bytes_accessed=2 * nx * D * lanes, transcendentals=0
+        cost_estimate=cost(12),
+    )(me, *args)
+    return keep, send
+
+
+def up_grads(me, h3, du, dm, g):
+    nx, rows, n = du.shape
+    ny = lax.axis_size("gy")
+    start = padded(n)
+    width = g.shape[1] // ny
+    fold = fold_width(width)
+    lanes = start if dm is None else start + fold
+    half = nx // 2
+    each = D // nx
+    args = (h3, du) if dm is None else (h3, du, dm, g)
+
+    def kernel(me_ref, h_ref, du_ref, *refs):
+        if dm is None:
+            send_ref, keep_ref, turn = refs
+        else:
+            dm_ref, g_ref, send_ref, keep_ref, turn, down_turn = refs
+        step = pl.program_id(0)
+
+        @pl.when(step == 0)
+        def _():
+            turn_rows(turn, h_ref[...], me_ref[1], ny)
+            if dm is not None:
+                down_turn[...] = dm_ref[...].astype(f32).T.astype(bf16)
+
+        def fill(out_ref):
+            out_ref[0, :, :n] = mm(turn[...], du_ref[0]).astype(bf16)
+            if n < lanes:
+                out_ref[0, :, n:] = jnp.zeros((D, lanes - n), bf16)
+            if dm is None:
+                return
+            x = step_block(step, me_ref[0], nx)
+            left = down_turn[pl.ds(pl.multiple_of(x * each, 16), each), :]
+            for y in range(ny):
+                block = mm(left, g_ref[:, y * width : (y + 1) * width]).astype(bf16)
+                top = pl.multiple_of((y ^ me_ref[1]) * 2 * each, 16)
+                out_ref[0, pl.ds(top, each), start:] = block[:, :fold]
+                low = pl.multiple_of((y ^ me_ref[1]) * 2 * each + each, 16)
+                out_ref[0, pl.ds(low, each), start : start + width - fold] = block[:, fold:]
+
+        @pl.when(step < half)
+        def _():
+            fill(send_ref)
+
+        @pl.when(step >= half)
+        def _():
+            fill(keep_ref)
+
+    send, keep = pl.pallas_call(
+        kernel,
+        out_shape=[shape(half, D, lanes, dtype=bf16)] * 2,
+        grid_spec=pltpu.PrefetchScalarGridSpec(
+            num_scalar_prefetch=1,
+            grid=(nx,),
+            in_specs=[
+                vmem(),
+                pl.BlockSpec((1, rows, n), lambda t, me: (step_block(t, me[0], nx), 0, 0)),
+            ]
+            + [vmem()] * (len(args) - 2),
+            out_specs=[
+                pl.BlockSpec((1, D, lanes), lambda t, me: (jnp.minimum(t, half - 1), 0, 0)),
+                pl.BlockSpec((1, D, lanes), lambda t, me: (jnp.maximum(t - half, 0), 0, 0)),
+            ],
+            scratch_shapes=[pltpu.VMEM((D, rows), bf16)] * (len(args) // 2),
         ),
-    )(*args)
-
-
-def ff_grads(h3, du, dm, g):
-    nx, rows, n = du.shape
-    lanes = padded(n)
-
-    def up_kernel(h_ref, du_ref, out_ref, turn):
-        @pl.when(pl.program_id(0) == 0)
-        def _():
-            turn[...] = h_ref[...].astype(f32).T.astype(bf16)
-
-        out_ref[0, :, :n] = mm(turn[...], du_ref[0]).astype(bf16)
-        if n < lanes:
-            out_ref[0, :, n:] = jnp.zeros((D, lanes - n), bf16)
-
-    d_up = pl.pallas_call(
-        up_kernel,
-        out_shape=shape(nx, D, lanes, dtype=bf16),
-        grid=(nx,),
-        in_specs=[vmem(), pl.BlockSpec((1, rows, n), lambda x: (x, 0, 0))],
-        out_specs=pl.BlockSpec((1, D, lanes), lambda x: (x, 0, 0)),
-        scratch_shapes=[pltpu.VMEM((D, rows), bf16)],
         compiler_params=pltpu.CompilerParams(vmem_limit_bytes=56 << 20),
-        cost_estimate=pl.CostEstimate(
-            flops=4 * rows * D * nx * n, bytes_accessed=2 * nx * D * n, transcendentals=0
-        ),
-    )(h3, du)
+        cost_estimate=cost(20),
+    )(me, *args)
+    return keep, send
+
+
+def down_grads(dm, g):
+    rows = g.shape[0]
     ny = lax.axis_size("gy")
     width = g.shape[1] // ny
 
-    def down_kernel(dm_ref, g_ref, out_ref, turn):
+    def kernel(dm_ref, g_ref, out_ref, turn):
         @pl.when(pl.program_id(0) == 0)
         def _():
             turn[...] = dm_ref[...].astype(f32).T.astype(bf16)
 
         out_ref[0] = mm(turn[...], g_ref[...]).astype(bf16)
 
-    d_down = pl.pallas_call(
-        down_kernel,
+    return pl.pallas_call(
+        kernel,
         out_shape=shape(ny, D, width, dtype=bf16),
         grid=(ny,),
         in_specs=[vmem(), pl.BlockSpec((rows, width), lambda i: (0, i))],
         out_specs=pl.BlockSpec((1, D, width), lambda i: (i, 0, 0)),
         scratch_shapes=[pltpu.VMEM((D, rows), bf16)],
         compiler_params=pltpu.CompilerParams(vmem_limit_bytes=56 << 20),
-        cost_estimate=pl.CostEstimate(
-            flops=4 * rows * D * ny * width, bytes_accessed=2 * ny * D * width, transcendentals=0
-        ),
+        cost_estimate=cost(12),
     )(dm, g)
-    return d_up, d_down
-
-
-def gather_columns(shard):
-    nx = lax.axis_size("gx")
-    whole = lax.all_gather(shard, col_axes, axis=0, tiled=True)
-    return whole.reshape(nx, -1, shard.shape[1])
+
+
+def after(value, *others):
+    return lax.optimization_barrier((value, others))[0]
+
+
+class Gather:
+    def __init__(self, shard):
+        self.line = [shard]
+
+    def along(self, fars, *others):
+        shard = after(self.line[0], *others)
+        new = [swap(shard, "gx", 2 * far) for far in fars]
+        self.line = self.line + new
+        return new
+
+    def first(self, *others):
+        line = after(self.line, *others)
+        half = len(line) // 2
+        some, rest = jnp.stack(line[:half]), jnp.stack(line[half:])
+        self.near = (some, rest)
+        self.far = [swap(some, "gy", 1), swap(rest, "gy", 2)]
+        return self.far
+
+    def second(self, *others):
+        far = after(self.far, *others)
+        some, rest = [jnp.stack(pair) for pair in zip(self.near, far)]
+        arrays = [swap(some, "gy", 2), swap(rest, "gy", 1)]
+        self.arrays = [some, arrays[0], rest, arrays[1]]
+        return arrays
+
+    def last(self, *others):
+        arrays = after(self.arrays, *others)
+        return tuple(arrays + [swap(array, "gx", 1) for array in arrays])
 
 
 def gather_rows(shard):
     ny = lax.axis_size("gy")
     whole = lax.all_gather(shard, row_axes, axis=0, tiled=True)
     return whole.reshape(ny, -1, shard.shape[1])
+
+
+def total(*terms):
+    return sum(term.astype(f32) for term in terms).astype(bf16)
+
+
+class Scatter:
+    def __init__(self, keep, send, *others):
+        nz, depth, lanes = keep.shape
+        ny = lax.axis_size("gy")
+        self.half = nz // 2
+        self.keep = keep.reshape(nz, ny, depth // ny, lanes)
+        self.come = swap(after(send, *others), "gx", 1).reshape(self.keep.shape)
+
+    def first(self, *others):
+        keep, half = self.keep, self.half
+        come = self.come = after(self.come, *others)
+        some = swap(total(keep[:half, 2:], come[:half, 2:]), "gy", 2)
+        self.some_come = some.reshape(half, 2, *some.shape[-2:])
+        self.rest_come = [
+            swap(total(keep[half:, y], come[half:, y]), "gy", 1) for y in (1, 3)
+        ]
+        return [self.some_come, *self.rest_come]
+
+    def second(self, *others):
+        keep, come, half = self.keep, self.come, self.half
+        some_come, rest_come = after((self.some_come, self.rest_come), *others)
+        some_end = swap(total(keep[:half, 1], come[:half, 1], some_come[:, 1]), "gy", 1)
+        rest_end = swap(total(keep[half:, 2], come[half:, 2], rest_come[1]), "gy", 2)
+        self.parts = (some_come, rest_come, some_end, rest_end)
+        return [some_end, rest_end]
+
+    def line(self, *others):
+        keep, come, half = self.keep, self.come, self.half
+        some_come, rest_come, some_end, rest_end = after(self.parts, *others)
+        some = total(keep[:half, 0], come[:half, 0], some_come[:, 0], some_end)
+        rest = total(keep[half:, 0], come[half:, 0], rest_come[0], rest_end)
+        self.ends = [some[i] for i in range(half)] + [rest[i] for i in range(half)]
+        self.got = []
+
+    def along(self, fars, *others):
+        new = [swap(after(self.ends[far], *others), "gx", 2 * far) for far in fars]
+        self.got = self.got + new
+        return new
+
+    def result(self):
+        return sum([term.astype(f32) for term in self.got], self.ends[0].astype(f32))
 
 
 def scatter(blocks, axes):
@@ -681,6 +879,7 @@
     nx, ny = lax.axis_size("gx"), lax.axis_size("gy")
     gx, gy = lax.axis_index("gx"), lax.axis_index("gy")
     devices = nx * ny
+    me = jnp.stack([gx, gy]).astype(jnp.int32)
     device = gy * nx + gx
     rows = tokens.shape[0]
     frame_devs = FRAME // rows
@@ -698,10 +897,41 @@
     row_clip = jnp.repeat(frame_clip, rows // frames)[:, None]
 
     n_sqkv, n_one, n_up = w_sqkv.shape[1], w_sout.shape[1], w_up.shape[1]
-    full_a = gather_columns(pad_lanes(jnp.concatenate([w_sqkv, w_sout, w_cq, w_cout], axis=1)))
-    full_b = gather_columns(pad_lanes(jnp.concatenate([w_up, w_tqkv, w_tout], axis=1)))
-    full_down = gather_rows(w_down.T)
-    ff_width = full_down.shape[2]
+    shard_a = pad_lanes(jnp.concatenate([w_sqkv, w_sout, w_cq, w_cout], axis=1))
+    shard_d = pad_lanes(jnp.concatenate([w_tqkv, w_tout], axis=1))
+    shard_up = pad_lanes(w_up)
+    trees = w_down.shape[1] % 16 == 0 and 2 * w_down.shape[1] == k_rows
+    if trees:
+        turned = w_down.T
+        fold = fold_width(turned.shape[1])
+        rest = jnp.pad(turned[:, fold:], ((0, 0), (0, 2 * fold - turned.shape[1])))
+        folded = jnp.concatenate([turned[:, :fold], rest])
+        shard_up = jnp.concatenate([shard_up, folded], axis=1)
+    fars = range(1, nx // 2)
+    get_a, get_up, get_d = Gather(shard_a), Gather(shard_up), Gather(shard_d)
+    get_a.along(fars)
+    cond_all = condition(timesteps, pooled_text)
+    cond_rows = lax.dynamic_slice_in_dim(cond_all, gy * k_rows, k_rows, axis=1)
+    mod_part = jnp.dot(cond_rows, w_ada.astype(f32), precision=highest)
+    mod_part = mod_part + swap(mod_part, "gy", 1)
+    mod_all = (mod_part + swap(mod_part, "gy", 2))[None]
+    bit = 1
+    while bit < nx:
+        come = swap(mod_all, "gx", bit)
+        mod_all = jnp.where(
+            gx & bit != 0,
+            jnp.concatenate([come, mod_all]),
+            jnp.concatenate([mod_all, come]),
+        )
+        bit *= 2
+    mod = lax.dynamic_index_in_dim(mod_all, clip_here, axis=1, keepdims=False).reshape(9, D)
+    done = [*get_a.line, mod_all]
+    done = get_a.first(*done) + get_up.along(fars[:1], *done)
+    done = get_a.second(*done) + get_up.along(fars[1:], *done)
+    full_a = get_a.last(*done)
+    held = done
+    done = get_up.first(*held) + get_d.along(fars, *held)
+    ff_width = w_down.shape[0]
     ff = ff_width * ny
     win_sqkv = Window(0, n_sqkv)
     at = n_sqkv
@@ -710,50 +940,47 @@
         Window(at + i * n_one, at + (i + 1) * n_one).inside(win_rest) for i in range(3)
     ]
     win_up = Window(0, n_up)
-    win_tqkv = Window(n_up, n_up + n_sqkv)
-    win_tout = Window(n_up + n_sqkv, n_up + n_sqkv + n_one)
-
-    cond_all = condition(timesteps, pooled_text)
-    cond_rows = lax.dynamic_slice_in_dim(cond_all, gy * k_rows, k_rows, axis=1)
-    mod_part = jnp.dot(cond_rows, w_ada.astype(f32), precision=highest)
-    mod_all = lax.all_gather(lax.psum(mod_part, "gy"), "gx", axis=1, tiled=True)
-    mod = jnp.dot(clip_pick, mod_all, precision=highest).reshape(9, D)
+    win_d = Window(0, n_sqkv + n_one)
+    win_tqkv = Window(0, n_sqkv)
+    win_tout = Window(n_sqkv, n_sqkv + n_one)
 
     own = text_states.shape[0]
     depth = w_ckv.shape[0]
-    pieces = text_states.reshape(own // CLIPS, CLIPS, ny, depth).transpose(2, 1, 0, 3)
-    pieces = lax.all_to_all(
-        pieces.reshape(ny, own, depth), "gy", split_axis=0, concat_axis=0, tiled=True
-    )
-    text_block = lax.all_gather(pieces, "gx", axis=0)
+    text_rows = text_states.reshape(own // CLIPS, CLIPS, -1).transpose(1, 0, 2)
+    text_rows = lax.all_gather(text_rows.reshape(own, -1), row_axes, axis=0)
+    text_rows = after(text_rows, *held)
+    text_block = lax.dynamic_slice_in_dim(text_rows, gy * depth, depth, axis=2)
     text_block = (
-        text_block.reshape(nx, ny, CLIPS, own // CLIPS, depth)
-        .transpose(2, 1, 0, 3, 4)
+        text_block.reshape(devices, CLIPS, own // CLIPS, depth)
+        .transpose(1, 0, 2, 3)
         .reshape(own * devices, depth)
     )
     text_part = jnp.dot(text_block, w_ckv, preferred_element_type=f32)
     text_sum = lax.psum_scatter(text_part, "gy", scatter_dimension=0, tiled=True).astype(bf16)
-    text_all = lax.all_gather(text_sum, row_axes, axis=0)
+
+    win = win_sqkv
+    hidden_a, query_a, pair_a = run(
+        functools.partial(qkv_kernel, win, nx),
+        [
+            shape(rows, D, dtype=bf16),
+            shape(rows, D, dtype=bf16),
+            shape(rows, 2 * D, dtype=bf16),
+        ],
+        [smem()] + [vmem(), vmem(), hbm()],
+        [pltpu.VMEM((nx, D, win.width), bf16), pltpu.SemaphoreType.DMA((nx,))],
+        (me, tokens, mod, full_a),
+        9,
+    )
+    done = done + [pair_a]
+    near_up = get_up.second(*done)
+    text_all = lax.all_gather(after(text_sum, *done), row_axes, axis=0)
+    grad_branch_d = (keep_here[0] * mod[8] * grad_out.astype(f32)).astype(bf16)
+    grad_branch_moved = reorder(after(grad_branch_d, *done))
     slots = own * devices // CLIPS
     text_all = text_all.reshape(ny, nx, -1, w_ckv.shape[1]).transpose(0, 2, 1, 3)
     text_all = text_all.reshape(CLIPS, slots, 2 * D)
     text_pairs = lax.dynamic_index_in_dim(text_all, clip_here, axis=0, keepdims=False)
-
-    win = win_sqkv
-    hidden_a, query_a, pair_a = run(
-        functools.partial(qkv_kernel, win, nx),
-        [
-            shape(rows, D, dtype=bf16),
-            shape(rows, D, dtype=bf16),
-            shape(rows, 2 * D, dtype=bf16),
-        ],
-        [vmem(), vmem(), hbm()],
-        [pltpu.VMEM((nx, D, win.width), bf16), pltpu.SemaphoreType.DMA((nx,))],
-        (tokens, mod, full_a),
-        4 * rows * D * 3 * D,
-        2 * D * 3 * D,
-    )
-    pairs = [pair_a]
+    pairs = [after(pair_a, *done)]
     bit = frame_devs // 2
     while bit:
         pairs = pairs + [swap(p, "gx", bit) for p in pairs]
@@ -771,10 +998,14 @@
             pltpu.VMEM((D, rows), f32),
         ],
         (query_a, *pairs),
-        16 * rows * keys * HEADS * 128,
-        4 * keys * D,
-    )
-
+        18,
+    )
+
+    done = near_up + [out_a, text_pairs, grad_branch_moved]
+    full_up = get_up.last(*done)
+    full_down = None if trees else gather_rows(after(w_down.T, *done))
+    far_d = get_d.first(*done)
+    out_a = after(out_a, *done)
     branch_a, after_a, hidden_b, query_b, out_b, after_b, hidden_c = run(
         functools.partial(text_kernel, win_rest, win_sout, win_cq, win_cout, nx),
         [
@@ -786,7 +1017,7 @@
             shape(rows, D),
             shape(rows, D, dtype=bf16),
         ],
-        [vmem(), vmem(), vmem(), hbm(), vmem(), smem()],
+        [smem()] + [vmem(), vmem(), vmem(), hbm(), vmem(), smem()],
         [
             pltpu.VMEM((nx, D, win_rest.width), bf16),
             pltpu.SemaphoreType.DMA((nx,)),
@@ -794,11 +1025,11 @@
             pltpu.VMEM((D, rows), f32),
             pltpu.VMEM((D, slots), f32),
         ],
-        (tokens, out_a, mod, full_a, text_pairs, length_here),
-        8 * rows * D * 3 * D,
-        2 * D * 4 * D,
-    )
-
+        (me, tokens, out_a, mod, full_a, text_pairs, length_here),
+        18,
+    )
+
+    near_d = get_d.second(hidden_c, *far_d)
     pre_act, activated, branch_c, after_c, hidden_d = run(
         functools.partial(ff_kernel, win_up, nx, ny),
         [
@@ -808,74 +1039,56 @@
             shape(rows, D),
             shape(rows, D, dtype=bf16),
         ],
-        [vmem(), vmem(), vmem(), hbm(), hbm()],
+        [smem()] + [vmem(), vmem(), vmem(), hbm(), hbm()],
         [
             pltpu.VMEM((nx, D, win_up.width), bf16),
             pltpu.VMEM((ny, D, ff_width), bf16),
             pltpu.SemaphoreType.DMA((nx,)),
             pltpu.SemaphoreType.DMA((ny,)),
         ],
-        (hidden_c, after_b, mod, full_b, full_down),
-        8 * rows * D * ff,
-        4 * D * ff,
-    )
-
-    win = win_tout
-    grad_branch_d, grad_out_d = run(
-        functools.partial(early_kernel, win, nx),
-        [shape(rows, D, dtype=bf16), shape(rows, D, dtype=bf16)],
-        [vmem(), vmem(), smem(), hbm()],
+        (me, hidden_c, after_b, mod, full_up, full_down),
+        20,
+    )
+
+    done = [*near_d, hidden_d]
+    full_d = get_d.last(*done)
+    moved_d = reorder(after(hidden_d, *done))
+    pad_width = max(win_tqkv.width, win_tout.width)
+    out_moved, branch_moved, grad_qkv_d, grad_hidden_moved = run(
+        functools.partial(temporal_kernel, win_d, win_tqkv, win_tout, nx, frames),
         [
-            pltpu.VMEM((nx, D, win.width), bf16),
-            pltpu.VMEM((rows, win.width), bf16),
+            shape(rows, D, dtype=bf16),
+            shape(rows, D, dtype=bf16),
+            shape(rows, 3 * D, dtype=bf16),
+            shape(rows, D, dtype=bf16),
+        ],
+        [smem()] + [vmem(), vmem(), hbm(), vmem(), smem()],
+        [
+            pltpu.VMEM((nx, D, win_d.width), bf16),
             pltpu.SemaphoreType.DMA((nx,)),
-        ],
-        (grad_out, mod, keep_here, full_b),
-        4 * rows * D * D,
-        2 * D * D,
-    )
-    grad_out_moved = reorder(grad_out_d)
-    moved_d = reorder(hidden_d)
-    win = win_tqkv
-    out_moved, grad_qkv_d, grad_hidden_moved = run(
-        functools.partial(temporal_kernel, win, nx, frames),
-        [
-            shape(rows, D, dtype=bf16),
-            shape(rows, 3 * D, dtype=bf16),
-            shape(rows, D, dtype=bf16),
-        ],
-        [vmem(), vmem(), hbm(), vmem(), smem()],
-        [
-            pltpu.VMEM((nx, D, win.width), bf16),
-            pltpu.SemaphoreType.DMA((nx,)),
-            pltpu.VMEM((rows, win.width), bf16),
+            pltpu.VMEM((rows, pad_width), bf16),
         ]
         + [pltpu.VMEM((rows, D), f32)] * 8
         + [pltpu.VMEM((rows, 3 * D), bf16)],
-        (moved_d, grad_out_moved, full_b, row_clip, frame_clip),
-        16 * rows * D * 3 * D,
-        2 * D * 3 * D,
+        (me, moved_d, grad_branch_moved, full_d, row_clip, frame_clip),
+        25,
     )
     grad_hidden_d = reorder(grad_hidden_moved)
-    out_d = reorder(out_moved)
-    win = win_tout
+    late_terms = weight_grads(
+        nx, me, [(moved_d, [grad_qkv_d]), (out_moved, [grad_branch_moved])]
+    )
+    done = [*late_terms, grad_hidden_d]
+    late = Scatter(*late_terms, *done)
+    grad_hidden_d = after(grad_hidden_d, *done)
+    branch_d = reorder(after(branch_moved, *done))
     mixed, d_gate3 = run(
-        functools.partial(mixed_kernel, win, nx),
+        mixed_kernel,
         [shape(rows, D, dtype=bf16), shape(1, D)],
-        [vmem(), vmem(), vmem(), vmem(), smem(), hbm()],
-        [
-            pltpu.VMEM((nx, D, win.width), bf16),
-            pltpu.SemaphoreType.DMA((nx,)),
-            pltpu.VMEM((rows, D), f32),
-        ],
-        (out_d, after_c, grad_out, mod, keep_here, full_b),
-        4 * rows * D * D,
-        2 * D * D,
-    )
-    late = scatter(
-        weight_grads(nx, [(moved_d, [grad_qkv_d]), (out_d, [grad_branch_d])]), col_axes
-    )
-    d_tqkv, d_tout = late[:, :n_sqkv], late[:, n_sqkv : n_sqkv + n_one]
+        [vmem(), vmem(), vmem(), vmem(), smem()],
+        [],
+        (branch_d, after_c, grad_out, mod, keep_here),
+        3,
+    )
 
     grad_branch_c, grad_pre, grad_b, sums_c = run(
         functools.partial(ff_back_kernel, win_up, nx, ny),
@@ -885,7 +1098,7 @@
             shape(rows, D),
             shape(8, D),
         ],
-        [vmem()] * 7 + [hbm(), hbm()],
+        [smem()] + [vmem()] * 7 + [hbm(), hbm()],
         [
             pltpu.VMEM((nx, D, win_up.width), bf16),
             pltpu.VMEM((ny, D, ff_width), bf16),
@@ -894,13 +1107,21 @@
             pltpu.VMEM((rows, ff), bf16),
             pltpu.VMEM((rows, win_up.width), bf16),
         ],
-        (grad_out, grad_hidden_d, after_c, after_b, pre_act, branch_c, mod, full_b, full_down),
-        8 * rows * D * ff,
-        4 * D * ff,
-    )
-    up_terms, down_terms = ff_grads(hidden_c, grad_pre, grad_branch_c, activated)
-    d_up = scatter(up_terms, col_axes)[:, :n_up]
-    d_down = scatter(down_terms, row_axes).T
+        (me, grad_out, grad_hidden_d, after_c, after_b, pre_act, branch_c, mod, full_up, full_down),
+        22,
+    )
+    done = [late.come, grad_b, branch_d]
+    late_first = late.first(*done)
+    grad_pre = after(grad_pre, *done)
+    if trees:
+        up_terms = up_grads(me, hidden_c, grad_pre, grad_branch_c, activated)
+    else:
+        up_terms = up_grads(me, hidden_c, grad_pre, None, activated)
+        d_down = scatter(down_grads(grad_branch_c, activated), row_axes).T
+    done = [*late_first, *up_terms]
+    late_second = late.second(*done)
+    up_sums = Scatter(*up_terms, *done)
+    grad_b = after(grad_b, *done)
 
     kv_width = w_ckv.shape[1]
     grad_cout_rows, grad_query_b, grad_a, grad_branch_a, grad_out_a, text_terms, d_gate1 = run(
@@ -914,7 +1135,7 @@
             shape(nx, slots, kv_width, dtype=bf16),
             shape(1, D),
         ],
-        [vmem()] * 4 + [hbm(), vmem(), vmem(), smem()],
+        [smem()] + [vmem()] * 4 + [hbm(), vmem(), vmem(), smem()],
         [
             pltpu.VMEM((nx, D, win_rest.width), bf16),
             pltpu.SemaphoreType.DMA((nx,)),
@@ -926,16 +1147,28 @@
             pltpu.VMEM((rows, D), bf16),
             pltpu.VMEM((slots, 2 * D), f32),
         ],
-        (grad_b, after_a, branch_a, mod, full_a, query_b, text_pairs, length_here),
-        8 * rows * D * 3 * D,
-        2 * D * 4 * D,
+        (me, grad_b, after_a, branch_a, mod, full_a, query_b, text_pairs, length_here),
+        20,
     )
     text_terms = jnp.where(clip_mark[None, :, None, None], text_terms[:, None], 0)
     text_terms = lax.psum_scatter(
         text_terms.reshape(nx, -1, kv_width), "gx", scatter_dimension=0, tiled=True
     )
-    text_grad = lax.psum(text_terms[0].astype(f32), "gy").astype(bf16)
+    text_terms = text_terms[0].astype(f32)
+    text_terms = text_terms + swap(text_terms.astype(bf16), "gy", 1).astype(f32)
+    text_terms = text_terms + swap(text_terms.astype(bf16), "gy", 2).astype(f32)
+    text_grad = text_terms.astype(bf16)
     d_ckv = jnp.einsum("rd,re->de", text_block, text_grad, preferred_element_type=f32)
+
+    cross_terms = weight_grads(
+        nx, me, [(hidden_b, [grad_query_b]), (out_b, [grad_cout_rows])]
+    )
+    done = [*late_second, up_sums.come, *cross_terms, grad_out_a]
+    late.line(*done)
+    late_done = late.along(fars, *done)
+    up_first = up_sums.first(*done)
+    cross = Scatter(*cross_terms, *done)
+    grad_out_a = after(grad_out_a, *done)
 
     grad_query_a, grad_pairs = run(
         functools.partial(spatial_back_kernel, count),
@@ -946,9 +1179,13 @@
         + [pltpu.VMEM((HEADS, rows, 128), bf16)] * 2
         + [pltpu.VMEM((HEADS, keys, 128), bf16)] * 4,
         (query_a, grad_out_a, out_a, lse_a, *pairs),
-        40 * rows * keys * HEADS * 128,
-        8 * keys * D,
-    )
+        28,
+    )
+    late = late.result()
+    d_tqkv, d_tout = late[:, :n_sqkv], late[:, n_sqkv : n_sqkv + n_one]
+    done = [*late_done, *up_first, cross.come, grad_pairs]
+    up_second = up_sums.second(*done)
+    grad_pairs = after(grad_pairs, *done)
     bit = 1
     while bit < frame_devs // 2:
         half = grad_pairs.shape[0] // 2
@@ -960,39 +1197,53 @@
     grad_pair_a, grad_tokens, sums_a = run(
         functools.partial(qkv_back_kernel, win, nx),
         [shape(rows, 2 * D, dtype=bf16), shape(rows, D, dtype=bf16), shape(2, D)],
-        [vmem()] * 6 + [hbm()],
+        [smem()] + [vmem()] * 6 + [hbm()],
         [
             pltpu.VMEM((nx, D, win.width), bf16),
             pltpu.SemaphoreType.DMA((nx,)),
             pltpu.VMEM((rows, win.width), bf16),
         ],
-        (grad_query_a, grad_pairs[0], come, tokens, mod, grad_a, full_a),
-        4 * rows * D * 3 * D,
-        2 * D * 3 * D,
-    )
-    early = scatter(
-        weight_grads(
-            nx,
-            [
-                (hidden_a, [grad_query_a, grad_pair_a]),
-                (out_a, [grad_branch_a]),
-                (hidden_b, [grad_query_b]),
-                (out_b, [grad_cout_rows]),
-            ],
-        ),
-        col_axes,
-    )
-    d_sqkv = early[:, :n_sqkv]
-    d_sout, d_cq, d_cout = [
-        early[:, n_sqkv + i * n_one : n_sqkv + (i + 1) * n_one] for i in range(3)
-    ]
+        (me, grad_query_a, grad_pairs[0], come, tokens, mod, grad_a, full_a),
+        11,
+    )
+    early_terms = weight_grads(
+        nx,
+        me,
+        [(hidden_a, [grad_query_a, grad_pair_a]), (out_a, [grad_branch_a])],
+    )
+    done = [*up_second, *early_terms]
+    early = Scatter(*early_terms, *done)
+    up_sums.line(*done)
+    done = up_sums.along(fars[:1], *done) + cross.first(*done) + [early.come]
+    done = up_sums.along(fars[1:2], *done) + cross.second(*done) + early.first(*done)
+    cross.line(*done)
+    done = (
+        up_sums.along(fars[2:], *done) + cross.along(fars, *done) + early.second(*done)
+    )
+    early.line(*done)
+    early.along(fars)
+    up, cross, early = up_sums.result(), cross.result(), early.result()
+    d_up = up[:, :n_up]
+    if trees:
+        start, each = win_up.stop, w_down.shape[1]
+        d_down = jnp.concatenate(
+            [up[:each, start:], up[each:, start : start + ff_width - fold]], axis=1
+        ).T
+    d_cq, d_cout = cross[:, :n_one], cross[:, n_one : 2 * n_one]
+    d_sqkv, d_sout = early[:, :n_sqkv], early[:, n_sqkv : n_sqkv + n_one]
 
     grad_mod = jnp.concatenate(
         [sums_a, d_gate1, sums_c[3:5], sums_c[2:3], sums_c[0:2], d_gate3]
     ).reshape(-1)
-    grad_mod = jnp.where(clip_mark[:, None], grad_mod[None, :], 0.0)
-    grad_mod = lax.psum_scatter(grad_mod, "gx", scatter_dimension=1, tiled=True)
-    grad_mod = lax.psum(grad_mod, "gy")
+    grad_mod = lax.all_gather(grad_mod, row_axes, axis=0)
+    width = w_ada.shape[1]
+    grad_mod = lax.dynamic_slice_in_dim(grad_mod, gx * width, width, axis=1)
+    device_clip = jnp.sum(
+        (clip_ends[None, :] <= (jnp.arange(devices) // frame_devs)[:, None]).astype(jnp.int32),
+        axis=1,
+    )
+    device_pick = (jnp.arange(CLIPS)[:, None] == device_clip[None, :]).astype(f32)
+    grad_mod = jnp.dot(device_pick, grad_mod, precision=highest)
     d_ada = lax.dot_general(
         cond_rows, grad_mod, (((0,), (0,)), ((), ())), precision=highest
     )

time: 1430 us -> 979 us (0.68)
  waiting for transfers between devices: 1010 us -> 446 us
  starting transfers between devices: 10.4 us -> 133 us
  blocking collectives: 93.9 us -> 0 us
  other arithmetic: 17.5 us -> 97 us
    ppermute x5 -> x81, waiting for transfers between devices: 45.7 us -> 407 us  [swap(): lax.ppermute(values, axis, [(i, i ^ mask) for i in range(lax.axis_size(ax...]
    unnamed x15 -> x5, waiting for transfers between devices: 348 us -> 0.08 us
    all_gather x5 -> x3, waiting for transfers between devices: 273 us -> 6.69 us  [the longest x1 6.68 us: local(): text_all = lax.all_gather(after(text_sum, *done), row_axes, axis=0)]
    reduce_scatter x2 -> x0, waiting for transfers between devices: 259 us -> none  [scatter(): lax.psum_scatter(flat, axes, scatter_dimension=0, tiled=True).astype(f32)]
    ppermute x5 -> x81, starting transfers between devices: 0.64 us -> 112 us  [swap(): lax.ppermute(values, axis, [(i, i ^ mask) for i in range(lax.axis_size(ax...]
    convert_element_type x1 -> x22, other arithmetic: 1.05 us -> 60.5 us  [the longest x20 58.4 us: total(): return sum((term.astype(f32) for term in terms)).astype(bf16)]
    psum x2 -> x0, blocking collectives: 47.9 us -> none  [the longest x1 31.8 us: local(): grad_mod = lax.psum(grad_mod, 'gy')]
    reduce_scatter x1, waiting for transfers between devices: 37.3 us -> 0.02 us  [local(): lax.psum_scatter(text_terms.reshape(nx, -1, kv_width), 'gx', scatter_dime...]
  transfers between devices with their start and end apart: 20 -> 90, of which waited for: 16 -> 33; matrix products, arithmetic and copies ran while one was open for 3% -> 12% of each run, Pallas kernels for 9% -> 21%
where the time goes in v2:
time: 979 us; the launch traced here: 971 us
  waiting for transfers between devices  446 us (46%)
  Pallas kernels  229 us (23%)
  starting transfers between devices  133 us (14%)
  other arithmetic  97 us (10%)
  local copies, waits for them, and re-layouts  40.6 us (4%)
  between operations  17.3 us (2%)
    ppermute x81, waiting for transfers between devices, swap(): lax.ppermute(values, axis, [(i, i ^ mask) for i in range(lax.axis_size(ax...  407 us
    pallas_call x10, Pallas kernels, run(): pl.pallas_call(grouped, out_shape=outs, in_specs=flat_specs, out_specs=[v...  175 us
    ppermute x81, starting transfers between devices, swap(): lax.ppermute(values, axis, [(i, i ^ mask) for i in range(lax.axis_size(ax...  112 us
    convert_element_type x20, other arithmetic, total(): return sum((term.astype(f32) for term in terms)).astype(bf16)  58.4 us
    pallas_call x3, Pallas kernels, weight_grads(): pl.pallas_call(functools.partial(weight_kernel, nx, lax.axis_size('gy'),...  36.9 us
    all_to_all x4, waiting for transfers between devices, reorder(): lax.all_to_all(values.reshape(devices, values.shape[0] // devices, values...  25.4 us
    all_to_all x4, starting transfers between devices, reorder(): lax.all_to_all(values.reshape(devices, values.shape[0] // devices, values...  20.6 us
  transfers between devices with their start and end apart: 90, of which 33 were waited for; matrix products, arithmetic and copies ran while one was open for 12% of the time, Pallas kernels for 21%

profile of v2, /device:TPU:0, one launch (start us, length us, event | category | flops | bytes accessed | tf_op | source)
XLA Modules:
  0.0 970.6 jit_solution(3256639996840852545)
XLA Ops:
  11.3 3.0 collective-permute-start
  23.8 3.0 collective-permute-start.6
  29.9 53.6 %collective-permute-done.4 = f32[4,4,1296]{2,1,0:T(4,128)S(1)} collective-permute-done((f32[4,4,1296]{2,1,0:T(4,128)S(1)}, f32[4,4,1296]{2,1,0:T(4,128)S(1)}, u32[]{:S(2)}, u32[]{:S(2)}) %collective-permute-start.4) | collective-permute-done | bytes 82976 | tf_op jit(solution)/shard_map/ppermute | solution.py:831
  88.7 23.1 %collective-permute-done.10 = bf16[288,1280]{1,0:T(8,128)(2,1)S(1)} collective-permute-done((bf16[288,1280]{1,0:T(8,128)(2,1)S(1)}, bf16[288,1280]{1,0:T(8,128)(2,1)S(1)}, u32[]{:S(2)}, u32[]{:S(2)}) %collective-permute-start.10) | collective-permute-done | bytes 737312 | tf_op jit(solution)/shard_map/ppermute | solution.py:831
  121.3 46.8 %collective-permute-done.13 = bf16[288,1280]{1,0:T(8,128)(2,1)S(1)} collective-permute-done((bf16[288,1280]{1,0:T(8,128)(2,1)S(1)}, bf16[288,1280]{1,0:T(8,128)(2,1)S(1)}, u32[]{:S(2)}, u32[]{:S(2)}) %collective-permute-start.13) | collective-permute-done | bytes 737312 | tf_op jit(solution)/shard_map/ppermute | solution.py:831
  174.8 4.5 copy.269
  184.1 15.5 %collective-permute-start.21 = (bf16[288,640]{1,0:T(8,128)(2,1)S(1)}, bf16[288,640]{1,0:T(8,128)(2,1)S(1)}, u32[]{:S(2)}, u32[]{:S(2)}) collective-permute-start(bf16[288,640]{1,0:T(8,128)(2,1)S(1)} %fusion.53), channel_id=1, source_target_pairs={{0,2},{1,3},{2,0},{3,1},{4,6},{5,7},{6,4},{7,5},{8,10},{9,11},{10,... | collective-permute-start | bytes 1105928 | tf_op jit(solution)/shard_map/ppermute | solution.py:831
  207.1 9.2 shard_map.265
  216.4 7.2 reduce-scatter.3.cloned.1.call-done
  232.4 3.3 pad_maximum_fusion.1.refs_6_.refs_10_
  236.4 6.5 collective-permute-start.24
  245.6 26.7 %collective-permute-done.24.refs_2_.refs_5_ = bf16[256,2304]{1,0:T(8,128)(2,1)} collective-permute-done((bf16[256,2304]{1,0:T(8,128)(2,1)}, bf16[256,2304]{1,0:T(8,128)(2,1)}, u32[]{:S(2)}, u32[]{:S(2)}) %collective-permute-start.24) | collective-permute-done | bytes 1179680 | tf_op jit(solution)/shard_map/ppermute | solution.py:831
  273.3 4.3 all-to-all-start
  277.6 18.1 %shard_map.266 = (bf16[256,1152]{1,0:T(8,128)(2,1)}, f32[16,256]{1,0:T(8,128)}) custom-call(bf16[256,1152]{1,0:T(8,128)(2,1)} %get-tuple-element.161.refs_0_, bf16[256,2304]{1,0:T(8,128)(2,1)} %get-tuple-element.168.refs_1_.refs_4_, bf16[256,2304]{1,0:T(8,128)(2,1)} %collective-permute-done.24.refs_2_.refs_5_, ...), custom_call_target="tpu_custom_call" | custom-call | flops 360000000 | tf_op jit(solution)/shard_map/pallas_call | solution.py:57
  295.7 6.7 all-gather.8.cloned.1.call-done
  308.4 4.3 all-to-all-done
  316.5 16.5 %collective-permute-done.33 = bf16[2,288,640]{2,1,0:T(8,128)(2,1)S(1)} collective-permute-done((bf16[2,288,640]{2,1,0:T(8,128)(2,1)S(1)}, bf16[2,288,640]{2,1,0:T(8,128)(2,1)S(1)}, u32[]{:S(2)}, u32[]{:S(2)}) %collective-permute-start.33) | collective-permute-done | bytes 737312 | tf_op jit(solution)/shard_map/ppermute | solution.py:831
  335.9 17.9 %shard_map.267 = (f32[256,1152]{1,0:T(8,128)}, f32[256,1152]{1,0:T(8,128)}, bf16[256,1152]{1,0:T(8,128)(2,1)}, bf16[256,1152]{1,0:T(8,128)(2,1)}, bf16[256,1152]...) custom-call(s32[2]{0:T(128)} %pad_add_fusion.refs_0_.me_ref, bf16[256,1152]{1,0:T(8,128)(2,1)} %refs_4_.1, ...), custom_call_target="tpu_custom_call" | custom-call | flops 360000000 | tf_op jit(solution)/shard_map/pallas_call | solution.py:57
  361.4 20.7 %shard_map.268 = (f32[256,4608]{1,0:T(8,128)}, bf16[256,4608]{1,0:T(8,128)(2,1)}, f32[256,1152]{1,0:T(8,128)}, f32[256,1152]{1,0:T(8,128)}, bf16[256,1152]{1,0:T(8,128)(2,1)}) custom-call(s32[2]{0:T(128)} %pad_add_fusion.refs_0_.me_ref, bf16[256,1152]{1,0:T(8,128)(2,1)} %get-tuple-element.176.refs_1_.h_ref, f32[256,1152]{1,0:T(8,128)} %get-tuple-element.177.refs_2_.refs_4_, ...), custom_call_target="tpu_custom_call" | custom-call | flops 400000000 | tf_op jit(solution)/shard_map/pallas_call | solution.py:57
  382.1 8.3 collective-permute-done.35.refs_4_
  390.4 3.2 collective-permute-done.36.refs_6_
  394.6 10.5 %all-to-all-start.1 = ((bf16[32,8,1152]{2,1,0:T(8,128)(2,1)}), bf16[32,8,1152]{2,1,0:T(8,128)(2,1)S(1)}, u32[]{:S(2)}, u32[]{:S(2)}) async-start(bf16[32,8,1152]{2,1,0:T(8,128)(2,1)} %bitcast.302), calls=%async_computation.2 | async-start | bytes 1179648 | tf_op jit(solution)/shard_map/all_to_all | solution.py:836
  406.5 16.3 %all-to-all-done.1 = bf16[32,8,1152]{2,1,0:T(8,128)(2,1)S(1)} async-done(((bf16[32,8,1152]{2,1,0:T(8,128)(2,1)}), bf16[32,8,1152]{2,1,0:T(8,128)(2,1)S(1)}, u32[]{:S(2)}, u32[]{:S(2)}) %all-to-all-start.1) | async-done | bytes 589856 | tf_op jit(solution)/shard_map/all_to_all | solution.py:836
  424.2 25.5 %shard_map.269 = (bf16[256,1152]{1,0:T(8,128)(2,1)}, bf16[256,1152]{1,0:T(8,128)(2,1)}, bf16[256,3456]{1,0:T(8,128)(2,1)}, bf16[256,1152]{1,0:T(8,128)(2,1)}) custom-call(s32[2]{0:T(128)} %pad_add_fusion.refs_0_.me_ref, bf16[256,1152]{1,0:T(8,128)(2,1)} %bitcast.279, bf16[256,1152]{1,0:T(8,128)(2,1)} %bitcast.277, ...), custom_call_target="tpu_custom_call" | custom-call | flops 500000000 | tf_op jit(solution)/shard_map/pallas_call | solution.py:57
  449.6 3.2 all-to-all-start.2
  452.8 13.0 %shard_map.270 = (bf16[4,1152,640]{2,1,0:T(8,128)(2,1)}, bf16[4,1152,640]{2,1,0:T(8,128)(2,1)}) custom-call(s32[2]{0:T(128)} %pad_add_fusion.refs_0_.me_ref, bf16[256,1152]{1,0:T(8,128)(2,1)} %bitcast.280, bf16[256,3456]{1,0:T(8,128)(2,1)} %get-tuple-element.195.refs_1_, bf16[256,1152]{1,0:T(8,128)(2,1)} %get-tuple-element.196.refs_2_, ...), custom_call_target="tpu_custom_call" | custom-call | flops 240000000 | tf_op jit(solution)/shard_map/pallas_call | solution.py:623
  465.8 4.8 all-to-all-done.2
  473.4 22.1 %shard_map.272 = (bf16[256,1152]{1,0:T(8,128)(2,1)}, bf16[8,256,576]{2,1,0:T(8,128)(2,1)}, f32[256,1152]{1,0:T(8,128)}, f32[8,1152]{1,0:T(8,128)}) custom-call(s32[2]{0:T(128)} %pad_add_fusion.refs_0_.me_ref, bf16[256,1152]{1,0:T(8,128)(2,1)} %refs_1_.5, bf16[256,1152]{1,0:T(8,128)(2,1)} %bitcast.292, f32[256,1152]{1,0:T(8,128)} %get-tuple-element.201.refs_1_.refs_3_, ...), custom_call_target="tpu_custom_call" | custom-call | flops 440000000 | tf_op jit(solution)/shard_map/pallas_call | solution.py:57
  495.6 3.5 add_convert_fusion.6
  501.4 3.3 fusion.33
  507.4 16.6 %shard_map.273 = (bf16[4,1152,1280]{2,1,0:T(8,128)(2,1)}, bf16[4,1152,1280]{2,1,0:T(8,128)(2,1)}) custom-call(s32[2]{0:T(128)} %pad_add_fusion.refs_0_.me_ref, bf16[256,1152]{1,0:T(8,128)(2,1)} %get-tuple-element.176.refs_1_.h_ref, bf16[8,256,576]{2,1,0:T(8,128)(2,1)} %get-tuple-element.210.du_ref, bf16[256,1152]{1,0:T(8,128)(2,1)} %get-tuple-element.211.refs_0_, ...), custom_call_target="tpu_custom_call" | custom-call | flops 400000000 | tf_op jit(solution)/shard_map/pallas_call | solution.py:691
  524.9 15.0 %collective-permute-done.44 = bf16[2,288,640]{2,1,0:T(8,128)(2,1)S(1)} collective-permute-done((bf16[2,288,640]{2,1,0:T(8,128)(2,1)}, bf16[2,288,640]{2,1,0:T(8,128)(2,1)S(1)}, u32[]{:S(2)}, u32[]{:S(2)}) %collective-permute-start.44) | collective-permute-done | bytes 737312 | tf_op jit(solution)/shard_map/ppermute | solution.py:831
  547.9 19.8 %shard_map.274 = (bf16[256,1152]{1,0:T(8,128)(2,1)}, bf16[256,1152]{1,0:T(8,128)(2,1)}, f32[256,1152]{1,0:T(8,128)}, bf16[256,1152]{1,0:T(8,128)(2,1)}, bf16[256...) custom-call(s32[2]{0:T(128)} %pad_add_fusion.refs_0_.me_ref, ...), custom_call_target="tpu_custom_call" | custom-call | flops 400000000 | tf_op jit(solution)/shard_map/pallas_call | solution.py:57
  567.7 10.7 %shard_map.275 = (bf16[4,1152,384]{2,1,0:T(8,128)(2,1)}, bf16[4,1152,384]{2,1,0:T(8,128)(2,1)}) custom-call(s32[2]{0:T(128)} %pad_add_fusion.refs_0_.me_ref, bf16[256,1152]{1,0:T(8,128)(2,1)} %get-tuple-element.223.refs_0_, bf16[256,1152]{1,0:T(8,128)(2,1)} %get-tuple-element.224.refs_1_, bf16[256,1152]{1,0:T(8,128)(2,1)} %get-tuple-element.225.refs_2_, ...), custom_call_target="tpu_custom_call" | custom-call | flops 240000000 | tf_op jit(solution)/shard_map/pallas_call | solution.py:623
  578.5 4.4 add_convert_fusion
  584.4 5.1 fusion.5
  596.0 8.3 collective-permute-done.48
  604.4 3.3 collective-permute-start.49
  607.7 15.3 %collective-permute-done.49 = bf16[288,640]{1,0:T(8,128)(2,1)} collective-permute-done((bf16[288,640]{1,0:T(8,128)(2,1)S(1)}, bf16[288,640]{1,0:T(8,128)(2,1)}, u32[]{:S(2)}, u32[]{:S(2)}) %collective-permute-start.49) | collective-permute-done | bytes 368672 | tf_op jit(solution)/shard_map/ppermute | solution.py:831
  623.0 3.5 collective-permute-start.50
  626.6 28.3 %shard_map.276 = (bf16[256,1152]{1,0:T(8,128)(2,1)}, bf16[4,256,2304]{2,1,0:T(8,128)(2,1)}) custom-call(bf16[256,1152]{1,0:T(8,128)(2,1)} %get-tuple-element.161.refs_0_, bf16[256,1152]{1,0:T(8,128)(2,1)} %get-tuple-element.229.refs_1_, bf16[256,1152]{1,0:T(8,128)(2,1)} %get-tuple-element.175.refs_2_.refs_3_, f32[16,256]{1,0:T(8,128)} %get-tuple-element.230.refs_3_, ...), custom_call_target="tpu_custom_call" | custom-call | flops 560000000 | tf_op jit(solution)/shard_map/pallas_call | solution.py:57
  655.7 3.3 slice.326
  668.3 2.9 add_convert_fusion.1
  674.2 51.1 %collective-permute-done.56.refs_3_ = bf16[256,2304]{1,0:T(8,128)(2,1)S(1)} collective-permute-done((bf16[256,2304]{1,0:T(8,128)(2,1)S(1)}, bf16[256,2304]{1,0:T(8,128)(2,1)S(1)}, u32[]{:S(2)}, u32[]{:S(2)}) %collective-permute-start.56) | collective-permute-done | bytes 1179680 | tf_op jit(solution)/shard_map/ppermute | solution.py:831
  726.3 10.9 %shard_map.277 = (bf16[256,2304]{1,0:T(8,128)(2,1)}, bf16[256,1152]{1,0:T(8,128)(2,1)}, f32[2,1152]{1,0:T(2,128)}) custom-call(s32[2]{0:T(128)} %pad_add_fusion.refs_0_.me_ref, bf16[256,1152]{1,0:T(8,128)(2,1)} %get-tuple-element.231.refs_1_, bf16[256,2304]{1,0:T(8,128)(2,1)} %get-tuple-element.363.refs_2_, bf16[256,2304]{1,0:T(8,128)(2,1)} %copy-done.17, ...), custom_call_target="tpu_custom_call" | custom-call | flops 220000000 | tf_op jit(solution)/shard_map/pallas_call | solution.py:57
  737.3 13.2 %shard_map.278 = (bf16[4,1152,640]{2,1,0:T(8,128)(2,1)}, bf16[4,1152,640]{2,1,0:T(8,128)(2,1)}) custom-call(s32[2]{0:T(128)} %pad_add_fusion.refs_0_.me_ref, bf16[256,1152]{1,0:T(8,128)(2,1)} %get-tuple-element.250.refs_0_, bf16[256,1152]{1,0:T(8,128)(2,1)} %get-tuple-element.231.refs_1_, bf16[256,2304]{1,0:T(8,128)(2,1)} %get-tuple-element.251.refs_2_, ...), custom_call_target="tpu_custom_call" | custom-call | flops 240000000 | tf_op jit(solution)/shard_map/pallas_call | solution.py:623
  752.2 10.1 %collective-permute-done.79 = bf16[512,288]{1,0:T(8,128)(2,1)S(1)} collective-permute-done((bf16[512,288]{1,0:T(8,128)(2,1)}, bf16[512,288]{1,0:T(8,128)(2,1)S(1)}, u32[]{:S(2)}, u32[]{:S(2)}) %collective-permute-start.79) | collective-permute-done | bytes 294944 | tf_op jit(solution)/shard_map/ppermute | solution.py:831
  767.7 6.5 collective-permute-done.80
  779.8 5.1 fusion.1
  790.5 9.9 %collective-permute-done.62 = bf16[2,288,384]{2,1,0:T(8,128)(2,1)S(1)} collective-permute-done((bf16[2,288,384]{2,1,0:T(8,128)(2,1)S(1)}, bf16[2,288,384]{2,1,0:T(8,128)(2,1)S(1)}, u32[]{:S(2)}, u32[]{:S(2)}) %collective-permute-start.62) | collective-permute-done | bytes 442400 | tf_op jit(solution)/shard_map/ppermute | solution.py:831
  800.4 8.1 collective-permute-done.63
  809.4 2.8 add_convert_fusion.2
  813.0 2.8 fusion.36
  817.8 3.6 collective-permute-start.67
  830.1 28.3 %collective-permute-done.68 = bf16[2,288,384]{2,1,0:T(8,128)(2,1)} collective-permute-done((bf16[2,288,384]{2,1,0:T(8,128)(2,1)}, bf16[2,288,384]{2,1,0:T(8,128)(2,1)}, u32[]{:S(2)}, u32[]{:S(2)}) %collective-permute-start.68) | collective-permute-done | bytes 442400 | tf_op jit(solution)/shard_map/ppermute | solution.py:831
  861.3 5.6 collective-permute-done.69
  875.5 4.0 collective-permute-start.72
  882.2 14.8 %collective-permute-done.73 = bf16[288,384]{1,0:T(8,128)(2,1)S(1)} collective-permute-done((bf16[288,384]{1,0:T(8,128)(2,1)S(1)}, bf16[288,384]{1,0:T(8,128)(2,1)S(1)}, u32[]{:S(2)}, u32[]{:S(2)}) %collective-permute-start.73) | collective-permute-done | bytes 221216 | tf_op jit(solution)/shard_map/ppermute | solution.py:831
  897.3 3.6 fusion.64
  900.9 19.7 %collective-permute-done.74 = bf16[288,384]{1,0:T(8,128)(2,1)S(1)} collective-permute-done((bf16[288,384]{1,0:T(8,128)(2,1)S(1)}, bf16[288,384]{1,0:T(8,128)(2,1)S(1)}, u32[]{:S(2)}, u32[]{:S(2)}) %collective-permute-start.74) | collective-permute-done | bytes 221216 | tf_op jit(solution)/shard_map/ppermute | solution.py:831
  922.5 3.4 fusion.13
  926.0 3.7 collective-permute-start.78
  929.7 3.0 collective-permute-start.77
  939.5 22.4 %collective-permute-done.77 = bf16[288,640]{1,0:T(8,128)(2,1)S(1)} collective-permute-done((bf16[288,640]{1,0:T(8,128)(2,1)S(1)}, bf16[288,640]{1,0:T(8,128)(2,1)S(1)}, u32[]{:S(2)}, u32[]{:S(2)}) %collective-permute-start.77) | collective-permute-done | bytes 368672 | tf_op jit(solution)/shard_map/ppermute | solution.py:831
  (380 shorter events, 179.6 us)
Async XLA Ops:
  7.2 167.5 %all-gather.6.cloned.1.call-start = ((), (), s32[]{:S(2)}) async-start(), calls=%async_computation.6 | async-start | bytes 4325376 | tf_op jit(solution)/shard_map/all_gather | solution.py:950
  9.2 214.4 %reduce-scatter.3.cloned.1.call-start = ((), (), s32[]{:S(2)}) async-start(), calls=%async_computation.7 | async-start | bytes 737280 | tf_op jit(solution)/shard_map/reduce_scatter | solution.py:959
  23.7 60.6 %collective-permute-start.5 = (bf16[288,896]{1,0:T(8,128)(2,1)S(1)}, bf16[288,896]{1,0:T(8,128)(2,1)S(1)}, u32[]{:S(2)}, u32[]{:S(2)}) collective-permute-start(bf16[288,896]{1,0:T(8,128)(2,1)S(1)} %fusion.46), channel_id=1, source_target_pairs={{0,2},{1,3},{2,0},{3,1},{4,6},{5,7},{6,4},{7,5},{8,10},{9,11},{10,... | collective-permute-start | bytes 1548296 | tf_op jit(solution)/shard_map/ppermute | solution.py:831
  23.8 60.5 %collective-permute-start.6 = (bf16[288,896]{1,0:T(8,128)(2,1)S(1)}, bf16[288,896]{1,0:T(8,128)(2,1)S(1)}, u32[]{:S(2)}, u32[]{:S(2)}) collective-permute-start(bf16[288,896]{1,0:T(8,128)(2,1)S(1)} %fusion.46), channel_id=1, source_target_pairs={{0,4},{1,5},{2,6},{3,7},{4,0},{5,1},{6,2},{7,3},{8,12},{9,13},{10,... | collective-permute-start | bytes 1548296 | tf_op jit(solution)/shard_map/ppermute | solution.py:831
  26.8 57.5 %collective-permute-start.7 = (bf16[288,896]{1,0:T(8,128)(2,1)S(1)}, bf16[288,896]{1,0:T(8,128)(2,1)S(1)}, u32[]{:S(2)}, u32[]{:S(2)}) collective-permute-start(bf16[288,896]{1,0:T(8,128)(2,1)S(1)} %fusion.46), channel_id=1, source_target_pairs={{0,6},{1,7},{2,4},{3,5},{4,2},{5,3},{6,0},{7,1},{8,14},{9,15},{10,... | collective-permute-start | bytes 1548296 | tf_op jit(solution)/shard_map/ppermute | solution.py:831
  28.2 55.4 %collective-permute-start.4 = (f32[4,4,1296]{2,1,0:T(4,128)S(1)}, f32[4,4,1296]{2,1,0:T(4,128)S(1)}, u32[]{:S(2)}, u32[]{:S(2)}) collective-permute-start(f32[4,4,1296]{2,1,0:T(4,128)S(1)} %maximum_select_fusion.1), channel_id=1, source_target_pairs={{0,4},{1,5},{2,6},{3,7},{4,0},{5,1},{6,2},{7,3},{8,12},{9,13},{10,... | collective-permute-start | bytes 248840 | tf_op jit(solution)/shard_map/ppermute | solution.py:831
  84.4 29.2 %collective-permute-start.8 = (bf16[2,288,896]{2,1,0:T(8,128)(2,1)S(1)}, bf16[2,288,896]{2,1,0:T(8,128)(2,1)S(1)}, u32[]{:S(2)}, u32[]{:S(2)}) collective-permute-start(bf16[2,288,896]{2,1,0:T(8,128)(2,1)S(1)} %get-tuple-element.373), channel_id=1, source_target_pairs={{0,8},{8,0},{16,24},{24,16},{1,9},{9,1},{17,25},{25,17},{2,10},{10... | collective-permute-start | bytes 3096584 | tf_op jit(solution)/shard_map/ppermute | solution.py:831
  86.2 27.4 %collective-permute-start.9 = (bf16[2,288,896]{2,1,0:T(8,128)(2,1)S(1)}, bf16[2,288,896]{2,1,0:T(8,128)(2,1)S(1)}, u32[]{:S(2)}, u32[]{:S(2)}) collective-permute-start(bf16[2,288,896]{2,1,0:T(8,128)(2,1)S(1)} %get-tuple-element.371), channel_id=1, source_target_pairs={{0,16},{8,24},{16,0},{24,8},{1,17},{9,25},{17,1},{25,9},{2,18},{10... | collective-permute-start | bytes 3096584 | tf_op jit(solution)/shard_map/ppermute | solution.py:831
  113.8 54.3 %collective-permute-start.11 = (bf16[2,2,288,896]{3,2,1,0:T(8,128)(2,1)S(1)}, bf16[2,2,288,896]{3,2,1,0:T(8,128)(2,1)}, u32[]{:S(2)}, u32[]{:S(2)}) collective-permute-start(bf16[2,2,288,896]{3,2,1,0:T(8,128)(2,1)S(1)} %pad_maximum_fusion.2.refs_3_.refs_4_.refs_5_.refs_7_), channel_id=1, source_target_pairs={{0,16},{8,24},{16,0},{24,8},{1,17},{9,25},{17,1},{25,9},{2,18},{10... | collective-permute-start | bytes 6193160 | tf_op jit(solution)/shard_map/ppermute | solution.py:831
  116.9 51.2 %collective-permute-start.12 = (bf16[2,2,288,896]{3,2,1,0:T(8,128)(2,1)}, bf16[2,2,288,896]{3,2,1,0:T(8,128)(2,1)}, u32[]{:S(2)}, u32[]{:S(2)}) collective-permute-start(bf16[2,2,288,896]{3,2,1,0:T(8,128)(2,1)} %pad_maximum_fusion.3.refs_5_.refs_6_.refs_7_.refs_9_), channel_id=1, source_target_pairs={{0,8},{8,0},{16,24},{24,16},{1,9},{9,1},{17,25},{25,17},{2,10},{10... | collective-permute-start | bytes 6193160 | tf_op jit(solution)/shard_map/ppermute | solution.py:831
  117.5 50.6 %collective-permute-start.13 = (bf16[288,1280]{1,0:T(8,128)(2,1)S(1)}, bf16[288,1280]{1,0:T(8,128)(2,1)S(1)}, u32[]{:S(2)}, u32[]{:S(2)}) collective-permute-start(bf16[288,1280]{1,0:T(8,128)(2,1)S(1)} %fusion.31), channel_id=1, source_target_pairs={{0,4},{1,5},{2,6},{3,7},{4,0},{5,1},{6,2},{7,3},{8,12},{9,13},{10,... | collective-permute-start | bytes 2211848 | tf_op jit(solution)/shard_map/ppermute | solution.py:831
  119.9 48.2 %collective-permute-start.14 = (bf16[288,1280]{1,0:T(8,128)(2,1)S(1)}, bf16[288,1280]{1,0:T(8,128)(2,1)S(1)}, u32[]{:S(2)}, u32[]{:S(2)}) collective-permute-start(bf16[288,1280]{1,0:T(8,128)(2,1)S(1)} %fusion.31), channel_id=1, source_target_pairs={{0,6},{1,7},{2,4},{3,5},{4,2},{5,3},{6,0},{7,1},{8,14},{9,15},{10,... | collective-permute-start | bytes 2211848 | tf_op jit(solution)/shard_map/ppermute | solution.py:831
  169.2 30.4 %collective-permute-start.17 = (bf16[2,2,288,896]{3,2,1,0:T(8,128)(2,1)}, bf16[2,2,288,896]{3,2,1,0:T(8,128)(2,1)}, u32[]{:S(2)}, u32[]{:S(2)}) collective-permute-start(bf16[2,2,288,896]{3,2,1,0:T(8,128)(2,1)} %pad_maximum_fusion.3.refs_5_.refs_6_.refs_7_.refs_9_), channel_id=1, source_target_pairs={{0,1},{1,0},{2,3},{3,2},{4,5},{5,4},{6,7},{7,6},{8,9},{9,8},{10,11... | collective-permute-start | bytes 6193160 | tf_op jit(solution)/shard_map/ppermute | solution.py:831
  169.5 31.3 %collective-permute-start.18 = (bf16[2,2,288,896]{3,2,1,0:T(8,128)(2,1)}, bf16[2,2,288,896]{3,2,1,0:T(8,128)(2,1)}, u32[]{:S(2)}, u32[]{:S(2)}) collective-permute-start(bf16[2,2,288,896]{3,2,1,0:T(8,128)(2,1)} %collective-permute-done.12.refs_6_.refs_7_.refs_8_.refs_10_), channel_id=1, source_target_pairs={{0,1},{1,0},{2,3},{3,2},{4,5},{5,4},{6,7},{7,6},{8,9},{9,8},{10,11... | collective-permute-start | bytes 6193160 | tf_op jit(solution)/shard_map/ppermute | solution.py:831
  171.5 56.3 %collective-permute-start.19 = (bf16[2,288,1280]{2,1,0:T(8,128)(2,1)}, bf16[2,288,1280]{2,1,0:T(8,128)(2,1)}, u32[]{:S(2)}, u32[]{:S(2)}) collective-permute-start(bf16[2,288,1280]{2,1,0:T(8,128)(2,1)} %get-tuple-element.369), channel_id=1, source_target_pairs={{0,8},{8,0},{16,24},{24,16},{1,9},{9,1},{17,25},{25,17},{2,10},{10... | collective-permute-start | bytes 4423688 | tf_op jit(solution)/shard_map/ppermute | solution.py:831
  179.3 48.6 %collective-permute-start.20 = (bf16[2,288,1280]{2,1,0:T(8,128)(2,1)}, bf16[2,288,1280]{2,1,0:T(8,128)(2,1)}, u32[]{:S(2)}, u32[]{:S(2)}) collective-permute-start(bf16[2,288,1280]{2,1,0:T(8,128)(2,1)} %get-tuple-element.367), channel_id=1, source_target_pairs={{0,16},{8,24},{16,0},{24,8},{1,17},{9,25},{17,1},{25,9},{2,18},{10... | collective-permute-start | bytes 4423688 | tf_op jit(solution)/shard_map/ppermute | solution.py:831
  183.3 119.1 %all-gather.8.cloned.1.call-start = ((), (), s32[]{:S(2)}) async-start(), calls=%async_computation.9 | async-start | bytes 2433024 | tf_op jit(solution)/shard_map/all_gather | solution.py:976
  184.1 41.1 %collective-permute-start.21 = (bf16[288,640]{1,0:T(8,128)(2,1)S(1)}, bf16[288,640]{1,0:T(8,128)(2,1)S(1)}, u32[]{:S(2)}, u32[]{:S(2)}) collective-permute-start(bf16[288,640]{1,0:T(8,128)(2,1)S(1)} %fusion.53), channel_id=1, source_target_pairs={{0,2},{1,3},{2,0},{3,1},{4,6},{5,7},{6,4},{7,5},{8,10},{9,11},{10,... | collective-permute-start | bytes 1105928 | tf_op jit(solution)/shard_map/ppermute | solution.py:831
  199.6 28.2 %collective-permute-start.22 = (bf16[288,640]{1,0:T(8,128)(2,1)S(1)}, bf16[288,640]{1,0:T(8,128)(2,1)S(1)}, u32[]{:S(2)}, u32[]{:S(2)}) collective-permute-start(bf16[288,640]{1,0:T(8,128)(2,1)S(1)} %fusion.53), channel_id=1, source_target_pairs={{0,4},{1,5},{2,6},{3,7},{4,0},{5,1},{6,2},{7,3},{8,12},{9,13},{10,... | collective-permute-start | bytes 1105928 | tf_op jit(solution)/shard_map/ppermute | solution.py:831
  200.8 27.0 %collective-permute-start.23 = (bf16[288,640]{1,0:T(8,128)(2,1)S(1)}, bf16[288,640]{1,0:T(8,128)(2,1)S(1)}, u32[]{:S(2)}, u32[]{:S(2)}) collective-permute-start(bf16[288,640]{1,0:T(8,128)(2,1)S(1)} %fusion.53), channel_id=1, source_target_pairs={{0,6},{1,7},{2,4},{3,5},{4,2},{5,3},{6,0},{7,1},{8,14},{9,15},{10,... | collective-permute-start | bytes 1105928 | tf_op jit(solution)/shard_map/ppermute | solution.py:831
  230.9 81.8 %collective-permute-start.27 = (bf16[2,2,288,1280]{3,2,1,0:T(8,128)(2,1)S(1)}, bf16[2,2,288,1280]{3,2,1,0:T(8,128)(2,1)}, u32[]{:S(2)}, u32[]{:S(2)}) collective-permute-start(bf16[2,2,288,1280]{3,2,1,0:T(8,128)(2,1)S(1)} %pad_maximum_fusion.refs_4_.refs_8_), channel_id=1, source_target_pairs={{0,16},{8,24},{16,0},{24,8},{1,17},{9,25},{17,1},{25,9},{2,18},{10... | collective-permute-start | bytes 8847368 | tf_op jit(solution)/shard_map/ppermute | solution.py:831
  235.7 77.0 %collective-permute-start.28 = (bf16[2,2,288,1280]{3,2,1,0:T(8,128)(2,1)}, bf16[2,2,288,1280]{3,2,1,0:T(8,128)(2,1)}, u32[]{:S(2)}, u32[]{:S(2)}) collective-permute-start(bf16[2,2,288,1280]{3,2,1,0:T(8,128)(2,1)} %pad_maximum_fusion.1.refs_6_.refs_10_), channel_id=1, source_target_pairs={{0,8},{8,0},{16,24},{24,16},{1,9},{9,1},{17,25},{25,17},{2,10},{10... | collective-permute-start | bytes 8847368 | tf_op jit(solution)/shard_map/ppermute | solution.py:831
  236.4 35.9 %collective-permute-start.24 = (bf16[256,2304]{1,0:T(8,128)(2,1)}, bf16[256,2304]{1,0:T(8,128)(2,1)}, u32[]{:S(2)}, u32[]{:S(2)}) collective-permute-start(bf16[256,2304]{1,0:T(8,128)(2,1)} %get-tuple-element.168.refs_1_.refs_4_), channel_id=1, source_target_pairs={{0,2},{1,3},{2,0},{3,1},{4,6},{5,7},{6,4},{7,5},{8,10},{9,11},{10,... | collective-permute-start | bytes 3538952 | tf_op jit(solution)/shard_map/ppermute | solution.py:831
  245.5 32.0 %collective-permute-start.25 = (bf16[256,2304]{1,0:T(8,128)(2,1)}, bf16[256,2304]{1,0:T(8,128)(2,1)}, u32[]{:S(2)}, u32[]{:S(2)}) collective-permute-start(bf16[256,2304]{1,0:T(8,128)(2,1)} %get-tuple-element.168.refs_1_.refs_4_), channel_id=1, source_target_pairs={{0,1},{1,0},{2,3},{3,2},{4,5},{5,4},{6,7},{7,6},{8,9},{9,8},{10,11... | collective-permute-start | bytes 3538952 | tf_op jit(solution)/shard_map/ppermute | solution.py:831
  273.3 39.5 %all-to-all-start = ((bf16[32,8,1152]{2,1,0:T(8,128)(2,1)}), bf16[32,8,1152]{2,1,0:T(8,128)(2,1)S(1)}, u32[]{:S(2)}, u32[]{:S(2)}) async-start(bf16[32,8,1152]{2,1,0:T(8,128)(2,1)} %bitcast.290), calls=%async_computation.1 | async-start | bytes 1179648 | tf_op jit(solution)/shard_map/all_to_all | solution.py:836
  312.8 47.0 %collective-permute-start.29 = (bf16[2,2,288,1280]{3,2,1,0:T(8,128)(2,1)S(1)}, bf16[2,2,288,1280]{3,2,1,0:T(8,128)(2,1)S(1)}, u32[]{:S(2)}, u32[]{:S(2)}) collective-permute-start(bf16[2,2,288,1280]{3,2,1,0:T(8,128)(2,1)S(1)} %pad_maximum_fusion.refs_4_.refs_8_), channel_id=1, source_target_pairs={{0,1},{1,0},{2,3},{3,2},{4,5},{5,4},{6,7},{7,6},{8,9},{9,8},{10,11... | collective-permute-start | bytes 8847368 | tf_op jit(solution)/shard_map/ppermute | solution.py:831
  315.0 45.4 %collective-permute-start.30 = (bf16[2,2,288,1280]{3,2,1,0:T(8,128)(2,1)}, bf16[2,2,288,1280]{3,2,1,0:T(8,128)(2,1)}, u32[]{:S(2)}, u32[]{:S(2)}) collective-permute-start(bf16[2,2,288,1280]{3,2,1,0:T(8,128)(2,1)} %collective-permute-done.27.refs_5_.refs_9_), channel_id=1, source_target_pairs={{0,1},{1,0},{2,3},{3,2},{4,5},{5,4},{6,7},{7,6},{8,9},{9,8},{10,11... | collective-permute-start | bytes 8847368 | tf_op jit(solution)/shard_map/ppermute | solution.py:831
  315.0 45.4 %collective-permute-start.31 = (bf16[2,2,288,1280]{3,2,1,0:T(8,128)(2,1)}, bf16[2,2,288,1280]{3,2,1,0:T(8,128)(2,1)}, u32[]{:S(2)}, u32[]{:S(2)}) collective-permute-start(bf16[2,2,288,1280]{3,2,1,0:T(8,128)(2,1)} %pad_maximum_fusion.1.refs_6_.refs_10_), channel_id=1, source_target_pairs={{0,1},{1,0},{2,3},{3,2},{4,5},{5,4},{6,7},{7,6},{8,9},{9,8},{10,11... | collective-permute-start | bytes 8847368 | tf_op jit(solution)/shard_map/ppermute | solution.py:831
  315.5 44.9 %collective-permute-start.32 = (bf16[2,2,288,1280]{3,2,1,0:T(8,128)(2,1)}, bf16[2,2,288,1280]{3,2,1,0:T(8,128)(2,1)}, u32[]{:S(2)}, u32[]{:S(2)}) collective-permute-start(bf16[2,2,288,1280]{3,2,1,0:T(8,128)(2,1)} %collective-permute-done.28.refs_7_.refs_11_), channel_id=1, source_target_pairs={{0,1},{1,0},{2,3},{3,2},{4,5},{5,4},{6,7},{7,6},{8,9},{9,8},{10,11... | collective-permute-start | bytes 8847368 | tf_op jit(solution)/shard_map/ppermute | solution.py:831
  356.2 34.2 %collective-permute-start.35 = (bf16[2,2,288,640]{3,2,1,0:T(8,128)(2,1)}, bf16[2,2,288,640]{3,2,1,0:T(8,128)(2,1)}, u32[]{:S(2)}, u32[]{:S(2)}) collective-permute-start(bf16[2,2,288,640]{3,2,1,0:T(8,128)(2,1)} %pad_maximum_fusion.6.refs_3_), channel_id=1, source_target_pairs={{0,16},{8,24},{16,0},{24,8},{1,17},{9,25},{17,1},{25,9},{2,18},{10... | collective-permute-start | bytes 4423688 | tf_op jit(solution)/shard_map/ppermute | solution.py:831
  359.8 33.8 %collective-permute-start.36 = (bf16[2,2,288,640]{3,2,1,0:T(8,128)(2,1)}, bf16[2,2,288,640]{3,2,1,0:T(8,128)(2,1)S(1)}, u32[]{:S(2)}, u32[]{:S(2)}) collective-permute-start(bf16[2,2,288,640]{3,2,1,0:T(8,128)(2,1)} %pad_maximum_fusion.7.refs_5_), channel_id=1, source_target_pairs={{0,8},{8,0},{16,24},{24,16},{1,9},{9,1},{17,25},{25,17},{2,10},{10... | collective-permute-start | bytes 4423688 | tf_op jit(solution)/shard_map/ppermute | solution.py:831
  393.6 29.2 %collective-permute-start.37 = (bf16[2,2,288,640]{3,2,1,0:T(8,128)(2,1)}, bf16[2,2,288,640]{3,2,1,0:T(8,128)(2,1)S(1)}, u32[]{:S(2)}, u32[]{:S(2)}) collective-permute-start(bf16[2,2,288,640]{3,2,1,0:T(8,128)(2,1)} %pad_maximum_fusion.6.refs_3_), channel_id=1, source_target_pairs={{0,1},{1,0},{2,3},{3,2},{4,5},{5,4},{6,7},{7,6},{8,9},{9,8},{10,11... | collective-permute-start | bytes 4423688 | tf_op jit(solution)/shard_map/ppermute | solution.py:831
  393.6 29.2 %collective-permute-start.38 = (bf16[2,2,288,640]{3,2,1,0:T(8,128)(2,1)}, bf16[2,2,288,640]{3,2,1,0:T(8,128)(2,1)}, u32[]{:S(2)}, u32[]{:S(2)}) collective-permute-start(bf16[2,2,288,640]{3,2,1,0:T(8,128)(2,1)} %collective-permute-done.35.refs_4_), channel_id=1, source_target_pairs={{0,1},{1,0},{2,3},{3,2},{4,5},{5,4},{6,7},{7,6},{8,9},{9,8},{10,11... | collective-permute-start | bytes 4423688 | tf_op jit(solution)/shard_map/ppermute | solution.py:831
  394.1 28.7 %collective-permute-start.39 = (bf16[2,2,288,640]{3,2,1,0:T(8,128)(2,1)}, bf16[2,2,288,640]{3,2,1,0:T(8,128)(2,1)}, u32[]{:S(2)}, u32[]{:S(2)}) collective-permute-start(bf16[2,2,288,640]{3,2,1,0:T(8,128)(2,1)} %pad_maximum_fusion.7.refs_5_), channel_id=1, source_target_pairs={{0,1},{1,0},{2,3},{3,2},{4,5},{5,4},{6,7},{7,6},{8,9},{9,8},{10,11... | collective-permute-start | bytes 4423688 | tf_op jit(solution)/shard_map/ppermute | solution.py:831
  394.1 28.7 %collective-permute-start.40 = (bf16[2,2,288,640]{3,2,1,0:T(8,128)(2,1)S(1)}, bf16[2,2,288,640]{3,2,1,0:T(8,128)(2,1)}, u32[]{:S(2)}, u32[]{:S(2)}) collective-permute-start(bf16[2,2,288,640]{3,2,1,0:T(8,128)(2,1)S(1)} %collective-permute-done.36.refs_6_), channel_id=1, source_target_pairs={{0,1},{1,0},{2,3},{3,2},{4,5},{5,4},{6,7},{7,6},{8,9},{9,8},{10,11... | collective-permute-start | bytes 4423688 | tf_op jit(solution)/shard_map/ppermute | solution.py:831
  394.6 28.2 %all-to-all-start.1 = ((bf16[32,8,1152]{2,1,0:T(8,128)(2,1)}), bf16[32,8,1152]{2,1,0:T(8,128)(2,1)S(1)}, u32[]{:S(2)}, u32[]{:S(2)}) async-start(bf16[32,8,1152]{2,1,0:T(8,128)(2,1)} %bitcast.302), calls=%async_computation.2 | async-start | bytes 1179648 | tf_op jit(solution)/shard_map/all_to_all | solution.py:836
  473.2 277.4 %reduce-scatter.5.cloned.1.call-start = ((), (), s32[]{:S(2)}) async-start(), calls=%async_computation.8 | async-start | bytes 3538944 | tf_op jit(solution)/shard_map/reduce_scatter | solution.py:1154
  499.2 40.8 %collective-permute-start.42 = (bf16[2,2,288,640]{3,2,1,0:T(8,128)(2,1)}, bf16[2,2,288,640]{3,2,1,0:T(8,128)(2,1)}, u32[]{:S(2)}, u32[]{:S(2)}) collective-permute-start(bf16[2,2,288,640]{3,2,1,0:T(8,128)(2,1)} %add_convert_fusion.6), channel_id=1, source_target_pairs={{0,16},{8,24},{16,0},{24,8},{1,17},{9,25},{17,1},{25,9},{2,18},{10... | collective-permute-start | bytes 4423688 | tf_op jit(solution)/shard_map/ppermute | solution.py:831
  507.4 32.5 %collective-permute-start.44 = (bf16[2,288,640]{2,1,0:T(8,128)(2,1)}, bf16[2,288,640]{2,1,0:T(8,128)(2,1)S(1)}, u32[]{:S(2)}, u32[]{:S(2)}) collective-permute-start(bf16[2,288,640]{2,1,0:T(8,128)(2,1)} %get-tuple-element.352), channel_id=1, source_target_pairs={{0,8},{8,0},{16,24},{24,16},{1,9},{9,1},{17,25},{25,17},{2,10},{10... | collective-permute-start | bytes 2211848 | tf_op jit(solution)/shard_map/ppermute | solution.py:831
  539.9 38.4 %collective-permute-start.47 = (bf16[4,1152,1280]{2,1,0:T(8,128)(2,1)}, bf16[4,1152,1280]{2,1,0:T(8,128)(2,1)}, u32[]{:S(2)}, u32[]{:S(2)}) collective-permute-start(bf16[4,1152,1280]{2,1,0:T(8,128)(2,1)} %get-tuple-element.222), channel_id=1, source_target_pairs={{0,1},{1,0},{2,3},{3,2},{4,5},{5,4},{6,7},{7,6},{8,9},{9,8},{10,11... | collective-permute-start | bytes 35389448 | tf_op jit(solution)/shard_map/ppermute | solution.py:831
  543.3 35.1 %collective-permute-start.45 = (bf16[2,288,640]{2,1,0:T(8,128)(2,1)}, bf16[2,288,640]{2,1,0:T(8,128)(2,1)S(1)}, u32[]{:S(2)}, u32[]{:S(2)}) collective-permute-start(bf16[2,288,640]{2,1,0:T(8,128)(2,1)} %fusion.34), channel_id=1, source_target_pairs={{0,8},{8,0},{16,24},{24,16},{1,9},{9,1},{17,25},{25,17},{2,10},{10... | collective-permute-start | bytes 2211848 | tf_op jit(solution)/shard_map/ppermute | solution.py:831
  547.5 30.9 %collective-permute-start.46 = (bf16[2,288,640]{2,1,0:T(8,128)(2,1)}, bf16[2,288,640]{2,1,0:T(8,128)(2,1)}, u32[]{:S(2)}, u32[]{:S(2)}) collective-permute-start(bf16[2,288,640]{2,1,0:T(8,128)(2,1)} %fusion.18), channel_id=1, source_target_pairs={{0,16},{8,24},{16,0},{24,8},{1,17},{9,25},{17,1},{25,9},{2,18},{10... | collective-permute-start | bytes 2211848 | tf_op jit(solution)/shard_map/ppermute | solution.py:831
  578.4 77.3 %collective-permute-start.54 = (bf16[4,1152,384]{2,1,0:T(8,128)(2,1)}, bf16[4,1152,384]{2,1,0:T(8,128)(2,1)}, u32[]{:S(2)}, u32[]{:S(2)}) collective-permute-start(bf16[4,1152,384]{2,1,0:T(8,128)(2,1)} %get-tuple-element.242), channel_id=1, source_target_pairs={{0,1},{1,0},{2,3},{3,2},{4,5},{5,4},{6,7},{7,6},{8,9},{9,8},{10,11... | collective-permute-start | bytes 10616840 | tf_op jit(solution)/shard_map/ppermute | solution.py:831
  582.8 72.8 %collective-permute-start.51 = (bf16[2,2,288,1280]{3,2,0,1:T(8,128)(2,1)}, bf16[2,2,288,1280]{3,2,0,1:T(8,128)(2,1)}, u32[]{:S(2)}, u32[]{:S(2)}) collective-permute-start(bf16[2,2,288,1280]{3,2,0,1:T(8,128)(2,1)} %add_convert_fusion), channel_id=1, source_target_pairs={{0,16},{8,24},{16,0},{24,8},{1,17},{9,25},{17,1},{25,9},{2,18},{10... | collective-permute-start | bytes 8847368 | tf_op jit(solution)/shard_map/ppermute | solution.py:831
  589.5 65.4 %collective-permute-start.52 = (bf16[2,288,1280]{2,1,0:T(8,128)(2,1)}, bf16[2,288,1280]{2,1,0:T(8,128)(2,1)}, u32[]{:S(2)}, u32[]{:S(2)}) collective-permute-start(bf16[2,288,1280]{2,1,0:T(8,128)(2,1)} %get-tuple-element.349), channel_id=1, source_target_pairs={{0,8},{8,0},{16,24},{24,16},{1,9},{9,1},{17,25},{25,17},{2,10},{10... | collective-permute-start | bytes 4423688 | tf_op jit(solution)/shard_map/ppermute | solution.py:831
  589.8 65.9 %collective-permute-start.53 = (bf16[2,288,1280]{2,1,0:T(8,128)(2,1)}, bf16[2,288,1280]{2,1,0:T(8,128)(2,1)}, u32[]{:S(2)}, u32[]{:S(2)}) collective-permute-start(bf16[2,288,1280]{2,1,0:T(8,128)(2,1)} %get-tuple-element.348), channel_id=1, source_target_pairs={{0,8},{8,0},{16,24},{24,16},{1,9},{9,1},{17,25},{25,17},{2,10},{10... | collective-permute-start | bytes 4423688 | tf_op jit(solution)/shard_map/ppermute | solution.py:831
  623.0 31.9 %collective-permute-start.50 = (bf16[288,640]{1,0:T(8,128)(2,1)S(1)}, bf16[288,640]{1,0:T(8,128)(2,1)S(1)}, u32[]{:S(2)}, u32[]{:S(2)}) collective-permute-start(bf16[288,640]{1,0:T(8,128)(2,1)S(1)} %get-tuple-element.240), channel_id=1, source_target_pairs={{0,6},{1,7},{2,4},{3,5},{4,2},{5,3},{6,0},{7,1},{8,14},{9,15},{10,... | collective-permute-start | bytes 1105928 | tf_op jit(solution)/shard_map/ppermute | solution.py:831
  661.8 197.9 %all-gather.10.cloned.1.call-start = ((), (), s32[]{:S(2)}) async-start(), calls=%async_computation.10 | async-start | bytes 1368576 | tf_op jit(solution)/shard_map/all_gather | solution.py:1238
  664.7 85.8 %collective-permute-start.57 = (bf16[2,288,1280]{2,1,0:T(8,128)(2,1)S(1)}, bf16[2,288,1280]{2,1,0:T(8,128)(2,1)}, u32[]{:S(2)}, u32[]{:S(2)}) collective-permute-start(bf16[2,288,1280]{2,1,0:T(8,128)(2,1)S(1)} %fusion.6), channel_id=1, source_target_pairs={{0,8},{8,0},{16,24},{24,16},{1,9},{9,1},{17,25},{25,17},{2,10},{10... | collective-permute-start | bytes 4423688 | tf_op jit(solution)/shard_map/ppermute | solution.py:831
  667.8 82.7 %collective-permute-start.58 = (bf16[2,288,1280]{2,1,0:T(8,128)(2,1)S(1)}, bf16[2,288,1280]{2,1,0:T(8,128)(2,1)}, u32[]{:S(2)}, u32[]{:S(2)}) collective-permute-start(bf16[2,288,1280]{2,1,0:T(8,128)(2,1)S(1)} %fusion.3), channel_id=1, source_target_pairs={{0,16},{8,24},{16,0},{24,8},{1,17},{9,25},{17,1},{25,9},{2,18},{10... | collective-permute-start | bytes 4423688 | tf_op jit(solution)/shard_map/ppermute | solution.py:831
  672.4 52.9 %collective-permute-start.56 = (bf16[256,2304]{1,0:T(8,128)(2,1)S(1)}, bf16[256,2304]{1,0:T(8,128)(2,1)S(1)}, u32[]{:S(2)}, u32[]{:S(2)}) collective-permute-start(bf16[256,2304]{1,0:T(8,128)(2,1)S(1)} %get-tuple-element.362), channel_id=1, source_target_pairs={{0,2},{1,3},{2,0},{3,1},{4,6},{5,7},{6,4},{7,5},{8,10},{9,11},{10,... | collective-permute-start | bytes 3538952 | tf_op jit(solution)/shard_map/ppermute | solution.py:831
  750.5 58.8 %collective-permute-start.59 = (bf16[4,1152,640]{2,1,0:T(8,128)(2,1)}, bf16[4,1152,640]{2,1,0:T(8,128)(2,1)}, u32[]{:S(2)}, u32[]{:S(2)}) collective-permute-start(bf16[4,1152,640]{2,1,0:T(8,128)(2,1)} %get-tuple-element.257), channel_id=1, source_target_pairs={{0,1},{1,0},{2,3},{3,2},{4,5},{5,4},{6,7},{7,6},{8,9},{9,8},{10,11... | collective-permute-start | bytes 17694728 | tf_op jit(solution)/shard_map/ppermute | solution.py:831
  778.3 30.1 %collective-permute-start.61 = (bf16[2,2,288,384]{3,2,1,0:T(8,128)(2,1)S(1)}, bf16[2,2,288,384]{3,2,1,0:T(8,128)(2,1)S(1)}, u32[]{:S(2)}, u32[]{:S(2)}) collective-permute-start(bf16[2,2,288,384]{3,2,1,0:T(8,128)(2,1)S(1)} %add_convert_fusion.7), channel_id=1, source_target_pairs={{0,16},{8,24},{16,0},{24,8},{1,17},{9,25},{17,1},{25,9},{2,18},{10... | collective-permute-start | bytes 2654216 | tf_op jit(solution)/shard_map/ppermute | solution.py:831
  812.3 54.7 %collective-permute-start.64 = (bf16[2,2,288,640]{3,2,1,0:T(8,128)(2,1)}, bf16[2,2,288,640]{3,2,1,0:T(8,128)(2,1)}, u32[]{:S(2)}, u32[]{:S(2)}) collective-permute-start(bf16[2,2,288,640]{3,2,1,0:T(8,128)(2,1)} %add_convert_fusion.2), channel_id=1, source_target_pairs={{0,16},{8,24},{16,0},{24,8},{1,17},{9,25},{17,1},{25,9},{2,18},{10... | collective-permute-start | bytes 4423688 | tf_op jit(solution)/shard_map/ppermute | solution.py:831
  815.8 51.1 %collective-permute-start.65 = (bf16[2,288,640]{2,1,0:T(8,128)(2,1)}, bf16[2,288,640]{2,1,0:T(8,128)(2,1)}, u32[]{:S(2)}, u32[]{:S(2)}) collective-permute-start(bf16[2,288,640]{2,1,0:T(8,128)(2,1)} %get-tuple-element.351), channel_id=1, source_target_pairs={{0,8},{8,0},{16,24},{24,16},{1,9},{9,1},{17,25},{25,17},{2,10},{10... | collective-permute-start | bytes 2211848 | tf_op jit(solution)/shard_map/ppermute | solution.py:831
  817.3 49.7 %collective-permute-start.66 = (bf16[2,288,640]{2,1,0:T(8,128)(2,1)}, bf16[2,288,640]{2,1,0:T(8,128)(2,1)}, u32[]{:S(2)}, u32[]{:S(2)}) collective-permute-start(bf16[2,288,640]{2,1,0:T(8,128)(2,1)} %get-tuple-element.350), channel_id=1, source_target_pairs={{0,8},{8,0},{16,24},{24,16},{1,9},{9,1},{17,25},{25,17},{2,10},{10... | collective-permute-start | bytes 2211848 | tf_op jit(solution)/shard_map/ppermute | solution.py:831
  817.8 49.1 %collective-permute-start.67 = (bf16[288,1280]{1,0:T(8,128)(2,1)}, bf16[288,1280]{1,0:T(8,128)(2,1)}, u32[]{:S(2)}, u32[]{:S(2)}) collective-permute-start(bf16[288,1280]{1,0:T(8,128)(2,1)} %get-tuple-element.266), channel_id=1, source_target_pairs={{0,4},{1,5},{2,6},{3,7},{4,0},{5,1},{6,2},{7,3},{8,12},{9,13},{10,... | collective-permute-start | bytes 2211848 | tf_op jit(solution)/shard_map/ppermute | solution.py:831
  823.5 35.0 %collective-permute-start.68 = (bf16[2,288,384]{2,1,0:T(8,128)(2,1)}, bf16[2,288,384]{2,1,0:T(8,128)(2,1)}, u32[]{:S(2)}, u32[]{:S(2)}) collective-permute-start(bf16[2,288,384]{2,1,0:T(8,128)(2,1)} %fusion.49), channel_id=1, source_target_pairs={{0,8},{8,0},{16,24},{24,16},{1,9},{9,1},{17,25},{25,17},{2,10},{10... | collective-permute-start | bytes 1327112 | tf_op jit(solution)/shard_map/ppermute | solution.py:831
  869.7 52.8 %collective-permute-start.70 = (bf16[2,288,640]{2,1,0:T(8,128)(2,1)}, bf16[2,288,640]{2,1,0:T(8,128)(2,1)}, u32[]{:S(2)}, u32[]{:S(2)}) collective-permute-start(bf16[2,288,640]{2,1,0:T(8,128)(2,1)} %fusion.37), channel_id=1, source_target_pairs={{0,8},{8,0},{16,24},{24,16},{1,9},{9,1},{17,25},{25,17},{2,10},{10... | collective-permute-start | bytes 2211848 | tf_op jit(solution)/shard_map/ppermute | solution.py:831
  873.8 48.6 %collective-permute-start.71 = (bf16[2,288,640]{2,1,0:T(8,128)(2,1)}, bf16[2,288,640]{2,1,0:T(8,128)(2,1)}, u32[]{:S(2)}, u32[]{:S(2)}) collective-permute-start(bf16[2,288,640]{2,1,0:T(8,128)(2,1)} %fusion.14), channel_id=1, source_target_pairs={{0,16},{8,24},{16,0},{24,8},{1,17},{9,25},{17,1},{25,9},{2,18},{10... | collective-permute-start | bytes 2211848 | tf_op jit(solution)/shard_map/ppermute | solution.py:831
  875.5 47.0 %collective-permute-start.72 = (bf16[288,1280]{1,0:T(8,128)(2,1)}, bf16[288,1280]{1,0:T(8,128)(2,1)}, u32[]{:S(2)}, u32[]{:S(2)}) collective-permute-start(bf16[288,1280]{1,0:T(8,128)(2,1)} %get-tuple-element.272), channel_id=1, source_target_pairs={{0,6},{1,7},{2,4},{3,5},{4,2},{5,3},{6,0},{7,1},{8,14},{9,15},{10,... | collective-permute-start | bytes 2211848 | tf_op jit(solution)/shard_map/ppermute | solution.py:831
  882.1 38.5 %collective-permute-start.74 = (bf16[288,384]{1,0:T(8,128)(2,1)S(1)}, bf16[288,384]{1,0:T(8,128)(2,1)S(1)}, u32[]{:S(2)}, u32[]{:S(2)}) collective-permute-start(bf16[288,384]{1,0:T(8,128)(2,1)S(1)} %get-tuple-element.279), channel_id=1, source_target_pairs={{0,4},{1,5},{2,6},{3,7},{4,0},{5,1},{6,2},{7,3},{8,12},{9,13},{10,... | collective-permute-start | bytes 663560 | tf_op jit(solution)/shard_map/ppermute | solution.py:831
  929.7 32.2 %collective-permute-start.77 = (bf16[288,640]{1,0:T(8,128)(2,1)S(1)}, bf16[288,640]{1,0:T(8,128)(2,1)S(1)}, u32[]{:S(2)}, u32[]{:S(2)}) collective-permute-start(bf16[288,640]{1,0:T(8,128)(2,1)S(1)} %get-tuple-element.374), channel_id=1, source_target_pairs={{0,4},{1,5},{2,6},{3,7},{4,0},{5,1},{6,2},{7,3},{8,12},{9,13},{10,... | collective-permute-start | bytes 1105928 | tf_op jit(solution)/shard_map/ppermute | solution.py:831
  932.7 29.2 %collective-permute-start.76 = (bf16[288,640]{1,0:T(8,128)(2,1)S(1)}, bf16[288,640]{1,0:T(8,128)(2,1)S(1)}, u32[]{:S(2)}, u32[]{:S(2)}) collective-permute-start(bf16[288,640]{1,0:T(8,128)(2,1)S(1)} %slice_bitcast_fusion.18), channel_id=1, source_target_pairs={{0,2},{1,3},{2,0},{3,1},{4,6},{5,7},{6,4},{7,5},{8,10},{9,11},{10,... | collective-permute-start | bytes 1105928 | tf_op jit(solution)/shard_map/ppermute | solution.py:831
  (89 other events, 1279.5 us)
Sparse Core Ops, SparseCore 0:
  11.6 96.3 all-gather.5
  183.4 40.1 reduce-scatter.2
  228.0 74.3 all-gather.7
  661.9 63.3 reduce-scatter.4
  776.6 69.9 all-gather.9

commit v3 on v2

--- a/solution.py
+++ b/solution.py
@@ -93,12 +93,12 @@
 
 class Pieces:
     def __init__(self, sources, me, window, buffer, sems, nx):
-        rows = sources[0].shape[2]
+        rows = buffer.shape[1] // 4
         columns = slice(window.start, window.stop)
         for k, i, j, far_x, far_y in piece_places(nx):
             x, y = me[0] ^ far_x, me[1] ^ far_y
             pltpu.make_async_copy(
-                sources[k].at[i, j, :, columns],
+                sources[k].at[i, j, :rows, columns],
                 buffer.at[x, pl.ds(pl.multiple_of(y * rows, 16), rows), :],
                 sems.at[x],
             ).start()
@@ -122,17 +122,17 @@
 
 
 class Folded:
-    def __init__(self, sources, me, start, buffer, sems, nx):
-        rows = sources[0].shape[2] // 2
+    def __init__(self, sources, me, buffer, sems, nx):
+        rows = buffer.shape[1] // nx
+        base = sources[0].shape[2] - 2 * rows
         width = buffer.shape[2]
         fold = fold_width(width)
         for k, i, j, far_x, far_y in piece_places(nx):
             x, y = me[0] ^ far_x, me[1] ^ far_y
             place = pl.ds(pl.multiple_of(x * rows, 16), rows)
-            for top, columns in ((0, slice(0, fold)), (rows, slice(fold, width))):
-                lanes = slice(start, start + columns.stop - columns.start)
+            for top, columns in ((base, slice(0, fold)), (base + rows, slice(fold, width))):
                 pltpu.make_async_copy(
-                    sources[k].at[i, j, top : top + rows, lanes],
+                    sources[k].at[i, j, top : top + rows, : columns.stop - columns.start],
                     buffer.at[y, place, columns],
                     sems.at[y],
                 ).start()
@@ -146,9 +146,9 @@
     return padded(width // 2)
 
 
-def down_blocks(up_refs, down_ref, me_ref, start, buf, sems, nx):
+def down_blocks(up_refs, down_ref, me_ref, buf, sems, nx):
     if down_ref is None:
-        return Folded(up_refs, me_ref, start, buf, sems, nx)
+        return Folded(up_refs, me_ref, buf, sems, nx)
     return Blocks(down_ref, buf, sems)
 
 
@@ -296,7 +296,7 @@
 ):
     ups = Pieces(up_refs, me_ref, win, up_buf, up_sems, nx)
     width = down_buf.shape[2]
-    downs = down_blocks(up_refs, down_ref, me_ref, win.stop, down_buf, down_sems, nx)
+    downs = down_blocks(up_refs, down_ref, me_ref, down_buf, down_sems, nx)
     hidden = h_ref[...]
     for x in range(nx):
         ups.wait(x)
@@ -316,10 +316,11 @@
 
 
 def temporal_kernel(
-    win_all, win, w_out, nx, frames, me_ref, h_ref, da_ref, w_refs, row_clip, frame_clip,
-    o_ref, at_ref, dqkv_ref, dh_ref, buf, sems, pad, q_s, k_s, v_s, do_s, o_s, dq_s, dk_s, dv_s, qkv_s,
+    win, w_out, nx, frames, h_ref, da_ref, w_ref, row_clip, frame_clip,
+    grad_ref, at_ref, dh_ref, buf, sems, pad, q_s, k_s, v_s, do_s, o_s, dq_s, dk_s, dv_s, qkv_s,
 ):
-    pieces = Pieces(w_refs, me_ref, win_all, buf, sems, nx)
+    pieces = Blocks(w_ref, buf, sems)
+    o_ref, dqkv_ref = grad_ref.at[:, :D], grad_ref.at[:, D:]
     rows = h_ref.shape[0]
     spots = rows // frames
     hidden = h_ref[...]
@@ -407,10 +408,12 @@
 
 def ff_back_kernel(
     win, nx, ny, me_ref, g_ref, dh4_ref, x3_ref, x2_ref, u_ref, m_ref, mod_ref, up_refs, down_ref,
-    dm_ref, du_ref, dx2_ref, sum_ref, up_buf, down_buf, up_sems, down_sems, du_s, pad,
+    grad_ref, dx2_ref, sum_ref, up_buf, down_buf, up_sems, down_sems, pad,
 ):
+    ff = u_ref.shape[1]
+    du_s, dm_ref = grad_ref.at[:, :ff], grad_ref.at[:, ff:]
     width = down_buf.shape[2]
-    downs = down_blocks(up_refs, down_ref, me_ref, win.stop, down_buf, down_sems, nx)
+    downs = down_blocks(up_refs, down_ref, me_ref, down_buf, down_sems, nx)
     ups = Pieces(up_refs, me_ref, win, up_buf, up_sems, nx)
     dh4 = dh4_ref[...].astype(f32)
     normed, inv_std = stats(x3_ref[...])
@@ -434,7 +437,6 @@
     for x in range(nx):
         ups.wait(x)
         take(pad, win.off, [du_s], x * win.n, win.n)
-        du_ref[x] = pad[:, win.off : win.off + win.n]
         total = total + mm_nt(pad[...], up_buf[x])
     normed, inv_std = stats(x2_ref[...])
     sum_ref[3:4, :] = column_sum(total)
@@ -445,9 +447,10 @@
 
 def text_back_kernel(
     outer, w_out, w_cq, w_cout, nx, me_ref, dx2_ref, x1_ref, a1_ref, mod_ref, w_refs, qc_ref, text_ref,
-    length_ref, dac_ref, dqc_ref, dx1_ref, da1_ref, do1_ref, dtext_ref, gate_ref,
+    length_ref, grad_ref, dx1_ref, do1_ref, dtext_ref, gate_ref,
     buf, sems, pad, acc, q_t, do_t, k_t, do_s, dtext_s,
 ):
+    dac_ref, dqc_ref, da1_ref = [grad_ref.at[:, i * D : (i + 1) * D] for i in range(3)]
     pieces = Pieces(w_refs, me_ref, outer, buf, sems, nx)
 
     def product(source, win, wait=False):
@@ -537,15 +540,17 @@
 
 def qkv_back_kernel(
     win, nx, me_ref, dq_ref, own_ref, come_ref, x_ref, mod_ref, dx1_ref, w_refs,
-    dkv_ref, gx_ref, sum_ref, buf, sems, pad,
+    grad_ref, gx_ref, sum_ref, buf, sems, pad,
 ):
+    dkv_ref = grad_ref.at[:, D:]
+    grad_ref[:, :D] = dq_ref[...]
     pieces = Pieces(w_refs, me_ref, win, buf, sems, nx)
     dkv_ref[...] = (own_ref[...].astype(f32) + come_ref[...].astype(f32)).astype(bf16)
     pad[...] = jnp.zeros(pad.shape, bf16)
     total = jnp.zeros(dx1_ref.shape, f32)
     for x in range(nx):
         pieces.wait(x)
-        take(pad, win.off, [dq_ref, dkv_ref], x * win.n, win.n)
+        take(pad, win.off, [grad_ref], x * win.n, win.n)
         total = total + mm_nt(pad[...], buf[x])
     normed, inv_std = stats(x_ref[...].astype(f32))
     sum_ref[0:1, :] = column_sum(total)
@@ -555,160 +560,214 @@
     ).astype(bf16)
 
 
-def step_block(step, me_x, nx):
-    half = nx // 2
-    return me_x ^ (2 * lax.rem(step, half) + (1 - step // half))
-
-
-def turn_rows(turn, value, me_y, ny):
+def turn_rows(turn, at, value, me_y, ny):
     rows = turn.shape[0] // ny
     flipped = value.astype(f32).T.astype(bf16)
     for y in range(ny):
-        turn[pl.ds(pl.multiple_of((y ^ me_y) * rows, 16), rows), :] = flipped[
-            y * rows : (y + 1) * rows
-        ]
-
-
-def weight_kernel(nx, ny, lanes, counts, me_ref, *refs):
-    lefts, k = [], 0
-    for count in counts:
-        lefts.append((refs[k], refs[k + 1 : k + 1 + count]))
-        k += 1 + count
-    send_ref, keep_ref = refs[k : k + 2]
-    pads, turned = refs[k + 2 :: 2], refs[k + 3 :: 2]
+        place = pl.ds(pl.multiple_of((y ^ me_y) * rows, 16), rows)
+        turn[place, at : at + value.shape[0]] = flipped[y * rows : (y + 1) * rows]
+
+
+def write_blocks(outs, half, columns, block, first=0):
+    some_send, rest_send, some_keep, rest_keep = outs
+    rows, each = block.shape[0] // 4, some_keep.shape[1] // 2
     step = pl.program_id(0)
-    x = step_block(step, me_ref[0], nx)
+
+    def write(ref, at, y):
+        start = at * each + first
+        ref[0, start : start + rows, columns] = block[y * rows : (y + 1) * rows]
+
+    @pl.when(step < half)
+    def _():
+        for at in range(2):
+            write(some_keep, at, at)
+            write(some_send, at, 2 + at)
+
+    @pl.when(step >= half)
+    def _():
+        for at in range(2):
+            write(rest_keep, at, 2 * at)
+            write(rest_send, at, 2 * at + 1)
+
+
+def block_outs(nx, depth, lanes):
+    half = nx // 4
+    size = (1, depth // 2, lanes)
+    some = pl.BlockSpec(size, lambda t, me: (jnp.minimum(t, half - 1), 0, 0))
+    rest = pl.BlockSpec(size, lambda t, me: (jnp.maximum(t - half, 0), 0, 0))
+    return [shape(half, depth // 2, lanes, dtype=bf16)] * 4, [some, rest, some, rest]
+
+
+def view(refs, place):
+    k, first, last = place
+    return refs[k].at[:, first:last]
+
+
+def weight_kernel(nx, ny, lanes, count, pairs, me_ref, *refs):
+    sides, outs = (refs[:count], refs[count : 2 * count]), refs[2 * count : 2 * count + 4]
+    pads, turned = refs[2 * count + 4 :: 2], refs[2 * count + 5 :: 2]
+    step = pl.program_id(0)
+    x = me_ref[0] ^ (2 * step)
+    rows = refs[0].shape[0]
 
     @pl.when(step == 0)
     def _():
-        for (left, _), turn in zip(lefts, turned):
-            turn_rows(turn, left[...], me_ref[1], ny)
-
-    for (_, rights), pad in zip(lefts, pads):
+        for (left, _), turn in zip(pairs, turned):
+            for i, side in enumerate(sides):
+                turn_rows(turn, i * rows, view(side, left)[...], me_ref[1], ny)
+
+    at = 0
+    for (_, right), pad, turn in zip(pairs, pads, turned):
         n = pad.shape[1]
         for i in range(nx):
 
             @pl.when(x == i)
             def _():
-                take(pad, 0, rights, i * n, n)
-
-    def fill(out_ref):
-        at = 0
-        for pad, turn in zip(pads, turned):
-            n = pad.shape[1]
-            out_ref[0, :, at : at + n] = mm(turn[...], pad[...]).astype(bf16)
-            at += n
-        if at < lanes:
-            out_ref[0, :, at:] = jnp.zeros((out_ref.shape[1], lanes - at), bf16)
-
-    @pl.when(step < nx // 2)
-    def _():
-        fill(send_ref)
-
-    @pl.when(step >= nx // 2)
-    def _():
-        fill(keep_ref)
-
-
-def weight_grads(nx, me, pairs):
-    widths = [sum(r.shape[1] for r in rights) // nx for _, rights in pairs]
+                for k, side in enumerate(sides):
+                    take(pad.at[k * rows : (k + 1) * rows], 0, [view(side, right)], i * n, n)
+
+        block = mm(turn[...], pad[...]).astype(bf16)
+        write_blocks(outs, nx // 4, slice(at, at + n), block)
+        at += n
+    if at < lanes:
+        write_blocks(outs, nx // 4, slice(at, lanes), jnp.zeros((D, lanes - at), bf16))
+
+
+def weight_grads(nx, me, own, other, pairs):
+    widths = [(last - first) // nx for _, (_, first, last) in pairs]
     lanes = padded(sum(widths))
-    rows = pairs[0][0].shape[0]
-    half = nx // 2
-    args, specs, scratch = [], [], []
-    for (left, rights), width in zip(pairs, widths):
-        args += [left, *rights]
-        specs += [vmem() for _ in range(1 + len(rights))]
-        scratch += [pltpu.VMEM((rows, width), bf16), pltpu.VMEM((D, rows), bf16)]
-    send, keep = pl.pallas_call(
-        functools.partial(
-            weight_kernel, nx, lax.axis_size("gy"), lanes, [len(r) for _, r in pairs]
-        ),
-        out_shape=[shape(half, D, lanes, dtype=bf16)] * 2,
+    rows = own[0].shape[0]
+    scratch = []
+    for width in widths:
+        scratch += [pltpu.VMEM((2 * rows, width), bf16), pltpu.VMEM((D, 2 * rows), bf16)]
+    outs, out_specs = block_outs(nx, D, lanes)
+    return pl.pallas_call(
+        functools.partial(weight_kernel, nx, lax.axis_size("gy"), lanes, len(own), pairs),
+        out_shape=outs,
         grid_spec=pltpu.PrefetchScalarGridSpec(
             num_scalar_prefetch=1,
-            grid=(nx,),
-            in_specs=specs,
-            out_specs=[
-                pl.BlockSpec((1, D, lanes), lambda t, me: (jnp.minimum(t, half - 1), 0, 0)),
-                pl.BlockSpec((1, D, lanes), lambda t, me: (jnp.maximum(t - half, 0), 0, 0)),
-            ],
+            grid=(nx // 2,),
+            in_specs=[vmem() for _ in range(2 * len(own))],
+            out_specs=out_specs,
             scratch_shapes=scratch,
         ),
         compiler_params=pltpu.CompilerParams(vmem_limit_bytes=56 << 20),
-        cost_estimate=cost(12),
-    )(me, *args)
-    return keep, send
-
-
-def up_grads(me, h3, du, dm, g):
-    nx, rows, n = du.shape
+        cost_estimate=cost(9),
+    )(me, *own, *other)
+
+
+def whole_kernel(nx, lanes, pairs, *refs):
+    count = 1 + max(k for pair in pairs for k, _, _ in pair)
+    ins, out_ref = refs[:count], refs[count]
+    pads, turned = refs[count + 1 :: 2], refs[count + 2 :: 2]
+    x = pl.program_id(0)
+
+    @pl.when(x == 0)
+    def _():
+        for (left, _), turn in zip(pairs, turned):
+            turn[...] = view(ins, left)[...].astype(f32).T.astype(bf16)
+
+    at = 0
+    for (_, right), pad, turn in zip(pairs, pads, turned):
+        n = pad.shape[1]
+        for i in range(nx):
+
+            @pl.when(x == i)
+            def _():
+                take(pad, 0, [view(ins, right)], i * n, n)
+
+        out_ref[0, :, at : at + n] = mm(turn[...], pad[...]).astype(bf16)
+        at += n
+    if at < lanes:
+        out_ref[0, :, at:] = jnp.zeros((D, lanes - at), bf16)
+
+
+def whole_grads(nx, arrays, pairs):
+    widths = [(last - first) // nx for _, (_, first, last) in pairs]
+    lanes = padded(sum(widths))
+    rows = arrays[0].shape[0]
+    scratch = []
+    for width in widths:
+        scratch += [pltpu.VMEM((rows, width), bf16), pltpu.VMEM((D, rows), bf16)]
+    return pl.pallas_call(
+        functools.partial(whole_kernel, nx, lanes, pairs),
+        out_shape=shape(nx, D, lanes, dtype=bf16),
+        grid=(nx,),
+        in_specs=[vmem() for _ in arrays],
+        out_specs=pl.BlockSpec((1, D, lanes), lambda x: (x, 0, 0)),
+        scratch_shapes=scratch,
+        compiler_params=pltpu.CompilerParams(vmem_limit_bytes=56 << 20),
+        cost_estimate=cost(13),
+    )(*arrays)
+
+
+def up_grads(nx, me, own, other, folding):
+    rows, ff = own[2].shape
+    n = ff // nx
     ny = lax.axis_size("gy")
     start = padded(n)
-    width = g.shape[1] // ny
+    width = ff // ny
     fold = fold_width(width)
-    lanes = start if dm is None else start + fold
-    half = nx // 2
     each = D // nx
-    args = (h3, du) if dm is None else (h3, du, dm, g)
-
-    def kernel(me_ref, h_ref, du_ref, *refs):
-        if dm is None:
-            send_ref, keep_ref, turn = refs
-        else:
-            dm_ref, g_ref, send_ref, keep_ref, turn, down_turn = refs
+
+    def kernel(me_ref, *refs):
+        sides, outs = (refs[:3], refs[3:6]), refs[6:10]
+        turn, pad, down_turn, down_pad = refs[-4:]
         step = pl.program_id(0)
+        x = me_ref[0] ^ (2 * step)
 
         @pl.when(step == 0)
         def _():
-            turn_rows(turn, h_ref[...], me_ref[1], ny)
-            if dm is not None:
-                down_turn[...] = dm_ref[...].astype(f32).T.astype(bf16)
-
-        def fill(out_ref):
-            out_ref[0, :, :n] = mm(turn[...], du_ref[0]).astype(bf16)
-            if n < lanes:
-                out_ref[0, :, n:] = jnp.zeros((D, lanes - n), bf16)
-            if dm is None:
-                return
-            x = step_block(step, me_ref[0], nx)
-            left = down_turn[pl.ds(pl.multiple_of(x * each, 16), each), :]
-            for y in range(ny):
-                block = mm(left, g_ref[:, y * width : (y + 1) * width]).astype(bf16)
-                top = pl.multiple_of((y ^ me_ref[1]) * 2 * each, 16)
-                out_ref[0, pl.ds(top, each), start:] = block[:, :fold]
-                low = pl.multiple_of((y ^ me_ref[1]) * 2 * each + each, 16)
-                out_ref[0, pl.ds(low, each), start : start + width - fold] = block[:, fold:]
-
-        @pl.when(step < half)
-        def _():
-            fill(send_ref)
-
-        @pl.when(step >= half)
-        def _():
-            fill(keep_ref)
-
-    send, keep = pl.pallas_call(
+            for k, (h_ref, grad_ref, _) in enumerate(sides):
+                turn_rows(turn, k * rows, h_ref[...], me_ref[1], ny)
+                if folding:
+                    down_turn[:, k * rows : (k + 1) * rows] = (
+                        grad_ref[:, ff:].astype(f32).T.astype(bf16)
+                    )
+
+        for i in range(nx):
+
+            @pl.when(x == i)
+            def _():
+                for k, (_, grad_ref, _) in enumerate(sides):
+                    pad[k * rows : (k + 1) * rows] = grad_ref[:, i * n : (i + 1) * n]
+
+        write_blocks(outs, nx // 4, slice(0, n), mm(turn[...], pad[...]).astype(bf16))
+        if n < start:
+            write_blocks(outs, nx // 4, slice(n, start), jnp.zeros((D, start - n), bf16))
+        if not folding:
+            return
+        left = down_turn[pl.ds(pl.multiple_of(x * each, 16), each), :]
+        for y in range(ny):
+            columns = slice(y * width, (y + 1) * width)
+            block = mm(left[:, :rows], sides[0][2][:, columns])
+            block = (block + mm(left[:, rows:], sides[1][2][:, columns])).astype(bf16)
+            top = (y ^ me_ref[1]) * 2 * each
+            down_pad[pl.ds(pl.multiple_of(top, 16), each), :] = block[:, :fold]
+            low = pl.multiple_of(top + each, 16)
+            down_pad[pl.ds(low, each), : width - fold] = block[:, fold:]
+            down_pad[pl.ds(low, each), width - fold :] = jnp.zeros((each, 2 * fold - width), bf16)
+        write_blocks(outs, nx // 4, slice(0, fold), down_pad[...], D // ny)
+
+    outs, out_specs = block_outs(nx, 2 * D if folding else D, start)
+    return pl.pallas_call(
         kernel,
-        out_shape=[shape(half, D, lanes, dtype=bf16)] * 2,
+        out_shape=outs,
         grid_spec=pltpu.PrefetchScalarGridSpec(
             num_scalar_prefetch=1,
-            grid=(nx,),
-            in_specs=[
-                vmem(),
-                pl.BlockSpec((1, rows, n), lambda t, me: (step_block(t, me[0], nx), 0, 0)),
-            ]
-            + [vmem()] * (len(args) - 2),
-            out_specs=[
-                pl.BlockSpec((1, D, lanes), lambda t, me: (jnp.minimum(t, half - 1), 0, 0)),
-                pl.BlockSpec((1, D, lanes), lambda t, me: (jnp.maximum(t - half, 0), 0, 0)),
+            grid=(nx // 2,),
+            in_specs=[vmem()] * 6,
+            out_specs=out_specs,
+            scratch_shapes=[
+                pltpu.VMEM((D, 2 * rows), bf16),
+                pltpu.VMEM((2 * rows, n), bf16),
+                pltpu.VMEM((D, 2 * rows), bf16),
+                pltpu.VMEM((D, fold), bf16),
             ],
-            scratch_shapes=[pltpu.VMEM((D, rows), bf16)] * (len(args) // 2),
         ),
         compiler_params=pltpu.CompilerParams(vmem_limit_bytes=56 << 20),
-        cost_estimate=cost(20),
-    )(me, *args)
-    return keep, send
+        cost_estimate=cost(16),
+    )(me, *own, *other)
 
 
 def down_grads(dm, g):
@@ -759,14 +818,21 @@
 
     def second(self, *others):
         far = after(self.far, *others)
-        some, rest = [jnp.stack(pair) for pair in zip(self.near, far)]
-        arrays = [swap(some, "gy", 2), swap(rest, "gy", 1)]
-        self.arrays = [some, arrays[0], rest, arrays[1]]
-        return arrays
-
-    def last(self, *others):
-        arrays = after(self.arrays, *others)
-        return tuple(arrays + [swap(array, "gx", 1) for array in arrays])
+        self.own = [jnp.stack(pair) for pair in zip(self.near, far)]
+        self.new = [swap(self.own[0], "gy", 2), swap(self.own[1], "gy", 1)]
+        return self.new
+
+    def own_core(self, *others):
+        self.own_other = [swap(array, "gx", 1) for array in after(self.own, *others)]
+        return self.own_other
+
+    def new_core(self, *others):
+        self.new_other = [swap(array, "gx", 1) for array in after(self.new, *others)]
+        return self.new_other
+
+    def arrays(self):
+        pairs = ((self.own, self.new), (self.own_other, self.new_other))
+        return tuple(side[i] for own, new in pairs for i in range(2) for side in (own, new))
 
 
 def gather_rows(shard):
@@ -780,37 +846,32 @@
 
 
 class Scatter:
-    def __init__(self, keep, send, *others):
-        nz, depth, lanes = keep.shape
-        ny = lax.axis_size("gy")
-        self.half = nz // 2
-        self.keep = keep.reshape(nz, ny, depth // ny, lanes)
-        self.come = swap(after(send, *others), "gx", 1).reshape(self.keep.shape)
+    def __init__(self, some_send, rest_send, some_keep, rest_keep):
+        self.sent = [some_send, rest_send]
+        self.kept = [some_keep, rest_keep]
+        half, depth, lanes = some_keep.shape
+        self.half, self.size = half, (half, 2, depth // 2, lanes)
 
     def first(self, *others):
-        keep, half = self.keep, self.half
-        come = self.come = after(self.come, *others)
-        some = swap(total(keep[:half, 2:], come[:half, 2:]), "gy", 2)
-        self.some_come = some.reshape(half, 2, *some.shape[-2:])
-        self.rest_come = [
-            swap(total(keep[half:, y], come[half:, y]), "gy", 1) for y in (1, 3)
+        some, rest = after(self.sent, *others)
+        self.come = [swap(some, "gy", 2), swap(rest, "gy", 1)]
+        return self.come
+
+    def second(self, *others):
+        kept = [array.reshape(self.size) for array in self.kept]
+        come = [array.reshape(self.size) for array in after(self.come, *others)]
+        self.near = list(zip(kept, come))
+        self.sent = [total(mine[:, 1], theirs[:, 1]) for mine, theirs in self.near]
+        self.come = [swap(self.sent[0], "gy", 1), swap(self.sent[1], "gy", 2)]
+        return self.come
+
+    def line(self, *others):
+        come = after(self.come, *others)
+        some, rest = [
+            total(mine[:, 0], theirs[:, 0], last)
+            for (mine, theirs), last in zip(self.near, come)
         ]
-        return [self.some_come, *self.rest_come]
-
-    def second(self, *others):
-        keep, come, half = self.keep, self.come, self.half
-        some_come, rest_come = after((self.some_come, self.rest_come), *others)
-        some_end = swap(total(keep[:half, 1], come[:half, 1], some_come[:, 1]), "gy", 1)
-        rest_end = swap(total(keep[half:, 2], come[half:, 2], rest_come[1]), "gy", 2)
-        self.parts = (some_come, rest_come, some_end, rest_end)
-        return [some_end, rest_end]
-
-    def line(self, *others):
-        keep, come, half = self.keep, self.come, self.half
-        some_come, rest_come, some_end, rest_end = after(self.parts, *others)
-        some = total(keep[:half, 0], come[:half, 0], some_come[:, 0], some_end)
-        rest = total(keep[half:, 0], come[half:, 0], rest_come[0], rest_end)
-        self.ends = [some[i] for i in range(half)] + [rest[i] for i in range(half)]
+        self.ends = [some[i] for i in range(self.half)] + [rest[i] for i in range(self.half)]
         self.got = []
 
     def along(self, fars, *others):
@@ -900,23 +961,32 @@
     shard_a = pad_lanes(jnp.concatenate([w_sqkv, w_sout, w_cq, w_cout], axis=1))
     shard_d = pad_lanes(jnp.concatenate([w_tqkv, w_tout], axis=1))
     shard_up = pad_lanes(w_up)
-    trees = w_down.shape[1] % 16 == 0 and 2 * w_down.shape[1] == k_rows
+    each = w_down.shape[1]
+    fold = fold_width(w_down.shape[0])
+    trees = each % 16 == 0 and 2 * each == k_rows and fold == padded(n_up)
     if trees:
         turned = w_down.T
-        fold = fold_width(turned.shape[1])
         rest = jnp.pad(turned[:, fold:], ((0, 0), (0, 2 * fold - turned.shape[1])))
-        folded = jnp.concatenate([turned[:, :fold], rest])
-        shard_up = jnp.concatenate([shard_up, folded], axis=1)
+        shard_up = jnp.concatenate([shard_up, turned[:, :fold], rest])
     fars = range(1, nx // 2)
-    get_a, get_up, get_d = Gather(shard_a), Gather(shard_up), Gather(shard_d)
+    get_a, get_up = Gather(shard_a), Gather(shard_up)
     get_a.along(fars)
     cond_all = condition(timesteps, pooled_text)
     cond_rows = lax.dynamic_slice_in_dim(cond_all, gy * k_rows, k_rows, axis=1)
     mod_part = jnp.dot(cond_rows, w_ada.astype(f32), precision=highest)
     mod_part = mod_part + swap(mod_part, "gy", 1)
     mod_all = (mod_part + swap(mod_part, "gy", 2))[None]
+    mod_first = mod_all
+    own_text = text_states.shape[0]
+    text_rows = text_states.reshape(own_text // CLIPS, CLIPS, -1).transpose(1, 0, 2)
+    depth = w_ckv.shape[0]
+    text_rows = after(text_rows.reshape(own_text, ny, depth).transpose(1, 0, 2), mod_first)
+    text_rows = lax.all_to_all(text_rows, "gy", split_axis=0, concat_axis=0, tiled=True)
+    text_rows = lax.all_gather(text_rows, "gx", axis=0)
     bit = 1
     while bit < nx:
+        if 2 * bit == nx:
+            mod_all = after(mod_all, text_rows, *get_a.line)
         come = swap(mod_all, "gx", bit)
         mod_all = jnp.where(
             gx & bit != 0,
@@ -925,12 +995,29 @@
         )
         bit *= 2
     mod = lax.dynamic_index_in_dim(mod_all, clip_here, axis=1, keepdims=False).reshape(9, D)
-    done = [*get_a.line, mod_all]
-    done = get_a.first(*done) + get_up.along(fars[:1], *done)
-    done = get_a.second(*done) + get_up.along(fars[1:], *done)
-    full_a = get_a.last(*done)
+    done = [mod_all]
     held = done
-    done = get_up.first(*held) + get_d.along(fars, *held)
+    done = get_a.first(*held) + get_up.along(fars[:2], *held)
+    text_block = (
+        after(text_rows, *held)
+        .reshape(nx, ny, CLIPS, own_text // CLIPS, depth)
+        .transpose(2, 1, 0, 3, 4)
+        .reshape(own_text * devices, depth)
+    )
+    text_part = jnp.dot(text_block, w_ckv, preferred_element_type=f32)
+    done += [text_part]
+    grad_branch_d = (keep_here[0] * mod[8] * grad_out.astype(f32)).astype(bf16)
+    held = done
+    done = get_a.second(*held) + get_a.own_core()
+    done += get_up.along(fars[2:], *held, *get_a.own_other)
+    text_sum = lax.psum_scatter(
+        after(text_part, *held), "gy", scatter_dimension=0, tiled=True
+    )
+    done += [text_sum]
+    held = done
+    up_far = get_up.first(*held)
+    done = get_a.new_core(*held, *get_up.near)
+    full_a = get_a.arrays()
     ff_width = w_down.shape[0]
     ff = ff_width * ny
     win_sqkv = Window(0, n_sqkv)
@@ -944,19 +1031,6 @@
     win_tqkv = Window(0, n_sqkv)
     win_tout = Window(n_sqkv, n_sqkv + n_one)
 
-    own = text_states.shape[0]
-    depth = w_ckv.shape[0]
-    text_rows = text_states.reshape(own // CLIPS, CLIPS, -1).transpose(1, 0, 2)
-    text_rows = lax.all_gather(text_rows.reshape(own, -1), row_axes, axis=0)
-    text_rows = after(text_rows, *held)
-    text_block = lax.dynamic_slice_in_dim(text_rows, gy * depth, depth, axis=2)
-    text_block = (
-        text_block.reshape(devices, CLIPS, own // CLIPS, depth)
-        .transpose(1, 0, 2, 3)
-        .reshape(own * devices, depth)
-    )
-    text_part = jnp.dot(text_block, w_ckv, preferred_element_type=f32)
-    text_sum = lax.psum_scatter(text_part, "gy", scatter_dimension=0, tiled=True).astype(bf16)
 
     win = win_sqkv
     hidden_a, query_a, pair_a = run(
@@ -968,23 +1042,26 @@
         ],
         [smem()] + [vmem(), vmem(), hbm()],
         [pltpu.VMEM((nx, D, win.width), bf16), pltpu.SemaphoreType.DMA((nx,))],
-        (me, tokens, mod, full_a),
+        (me, tokens, after(mod, *done), full_a),
         9,
     )
-    done = done + [pair_a]
-    near_up = get_up.second(*done)
-    text_all = lax.all_gather(after(text_sum, *done), row_axes, axis=0)
-    grad_branch_d = (keep_here[0] * mod[8] * grad_out.astype(f32)).astype(bf16)
-    grad_branch_moved = reorder(after(grad_branch_d, *done))
-    slots = own * devices // CLIPS
-    text_all = text_all.reshape(ny, nx, -1, w_ckv.shape[1]).transpose(0, 2, 1, 3)
-    text_all = text_all.reshape(CLIPS, slots, 2 * D)
-    text_pairs = lax.dynamic_index_in_dim(text_all, clip_here, axis=0, keepdims=False)
-    pairs = [after(pair_a, *done)]
+    up_near = get_up.second(*up_far, pair_a)
+    up_own = get_up.own_core()
+    pairs = [after(pair_a, *up_far)]
     bit = frame_devs // 2
     while bit:
         pairs = pairs + [swap(p, "gx", bit) for p in pairs]
         bit //= 2
+    text_all = lax.all_gather(after(text_sum, *held).astype(bf16), row_axes, axis=0)
+    full_d = lax.all_gather(after(shard_d, text_all), ("gx", "gy"), axis=0, tiled=True)
+    full_d = full_d.reshape(nx, D, -1)
+    slots = own_text * devices // CLIPS
+    text_all = text_all.reshape(ny, nx, -1, w_ckv.shape[1]).transpose(0, 2, 1, 3)
+    text_all = text_all.reshape(CLIPS, slots, 2 * D)
+    text_pairs = lax.dynamic_index_in_dim(text_all, clip_here, axis=0, keepdims=False)
+    done = [*pairs, *up_own]
+    query_a = after(query_a, *done)
+    grad_branch_moved = reorder(after(grad_branch_d, *done))
     count = len(pairs)
     keys = count * rows
     out_a, lse_a = run(
@@ -1001,10 +1078,7 @@
         18,
     )
 
-    done = near_up + [out_a, text_pairs, grad_branch_moved]
-    full_up = get_up.last(*done)
-    full_down = None if trees else gather_rows(after(w_down.T, *done))
-    far_d = get_d.first(*done)
+    done = [out_a, text_pairs, grad_branch_moved]
     out_a = after(out_a, *done)
     branch_a, after_a, hidden_b, query_b, out_b, after_b, hidden_c = run(
         functools.partial(text_kernel, win_rest, win_sout, win_cq, win_cout, nx),
@@ -1029,7 +1103,11 @@
         18,
     )
 
-    near_d = get_d.second(hidden_c, *far_d)
+    done = [hidden_c, *up_near]
+    done = get_up.new_core(*done)
+    full_up = get_up.arrays()
+    full_down = None if trees else gather_rows(after(w_down.T, *up_near))
+    hidden_c = after(hidden_c, *done)
     pre_act, activated, branch_c, after_c, hidden_d = run(
         functools.partial(ff_kernel, win_up, nx, ny),
         [
@@ -1050,19 +1128,20 @@
         20,
     )
 
-    done = [*near_d, hidden_d]
-    full_d = get_d.last(*done)
-    moved_d = reorder(after(hidden_d, *done))
+    rows_own = [hidden_a, out_a, hidden_b, out_b, hidden_c]
+    rows_other = swap(after(jnp.stack(rows_own), hidden_d), "gx", 1)
+    g_other = swap(after(activated, hidden_d), "gx", 1)
+    moved_d = reorder(hidden_d)
+    moved_d = after(moved_d, rows_other, g_other, grad_branch_moved)
     pad_width = max(win_tqkv.width, win_tout.width)
-    out_moved, branch_moved, grad_qkv_d, grad_hidden_moved = run(
-        functools.partial(temporal_kernel, win_d, win_tqkv, win_tout, nx, frames),
+    grads_d, branch_moved, grad_hidden_moved = run(
+        functools.partial(temporal_kernel, win_tqkv, win_tout, nx, frames),
         [
+            shape(rows, 4 * D, dtype=bf16),
             shape(rows, D, dtype=bf16),
             shape(rows, D, dtype=bf16),
-            shape(rows, 3 * D, dtype=bf16),
-            shape(rows, D, dtype=bf16),
         ],
-        [smem()] + [vmem(), vmem(), hbm(), vmem(), smem()],
+        [vmem(), vmem(), hbm(), vmem(), smem()],
         [
             pltpu.VMEM((nx, D, win_d.width), bf16),
             pltpu.SemaphoreType.DMA((nx,)),
@@ -1070,31 +1149,20 @@
         ]
         + [pltpu.VMEM((rows, D), f32)] * 8
         + [pltpu.VMEM((rows, 3 * D), bf16)],
-        (me, moved_d, grad_branch_moved, full_d, row_clip, frame_clip),
+        (moved_d, grad_branch_moved, full_d, row_clip, frame_clip),
         25,
     )
     grad_hidden_d = reorder(grad_hidden_moved)
-    late_terms = weight_grads(
-        nx, me, [(moved_d, [grad_qkv_d]), (out_moved, [grad_branch_moved])]
-    )
-    done = [*late_terms, grad_hidden_d]
-    late = Scatter(*late_terms, *done)
-    grad_hidden_d = after(grad_hidden_d, *done)
-    branch_d = reorder(after(branch_moved, *done))
-    mixed, d_gate3 = run(
-        mixed_kernel,
-        [shape(rows, D, dtype=bf16), shape(1, D)],
-        [vmem(), vmem(), vmem(), vmem(), smem()],
-        [],
-        (branch_d, after_c, grad_out, mod, keep_here),
-        3,
-    )
-
-    grad_branch_c, grad_pre, grad_b, sums_c = run(
+    late = whole_grads(
+        nx, [moved_d, grad_branch_moved, grads_d], [((0, 0, D), (2, D, 4 * D)), ((2, 0, D), (1, 0, D))]
+    )
+    late = scatter(after(late, grad_hidden_d), ("gx", "gy"))
+    d_tqkv, d_tout = late[:, :n_sqkv], late[:, n_sqkv : n_sqkv + n_one]
+
+    grads_c, grad_b, sums_c = run(
         functools.partial(ff_back_kernel, win_up, nx, ny),
         [
-            shape(rows, D, dtype=bf16),
-            shape(nx, rows, n_up, dtype=bf16),
+            shape(rows, ff + D, dtype=bf16),
             shape(rows, D),
             shape(8, D),
         ],
@@ -1104,33 +1172,31 @@
             pltpu.VMEM((ny, D, ff_width), bf16),
             pltpu.SemaphoreType.DMA((nx,)),
             pltpu.SemaphoreType.DMA((ny,)),
-            pltpu.VMEM((rows, ff), bf16),
             pltpu.VMEM((rows, win_up.width), bf16),
         ],
         (me, grad_out, grad_hidden_d, after_c, after_b, pre_act, branch_c, mod, full_up, full_down),
         22,
     )
-    done = [late.come, grad_b, branch_d]
-    late_first = late.first(*done)
-    grad_pre = after(grad_pre, *done)
-    if trees:
-        up_terms = up_grads(me, hidden_c, grad_pre, grad_branch_c, activated)
-    else:
-        up_terms = up_grads(me, hidden_c, grad_pre, None, activated)
-        d_down = scatter(down_grads(grad_branch_c, activated), row_axes).T
-    done = [*late_first, *up_terms]
-    late_second = late.second(*done)
-    up_sums = Scatter(*up_terms, *done)
-    grad_b = after(grad_b, *done)
+    grads_other = swap(grads_c, "gx", 1)
+    up_terms = up_grads(
+        nx,
+        me,
+        [hidden_c, grads_c, activated],
+        [rows_other[4], grads_other, g_other],
+        trees,
+    )
+    if not trees:
+        d_down = scatter(down_grads(grads_c[:, ff:], activated), row_axes).T
+    up_sums = Scatter(*up_terms)
+    up_first = up_sums.first()
+    grad_b = after(grad_b, *up_terms)
 
     kv_width = w_ckv.shape[1]
-    grad_cout_rows, grad_query_b, grad_a, grad_branch_a, grad_out_a, text_terms, d_gate1 = run(
+    grads_b, grad_a, grad_out_a, text_terms, d_gate1 = run(
         functools.partial(text_back_kernel, win_rest, win_sout, win_cq, win_cout, nx),
         [
-            shape(rows, D, dtype=bf16),
-            shape(rows, D, dtype=bf16),
+            shape(rows, 3 * D, dtype=bf16),
             shape(rows, D),
-            shape(rows, D, dtype=bf16),
             shape(rows, D, dtype=bf16),
             shape(nx, slots, kv_width, dtype=bf16),
             shape(1, D),
@@ -1151,23 +1217,13 @@
         20,
     )
     text_terms = jnp.where(clip_mark[None, :, None, None], text_terms[:, None], 0)
+
+    done = [grad_out_a]
+    grads_b_other = swap(grads_b, "gx", 1)
     text_terms = lax.psum_scatter(
-        text_terms.reshape(nx, -1, kv_width), "gx", scatter_dimension=0, tiled=True
-    )
-    text_terms = text_terms[0].astype(f32)
-    text_terms = text_terms + swap(text_terms.astype(bf16), "gy", 1).astype(f32)
-    text_terms = text_terms + swap(text_terms.astype(bf16), "gy", 2).astype(f32)
-    text_grad = text_terms.astype(bf16)
-    d_ckv = jnp.einsum("rd,re->de", text_block, text_grad, preferred_element_type=f32)
-
-    cross_terms = weight_grads(
-        nx, me, [(hidden_b, [grad_query_b]), (out_b, [grad_cout_rows])]
-    )
-    done = [*late_second, up_sums.come, *cross_terms, grad_out_a]
-    late.line(*done)
-    late_done = late.along(fars, *done)
-    up_first = up_sums.first(*done)
-    cross = Scatter(*cross_terms, *done)
+        after(text_terms, late).reshape(nx, -1, kv_width), "gx", scatter_dimension=0, tiled=True
+    )
+    branch_d = reorder(after(branch_moved, *done))
     grad_out_a = after(grad_out_a, *done)
 
     grad_query_a, grad_pairs = run(
@@ -1181,11 +1237,10 @@
         (query_a, grad_out_a, out_a, lse_a, *pairs),
         28,
     )
-    late = late.result()
-    d_tqkv, d_tout = late[:, :n_sqkv], late[:, n_sqkv : n_sqkv + n_one]
-    done = [*late_done, *up_first, cross.come, grad_pairs]
+    done = [grad_pairs, grads_b_other, branch_d]
+    grad_pairs = after(grad_pairs, *done)
     up_second = up_sums.second(*done)
-    grad_pairs = after(grad_pairs, *done)
+    done = up_sums.sent
     bit = 1
     while bit < frame_devs // 2:
         half = grad_pairs.shape[0] // 2
@@ -1193,10 +1248,33 @@
         grad_pairs = (grad_pairs[:half].astype(f32) + come.astype(f32)).astype(bf16)
         bit *= 2
     come = swap(grad_pairs[1], "gx", bit)
+    mixed, d_gate3 = run(
+        mixed_kernel,
+        [shape(rows, D, dtype=bf16), shape(1, D)],
+        [vmem(), vmem(), vmem(), vmem(), smem()],
+        [],
+        (branch_d, after_c, grad_out, mod, keep_here),
+        3,
+    )
+
+    cross = Scatter(
+        *weight_grads(
+            nx,
+            me,
+            [hidden_b, out_b, after(grads_b, grad_pairs, *done)],
+            [rows_other[2], rows_other[3], grads_b_other],
+            [((0, 0, D), (2, D, 2 * D)), ((1, 0, D), (2, 0, D))],
+        )
+    )
+    done = [come, *cross.sent, *up_second]
+    cross_first = cross.first(*done)
+    up_sums.line(*done)
+    up_done = up_sums.along(fars[2:])
+    grad_query_a = after(grad_query_a, *done, *up_sums.ends)
     win = win_sqkv
-    grad_pair_a, grad_tokens, sums_a = run(
+    grads_a, grad_tokens, sums_a = run(
         functools.partial(qkv_back_kernel, win, nx),
-        [shape(rows, 2 * D, dtype=bf16), shape(rows, D, dtype=bf16), shape(2, D)],
+        [shape(rows, 3 * D, dtype=bf16), shape(rows, D, dtype=bf16), shape(2, D)],
         [smem()] + [vmem()] * 6 + [hbm()],
         [
             pltpu.VMEM((nx, D, win.width), bf16),
@@ -1206,36 +1284,31 @@
         (me, grad_query_a, grad_pairs[0], come, tokens, mod, grad_a, full_a),
         11,
     )
-    early_terms = weight_grads(
-        nx,
-        me,
-        [(hidden_a, [grad_query_a, grad_pair_a]), (out_a, [grad_branch_a])],
-    )
-    done = [*up_second, *early_terms]
-    early = Scatter(*early_terms, *done)
-    up_sums.line(*done)
-    done = up_sums.along(fars[:1], *done) + cross.first(*done) + [early.come]
-    done = up_sums.along(fars[1:2], *done) + cross.second(*done) + early.first(*done)
+    grads_a_other = swap(grads_a, "gx", 1)
+    early = Scatter(
+        *weight_grads(
+            nx,
+            me,
+            [hidden_a, out_a, grads_a, grads_b],
+            [rows_other[0], rows_other[1], grads_a_other, grads_b_other],
+            [((0, 0, D), (2, 0, 3 * D)), ((1, 0, D), (3, 2 * D, 3 * D))],
+        )
+    )
+    done = [*cross_first, *early.sent]
+    cross_second = cross.second(*done)
+    done = [*cross_second, *up_done]
+    up_done = up_done + up_sums.along(fars[:2])
+    early_first = early.first(*done)
     cross.line(*done)
-    done = (
-        up_sums.along(fars[2:], *done) + cross.along(fars, *done) + early.second(*done)
-    )
-    early.line(*done)
-    early.along(fars)
-    up, cross, early = up_sums.result(), cross.result(), early.result()
-    d_up = up[:, :n_up]
-    if trees:
-        start, each = win_up.stop, w_down.shape[1]
-        d_down = jnp.concatenate(
-            [up[:each, start:], up[each:, start : start + ff_width - fold]], axis=1
-        ).T
-    d_cq, d_cout = cross[:, :n_one], cross[:, n_one : 2 * n_one]
-    d_sqkv, d_sout = early[:, :n_sqkv], early[:, n_sqkv : n_sqkv + n_one]
-
+    cross_done = cross.along(fars, *up_done)
+    done = [*early_first, *up_done]
+    early_second = early.second(*done)
+    early.line(*early_second)
+    early_done = early.along(fars)
     grad_mod = jnp.concatenate(
         [sums_a, d_gate1, sums_c[3:5], sums_c[2:3], sums_c[0:2], d_gate3]
     ).reshape(-1)
-    grad_mod = lax.all_gather(grad_mod, row_axes, axis=0)
+    grad_mod = after(lax.all_gather(grad_mod, row_axes, axis=0), *early.ends)
     width = w_ada.shape[1]
     grad_mod = lax.dynamic_slice_in_dim(grad_mod, gx * width, width, axis=1)
     device_clip = jnp.sum(
@@ -1247,6 +1320,19 @@
     d_ada = lax.dot_general(
         cond_rows, grad_mod, (((0,), (0,)), ((), ())), precision=highest
     )
+    text_terms = after(text_terms[0], *early.ends).astype(f32)
+    text_terms = text_terms + swap(text_terms.astype(bf16), "gy", 1).astype(f32)
+    text_terms = text_terms + swap(text_terms.astype(bf16), "gy", 2).astype(f32)
+    text_grad = text_terms.astype(bf16)
+    d_ckv = jnp.einsum("rd,re->de", text_block, text_grad, preferred_element_type=f32)
+    up, cross, early = up_sums.result(), cross.result(), early.result()
+    d_up = up[:k_rows, :n_up]
+    if trees:
+        down = up[k_rows:]
+        d_down = jnp.concatenate([down[:each], down[each:, : ff_width - fold]], axis=1).T
+    d_cq, d_cout = cross[:, :n_one], cross[:, n_one : 2 * n_one]
+    d_sqkv, d_sout = early[:, :n_sqkv], early[:, n_sqkv : n_sqkv + n_one]
+
     return (
         mixed,
         grad_tokens,

time: 979 us -> 861 us (0.88)
  waiting for transfers between devices: 446 us -> 379 us
  starting transfers between devices: 133 us -> 82.9 us
  other arithmetic: 97 us -> 59.1 us
  Pallas kernels: 229 us -> 245 us
    ppermute x81 -> x60, waiting for transfers between devices: 407 us -> 261 us  [swap(): lax.ppermute(values, axis, [(i, i ^ mask) for i in range(lax.axis_size(ax...]
    all_to_all x4, waiting for transfers between devices: 25.4 us -> 96.8 us  [reorder(): lax.all_to_all(values.reshape(devices, values.shape[0] // devices, values...]
    ppermute x81 -> x60, starting transfers between devices: 112 us -> 63.5 us  [swap(): lax.ppermute(values, axis, [(i, i ^ mask) for i in range(lax.axis_size(ax...]
    convert_element_type x20 -> x12, other arithmetic: 58.4 us -> 21.4 us  [total(): return sum((term.astype(f32) for term in terms)).astype(bf16)]
    pallas_call x1 -> x2, Pallas kernels: 16.6 us -> 36.8 us  [the longest x1 21.5 us: up_grads(): pl.pallas_call(kernel, out_shape=outs, grid_spec=pltpu.PrefetchScalarGrid...]
    reduce_scatter x2, waiting for transfers between devices: 7.23 us -> 20.6 us  [the longest x1 20.6 us: local(): lax.psum_scatter(after(text_part, *held), 'gy', scatter_dimension=0, tile...]
    unnamed x136 -> x160, local copies, waits for them, and re-layouts: 15.9 us -> 21.5 us
    pallas_call x3 -> x2, Pallas kernels: 36.9 us -> 32 us  [weight_grads(): pl.pallas_call(functools.partial(weight_kernel, nx, lax.axis_size('gy'),...]
  transfers between devices with their start and end apart: 90 -> 71, of which waited for: 33 -> 35; matrix products, arithmetic and copies ran while one was open for 12% -> 11% of each run, Pallas kernels for 21% -> 26%
where the time goes in v3:
time: 861 us; the launch traced here: 850 us
  waiting for transfers between devices  379 us (44%)
  Pallas kernels  245 us (28%)
  starting transfers between devices  82.9 us (10%)
  other arithmetic  59.1 us (7%)
  local copies, waits for them, and re-layouts  46.9 us (5%)
  between operations  18.1 us (2%)
  matrix products  10.6 us (1%)
  blocking collectives  9.14 us (1%)
    ppermute x60, waiting for transfers between devices, swap(): lax.ppermute(values, axis, [(i, i ^ mask) for i in range(lax.axis_size(ax...  261 us
    pallas_call x10, Pallas kernels, run(): pl.pallas_call(grouped, out_shape=outs, in_specs=flat_specs, out_specs=[v...  176 us
    all_to_all x4, waiting for transfers between devices, reorder(): lax.all_to_all(values.reshape(devices, values.shape[0] // devices, values...  96.8 us
    ppermute x60, starting transfers between devices, swap(): lax.ppermute(values, axis, [(i, i ^ mask) for i in range(lax.axis_size(ax...  63.5 us
    pallas_call x2, Pallas kernels, weight_grads(): pl.pallas_call(functools.partial(weight_kernel, nx, lax.axis_size('gy'),...  32 us
    unnamed x160, local copies, waits for them, and re-layouts  21.5 us
    pallas_call x1, Pallas kernels, up_grads(): pl.pallas_call(kernel, out_shape=outs, grid_spec=pltpu.PrefetchScalarGrid...  21.5 us
    convert_element_type x12, other arithmetic, total(): return sum((term.astype(f32) for term in terms)).astype(bf16)  21.4 us
  transfers between devices with their start and end apart: 71, of which 35 were waited for; matrix products, arithmetic and copies ran while one was open for 11% of the time, Pallas kernels for 26%

profile of v3, /device:TPU:0, one launch (start us, length us, event | category | flops | bytes accessed | tf_op | source)
XLA Modules:
  0.0 850.4 jit_solution(1894662903741637045)
XLA Ops:
  9.6 3.0 collective-permute-start
  18.4 9.1 %all_to_all.25 = bf16[4,16,1024]{2,1,0:T(8,128)(2,1)} all-to-all(bf16[4,16,1024]{2,1,0:T(8,128)(2,1)S(1)} %copy.214), channel_id=1, replica_groups=mesh['gy'=4,'gx'=8] {'gy'}, dimensions={0} | all-to-all | bytes 262144 | tf_op jit(solution)/shard_map/all_to_all | solution.py:984
  28.3 3.7 collective-permute-start.6
  35.2 35.6 %collective-permute-done.3 = f32[2,4,1296]{2,1,0:T(4,128)S(1)} collective-permute-done((f32[2,4,1296]{2,1,0:T(4,128)S(1)}, f32[2,4,1296]{2,1,0:T(4,128)S(1)}, u32[]{:S(2)}, u32[]{:S(2)}) %collective-permute-start.3) | collective-permute-done | bytes 41504 | tf_op jit(solution)/shard_map/ppermute | solution.py:892
  70.9 9.9 %collective-permute-done.5 = bf16[288,896]{1,0:T(8,128)(2,1)S(1)} collective-permute-done((bf16[288,896]{1,0:T(8,128)(2,1)S(1)}, bf16[288,896]{1,0:T(8,128)(2,1)S(1)}, u32[]{:S(2)}, u32[]{:S(2)}) %collective-permute-start.5) | collective-permute-done | bytes 516128 | tf_op jit(solution)/shard_map/ppermute | solution.py:892
  80.7 5.9 collective-permute-done.7
  92.4 2.5 collective-permute-start.10
  96.7 2.8 fusion.46
  99.5 25.3 %collective-permute-done.11 = bf16[576,640]{1,0:T(8,128)(2,1)} collective-permute-done((bf16[576,640]{1,0:T(8,128)(2,1)}, bf16[576,640]{1,0:T(8,128)(2,1)}, u32[]{:S(2)}, u32[]{:S(2)}) %collective-permute-start.11) | collective-permute-done | bytes 737312 | tf_op jit(solution)/shard_map/ppermute | solution.py:892
  126.7 3.5 pad_maximum_fusion.2.refs_3_.refs_4_.refs_5_.refs_7_
  133.3 4.2 collective-permute-done.14.refs_7_.refs_8_.refs_9_.refs_11_
  139.5 20.6 %reduce-scatter.6.cloned.1.call-done = f32[128,288]{0,1:T(8,128)} async-done(((f32[512,288]{0,1:T(8,128)}), f32[128,288]{0,1:T(8,128)}) %reduce-scatter.6.cloned.1.call-update) | async-done | bytes 147472 | tf_op jit(solution)/shard_map/reduce_scatter | solution.py:1013
  160.1 22.4 %collective-permute-done.12.refs_4_.refs_5_.refs_6_.refs_8_ = bf16[2,2,288,896]{3,2,1,0:T(8,128)(2,1)} collective-permute-done((bf16[2,2,288,896]{3,2,1,0:T(8,128)(2,1)}, bf16[2,2,288,896]{3,2,1,0:T(8,128)(2,1)}, u32[]{:S(2)}, u32[]{:S(2)}) %collective-permute-start.12) | collective-permute-done | bytes 2064416 | tf_op jit(solution)/shard_map/ppermute | solution.py:892
  186.6 4.1 fusion.42
  202.4 9.2 %shard_map.265 = (bf16[256,1152]{1,0:T(8,128)(2,1)}, bf16[256,1152]{1,0:T(8,128)(2,1)}, bf16[256,2304]{1,0:T(8,128)(2,1)}) custom-call(s32[2]{0:T(128)} %pad_add_fusion.refs_0_.me_ref, bf16[256,1152]{1,0:T(8,128)(2,1)} %refs_4_.1, f32[9,1152]{1,0:T(8,128)} %reshape.218.refs_2_.refs_3_.refs_7_.refs_4_.refs_5_, ...), custom_call_target="tpu_custom_call" | custom-call | flops 180000000 | tf_op jit(solution)/shard_map/pallas_call | solution.py:57
  211.6 16.5 %collective-permute-done.20 = bf16[2,576,640]{2,1,0:T(8,128)(2,1)} collective-permute-done((bf16[2,576,640]{2,1,0:T(8,128)(2,1)}, bf16[2,576,640]{2,1,0:T(8,128)(2,1)}, u32[]{:S(2)}, u32[]{:S(2)}) %collective-permute-start.20) | collective-permute-done | bytes 1474592 | tf_op jit(solution)/shard_map/ppermute | solution.py:892
  230.0 4.3 pad_maximum_fusion.refs_4_.refs_8_
  237.3 32.9 %collective-permute-done.21.refs_2_.refs_5_ = bf16[256,2304]{1,0:T(8,128)(2,1)} collective-permute-done((bf16[256,2304]{1,0:T(8,128)(2,1)S(1)}, bf16[256,2304]{1,0:T(8,128)(2,1)}, u32[]{:S(2)}, u32[]{:S(2)}) %collective-permute-start.21) | collective-permute-done | bytes 1179680 | tf_op jit(solution)/shard_map/ppermute | solution.py:892
  273.8 4.4 all-to-all-start.1
  285.7 18.3 %shard_map.266 = (bf16[256,1152]{1,0:T(8,128)(2,1)}, f32[16,256]{1,0:T(8,128)}) custom-call(bf16[256,1152]{1,0:T(8,128)(2,1)} %get-tuple-element.155.refs_0_, bf16[256,2304]{1,0:T(8,128)(2,1)} %get-tuple-element.150.refs_1_.refs_4_, bf16[256,2304]{1,0:T(8,128)(2,1)} %collective-permute-done.21.refs_2_.refs_5_, bf16[256,2304]{1,0:T(8,128)(2,1)} %copy-done.19, ...), custom_call_target="tpu_custom_call" | custom-call | flops 360000000 | tf_op jit(solution)/shard_map/pallas_call | solution.py:57
  304.0 17.9 %all-to-all-done.1 = bf16[32,8,1152]{2,1,0:T(8,128)(2,1)S(1)} async-done(((bf16[32,8,1152]{2,1,0:T(8,128)(2,1)}), bf16[32,8,1152]{2,1,0:T(8,128)(2,1)S(1)}, u32[]{:S(2)}, u32[]{:S(2)}) %all-to-all-start.1) | async-done | bytes 589856 | tf_op jit(solution)/shard_map/all_to_all | solution.py:897
  322.8 18.0 %shard_map.267 = (f32[256,1152]{1,0:T(8,128)}, f32[256,1152]{1,0:T(8,128)}, bf16[256,1152]{1,0:T(8,128)(2,1)}, bf16[256,1152]{1,0:T(8,128)(2,1)}, bf16[256,1152]...) custom-call(s32[2]{0:T(128)} %pad_add_fusion.refs_0_.me_ref, bf16[256,1152]{1,0:T(8,128)(2,1)} %refs_4_.1, ...), custom_call_target="tpu_custom_call" | custom-call | flops 360000000 | tf_op jit(solution)/shard_map/pallas_call | solution.py:57
  343.0 3.4 collective-permute-done.28.refs_9_.refs_13_
  346.5 5.0 collective-permute-done.29.refs_11_.refs_15_
  353.1 20.9 %shard_map.268 = (f32[256,4608]{1,0:T(8,128)}, bf16[256,4608]{1,0:T(8,128)(2,1)}, f32[256,1152]{1,0:T(8,128)}, f32[256,1152]{1,0:T(8,128)}, bf16[256,1152]{1,0:T(8,128)(2,1)}) custom-call(s32[2]{0:T(128)} %pad_add_fusion.refs_0_.me_ref, bf16[256,1152]{1,0:T(8,128)(2,1)} %get-tuple-element.163.refs_1_.refs_0_, ...), custom_call_target="tpu_custom_call" | custom-call | flops 400000000 | tf_op jit(solution)/shard_map/pallas_call | solution.py:57
  375.5 7.2 all-to-all-start.2
  384.2 16.3 %all-to-all-done.2 = bf16[32,8,1152]{2,1,0:T(8,128)(2,1)S(1)} async-done(((bf16[32,8,1152]{2,1,0:T(8,128)(2,1)}), bf16[32,8,1152]{2,1,0:T(8,128)(2,1)S(1)}, u32[]{:S(2)}, u32[]{:S(2)}) %all-to-all-start.2) | async-done | bytes 589856 | tf_op jit(solution)/shard_map/all_to_all | solution.py:897
  401.3 24.0 %shard_map.269 = (bf16[256,4608]{1,0:T(8,128)(2,1)}, bf16[256,1152]{1,0:T(8,128)(2,1)}, bf16[256,1152]{1,0:T(8,128)(2,1)}) custom-call(bf16[256,1152]{1,0:T(8,128)(2,1)} %bitcast.277, bf16[256,1152]{1,0:T(8,128)(2,1)} %bitcast.275, bf16[8,1152,640]{2,1,0:T(8,128)(2,1)} %bitcast.271, f32[256,1]{1,0:T(8,128)} %broadcast_in_dim_reshape.4.refs_3_, f32[8]{0:T(128)} %copy-done.63), custom_call_target="tpu_custom_call" | custom-call | flops 500000000 | tf_op jit(solution)/shard_map/pallas_call | solution.py:57
  425.3 2.6 all-to-all-start.3
  428.0 15.3 %shard_map.278 = bf16[8,1152,640]{2,1,0:T(8,128)(2,1)} custom-call(bf16[256,1152]{1,0:T(8,128)(2,1)} %bitcast.278, bf16[256,1152]{1,0:T(8,128)(2,1)} %bitcast.276, bf16[256,4608]{1,0:T(8,128)(2,1)} %get-tuple-element.238.refs_2_), custom_call_target="tpu_custom_call" | custom-call | flops 260000000 | tf_op jit(solution)/shard_map/pallas_call | solution.py:692
  443.3 2.4 all-to-all-done.3
  446.6 22.9 %shard_map.270 = (bf16[256,5760]{1,0:T(8,128)(2,1)}, f32[256,1152]{1,0:T(8,128)}, f32[8,1152]{1,0:T(8,128)}) custom-call(s32[2]{0:T(128)} %pad_add_fusion.refs_0_.me_ref, bf16[256,1152]{1,0:T(8,128)(2,1)} %refs_2_.1, bf16[256,1152]{1,0:T(8,128)(2,1)} %bitcast.290, f32[256,1152]{1,0:T(8,128)} %get-tuple-element.176.refs_3_.refs_1_, ...), custom_call_target="tpu_custom_call" | custom-call | flops 440000000 | tf_op jit(solution)/shard_map/pallas_call | solution.py:57
  471.3 4.3 collective-permute-done.32.refs_4_
  477.1 21.5 %shard_map.271 = (bf16[2,1152,640]{2,1,0:T(8,128)(2,1)}, bf16[2,1152,640]{2,1,0:T(8,128)(2,1)}, bf16[2,1152,640]{2,1,0:T(8,128)(2,1)}, bf16[2,1152,640]{2,1,0:T(8,128)(2,1)}) custom-call(s32[2]{0:T(128)} %pad_add_fusion.refs_0_.me_ref, bf16[256,1152]{1,0:T(8,128)(2,1)} %get-tuple-element.163.refs_1_.refs_0_, bf16[256,5760]{1,0:T(8,128)(2,1)} %get-tuple-element.180.refs_1_, ...), custom_call_target="tpu_custom_call" | custom-call | flops 320000000 | tf_op jit(solution)/shard_map/pallas_call | solution.py:753
  498.6 20.2 %shard_map.272 = (bf16[256,3456]{1,0:T(8,128)(2,1)}, f32[256,1152]{1,0:T(8,128)}, bf16[256,1152]{1,0:T(8,128)(2,1)}, bf16[8,128,288]{2,1,0:T(8,128)(2,1)}, f32[1,1152]{1,0:T(1,128)}) custom-call(s32[2]{0:T(128)} %pad_add_fusion.refs_0_.me_ref, f32[256,1152]{1,0:T(8,128)} %get-tuple-element.185.refs_1_, f32[256,1152]{1,0:T(8,128)} %get-tuple-element.186.refs_2_, ...), custom_call_target="tpu_custom_call" | custom-call | flops 400000000 | tf_op jit(solution)/shard_map/pallas_call | solution.py:57
  523.3 4.4 all-to-all-start.4
  528.0 28.4 %shard_map.274 = (bf16[256,1152]{1,0:T(8,128)(2,1)}, bf16[4,256,2304]{2,1,0:T(8,128)(2,1)}) custom-call(bf16[256,1152]{1,0:T(8,128)(2,1)} %get-tuple-element.155.refs_0_, bf16[256,1152]{1,0:T(8,128)(2,1)} %get-tuple-element.192.refs_1_, bf16[256,1152]{1,0:T(8,128)(2,1)} %get-tuple-element.159.refs_2_.refs_1_, f32[16,256]{1,0:T(8,128)} %get-tuple-element.193.refs_3_, ...), custom_call_target="tpu_custom_call" | custom-call | flops 560000000 | tf_op jit(solution)/shard_map/pallas_call | solution.py:57
  556.4 60.3 %all-to-all-done.4 = bf16[32,8,1152]{2,1,0:T(8,128)(2,1)S(1)} async-done(((bf16[32,8,1152]{2,1,0:T(8,128)(2,1)}), bf16[32,8,1152]{2,1,0:T(8,128)(2,1)S(1)}, u32[]{:S(2)}, u32[]{:S(2)}) %all-to-all-start.4) | async-done | bytes 589856 | tf_op jit(solution)/shard_map/all_to_all | solution.py:897
  616.7 2.7 slice.188
  619.6 3.5 fusion.2
  625.2 2.9 fusion.3
  635.2 14.3 %shard_map.275 = (bf16[2,576,384]{2,1,0:T(8,128)(2,1)}, bf16[2,576,384]{2,1,0:T(8,128)(2,1)}, bf16[2,576,384]{2,1,0:T(8,128)(2,1)}, bf16[2,576,384]{2,1,0:T(8,128)(2,1)}) custom-call(s32[2]{0:T(128)} %pad_add_fusion.refs_0_.me_ref, bf16[256,1152]{1,0:T(8,128)(2,1)} %get-tuple-element.167.refs_0_, bf16[256,1152]{1,0:T(8,128)(2,1)} %get-tuple-element.168.refs_1_, ...), custom_call_target="tpu_custom_call" | custom-call | flops 180000000 | tf_op jit(solution)/shard_map/pallas_call | solution.py:644
  649.5 8.8 %collective-permute-done.38 = bf16[2,576,640]{2,1,0:T(8,128)(2,1)S(1)} collective-permute-done((bf16[2,576,640]{2,1,0:T(8,128)(2,1)}, bf16[2,576,640]{2,1,0:T(8,128)(2,1)S(1)}, u32[]{:S(2)}, u32[]{:S(2)}) %collective-permute-start.38) | collective-permute-done | bytes 1474592 | tf_op jit(solution)/shard_map/ppermute | solution.py:892
  658.3 4.4 collective-permute-done.39
  662.7 11.2 %collective-permute-done.35.refs_3_ = bf16[256,2304]{1,0:T(8,128)(2,1)S(1)} collective-permute-done((bf16[256,2304]{1,0:T(8,128)(2,1)}, bf16[256,2304]{1,0:T(8,128)(2,1)S(1)}, u32[]{:S(2)}, u32[]{:S(2)}) %collective-permute-start.35) | collective-permute-done | bytes 1179680 | tf_op jit(solution)/shard_map/ppermute | solution.py:892
  674.0 2.8 fusion.1
  677.8 2.4 fusion
  681.4 11.1 %shard_map.276 = (bf16[256,3456]{1,0:T(8,128)(2,1)}, bf16[256,1152]{1,0:T(8,128)(2,1)}, f32[2,1152]{1,0:T(2,128)}) custom-call(s32[2]{0:T(128)} %pad_add_fusion.refs_0_.me_ref, bf16[256,1152]{1,0:T(8,128)(2,1)} %get-tuple-element.207.refs_1_, bf16[256,2304]{1,0:T(8,128)(2,1)} %get-tuple-element.319.refs_2_, bf16[256,2304]{1,0:T(8,128)(2,1)} %copy-done.35, ...), custom_call_target="tpu_custom_call" | custom-call | flops 220000000 | tf_op jit(solution)/shard_map/pallas_call | solution.py:57
  694.3 6.6 collective-permute-start.45
  702.1 17.6 %shard_map.277 = (bf16[2,576,640]{2,1,0:T(8,128)(2,1)}, bf16[2,576,640]{2,1,0:T(8,128)(2,1)}, bf16[2,576,640]{2,1,0:T(8,128)(2,1)}, bf16[2,576,640]{2,1,0:T(8,128)(2,1)}) custom-call(s32[2]{0:T(128)} %pad_add_fusion.refs_0_.me_ref, bf16[256,1152]{1,0:T(8,128)(2,1)} %get-tuple-element.166.refs_0_, bf16[256,1152]{1,0:T(8,128)(2,1)} %get-tuple-element.159.refs_2_.refs_1_, ...), custom_call_target="tpu_custom_call" | custom-call | flops 180000000 | tf_op jit(solution)/shard_map/pallas_call | solution.py:644
  727.4 6.0 collective-permute-done.43
  733.4 2.3 collective-permute-done.44
  738.5 2.7 shard_map.273
  742.7 12.9 %collective-permute-done.48 = bf16[576,640]{1,0:T(8,128)(2,1)} collective-permute-done((bf16[576,640]{1,0:T(8,128)(2,1)}, bf16[576,640]{1,0:T(8,128)(2,1)}, u32[]{:S(2)}, u32[]{:S(2)}) %collective-permute-start.48) | collective-permute-done | bytes 737312 | tf_op jit(solution)/shard_map/ppermute | solution.py:892
  755.6 8.1 collective-permute-done.49
  777.3 2.8 collective-permute-start.57
  781.7 6.2 collective-permute-done.55
  787.9 3.6 collective-permute-done.57
  791.5 11.6 %collective-permute-done.56 = bf16[288,384]{1,0:T(8,128)(2,1)S(1)} collective-permute-done((bf16[288,384]{1,0:T(8,128)(2,1)S(1)}, bf16[288,384]{1,0:T(8,128)(2,1)S(1)}, u32[]{:S(2)}, u32[]{:S(2)}) %collective-permute-start.56) | collective-permute-done | bytes 221216 | tf_op jit(solution)/shard_map/ppermute | solution.py:892
  811.7 2.2 collective-permute-start.54
  818.1 3.6 fusion.39
  821.7 12.8 %collective-permute-done.53 = bf16[288,640]{1,0:T(8,128)(2,1)S(1)} collective-permute-done((bf16[288,640]{1,0:T(8,128)(2,1)S(1)}, bf16[288,640]{1,0:T(8,128)(2,1)S(1)}, u32[]{:S(2)}, u32[]{:S(2)}) %collective-permute-start.53) | collective-permute-done | bytes 368672 | tf_op jit(solution)/shard_map/ppermute | solution.py:892
  834.6 2.2 collective-permute-done.52
  840.6 2.7 fusion.28
  (354 shorter events, 130.6 us)
Async XLA Ops:
  7.2 73.5 %all-gather.10.cloned.1.call-start = ((), (), s32[]{:S(2)}) async-start(), calls=%async_computation.11 | async-start | bytes 1179648 | tf_op jit(solution)/shard_map/all_gather | solution.py:985
  27.5 132.6 %reduce-scatter.6.cloned.1.call-start = ((), (), s32[]{:S(2)}) async-start(), calls=%async_computation.8 | async-start | bytes 737280 | tf_op jit(solution)/shard_map/reduce_scatter | solution.py:1013
  28.3 42.6 %collective-permute-start.6 = (bf16[288,896]{1,0:T(8,128)(2,1)S(1)}, bf16[288,896]{1,0:T(8,128)(2,1)S(1)}, u32[]{:S(2)}, u32[]{:S(2)}) collective-permute-start(bf16[288,896]{1,0:T(8,128)(2,1)S(1)} %fusion.23), channel_id=1, source_target_pairs={{0,6},{1,7},{2,4},{3,5},{4,2},{5,3},{6,0},{7,1},{8,14},{9,15},{10,... | collective-permute-start | bytes 1548296 | tf_op jit(solution)/shard_map/ppermute | solution.py:892
  31.9 48.8 %collective-permute-start.5 = (bf16[288,896]{1,0:T(8,128)(2,1)S(1)}, bf16[288,896]{1,0:T(8,128)(2,1)S(1)}, u32[]{:S(2)}, u32[]{:S(2)}) collective-permute-start(bf16[288,896]{1,0:T(8,128)(2,1)S(1)} %fusion.23), channel_id=1, source_target_pairs={{0,4},{1,5},{2,6},{3,7},{4,0},{5,1},{6,2},{7,3},{8,12},{9,13},{10,... | collective-permute-start | bytes 1548296 | tf_op jit(solution)/shard_map/ppermute | solution.py:892
  31.9 48.8 %collective-permute-start.4 = (bf16[288,896]{1,0:T(8,128)(2,1)S(1)}, bf16[288,896]{1,0:T(8,128)(2,1)S(1)}, u32[]{:S(2)}, u32[]{:S(2)}) collective-permute-start(bf16[288,896]{1,0:T(8,128)(2,1)S(1)} %fusion.23), channel_id=1, source_target_pairs={{0,2},{1,3},{2,0},{3,1},{4,6},{5,7},{6,4},{7,5},{8,10},{9,11},{10,... | collective-permute-start | bytes 1548296 | tf_op jit(solution)/shard_map/ppermute | solution.py:892
  33.9 36.9 %collective-permute-start.3 = (f32[2,4,1296]{2,1,0:T(4,128)S(1)}, f32[2,4,1296]{2,1,0:T(4,128)S(1)}, u32[]{:S(2)}, u32[]{:S(2)}) collective-permute-start(f32[2,4,1296]{2,1,0:T(4,128)S(1)} %maximum_select_fusion.2), channel_id=1, source_target_pairs={{0,2},{1,3},{2,0},{3,1},{4,6},{5,7},{6,4},{7,5},{8,10},{9,11},{10,... | collective-permute-start | bytes 124424 | tf_op jit(solution)/shard_map/ppermute | solution.py:892
  88.5 36.4 %collective-permute-start.8 = (bf16[2,288,896]{2,1,0:T(8,128)(2,1)}, bf16[2,288,896]{2,1,0:T(8,128)(2,1)}, u32[]{:S(2)}, u32[]{:S(2)}) collective-permute-start(bf16[2,288,896]{2,1,0:T(8,128)(2,1)} %get-tuple-element.330), channel_id=1, source_target_pairs={{0,8},{8,0},{16,24},{24,16},{1,9},{9,1},{17,25},{25,17},{2,10},{10... | collective-permute-start | bytes 3096584 | tf_op jit(solution)/shard_map/ppermute | solution.py:892
  90.9 34.0 %collective-permute-start.9 = (bf16[2,288,896]{2,1,0:T(8,128)(2,1)}, bf16[2,288,896]{2,1,0:T(8,128)(2,1)}, u32[]{:S(2)}, u32[]{:S(2)}) collective-permute-start(bf16[2,288,896]{2,1,0:T(8,128)(2,1)} %get-tuple-element.328), channel_id=1, source_target_pairs={{0,16},{8,24},{16,0},{24,8},{1,17},{9,25},{17,1},{25,9},{2,18},{10... | collective-permute-start | bytes 3096584 | tf_op jit(solution)/shard_map/ppermute | solution.py:892
  92.4 32.3 %collective-permute-start.11 = (bf16[576,640]{1,0:T(8,128)(2,1)}, bf16[576,640]{1,0:T(8,128)(2,1)}, u32[]{:S(2)}, u32[]{:S(2)}) collective-permute-start(bf16[576,640]{1,0:T(8,128)(2,1)} %fusion.15), channel_id=1, source_target_pairs={{0,4},{1,5},{2,6},{3,7},{4,0},{5,1},{6,2},{7,3},{8,12},{9,13},{10,... | collective-permute-start | bytes 2211848 | tf_op jit(solution)/shard_map/ppermute | solution.py:892
  92.4 32.4 %collective-permute-start.10 = (bf16[576,640]{1,0:T(8,128)(2,1)}, bf16[576,640]{1,0:T(8,128)(2,1)}, u32[]{:S(2)}, u32[]{:S(2)}) collective-permute-start(bf16[576,640]{1,0:T(8,128)(2,1)} %fusion.15), channel_id=1, source_target_pairs={{0,2},{1,3},{2,0},{3,1},{4,6},{5,7},{6,4},{7,5},{8,10},{9,11},{10,... | collective-permute-start | bytes 2211848 | tf_op jit(solution)/shard_map/ppermute | solution.py:892
  130.2 7.4 collective-permute-start.14
  130.2 7.4 collective-permute-start.15
  130.7 51.9 %collective-permute-start.12 = (bf16[2,2,288,896]{3,2,1,0:T(8,128)(2,1)}, bf16[2,2,288,896]{3,2,1,0:T(8,128)(2,1)}, u32[]{:S(2)}, u32[]{:S(2)}) collective-permute-start(bf16[2,2,288,896]{3,2,1,0:T(8,128)(2,1)} %pad_maximum_fusion.2.refs_3_.refs_4_.refs_5_.refs_7_), channel_id=1, source_target_pairs={{0,16},{8,24},{16,0},{24,8},{1,17},{9,25},{17,1},{25,9},{2,18},{10... | collective-permute-start | bytes 6193160 | tf_op jit(solution)/shard_map/ppermute | solution.py:892
  132.1 51.4 %collective-permute-start.13 = (bf16[2,2,288,896]{3,2,1,0:T(8,128)(2,1)S(1)}, bf16[2,2,288,896]{3,2,1,0:T(8,128)(2,1)}, u32[]{:S(2)}, u32[]{:S(2)}) collective-permute-start(bf16[2,2,288,896]{3,2,1,0:T(8,128)(2,1)S(1)} %pad_maximum_fusion.3.refs_5_.refs_6_.refs_7_.refs_9_), channel_id=1, source_target_pairs={{0,8},{8,0},{16,24},{24,16},{1,9},{9,1},{17,25},{25,17},{2,10},{10... | collective-permute-start | bytes 6193160 | tf_op jit(solution)/shard_map/ppermute | solution.py:892
  133.3 146.4 %all-gather.12.cloned.1.call-start = ((), (), s32[]{:S(2)}) async-start(), calls=%async_computation.12 | async-start | bytes 2433024 | tf_op jit(solution)/shard_map/all_gather | solution.py:1055
  137.5 46.0 %collective-permute-start.16 = (bf16[576,640]{1,0:T(8,128)(2,1)}, bf16[576,640]{1,0:T(8,128)(2,1)S(1)}, u32[]{:S(2)}, u32[]{:S(2)}) collective-permute-start(bf16[576,640]{1,0:T(8,128)(2,1)} %fusion.15), channel_id=1, source_target_pairs={{0,6},{1,7},{2,4},{3,5},{4,2},{5,3},{6,0},{7,1},{8,14},{9,15},{10,... | collective-permute-start | bytes 2211848 | tf_op jit(solution)/shard_map/ppermute | solution.py:892
  185.3 215.3 %all-gather.8.cloned.1.call-start = ((), (), s32[]{:S(2)}) async-start(), calls=%async_computation.9 | async-start | bytes 12165120 | tf_op jit(solution)/shard_map/all_gather | solution.py:1056
  190.7 10.3 %collective-permute-start.17 = (bf16[2,2,288,896]{3,2,1,0:T(8,128)(2,1)}, bf16[2,2,288,896]{3,2,1,0:T(8,128)(2,1)S(1)}, u32[]{:S(2)}, u32[]{:S(2)}) collective-permute-start(bf16[2,2,288,896]{3,2,1,0:T(8,128)(2,1)} %collective-permute-done.12.refs_4_.refs_5_.refs_6_.refs_8_), channel_id=1, source_target_pairs={{0,1},{1,0},{2,3},{3,2},{4,5},{5,4},{6,7},{7,6},{8,9},{9,8},{10,11... | collective-permute-start | bytes 6193160 | tf_op jit(solution)/shard_map/ppermute | solution.py:892
  190.7 10.4 %collective-permute-start.18 = (bf16[2,2,288,896]{3,2,1,0:T(8,128)(2,1)}, bf16[2,2,288,896]{3,2,1,0:T(8,128)(2,1)}, u32[]{:S(2)}, u32[]{:S(2)}) collective-permute-start(bf16[2,2,288,896]{3,2,1,0:T(8,128)(2,1)} %collective-permute-done.13.refs_6_.refs_7_.refs_8_.refs_10_), channel_id=1, source_target_pairs={{0,1},{1,0},{2,3},{3,2},{4,5},{5,4},{6,7},{7,6},{8,9},{9,8},{10,11... | collective-permute-start | bytes 6193160 | tf_op jit(solution)/shard_map/ppermute | solution.py:892
  191.2 36.9 %collective-permute-start.20 = (bf16[2,576,640]{2,1,0:T(8,128)(2,1)}, bf16[2,576,640]{2,1,0:T(8,128)(2,1)}, u32[]{:S(2)}, u32[]{:S(2)}) collective-permute-start(bf16[2,576,640]{2,1,0:T(8,128)(2,1)} %get-tuple-element.324), channel_id=1, source_target_pairs={{0,16},{8,24},{16,0},{24,8},{1,17},{9,25},{17,1},{25,9},{2,18},{10... | collective-permute-start | bytes 4423688 | tf_op jit(solution)/shard_map/ppermute | solution.py:892
  191.8 36.3 %collective-permute-start.19 = (bf16[2,576,640]{2,1,0:T(8,128)(2,1)S(1)}, bf16[2,576,640]{2,1,0:T(8,128)(2,1)}, u32[]{:S(2)}, u32[]{:S(2)}) collective-permute-start(bf16[2,576,640]{2,1,0:T(8,128)(2,1)S(1)} %get-tuple-element.343), channel_id=1, source_target_pairs={{0,8},{8,0},{16,24},{24,16},{1,9},{9,1},{17,25},{25,17},{2,10},{10... | collective-permute-start | bytes 4423688 | tf_op jit(solution)/shard_map/ppermute | solution.py:892
  228.1 7.3 collective-permute-start.22
  234.3 39.5 %collective-permute-start.24 = (bf16[2,2,576,640]{3,2,1,0:T(8,128)(2,1)}, bf16[2,2,576,640]{3,2,1,0:T(8,128)(2,1)}, u32[]{:S(2)}, u32[]{:S(2)}) collective-permute-start(bf16[2,2,576,640]{3,2,1,0:T(8,128)(2,1)} %pad_maximum_fusion.refs_4_.refs_8_), channel_id=1, source_target_pairs={{0,1},{1,0},{2,3},{3,2},{4,5},{5,4},{6,7},{7,6},{8,9},{9,8},{10,11... | collective-permute-start | bytes 8847368 | tf_op jit(solution)/shard_map/ppermute | solution.py:892
  234.8 39.0 %collective-permute-start.25 = (bf16[2,2,576,640]{3,2,1,0:T(8,128)(2,1)S(1)}, bf16[2,2,576,640]{3,2,1,0:T(8,128)(2,1)}, u32[]{:S(2)}, u32[]{:S(2)}) collective-permute-start(bf16[2,2,576,640]{3,2,1,0:T(8,128)(2,1)S(1)} %pad_maximum_fusion.1.refs_6_.refs_10_), channel_id=1, source_target_pairs={{0,1},{1,0},{2,3},{3,2},{4,5},{5,4},{6,7},{7,6},{8,9},{9,8},{10,11... | collective-permute-start | bytes 8847368 | tf_op jit(solution)/shard_map/ppermute | solution.py:892
  234.8 35.3 %collective-permute-start.21 = (bf16[256,2304]{1,0:T(8,128)(2,1)S(1)}, bf16[256,2304]{1,0:T(8,128)(2,1)}, u32[]{:S(2)}, u32[]{:S(2)}) collective-permute-start(bf16[256,2304]{1,0:T(8,128)(2,1)S(1)} %copy-done.18), channel_id=1, source_target_pairs={{0,2},{1,3},{2,0},{3,1},{4,6},{5,7},{6,4},{7,5},{8,10},{9,11},{10,... | collective-permute-start | bytes 3538952 | tf_op jit(solution)/shard_map/ppermute | solution.py:892
  234.8 106.0 %collective-permute-start.26 = (bf16[2,2,576,640]{3,2,1,0:T(8,128)(2,1)}, bf16[2,2,576,640]{3,2,1,0:T(8,128)(2,1)}, u32[]{:S(2)}, u32[]{:S(2)}) collective-permute-start(bf16[2,2,576,640]{3,2,1,0:T(8,128)(2,1)} %pad_maximum_fusion.refs_4_.refs_8_), channel_id=1, source_target_pairs={{0,16},{8,24},{16,0},{24,8},{1,17},{9,25},{17,1},{25,9},{2,18},{10... | collective-permute-start | bytes 8847368 | tf_op jit(solution)/shard_map/ppermute | solution.py:892
  235.4 105.4 %collective-permute-start.27 = (bf16[2,2,576,640]{3,2,1,0:T(8,128)(2,1)S(1)}, bf16[2,2,576,640]{3,2,1,0:T(8,128)(2,1)}, u32[]{:S(2)}, u32[]{:S(2)}) collective-permute-start(bf16[2,2,576,640]{3,2,1,0:T(8,128)(2,1)S(1)} %pad_maximum_fusion.1.refs_6_.refs_10_), channel_id=1, source_target_pairs={{0,8},{8,0},{16,24},{24,16},{1,9},{9,1},{17,25},{25,17},{2,10},{10... | collective-permute-start | bytes 8847368 | tf_op jit(solution)/shard_map/ppermute | solution.py:892
  273.8 48.1 %all-to-all-start.1 = ((bf16[32,8,1152]{2,1,0:T(8,128)(2,1)}), bf16[32,8,1152]{2,1,0:T(8,128)(2,1)S(1)}, u32[]{:S(2)}, u32[]{:S(2)}) async-start(bf16[32,8,1152]{2,1,0:T(8,128)(2,1)} %bitcast.288), calls=%async_computation.2 | async-start | bytes 1179648 | tf_op jit(solution)/shard_map/all_to_all | solution.py:897
  340.9 10.6 %collective-permute-start.29 = (bf16[2,2,576,640]{3,2,1,0:T(8,128)(2,1)}, bf16[2,2,576,640]{3,2,1,0:T(8,128)(2,1)S(1)}, u32[]{:S(2)}, u32[]{:S(2)}) collective-permute-start(bf16[2,2,576,640]{3,2,1,0:T(8,128)(2,1)} %collective-permute-done.27.refs_7_.refs_11_), channel_id=1, source_target_pairs={{0,1},{1,0},{2,3},{3,2},{4,5},{5,4},{6,7},{7,6},{8,9},{9,8},{10,11... | collective-permute-start | bytes 8847368 | tf_op jit(solution)/shard_map/ppermute | solution.py:892
  374.9 25.6 %collective-permute-start.30 = (bf16[5,256,1152]{2,1,0:T(8,128)(2,1)}, bf16[5,256,1152]{2,1,0:T(8,128)(2,1)S(1)}, u32[]{:S(2)}, u32[]{:S(2)}) collective-permute-start(bf16[5,256,1152]{2,1,0:T(8,128)(2,1)} %bitcast_dynamic-update-slice_fusion), channel_id=1, source_target_pairs={{0,1},{1,0},{2,3},{3,2},{4,5},{5,4},{6,7},{7,6},{8,9},{9,8},{10,11... | collective-permute-start | bytes 8847368 | tf_op jit(solution)/shard_map/ppermute | solution.py:892
  375.5 25.0 %collective-permute-start.31 = (bf16[256,4608]{1,0:T(8,128)(2,1)}, bf16[256,4608]{1,0:T(8,128)(2,1)}, u32[]{:S(2)}, u32[]{:S(2)}) collective-permute-start(bf16[256,4608]{1,0:T(8,128)(2,1)} %get-tuple-element.171.refs_2_), channel_id=1, source_target_pairs={{0,1},{1,0},{2,3},{3,2},{4,5},{5,4},{6,7},{7,6},{8,9},{9,8},{10,11... | collective-permute-start | bytes 7077896 | tf_op jit(solution)/shard_map/ppermute | solution.py:892
  375.5 25.0 %all-to-all-start.2 = ((bf16[32,8,1152]{2,1,0:T(8,128)(2,1)}), bf16[32,8,1152]{2,1,0:T(8,128)(2,1)S(1)}, u32[]{:S(2)}, u32[]{:S(2)}) async-start(bf16[32,8,1152]{2,1,0:T(8,128)(2,1)} %bitcast.310), calls=%async_computation.3 | async-start | bytes 1179648 | tf_op jit(solution)/shard_map/all_to_all | solution.py:897
  425.3 20.4 %all-to-all-start.3 = ((bf16[32,8,1152]{2,1,0:T(8,128)(2,1)}), bf16[32,8,1152]{2,1,0:T(8,128)(2,1)S(1)}, u32[]{:S(2)}, u32[]{:S(2)}) async-start(bf16[32,8,1152]{2,1,0:T(8,128)(2,1)} %bitcast.311), calls=%async_computation.4 | async-start | bytes 1179648 | tf_op jit(solution)/shard_map/all_to_all | solution.py:897
  428.0 205.9 %reduce-scatter.10.cloned.1.call-start = ((), (), s32[]{:S(2)}) async-start(), calls=%async_computation.14 | async-start | bytes 12165120
  518.8 97.8 %collective-permute-start.33 = (bf16[256,3456]{1,0:T(8,128)(2,1)}, bf16[256,3456]{1,0:T(8,128)(2,1)S(1)}, u32[]{:S(2)}, u32[]{:S(2)}) collective-permute-start(bf16[256,3456]{1,0:T(8,128)(2,1)} %get-tuple-element.202.refs_2_.refs_3_), channel_id=1, source_target_pairs={{0,1},{1,0},{2,3},{3,2},{4,5},{5,4},{6,7},{7,6},{8,9},{9,8},{10,11... | collective-permute-start | bytes 5308424 | tf_op jit(solution)/shard_map/ppermute | solution.py:892
  520.5 99.0 %collective-permute-start.36 = (bf16[2,1152,640]{2,1,0:T(8,128)(2,1)}, bf16[2,1152,640]{2,1,0:T(8,128)(2,1)}, u32[]{:S(2)}, u32[]{:S(2)}) collective-permute-start(bf16[2,1152,640]{2,1,0:T(8,128)(2,1)} %get-tuple-element.198), channel_id=1, source_target_pairs={{0,16},{8,24},{16,0},{24,8},{1,17},{9,25},{17,1},{25,9},{2,18},{10... | collective-permute-start | bytes 8847368 | tf_op jit(solution)/shard_map/ppermute | solution.py:892
  522.2 97.3 %collective-permute-start.37 = (bf16[2,1152,640]{2,1,0:T(8,128)(2,1)}, bf16[2,1152,640]{2,1,0:T(8,128)(2,1)}, u32[]{:S(2)}, u32[]{:S(2)}) collective-permute-start(bf16[2,1152,640]{2,1,0:T(8,128)(2,1)} %get-tuple-element.199), channel_id=1, source_target_pairs={{0,8},{8,0},{16,24},{24,16},{1,9},{9,1},{17,25},{25,17},{2,10},{10... | collective-permute-start | bytes 8847368 | tf_op jit(solution)/shard_map/ppermute | solution.py:892
  523.3 93.4 %all-to-all-start.4 = ((bf16[32,8,1152]{2,1,0:T(8,128)(2,1)}), bf16[32,8,1152]{2,1,0:T(8,128)(2,1)S(1)}, u32[]{:S(2)}, u32[]{:S(2)}) async-start(bf16[32,8,1152]{2,1,0:T(8,128)(2,1)} %bitcast.44), calls=%async_computation.5 | async-start | bytes 1179648 | tf_op jit(solution)/shard_map/all_to_all | solution.py:897
  527.7 280.0 %reduce-scatter.8.cloned.1.call-start = ((), (), s32[]{:S(2)}) async-start(), calls=%async_computation.10 | async-start | bytes 3538944 | tf_op jit(solution)/shard_map/reduce_scatter | solution.py:1223
  619.4 9.2 %collective-permute-start.34 = (bf16[2,256,2304]{2,1,0:T(8,128)(2,1)S(1)}, bf16[2,256,2304]{2,1,0:T(8,128)(2,1)S(1)}, u32[]{:S(2)}, u32[]{:S(2)}) collective-permute-start(bf16[2,256,2304]{2,1,0:T(8,128)(2,1)S(1)} %slice.188), channel_id=1, source_target_pairs={{0,1},{1,0},{2,3},{3,2},{4,5},{5,4},{6,7},{7,6},{8,9},{9,8},{10,11... | collective-permute-start | bytes 7077896 | tf_op jit(solution)/shard_map/ppermute | solution.py:892
  623.0 35.3 %collective-permute-start.38 = (bf16[2,576,640]{2,1,0:T(8,128)(2,1)}, bf16[2,576,640]{2,1,0:T(8,128)(2,1)S(1)}, u32[]{:S(2)}, u32[]{:S(2)}) collective-permute-start(bf16[2,576,640]{2,1,0:T(8,128)(2,1)} %fusion.2), channel_id=1, source_target_pairs={{0,8},{8,0},{16,24},{24,16},{1,9},{9,1},{17,25},{25,17},{2,10},{10... | collective-permute-start | bytes 4423688 | tf_op jit(solution)/shard_map/ppermute | solution.py:892
  628.0 34.7 %collective-permute-start.39 = (bf16[2,576,640]{2,1,0:T(8,128)(2,1)}, bf16[2,576,640]{2,1,0:T(8,128)(2,1)}, u32[]{:S(2)}, u32[]{:S(2)}) collective-permute-start(bf16[2,576,640]{2,1,0:T(8,128)(2,1)} %fusion.3), channel_id=1, source_target_pairs={{0,16},{8,24},{16,0},{24,8},{1,17},{9,25},{17,1},{25,9},{2,18},{10... | collective-permute-start | bytes 4423688 | tf_op jit(solution)/shard_map/ppermute | solution.py:892
  630.7 43.2 %collective-permute-start.35 = (bf16[256,2304]{1,0:T(8,128)(2,1)}, bf16[256,2304]{1,0:T(8,128)(2,1)S(1)}, u32[]{:S(2)}, u32[]{:S(2)}) collective-permute-start(bf16[256,2304]{1,0:T(8,128)(2,1)} %get-tuple-element.320), channel_id=1, source_target_pairs={{0,2},{1,3},{2,0},{3,1},{4,6},{5,7},{6,4},{7,5},{8,10},{9,11},{10,... | collective-permute-start | bytes 3538952 | tf_op jit(solution)/shard_map/ppermute | solution.py:892
  635.1 175.0 %all-gather.14.cloned.1.call-start = ((), (), s32[]{:S(2)}) async-start(), calls=%async_computation.13 | async-start | bytes 1368576 | tf_op jit(solution)/shard_map/all_gather | solution.py:1311
  692.6 8.3 collective-permute-start.40
  692.7 27.1 %collective-permute-start.41 = (bf16[2,576,384]{2,1,0:T(8,128)(2,1)}, bf16[2,576,384]{2,1,0:T(8,128)(2,1)S(1)}, u32[]{:S(2)}, u32[]{:S(2)}) collective-permute-start(bf16[2,576,384]{2,1,0:T(8,128)(2,1)} %get-tuple-element.219), channel_id=1, source_target_pairs={{0,16},{8,24},{16,0},{24,8},{1,17},{9,25},{17,1},{25,9},{2,18},{10... | collective-permute-start | bytes 2654216 | tf_op jit(solution)/shard_map/ppermute | solution.py:892
  694.3 25.5 %collective-permute-start.42 = (bf16[2,576,384]{2,1,0:T(8,128)(2,1)S(1)}, bf16[2,576,384]{2,1,0:T(8,128)(2,1)S(1)}, u32[]{:S(2)}, u32[]{:S(2)}) collective-permute-start(bf16[2,576,384]{2,1,0:T(8,128)(2,1)S(1)} %copy-done.64), channel_id=1, source_target_pairs={{0,8},{8,0},{16,24},{24,16},{1,9},{9,1},{17,25},{25,17},{2,10},{10... | collective-permute-start | bytes 2654216 | tf_op jit(solution)/shard_map/ppermute | solution.py:892
  694.3 33.1 %collective-permute-start.45 = (bf16[576,640]{1,0:T(8,128)(2,1)}, bf16[576,640]{1,0:T(8,128)(2,1)}, u32[]{:S(2)}, u32[]{:S(2)}) collective-permute-start(bf16[576,640]{1,0:T(8,128)(2,1)} %get-tuple-element.321), channel_id=1, source_target_pairs={{0,6},{1,7},{2,4},{3,5},{4,2},{5,3},{6,0},{7,1},{8,14},{9,15},{10,... | collective-permute-start | bytes 2211848 | tf_op jit(solution)/shard_map/ppermute | solution.py:892
  720.7 12.7 %collective-permute-start.43 = (bf16[2,288,384]{2,1,0:T(8,128)(2,1)}, bf16[2,288,384]{2,1,0:T(8,128)(2,1)}, u32[]{:S(2)}, u32[]{:S(2)}) collective-permute-start(bf16[2,288,384]{2,1,0:T(8,128)(2,1)} %fusion.24), channel_id=1, source_target_pairs={{0,8},{8,0},{16,24},{24,16},{1,9},{9,1},{17,25},{25,17},{2,10},{10... | collective-permute-start | bytes 1327112 | tf_op jit(solution)/shard_map/ppermute | solution.py:892
  723.5 12.2 %collective-permute-start.44 = (bf16[2,288,384]{2,1,0:T(8,128)(2,1)}, bf16[2,288,384]{2,1,0:T(8,128)(2,1)}, u32[]{:S(2)}, u32[]{:S(2)}) collective-permute-start(bf16[2,288,384]{2,1,0:T(8,128)(2,1)} %fusion.25), channel_id=1, source_target_pairs={{0,16},{8,24},{16,0},{24,8},{1,17},{9,25},{17,1},{25,9},{2,18},{10... | collective-permute-start | bytes 1327112 | tf_op jit(solution)/shard_map/ppermute | solution.py:892
  725.5 30.1 %collective-permute-start.48 = (bf16[576,640]{1,0:T(8,128)(2,1)}, bf16[576,640]{1,0:T(8,128)(2,1)}, u32[]{:S(2)}, u32[]{:S(2)}) collective-permute-start(bf16[576,640]{1,0:T(8,128)(2,1)} %slice_bitcast_fusion.20), channel_id=1, source_target_pairs={{0,2},{1,3},{2,0},{3,1},{4,6},{5,7},{6,4},{7,5},{8,10},{9,11},{10,... | collective-permute-start | bytes 2211848 | tf_op jit(solution)/shard_map/ppermute | solution.py:892
  725.5 38.3 %collective-permute-start.49 = (bf16[576,640]{1,0:T(8,128)(2,1)}, bf16[576,640]{1,0:T(8,128)(2,1)}, u32[]{:S(2)}, u32[]{:S(2)}) collective-permute-start(bf16[576,640]{1,0:T(8,128)(2,1)} %get-tuple-element.322), channel_id=1, source_target_pairs={{0,4},{1,5},{2,6},{3,7},{4,0},{5,1},{6,2},{7,3},{8,12},{9,13},{10,... | collective-permute-start | bytes 2211848 | tf_op jit(solution)/shard_map/ppermute | solution.py:892
  735.7 34.8 %collective-permute-start.46 = (bf16[2,576,640]{2,1,0:T(8,128)(2,1)}, bf16[2,576,640]{2,1,0:T(8,128)(2,1)}, u32[]{:S(2)}, u32[]{:S(2)}) collective-permute-start(bf16[2,576,640]{2,1,0:T(8,128)(2,1)} %get-tuple-element.224), channel_id=1, source_target_pairs={{0,16},{8,24},{16,0},{24,8},{1,17},{9,25},{17,1},{25,9},{2,18},{10... | collective-permute-start | bytes 4423688 | tf_op jit(solution)/shard_map/ppermute | solution.py:892
  737.5 33.2 %collective-permute-start.47 = (bf16[2,576,640]{2,1,0:T(8,128)(2,1)}, bf16[2,576,640]{2,1,0:T(8,128)(2,1)}, u32[]{:S(2)}, u32[]{:S(2)}) collective-permute-start(bf16[2,576,640]{2,1,0:T(8,128)(2,1)} %get-tuple-element.225), channel_id=1, source_target_pairs={{0,8},{8,0},{16,24},{24,16},{1,9},{9,1},{17,25},{25,17},{2,10},{10... | collective-permute-start | bytes 4423688 | tf_op jit(solution)/shard_map/ppermute | solution.py:892
  772.2 31.0 %collective-permute-start.50 = (bf16[2,288,640]{2,1,0:T(8,128)(2,1)S(1)}, bf16[2,288,640]{2,1,0:T(8,128)(2,1)S(1)}, u32[]{:S(2)}, u32[]{:S(2)}) collective-permute-start(bf16[2,288,640]{2,1,0:T(8,128)(2,1)S(1)} %fusion.17), channel_id=1, source_target_pairs={{0,8},{8,0},{16,24},{24,16},{1,9},{9,1},{17,25},{25,17},{2,10},{10... | collective-permute-start | bytes 2211848 | tf_op jit(solution)/shard_map/ppermute | solution.py:892
  775.3 27.8 %collective-permute-start.51 = (bf16[2,288,640]{2,1,0:T(8,128)(2,1)S(1)}, bf16[2,288,640]{2,1,0:T(8,128)(2,1)S(1)}, u32[]{:S(2)}, u32[]{:S(2)}) collective-permute-start(bf16[2,288,640]{2,1,0:T(8,128)(2,1)S(1)} %fusion.18), channel_id=1, source_target_pairs={{0,16},{8,24},{16,0},{24,8},{1,17},{9,25},{17,1},{25,9},{2,18},{10... | collective-permute-start | bytes 2211848 | tf_op jit(solution)/shard_map/ppermute | solution.py:892
  777.2 10.6 %collective-permute-start.55 = (bf16[288,384]{1,0:T(8,128)(2,1)S(1)}, bf16[288,384]{1,0:T(8,128)(2,1)S(1)}, u32[]{:S(2)}, u32[]{:S(2)}) collective-permute-start(bf16[288,384]{1,0:T(8,128)(2,1)S(1)} %slice_bitcast_fusion.41), channel_id=1, source_target_pairs={{0,2},{1,3},{2,0},{3,1},{4,6},{5,7},{6,4},{7,5},{8,10},{9,11},{10,... | collective-permute-start | bytes 663560 | tf_op jit(solution)/shard_map/ppermute | solution.py:892
  777.3 14.1 %collective-permute-start.57 = (bf16[288,384]{1,0:T(8,128)(2,1)S(1)}, bf16[288,384]{1,0:T(8,128)(2,1)S(1)}, u32[]{:S(2)}, u32[]{:S(2)}) collective-permute-start(bf16[288,384]{1,0:T(8,128)(2,1)S(1)} %get-tuple-element.236), channel_id=1, source_target_pairs={{0,6},{1,7},{2,4},{3,5},{4,2},{5,3},{6,0},{7,1},{8,14},{9,15},{10,... | collective-permute-start | bytes 663560 | tf_op jit(solution)/shard_map/ppermute | solution.py:892
  780.1 22.9 %collective-permute-start.56 = (bf16[288,384]{1,0:T(8,128)(2,1)S(1)}, bf16[288,384]{1,0:T(8,128)(2,1)S(1)}, u32[]{:S(2)}, u32[]{:S(2)}) collective-permute-start(bf16[288,384]{1,0:T(8,128)(2,1)S(1)} %get-tuple-element.235), channel_id=1, source_target_pairs={{0,4},{1,5},{2,6},{3,7},{4,0},{5,1},{6,2},{7,3},{8,12},{9,13},{10,... | collective-permute-start | bytes 663560 | tf_op jit(solution)/shard_map/ppermute | solution.py:892
  807.7 8.7 %collective-permute-start.58 = (bf16[512,288]{1,0:T(8,128)(2,1)}, bf16[512,288]{1,0:T(8,128)(2,1)S(1)}, u32[]{:S(2)}, u32[]{:S(2)}) collective-permute-start(bf16[512,288]{1,0:T(8,128)(2,1)} %bitcast.293), channel_id=1, source_target_pairs={{0,8},{8,0},{16,24},{24,16},{1,9},{9,1},{17,25},{25,17},{2,10},{10... | collective-permute-start | bytes 884744 | tf_op jit(solution)/shard_map/ppermute | solution.py:892
  811.7 22.9 %collective-permute-start.53 = (bf16[288,640]{1,0:T(8,128)(2,1)S(1)}, bf16[288,640]{1,0:T(8,128)(2,1)S(1)}, u32[]{:S(2)}, u32[]{:S(2)}) collective-permute-start(bf16[288,640]{1,0:T(8,128)(2,1)S(1)} %copy-done.49), channel_id=1, source_target_pairs={{0,4},{1,5},{2,6},{3,7},{4,0},{5,1},{6,2},{7,3},{8,12},{9,13},{10,... | collective-permute-start | bytes 1105928 | tf_op jit(solution)/shard_map/ppermute | solution.py:892
  811.7 22.8 %collective-permute-start.54 = (bf16[288,640]{1,0:T(8,128)(2,1)S(1)}, bf16[288,640]{1,0:T(8,128)(2,1)S(1)}, u32[]{:S(2)}, u32[]{:S(2)}) collective-permute-start(bf16[288,640]{1,0:T(8,128)(2,1)S(1)} %copy-done.47), channel_id=1, source_target_pairs={{0,6},{1,7},{2,4},{3,5},{4,2},{5,3},{6,0},{7,1},{8,14},{9,15},{10,... | collective-permute-start | bytes 1105928 | tf_op jit(solution)/shard_map/ppermute | solution.py:892
  814.0 22.8 %collective-permute-start.52 = (bf16[288,640]{1,0:T(8,128)(2,1)S(1)}, bf16[288,640]{1,0:T(8,128)(2,1)S(1)}, u32[]{:S(2)}, u32[]{:S(2)}) collective-permute-start(bf16[288,640]{1,0:T(8,128)(2,1)S(1)} %copy-done.48), channel_id=1, source_target_pairs={{0,2},{1,3},{2,0},{3,1},{4,6},{5,7},{6,4},{7,5},{8,10},{9,11},{10,... | collective-permute-start | bytes 1105928 | tf_op jit(solution)/shard_map/ppermute | solution.py:892
  817.3 23.4 %collective-permute-start.59 = (bf16[512,288]{1,0:T(8,128)(2,1)}, bf16[512,288]{1,0:T(8,128)(2,1)}, u32[]{:S(2)}, u32[]{:S(2)}) collective-permute-start(bf16[512,288]{1,0:T(8,128)(2,1)} %fusion.14), channel_id=1, source_target_pairs={{0,16},{8,24},{16,0},{24,8},{1,17},{9,25},{17,1},{25,9},{2,18},{10... | collective-permute-start | bytes 884744 | tf_op jit(solution)/shard_map/ppermute | solution.py:892
  (80 other events, 837.3 us)
Sparse Core Ops, SparseCore 0:
  27.7 37.3 all-gather.9
  133.4 26.7 reduce-scatter.5
  185.4 59.6 all-gather.11
  248.3 110.8 all-gather.7
  445.9 178.5 reduce-scatter.9
  635.3 56.1 reduce-scatter.7
  742.8 62.3 all-gather.13

commit v4 on v3

--- a/solution.py
+++ b/solution.py
@@ -1078,7 +1078,7 @@
         18,
     )
 
-    done = [out_a, text_pairs, grad_branch_moved]
+    done = [out_a, text_pairs]
     out_a = after(out_a, *done)
     branch_a, after_a, hidden_b, query_b, out_b, after_b, hidden_c = run(
         functools.partial(text_kernel, win_rest, win_sout, win_cq, win_cout, nx),
@@ -1177,6 +1177,8 @@
         (me, grad_out, grad_hidden_d, after_c, after_b, pre_act, branch_c, mod, full_up, full_down),
         22,
     )
+    branch_d = reorder(after(branch_moved, grad_hidden_d))
+    grads_c = after(grads_c, branch_d)
     grads_other = swap(grads_c, "gx", 1)
     up_terms = up_grads(
         nx,
@@ -1223,7 +1225,6 @@
     text_terms = lax.psum_scatter(
         after(text_terms, late).reshape(nx, -1, kv_width), "gx", scatter_dimension=0, tiled=True
     )
-    branch_d = reorder(after(branch_moved, *done))
     grad_out_a = after(grad_out_a, *done)
 
     grad_query_a, grad_pairs = run(
@@ -1237,7 +1238,7 @@
         (query_a, grad_out_a, out_a, lse_a, *pairs),
         28,
     )
-    done = [grad_pairs, grads_b_other, branch_d]
+    done = [grad_pairs, grads_b_other]
     grad_pairs = after(grad_pairs, *done)
     up_second = up_sums.second(*done)
     done = up_sums.sent

time: 861 us -> 855 us (level)
  blocking collectives: 9.14 us -> 33.5 us
  waiting for transfers between devices: 379 us -> 360 us
    all_to_all x4 -> x3, waiting for transfers between devices: 96.8 us -> 19.6 us  [reorder(): lax.all_to_all(values.reshape(devices, values.shape[0] // devices, values...]
    ppermute x60, waiting for transfers between devices: 261 us -> 320 us  [swap(): lax.ppermute(values, axis, [(i, i ^ mask) for i in range(lax.axis_size(ax...]
    all_to_all x0 -> x1, blocking collectives: none -> 24.3 us  [reorder(): lax.all_to_all(values.reshape(devices, values.shape[0] // devices, values...]
    all_to_all x4 -> x3, starting transfers between devices: 18.7 us -> 8.3 us  [reorder(): lax.all_to_all(values.reshape(devices, values.shape[0] // devices, values...]
    unnamed x160 -> x158, local copies, waits for them, and re-layouts: 21.5 us -> 20.2 us
  transfers between devices with their start and end apart: 71 -> 70, of which waited for: 35 -> 34; matrix products, arithmetic and copies ran while one was open for 11% -> 11% of each run, Pallas kernels for 26% -> 26%
where the time goes in v4:
time: 855 us; the launch traced here: 844 us
  waiting for transfers between devices  360 us (42%)
  Pallas kernels  244 us (29%)
  starting transfers between devices  74.6 us (9%)
  other arithmetic  57.6 us (7%)
  local copies, waits for them, and re-layouts  45.4 us (5%)
  blocking collectives  33.5 us (4%)
  between operations  18 us (2%)
  matrix products  10.6 us (1%)
    ppermute x60, waiting for transfers between devices, swap(): lax.ppermute(values, axis, [(i, i ^ mask) for i in range(lax.axis_size(ax...  320 us
    pallas_call x10, Pallas kernels, run(): pl.pallas_call(grouped, out_shape=outs, in_specs=flat_specs, out_specs=[v...  176 us
    ppermute x60, starting transfers between devices, swap(): lax.ppermute(values, axis, [(i, i ^ mask) for i in range(lax.axis_size(ax...  65.4 us
    pallas_call x2, Pallas kernels, weight_grads(): pl.pallas_call(functools.partial(weight_kernel, nx, lax.axis_size('gy'),...  31.8 us
    all_to_all x1, blocking collectives, reorder(): lax.all_to_all(values.reshape(devices, values.shape[0] // devices, values...  24.3 us
    pallas_call x1, Pallas kernels, up_grads(): pl.pallas_call(kernel, out_shape=outs, grid_spec=pltpu.PrefetchScalarGrid...  21.7 us
    convert_element_type x12, other arithmetic, total(): return sum((term.astype(f32) for term in terms)).astype(bf16)  20.9 us
    reduce_scatter x1, waiting for transfers between devices, local(): lax.psum_scatter(after(text_part, *held), 'gy', scatter_dimension=0, tile...  20.6 us
  transfers between devices with their start and end apart: 70, of which 34 were waited for; matrix products, arithmetic and copies ran while one was open for 11% of the time, Pallas kernels for 26%

profile of v4, /device:TPU:0, one launch (start us, length us, event | category | flops | bytes accessed | tf_op | source)
XLA Modules:
  0.0 844.2 jit_solution(12723720197586946030)
XLA Ops:
  9.6 3.0 collective-permute-start
  18.4 9.1 %all_to_all.25 = bf16[4,16,1024]{2,1,0:T(8,128)(2,1)} all-to-all(bf16[4,16,1024]{2,1,0:T(8,128)(2,1)S(1)} %copy.214), channel_id=1, replica_groups=mesh['gy'=4,'gx'=8] {'gy'}, dimensions={0} | all-to-all | bytes 262144 | tf_op jit(solution)/shard_map/all_to_all | solution.py:984
  28.3 3.7 collective-permute-start.6
  35.2 35.6 %collective-permute-done.3 = f32[2,4,1296]{2,1,0:T(4,128)S(1)} collective-permute-done((f32[2,4,1296]{2,1,0:T(4,128)S(1)}, f32[2,4,1296]{2,1,0:T(4,128)S(1)}, u32[]{:S(2)}, u32[]{:S(2)}) %collective-permute-start.3) | collective-permute-done | bytes 41504 | tf_op jit(solution)/shard_map/ppermute | solution.py:892
  70.9 9.9 %collective-permute-done.5 = bf16[288,896]{1,0:T(8,128)(2,1)S(1)} collective-permute-done((bf16[288,896]{1,0:T(8,128)(2,1)S(1)}, bf16[288,896]{1,0:T(8,128)(2,1)S(1)}, u32[]{:S(2)}, u32[]{:S(2)}) %collective-permute-start.5) | collective-permute-done | bytes 516128 | tf_op jit(solution)/shard_map/ppermute | solution.py:892
  80.7 5.9 collective-permute-done.7
  92.4 2.5 collective-permute-start.10
  96.7 2.8 fusion.46
  99.5 25.3 %collective-permute-done.11 = bf16[576,640]{1,0:T(8,128)(2,1)} collective-permute-done((bf16[576,640]{1,0:T(8,128)(2,1)}, bf16[576,640]{1,0:T(8,128)(2,1)}, u32[]{:S(2)}, u32[]{:S(2)}) %collective-permute-start.11) | collective-permute-done | bytes 737312 | tf_op jit(solution)/shard_map/ppermute | solution.py:892
  126.7 3.5 pad_maximum_fusion.2.refs_3_.refs_4_.refs_5_.refs_7_
  133.4 4.2 collective-permute-done.14.refs_7_.refs_8_.refs_9_.refs_11_
  139.6 20.6 %reduce-scatter.6.cloned.1.call-done = f32[128,288]{0,1:T(8,128)} async-done(((f32[512,288]{0,1:T(8,128)}), f32[128,288]{0,1:T(8,128)}) %reduce-scatter.6.cloned.1.call-update) | async-done | bytes 147472 | tf_op jit(solution)/shard_map/reduce_scatter | solution.py:1013
  160.2 22.4 %collective-permute-done.12.refs_4_.refs_5_.refs_6_.refs_8_ = bf16[2,2,288,896]{3,2,1,0:T(8,128)(2,1)} collective-permute-done((bf16[2,2,288,896]{3,2,1,0:T(8,128)(2,1)}, bf16[2,2,288,896]{3,2,1,0:T(8,128)(2,1)}, u32[]{:S(2)}, u32[]{:S(2)}) %collective-permute-start.12) | collective-permute-done | bytes 2064416 | tf_op jit(solution)/shard_map/ppermute | solution.py:892
  186.6 4.1 fusion.42
  202.3 9.2 %shard_map.265 = (bf16[256,1152]{1,0:T(8,128)(2,1)}, bf16[256,1152]{1,0:T(8,128)(2,1)}, bf16[256,2304]{1,0:T(8,128)(2,1)}) custom-call(s32[2]{0:T(128)} %pad_add_fusion.refs_0_.me_ref, bf16[256,1152]{1,0:T(8,128)(2,1)} %refs_4_.1, f32[9,1152]{1,0:T(8,128)} %reshape.218.refs_2_.refs_3_.refs_7_.refs_4_.refs_5_, ...), custom_call_target="tpu_custom_call" | custom-call | flops 180000000 | tf_op jit(solution)/shard_map/pallas_call | solution.py:57
  211.5 16.6 %collective-permute-done.20 = bf16[2,576,640]{2,1,0:T(8,128)(2,1)} collective-permute-done((bf16[2,576,640]{2,1,0:T(8,128)(2,1)}, bf16[2,576,640]{2,1,0:T(8,128)(2,1)}, u32[]{:S(2)}, u32[]{:S(2)}) %collective-permute-start.20) | collective-permute-done | bytes 1474592 | tf_op jit(solution)/shard_map/ppermute | solution.py:892
  230.0 4.3 pad_maximum_fusion.refs_4_.refs_8_
  237.2 35.1 %collective-permute-done.21.refs_2_.refs_5_ = bf16[256,2304]{1,0:T(8,128)(2,1)} collective-permute-done((bf16[256,2304]{1,0:T(8,128)(2,1)S(1)}, bf16[256,2304]{1,0:T(8,128)(2,1)}, u32[]{:S(2)}, u32[]{:S(2)}) %collective-permute-start.21) | collective-permute-done | bytes 1179680 | tf_op jit(solution)/shard_map/ppermute | solution.py:892
  277.8 18.5 %shard_map.266 = (bf16[256,1152]{1,0:T(8,128)(2,1)}, f32[16,256]{1,0:T(8,128)}) custom-call(bf16[256,1152]{1,0:T(8,128)(2,1)} %get-tuple-element.155.refs_0_, bf16[256,2304]{1,0:T(8,128)(2,1)} %get-tuple-element.150.refs_1_.refs_4_, bf16[256,2304]{1,0:T(8,128)(2,1)} %collective-permute-done.21.refs_2_.refs_5_, bf16[256,2304]{1,0:T(8,128)(2,1)} %copy-done.18, ...), custom_call_target="tpu_custom_call" | custom-call | flops 360000000 | tf_op jit(solution)/shard_map/pallas_call | solution.py:57
  296.4 18.0 %shard_map.267 = (f32[256,1152]{1,0:T(8,128)}, f32[256,1152]{1,0:T(8,128)}, bf16[256,1152]{1,0:T(8,128)(2,1)}, bf16[256,1152]{1,0:T(8,128)(2,1)}, bf16[256,1152]...) custom-call(s32[2]{0:T(128)} %pad_add_fusion.refs_0_.me_ref, bf16[256,1152]{1,0:T(8,128)(2,1)} %refs_4_.1, ...), custom_call_target="tpu_custom_call" | custom-call | flops 360000000 | tf_op jit(solution)/shard_map/pallas_call | solution.py:57
  316.9 6.1 collective-permute-done.28.refs_9_.refs_13_
  323.1 4.3 collective-permute-done.29.refs_11_.refs_15_
  328.9 20.8 %shard_map.268 = (f32[256,4608]{1,0:T(8,128)}, bf16[256,4608]{1,0:T(8,128)(2,1)}, f32[256,1152]{1,0:T(8,128)}, f32[256,1152]{1,0:T(8,128)}, bf16[256,1152]{1,0:T(8,128)(2,1)}) custom-call(s32[2]{0:T(128)} %pad_add_fusion.refs_0_.me_ref, bf16[256,1152]{1,0:T(8,128)(2,1)} %get-tuple-element.162.refs_1_.refs_0_, ...), custom_call_target="tpu_custom_call" | custom-call | flops 400000000 | tf_op jit(solution)/shard_map/pallas_call | solution.py:57
  354.4 24.3 %all_to_all.26 = bf16[32,8,1152]{2,1,0:T(8,128)(2,1)} all-to-all(bf16[32,8,1152]{2,1,0:T(8,128)(2,1)S(1)} %bitcast.288), channel_id=1, replica_groups=mesh['gy'=4,'gx'=8] {'gy','gx'}, dimensions={0} | all-to-all | bytes 1179648 | tf_op jit(solution)/shard_map/all_to_all | solution.py:897
  378.7 2.6 all-to-all-start.1
  382.3 16.8 %all-to-all-done.1 = bf16[32,8,1152]{2,1,0:T(8,128)(2,1)S(1)} async-done(((bf16[32,8,1152]{2,1,0:T(8,128)(2,1)}), bf16[32,8,1152]{2,1,0:T(8,128)(2,1)S(1)}, u32[]{:S(2)}, u32[]{:S(2)}) %all-to-all-start.1) | async-done | bytes 589856 | tf_op jit(solution)/shard_map/all_to_all | solution.py:897
  399.9 24.0 %shard_map.269 = (bf16[256,4608]{1,0:T(8,128)(2,1)}, bf16[256,1152]{1,0:T(8,128)(2,1)}, bf16[256,1152]{1,0:T(8,128)(2,1)}) custom-call(bf16[256,1152]{1,0:T(8,128)(2,1)} %bitcast.277, bf16[256,1152]{1,0:T(8,128)(2,1)} %bitcast.275, bf16[8,1152,640]{2,1,0:T(8,128)(2,1)} %bitcast.271, f32[256,1]{1,0:T(8,128)} %broadcast_in_dim_reshape.4.refs_3_, f32[8]{0:T(128)} %copy-done.63), custom_call_target="tpu_custom_call" | custom-call | flops 500000000 | tf_op jit(solution)/shard_map/pallas_call | solution.py:57
  424.0 2.6 all-to-all-start.3
  426.7 14.9 %shard_map.278 = bf16[8,1152,640]{2,1,0:T(8,128)(2,1)} custom-call(bf16[256,1152]{1,0:T(8,128)(2,1)} %bitcast.278, bf16[256,1152]{1,0:T(8,128)(2,1)} %bitcast.276, bf16[256,4608]{1,0:T(8,128)(2,1)} %get-tuple-element.238.refs_2_), custom_call_target="tpu_custom_call" | custom-call | flops 260000000 | tf_op jit(solution)/shard_map/pallas_call | solution.py:692
  441.6 2.8 all-to-all-done.3
  445.2 3.1 all-to-all-start.4
  448.7 23.4 %shard_map.271 = (bf16[256,5760]{1,0:T(8,128)(2,1)}, f32[256,1152]{1,0:T(8,128)}, f32[8,1152]{1,0:T(8,128)}) custom-call(s32[2]{0:T(128)} %pad_add_fusion.refs_0_.me_ref, bf16[256,1152]{1,0:T(8,128)(2,1)} %refs_1_.5, bf16[256,1152]{1,0:T(8,128)(2,1)} %bitcast.290, f32[256,1152]{1,0:T(8,128)} %get-tuple-element.177.refs_1_.refs_3_, ...), custom_call_target="tpu_custom_call" | custom-call | flops 440000000 | tf_op jit(solution)/shard_map/pallas_call | solution.py:57
  472.5 3.6 slice_bitcast_fusion.22
  479.9 21.7 %shard_map.272 = (bf16[2,1152,640]{2,1,0:T(8,128)(2,1)}, bf16[2,1152,640]{2,1,0:T(8,128)(2,1)}, bf16[2,1152,640]{2,1,0:T(8,128)(2,1)}, bf16[2,1152,640]{2,1,0:T(8,128)(2,1)}) custom-call(s32[2]{0:T(128)} %pad_add_fusion.refs_0_.me_ref, bf16[256,1152]{1,0:T(8,128)(2,1)} %get-tuple-element.162.refs_1_.refs_0_, bf16[256,5760]{1,0:T(8,128)(2,1)} %get-tuple-element.183.refs_1_, ...), custom_call_target="tpu_custom_call" | custom-call | flops 320000000 | tf_op jit(solution)/shard_map/pallas_call | solution.py:753
  501.6 19.8 %shard_map.273 = (bf16[256,3456]{1,0:T(8,128)(2,1)}, f32[256,1152]{1,0:T(8,128)}, bf16[256,1152]{1,0:T(8,128)(2,1)}, bf16[8,128,288]{2,1,0:T(8,128)(2,1)}, f32[1,1152]{1,0:T(1,128)}) custom-call(s32[2]{0:T(128)} %pad_add_fusion.refs_0_.me_ref, f32[256,1152]{1,0:T(8,128)} %get-tuple-element.188.refs_1_, f32[256,1152]{1,0:T(8,128)} %get-tuple-element.189.refs_2_, ...), custom_call_target="tpu_custom_call" | custom-call | flops 400000000 | tf_op jit(solution)/shard_map/pallas_call | solution.py:57
  522.5 2.4 collective-permute-start.36
  524.9 2.8 collective-permute-start.37
  527.7 28.4 %shard_map.274 = (bf16[256,1152]{1,0:T(8,128)(2,1)}, bf16[4,256,2304]{2,1,0:T(8,128)(2,1)}) custom-call(bf16[256,1152]{1,0:T(8,128)(2,1)} %get-tuple-element.155.refs_0_, bf16[256,1152]{1,0:T(8,128)(2,1)} %get-tuple-element.192.refs_1_, bf16[256,1152]{1,0:T(8,128)(2,1)} %get-tuple-element.158.refs_2_.refs_1_, f32[16,256]{1,0:T(8,128)} %get-tuple-element.193.refs_3_, ...), custom_call_target="tpu_custom_call" | custom-call | flops 560000000 | tf_op jit(solution)/shard_map/pallas_call | solution.py:57
  556.2 2.5 slice.188
  558.8 54.3 %collective-permute-done.36 = bf16[2,1152,640]{2,1,0:T(8,128)(2,1)} collective-permute-done((bf16[2,1152,640]{2,1,0:T(8,128)(2,1)}, bf16[2,1152,640]{2,1,0:T(8,128)(2,1)}, u32[]{:S(2)}, u32[]{:S(2)}) %collective-permute-start.36) | collective-permute-done | bytes 2949152 | tf_op jit(solution)/shard_map/ppermute | solution.py:892
  613.1 3.0 fusion.2
  616.1 2.8 collective-permute-start.38
  618.9 2.9 fusion.3
  630.6 14.3 %shard_map.275 = (bf16[2,576,384]{2,1,0:T(8,128)(2,1)}, bf16[2,576,384]{2,1,0:T(8,128)(2,1)}, bf16[2,576,384]{2,1,0:T(8,128)(2,1)}, bf16[2,576,384]{2,1,0:T(8,128)(2,1)}) custom-call(s32[2]{0:T(128)} %pad_add_fusion.refs_0_.me_ref, bf16[256,1152]{1,0:T(8,128)(2,1)} %get-tuple-element.166.refs_0_, bf16[256,1152]{1,0:T(8,128)(2,1)} %get-tuple-element.167.refs_1_, ...), custom_call_target="tpu_custom_call" | custom-call | flops 180000000 | tf_op jit(solution)/shard_map/pallas_call | solution.py:644
  644.9 6.2 collective-permute-done.38
  651.1 4.4 collective-permute-done.39
  655.5 13.7 %collective-permute-done.35.refs_3_ = bf16[256,2304]{1,0:T(8,128)(2,1)S(1)} collective-permute-done((bf16[256,2304]{1,0:T(8,128)(2,1)}, bf16[256,2304]{1,0:T(8,128)(2,1)S(1)}, u32[]{:S(2)}, u32[]{:S(2)}) %collective-permute-start.35) | collective-permute-done | bytes 1179680 | tf_op jit(solution)/shard_map/ppermute | solution.py:892
  669.3 2.8 fusion.1
  676.7 11.1 %shard_map.276 = (bf16[256,3456]{1,0:T(8,128)(2,1)}, bf16[256,1152]{1,0:T(8,128)(2,1)}, f32[2,1152]{1,0:T(2,128)}) custom-call(s32[2]{0:T(128)} %pad_add_fusion.refs_0_.me_ref, bf16[256,1152]{1,0:T(8,128)(2,1)} %get-tuple-element.207.refs_1_, bf16[256,2304]{1,0:T(8,128)(2,1)} %get-tuple-element.319.refs_2_, bf16[256,2304]{1,0:T(8,128)(2,1)} %copy-done.35, ...), custom_call_target="tpu_custom_call" | custom-call | flops 220000000 | tf_op jit(solution)/shard_map/pallas_call | solution.py:57
  688.0 6.3 collective-permute-start.45
  695.6 17.6 %shard_map.277 = (bf16[2,576,640]{2,1,0:T(8,128)(2,1)}, bf16[2,576,640]{2,1,0:T(8,128)(2,1)}, bf16[2,576,640]{2,1,0:T(8,128)(2,1)}, bf16[2,576,640]{2,1,0:T(8,128)(2,1)}) custom-call(s32[2]{0:T(128)} %pad_add_fusion.refs_0_.me_ref, bf16[256,1152]{1,0:T(8,128)(2,1)} %get-tuple-element.165.refs_0_, bf16[256,1152]{1,0:T(8,128)(2,1)} %get-tuple-element.158.refs_2_.refs_1_, ...), custom_call_target="tpu_custom_call" | custom-call | flops 180000000 | tf_op jit(solution)/shard_map/pallas_call | solution.py:644
  717.1 3.1 collective-permute-start.49
  720.3 6.4 collective-permute-done.43
  730.4 2.7 shard_map.270
  734.5 12.8 %collective-permute-done.48 = bf16[576,640]{1,0:T(8,128)(2,1)} collective-permute-done((bf16[576,640]{1,0:T(8,128)(2,1)}, bf16[576,640]{1,0:T(8,128)(2,1)}, u32[]{:S(2)}, u32[]{:S(2)}) %collective-permute-start.48) | collective-permute-done | bytes 737312 | tf_op jit(solution)/shard_map/ppermute | solution.py:892
  747.3 10.1 %collective-permute-done.49 = bf16[576,640]{1,0:T(8,128)(2,1)} collective-permute-done((bf16[576,640]{1,0:T(8,128)(2,1)}, bf16[576,640]{1,0:T(8,128)(2,1)}, u32[]{:S(2)}, u32[]{:S(2)}) %collective-permute-start.49) | collective-permute-done | bytes 737312 | tf_op jit(solution)/shard_map/ppermute | solution.py:892
  770.8 2.7 collective-permute-start.57
  775.2 6.2 collective-permute-done.55
  781.4 3.8 collective-permute-done.57
  785.2 10.7 %collective-permute-done.56 = bf16[288,384]{1,0:T(8,128)(2,1)S(1)} collective-permute-done((bf16[288,384]{1,0:T(8,128)(2,1)S(1)}, bf16[288,384]{1,0:T(8,128)(2,1)S(1)}, u32[]{:S(2)}, u32[]{:S(2)}) %collective-permute-start.56) | collective-permute-done | bytes 221216 | tf_op jit(solution)/shard_map/ppermute | solution.py:892
  804.7 2.7 collective-permute-start.54
  810.9 3.6 fusion.39
  814.5 15.0 %collective-permute-done.53 = bf16[288,640]{1,0:T(8,128)(2,1)S(1)} collective-permute-done((bf16[288,640]{1,0:T(8,128)(2,1)S(1)}, bf16[288,640]{1,0:T(8,128)(2,1)S(1)}, u32[]{:S(2)}, u32[]{:S(2)}) %collective-permute-start.53) | collective-permute-done | bytes 368672 | tf_op jit(solution)/shard_map/ppermute | solution.py:892
  834.5 2.7 fusion.28
  (351 shorter events, 123.2 us)
Async XLA Ops:
  7.2 73.5 %all-gather.10.cloned.1.call-start = ((), (), s32[]{:S(2)}) async-start(), calls=%async_computation.11 | async-start | bytes 1179648 | tf_op jit(solution)/shard_map/all_gather | solution.py:985
  27.5 132.7 %reduce-scatter.6.cloned.1.call-start = ((), (), s32[]{:S(2)}) async-start(), calls=%async_computation.8 | async-start | bytes 737280 | tf_op jit(solution)/shard_map/reduce_scatter | solution.py:1013
  28.3 42.6 %collective-permute-start.6 = (bf16[288,896]{1,0:T(8,128)(2,1)S(1)}, bf16[288,896]{1,0:T(8,128)(2,1)S(1)}, u32[]{:S(2)}, u32[]{:S(2)}) collective-permute-start(bf16[288,896]{1,0:T(8,128)(2,1)S(1)} %fusion.23), channel_id=1, source_target_pairs={{0,6},{1,7},{2,4},{3,5},{4,2},{5,3},{6,0},{7,1},{8,14},{9,15},{10,... | collective-permute-start | bytes 1548296 | tf_op jit(solution)/shard_map/ppermute | solution.py:892
  31.9 48.8 %collective-permute-start.5 = (bf16[288,896]{1,0:T(8,128)(2,1)S(1)}, bf16[288,896]{1,0:T(8,128)(2,1)S(1)}, u32[]{:S(2)}, u32[]{:S(2)}) collective-permute-start(bf16[288,896]{1,0:T(8,128)(2,1)S(1)} %fusion.23), channel_id=1, source_target_pairs={{0,4},{1,5},{2,6},{3,7},{4,0},{5,1},{6,2},{7,3},{8,12},{9,13},{10,... | collective-permute-start | bytes 1548296 | tf_op jit(solution)/shard_map/ppermute | solution.py:892
  31.9 48.8 %collective-permute-start.4 = (bf16[288,896]{1,0:T(8,128)(2,1)S(1)}, bf16[288,896]{1,0:T(8,128)(2,1)S(1)}, u32[]{:S(2)}, u32[]{:S(2)}) collective-permute-start(bf16[288,896]{1,0:T(8,128)(2,1)S(1)} %fusion.23), channel_id=1, source_target_pairs={{0,2},{1,3},{2,0},{3,1},{4,6},{5,7},{6,4},{7,5},{8,10},{9,11},{10,... | collective-permute-start | bytes 1548296 | tf_op jit(solution)/shard_map/ppermute | solution.py:892
  33.9 36.9 %collective-permute-start.3 = (f32[2,4,1296]{2,1,0:T(4,128)S(1)}, f32[2,4,1296]{2,1,0:T(4,128)S(1)}, u32[]{:S(2)}, u32[]{:S(2)}) collective-permute-start(f32[2,4,1296]{2,1,0:T(4,128)S(1)} %maximum_select_fusion.2), channel_id=1, source_target_pairs={{0,2},{1,3},{2,0},{3,1},{4,6},{5,7},{6,4},{7,5},{8,10},{9,11},{10,... | collective-permute-start | bytes 124424 | tf_op jit(solution)/shard_map/ppermute | solution.py:892
  88.5 36.4 %collective-permute-start.8 = (bf16[2,288,896]{2,1,0:T(8,128)(2,1)}, bf16[2,288,896]{2,1,0:T(8,128)(2,1)}, u32[]{:S(2)}, u32[]{:S(2)}) collective-permute-start(bf16[2,288,896]{2,1,0:T(8,128)(2,1)} %get-tuple-element.330), channel_id=1, source_target_pairs={{0,8},{8,0},{16,24},{24,16},{1,9},{9,1},{17,25},{25,17},{2,10},{10... | collective-permute-start | bytes 3096584 | tf_op jit(solution)/shard_map/ppermute | solution.py:892
  90.9 34.0 %collective-permute-start.9 = (bf16[2,288,896]{2,1,0:T(8,128)(2,1)}, bf16[2,288,896]{2,1,0:T(8,128)(2,1)}, u32[]{:S(2)}, u32[]{:S(2)}) collective-permute-start(bf16[2,288,896]{2,1,0:T(8,128)(2,1)} %get-tuple-element.328), channel_id=1, source_target_pairs={{0,16},{8,24},{16,0},{24,8},{1,17},{9,25},{17,1},{25,9},{2,18},{10... | collective-permute-start | bytes 3096584 | tf_op jit(solution)/shard_map/ppermute | solution.py:892
  92.4 32.3 %collective-permute-start.11 = (bf16[576,640]{1,0:T(8,128)(2,1)}, bf16[576,640]{1,0:T(8,128)(2,1)}, u32[]{:S(2)}, u32[]{:S(2)}) collective-permute-start(bf16[576,640]{1,0:T(8,128)(2,1)} %fusion.15), channel_id=1, source_target_pairs={{0,4},{1,5},{2,6},{3,7},{4,0},{5,1},{6,2},{7,3},{8,12},{9,13},{10,... | collective-permute-start | bytes 2211848 | tf_op jit(solution)/shard_map/ppermute | solution.py:892
  92.4 32.4 %collective-permute-start.10 = (bf16[576,640]{1,0:T(8,128)(2,1)}, bf16[576,640]{1,0:T(8,128)(2,1)}, u32[]{:S(2)}, u32[]{:S(2)}) collective-permute-start(bf16[576,640]{1,0:T(8,128)(2,1)} %fusion.15), channel_id=1, source_target_pairs={{0,2},{1,3},{2,0},{3,1},{4,6},{5,7},{6,4},{7,5},{8,10},{9,11},{10,... | collective-permute-start | bytes 2211848 | tf_op jit(solution)/shard_map/ppermute | solution.py:892
  130.2 7.4 collective-permute-start.14
  130.2 7.4 collective-permute-start.15
  130.7 51.9 %collective-permute-start.12 = (bf16[2,2,288,896]{3,2,1,0:T(8,128)(2,1)}, bf16[2,2,288,896]{3,2,1,0:T(8,128)(2,1)}, u32[]{:S(2)}, u32[]{:S(2)}) collective-permute-start(bf16[2,2,288,896]{3,2,1,0:T(8,128)(2,1)} %pad_maximum_fusion.2.refs_3_.refs_4_.refs_5_.refs_7_), channel_id=1, source_target_pairs={{0,16},{8,24},{16,0},{24,8},{1,17},{9,25},{17,1},{25,9},{2,18},{10... | collective-permute-start | bytes 6193160 | tf_op jit(solution)/shard_map/ppermute | solution.py:892
  132.2 51.4 %collective-permute-start.13 = (bf16[2,2,288,896]{3,2,1,0:T(8,128)(2,1)S(1)}, bf16[2,2,288,896]{3,2,1,0:T(8,128)(2,1)}, u32[]{:S(2)}, u32[]{:S(2)}) collective-permute-start(bf16[2,2,288,896]{3,2,1,0:T(8,128)(2,1)S(1)} %pad_maximum_fusion.3.refs_5_.refs_6_.refs_7_.refs_9_), channel_id=1, source_target_pairs={{0,8},{8,0},{16,24},{24,16},{1,9},{9,1},{17,25},{25,17},{2,10},{10... | collective-permute-start | bytes 6193160 | tf_op jit(solution)/shard_map/ppermute | solution.py:892
  133.3 140.3 %all-gather.12.cloned.1.call-start = ((), (), s32[]{:S(2)}) async-start(), calls=%async_computation.12 | async-start | bytes 2433024 | tf_op jit(solution)/shard_map/all_gather | solution.py:1055
  137.6 46.0 %collective-permute-start.16 = (bf16[576,640]{1,0:T(8,128)(2,1)}, bf16[576,640]{1,0:T(8,128)(2,1)S(1)}, u32[]{:S(2)}, u32[]{:S(2)}) collective-permute-start(bf16[576,640]{1,0:T(8,128)(2,1)} %fusion.15), channel_id=1, source_target_pairs={{0,6},{1,7},{2,4},{3,5},{4,2},{5,3},{6,0},{7,1},{8,14},{9,15},{10,... | collective-permute-start | bytes 2211848 | tf_op jit(solution)/shard_map/ppermute | solution.py:892
  185.3 213.8 %all-gather.8.cloned.1.call-start = ((), (), s32[]{:S(2)}) async-start(), calls=%async_computation.9 | async-start | bytes 12165120 | tf_op jit(solution)/shard_map/all_gather | solution.py:1056
  190.7 10.2 %collective-permute-start.17 = (bf16[2,2,288,896]{3,2,1,0:T(8,128)(2,1)}, bf16[2,2,288,896]{3,2,1,0:T(8,128)(2,1)S(1)}, u32[]{:S(2)}, u32[]{:S(2)}) collective-permute-start(bf16[2,2,288,896]{3,2,1,0:T(8,128)(2,1)} %collective-permute-done.12.refs_4_.refs_5_.refs_6_.refs_8_), channel_id=1, source_target_pairs={{0,1},{1,0},{2,3},{3,2},{4,5},{5,4},{6,7},{7,6},{8,9},{9,8},{10,11... | collective-permute-start | bytes 6193160 | tf_op jit(solution)/shard_map/ppermute | solution.py:892
  190.7 10.2 %collective-permute-start.18 = (bf16[2,2,288,896]{3,2,1,0:T(8,128)(2,1)}, bf16[2,2,288,896]{3,2,1,0:T(8,128)(2,1)}, u32[]{:S(2)}, u32[]{:S(2)}) collective-permute-start(bf16[2,2,288,896]{3,2,1,0:T(8,128)(2,1)} %collective-permute-done.13.refs_6_.refs_7_.refs_8_.refs_10_), channel_id=1, source_target_pairs={{0,1},{1,0},{2,3},{3,2},{4,5},{5,4},{6,7},{7,6},{8,9},{9,8},{10,11... | collective-permute-start | bytes 6193160 | tf_op jit(solution)/shard_map/ppermute | solution.py:892
  191.2 36.9 %collective-permute-start.20 = (bf16[2,576,640]{2,1,0:T(8,128)(2,1)}, bf16[2,576,640]{2,1,0:T(8,128)(2,1)}, u32[]{:S(2)}, u32[]{:S(2)}) collective-permute-start(bf16[2,576,640]{2,1,0:T(8,128)(2,1)} %get-tuple-element.324), channel_id=1, source_target_pairs={{0,16},{8,24},{16,0},{24,8},{1,17},{9,25},{17,1},{25,9},{2,18},{10... | collective-permute-start | bytes 4423688 | tf_op jit(solution)/shard_map/ppermute | solution.py:892
  191.8 36.3 %collective-permute-start.19 = (bf16[2,576,640]{2,1,0:T(8,128)(2,1)S(1)}, bf16[2,576,640]{2,1,0:T(8,128)(2,1)}, u32[]{:S(2)}, u32[]{:S(2)}) collective-permute-start(bf16[2,576,640]{2,1,0:T(8,128)(2,1)S(1)} %get-tuple-element.343), channel_id=1, source_target_pairs={{0,8},{8,0},{16,24},{24,16},{1,9},{9,1},{17,25},{25,17},{2,10},{10... | collective-permute-start | bytes 4423688 | tf_op jit(solution)/shard_map/ppermute | solution.py:892
  228.1 9.0 %collective-permute-start.22 = (bf16[256,2304]{1,0:T(8,128)(2,1)}, bf16[256,2304]{1,0:T(8,128)(2,1)S(1)}, u32[]{:S(2)}, u32[]{:S(2)}) collective-permute-start(bf16[256,2304]{1,0:T(8,128)(2,1)} %get-tuple-element.150.refs_1_.refs_4_), channel_id=1, source_target_pairs={{0,1},{1,0},{2,3},{3,2},{4,5},{5,4},{6,7},{7,6},{8,9},{9,8},{10,11... | collective-permute-start | bytes 3538952 | tf_op jit(solution)/shard_map/ppermute | solution.py:892
  234.3 43.5 %collective-permute-start.24 = (bf16[2,2,576,640]{3,2,1,0:T(8,128)(2,1)}, bf16[2,2,576,640]{3,2,1,0:T(8,128)(2,1)}, u32[]{:S(2)}, u32[]{:S(2)}) collective-permute-start(bf16[2,2,576,640]{3,2,1,0:T(8,128)(2,1)} %pad_maximum_fusion.refs_4_.refs_8_), channel_id=1, source_target_pairs={{0,1},{1,0},{2,3},{3,2},{4,5},{5,4},{6,7},{7,6},{8,9},{9,8},{10,11... | collective-permute-start | bytes 8847368 | tf_op jit(solution)/shard_map/ppermute | solution.py:892
  234.8 43.0 %collective-permute-start.25 = (bf16[2,2,576,640]{3,2,1,0:T(8,128)(2,1)S(1)}, bf16[2,2,576,640]{3,2,1,0:T(8,128)(2,1)}, u32[]{:S(2)}, u32[]{:S(2)}) collective-permute-start(bf16[2,2,576,640]{3,2,1,0:T(8,128)(2,1)S(1)} %pad_maximum_fusion.1.refs_6_.refs_10_), channel_id=1, source_target_pairs={{0,1},{1,0},{2,3},{3,2},{4,5},{5,4},{6,7},{7,6},{8,9},{9,8},{10,11... | collective-permute-start | bytes 8847368 | tf_op jit(solution)/shard_map/ppermute | solution.py:892
  234.8 79.5 %collective-permute-start.26 = (bf16[2,2,576,640]{3,2,1,0:T(8,128)(2,1)}, bf16[2,2,576,640]{3,2,1,0:T(8,128)(2,1)}, u32[]{:S(2)}, u32[]{:S(2)}) collective-permute-start(bf16[2,2,576,640]{3,2,1,0:T(8,128)(2,1)} %pad_maximum_fusion.refs_4_.refs_8_), channel_id=1, source_target_pairs={{0,16},{8,24},{16,0},{24,8},{1,17},{9,25},{17,1},{25,9},{2,18},{10... | collective-permute-start | bytes 8847368 | tf_op jit(solution)/shard_map/ppermute | solution.py:892
  235.4 79.3 %collective-permute-start.27 = (bf16[2,2,576,640]{3,2,1,0:T(8,128)(2,1)S(1)}, bf16[2,2,576,640]{3,2,1,0:T(8,128)(2,1)}, u32[]{:S(2)}, u32[]{:S(2)}) collective-permute-start(bf16[2,2,576,640]{3,2,1,0:T(8,128)(2,1)S(1)} %pad_maximum_fusion.1.refs_6_.refs_10_), channel_id=1, source_target_pairs={{0,8},{8,0},{16,24},{24,16},{1,9},{9,1},{17,25},{25,17},{2,10},{10... | collective-permute-start | bytes 8847368 | tf_op jit(solution)/shard_map/ppermute | solution.py:892
  237.1 35.2 %collective-permute-start.21 = (bf16[256,2304]{1,0:T(8,128)(2,1)S(1)}, bf16[256,2304]{1,0:T(8,128)(2,1)}, u32[]{:S(2)}, u32[]{:S(2)}) collective-permute-start(bf16[256,2304]{1,0:T(8,128)(2,1)S(1)} %copy-done.17), channel_id=1, source_target_pairs={{0,2},{1,3},{2,0},{3,1},{4,6},{5,7},{6,4},{7,5},{8,10},{9,11},{10,... | collective-permute-start | bytes 3538952 | tf_op jit(solution)/shard_map/ppermute | solution.py:892
  314.7 8.4 collective-permute-start.28
  315.4 12.0 %collective-permute-start.29 = (bf16[2,2,576,640]{3,2,1,0:T(8,128)(2,1)}, bf16[2,2,576,640]{3,2,1,0:T(8,128)(2,1)S(1)}, u32[]{:S(2)}, u32[]{:S(2)}) collective-permute-start(bf16[2,2,576,640]{3,2,1,0:T(8,128)(2,1)} %collective-permute-done.27.refs_7_.refs_11_), channel_id=1, source_target_pairs={{0,1},{1,0},{2,3},{3,2},{4,5},{5,4},{6,7},{7,6},{8,9},{9,8},{10,11... | collective-permute-start | bytes 8847368 | tf_op jit(solution)/shard_map/ppermute | solution.py:892
  350.6 48.5 %collective-permute-start.30 = (bf16[5,256,1152]{2,1,0:T(8,128)(2,1)}, bf16[5,256,1152]{2,1,0:T(8,128)(2,1)}, u32[]{:S(2)}, u32[]{:S(2)}) collective-permute-start(bf16[5,256,1152]{2,1,0:T(8,128)(2,1)} %bitcast_dynamic-update-slice_fusion), channel_id=1, source_target_pairs={{0,1},{1,0},{2,3},{3,2},{4,5},{5,4},{6,7},{7,6},{8,9},{9,8},{10,11... | collective-permute-start | bytes 8847368 | tf_op jit(solution)/shard_map/ppermute | solution.py:892
  354.2 44.9 %collective-permute-start.31 = (bf16[256,4608]{1,0:T(8,128)(2,1)}, bf16[256,4608]{1,0:T(8,128)(2,1)}, u32[]{:S(2)}, u32[]{:S(2)}) collective-permute-start(bf16[256,4608]{1,0:T(8,128)(2,1)} %get-tuple-element.170.refs_2_), channel_id=1, source_target_pairs={{0,1},{1,0},{2,3},{3,2},{4,5},{5,4},{6,7},{7,6},{8,9},{9,8},{10,11... | collective-permute-start | bytes 7077896 | tf_op jit(solution)/shard_map/ppermute | solution.py:892
  378.7 20.4 %all-to-all-start.1 = ((bf16[32,8,1152]{2,1,0:T(8,128)(2,1)}), bf16[32,8,1152]{2,1,0:T(8,128)(2,1)S(1)}, u32[]{:S(2)}, u32[]{:S(2)}) async-start(bf16[32,8,1152]{2,1,0:T(8,128)(2,1)} %bitcast.31), calls=%async_computation.2 | async-start | bytes 1179648 | tf_op jit(solution)/shard_map/all_to_all | solution.py:897
  424.0 20.4 %all-to-all-start.3 = ((bf16[32,8,1152]{2,1,0:T(8,128)(2,1)}), bf16[32,8,1152]{2,1,0:T(8,128)(2,1)S(1)}, u32[]{:S(2)}, u32[]{:S(2)}) async-start(bf16[32,8,1152]{2,1,0:T(8,128)(2,1)} %bitcast.310), calls=%async_computation.4 | async-start | bytes 1179648 | tf_op jit(solution)/shard_map/all_to_all | solution.py:897
  426.6 202.7 %reduce-scatter.10.cloned.1.call-start = ((), (), s32[]{:S(2)}) async-start(), calls=%async_computation.14 | async-start | bytes 12165120
  445.2 26.9 %all-to-all-start.4 = ((bf16[32,8,1152]{2,1,0:T(8,128)(2,1)}), bf16[32,8,1152]{2,1,0:T(8,128)(2,1)S(1)}, u32[]{:S(2)}, u32[]{:S(2)}) async-start(bf16[32,8,1152]{2,1,0:T(8,128)(2,1)} %bitcast.43), calls=%async_computation.5 | async-start | bytes 1179648 | tf_op jit(solution)/shard_map/all_to_all | solution.py:897
  448.3 352.4 %reduce-scatter.8.cloned.1.call-start = ((), (), s32[]{:S(2)}) async-start(), calls=%async_computation.10 | async-start | bytes 3538944 | tf_op jit(solution)/shard_map/reduce_scatter | solution.py:1225
  521.4 34.8 %collective-permute-start.33 = (bf16[256,3456]{1,0:T(8,128)(2,1)}, bf16[256,3456]{1,0:T(8,128)(2,1)S(1)}, u32[]{:S(2)}, u32[]{:S(2)}) collective-permute-start(bf16[256,3456]{1,0:T(8,128)(2,1)} %get-tuple-element.202.refs_2_.refs_3_), channel_id=1, source_target_pairs={{0,1},{1,0},{2,3},{3,2},{4,5},{5,4},{6,7},{7,6},{8,9},{9,8},{10,11... | collective-permute-start | bytes 5308424 | tf_op jit(solution)/shard_map/ppermute | solution.py:892
  522.5 90.5 %collective-permute-start.36 = (bf16[2,1152,640]{2,1,0:T(8,128)(2,1)}, bf16[2,1152,640]{2,1,0:T(8,128)(2,1)}, u32[]{:S(2)}, u32[]{:S(2)}) collective-permute-start(bf16[2,1152,640]{2,1,0:T(8,128)(2,1)} %get-tuple-element.198), channel_id=1, source_target_pairs={{0,16},{8,24},{16,0},{24,8},{1,17},{9,25},{17,1},{25,9},{2,18},{10... | collective-permute-start | bytes 8847368 | tf_op jit(solution)/shard_map/ppermute | solution.py:892
  524.9 88.1 %collective-permute-start.37 = (bf16[2,1152,640]{2,1,0:T(8,128)(2,1)}, bf16[2,1152,640]{2,1,0:T(8,128)(2,1)}, u32[]{:S(2)}, u32[]{:S(2)}) collective-permute-start(bf16[2,1152,640]{2,1,0:T(8,128)(2,1)} %get-tuple-element.199), channel_id=1, source_target_pairs={{0,8},{8,0},{16,24},{24,16},{1,9},{9,1},{17,25},{25,17},{2,10},{10... | collective-permute-start | bytes 8847368 | tf_op jit(solution)/shard_map/ppermute | solution.py:892
  558.7 64.8 %collective-permute-start.34 = (bf16[2,256,2304]{2,1,0:T(8,128)(2,1)S(1)}, bf16[2,256,2304]{2,1,0:T(8,128)(2,1)S(1)}, u32[]{:S(2)}, u32[]{:S(2)}) collective-permute-start(bf16[2,256,2304]{2,1,0:T(8,128)(2,1)S(1)} %slice.188), channel_id=1, source_target_pairs={{0,1},{1,0},{2,3},{3,2},{4,5},{5,4},{6,7},{7,6},{8,9},{9,8},{10,11... | collective-permute-start | bytes 7077896 | tf_op jit(solution)/shard_map/ppermute | solution.py:892
  616.1 35.0 %collective-permute-start.38 = (bf16[2,576,640]{2,1,0:T(8,128)(2,1)}, bf16[2,576,640]{2,1,0:T(8,128)(2,1)S(1)}, u32[]{:S(2)}, u32[]{:S(2)}) collective-permute-start(bf16[2,576,640]{2,1,0:T(8,128)(2,1)} %fusion.2), channel_id=1, source_target_pairs={{0,8},{8,0},{16,24},{24,16},{1,9},{9,1},{17,25},{25,17},{2,10},{10... | collective-permute-start | bytes 4423688 | tf_op jit(solution)/shard_map/ppermute | solution.py:892
  621.8 33.8 %collective-permute-start.39 = (bf16[2,576,640]{2,1,0:T(8,128)(2,1)}, bf16[2,576,640]{2,1,0:T(8,128)(2,1)}, u32[]{:S(2)}, u32[]{:S(2)}) collective-permute-start(bf16[2,576,640]{2,1,0:T(8,128)(2,1)} %fusion.3), channel_id=1, source_target_pairs={{0,16},{8,24},{16,0},{24,8},{1,17},{9,25},{17,1},{25,9},{2,18},{10... | collective-permute-start | bytes 4423688 | tf_op jit(solution)/shard_map/ppermute | solution.py:892
  625.7 43.6 %collective-permute-start.35 = (bf16[256,2304]{1,0:T(8,128)(2,1)}, bf16[256,2304]{1,0:T(8,128)(2,1)S(1)}, u32[]{:S(2)}, u32[]{:S(2)}) collective-permute-start(bf16[256,2304]{1,0:T(8,128)(2,1)} %get-tuple-element.320), channel_id=1, source_target_pairs={{0,2},{1,3},{2,0},{3,1},{4,6},{5,7},{6,4},{7,5},{8,10},{9,11},{10,... | collective-permute-start | bytes 3538952 | tf_op jit(solution)/shard_map/ppermute | solution.py:892
  630.6 172.6 %all-gather.14.cloned.1.call-start = ((), (), s32[]{:S(2)}) async-start(), calls=%async_computation.13 | async-start | bytes 1368576 | tf_op jit(solution)/shard_map/all_gather | solution.py:1312
  687.8 6.5 collective-permute-start.40
  687.9 25.3 %collective-permute-start.41 = (bf16[2,576,384]{2,1,0:T(8,128)(2,1)}, bf16[2,576,384]{2,1,0:T(8,128)(2,1)S(1)}, u32[]{:S(2)}, u32[]{:S(2)}) collective-permute-start(bf16[2,576,384]{2,1,0:T(8,128)(2,1)} %get-tuple-element.219), channel_id=1, source_target_pairs={{0,16},{8,24},{16,0},{24,8},{1,17},{9,25},{17,1},{25,9},{2,18},{10... | collective-permute-start | bytes 2654216 | tf_op jit(solution)/shard_map/ppermute | solution.py:892
  688.0 25.2 %collective-permute-start.42 = (bf16[2,576,384]{2,1,0:T(8,128)(2,1)S(1)}, bf16[2,576,384]{2,1,0:T(8,128)(2,1)S(1)}, u32[]{:S(2)}, u32[]{:S(2)}) collective-permute-start(bf16[2,576,384]{2,1,0:T(8,128)(2,1)S(1)} %copy-done.64), channel_id=1, source_target_pairs={{0,8},{8,0},{16,24},{24,16},{1,9},{9,1},{17,25},{25,17},{2,10},{10... | collective-permute-start | bytes 2654216 | tf_op jit(solution)/shard_map/ppermute | solution.py:892
  688.0 32.2 %collective-permute-start.45 = (bf16[576,640]{1,0:T(8,128)(2,1)}, bf16[576,640]{1,0:T(8,128)(2,1)}, u32[]{:S(2)}, u32[]{:S(2)}) collective-permute-start(bf16[576,640]{1,0:T(8,128)(2,1)} %get-tuple-element.321), channel_id=1, source_target_pairs={{0,6},{1,7},{2,4},{3,5},{4,2},{5,3},{6,0},{7,1},{8,14},{9,15},{10,... | collective-permute-start | bytes 2211848 | tf_op jit(solution)/shard_map/ppermute | solution.py:892
  714.1 12.6 %collective-permute-start.43 = (bf16[2,288,384]{2,1,0:T(8,128)(2,1)}, bf16[2,288,384]{2,1,0:T(8,128)(2,1)}, u32[]{:S(2)}, u32[]{:S(2)}) collective-permute-start(bf16[2,288,384]{2,1,0:T(8,128)(2,1)} %fusion.24), channel_id=1, source_target_pairs={{0,8},{8,0},{16,24},{24,16},{1,9},{9,1},{17,25},{25,17},{2,10},{10... | collective-permute-start | bytes 1327112 | tf_op jit(solution)/shard_map/ppermute | solution.py:892
  717.0 12.0 %collective-permute-start.44 = (bf16[2,288,384]{2,1,0:T(8,128)(2,1)}, bf16[2,288,384]{2,1,0:T(8,128)(2,1)}, u32[]{:S(2)}, u32[]{:S(2)}) collective-permute-start(bf16[2,288,384]{2,1,0:T(8,128)(2,1)} %fusion.25), channel_id=1, source_target_pairs={{0,16},{8,24},{16,0},{24,8},{1,17},{9,25},{17,1},{25,9},{2,18},{10... | collective-permute-start | bytes 1327112 | tf_op jit(solution)/shard_map/ppermute | solution.py:892
  717.1 30.2 %collective-permute-start.48 = (bf16[576,640]{1,0:T(8,128)(2,1)}, bf16[576,640]{1,0:T(8,128)(2,1)}, u32[]{:S(2)}, u32[]{:S(2)}) collective-permute-start(bf16[576,640]{1,0:T(8,128)(2,1)} %slice_bitcast_fusion.20), channel_id=1, source_target_pairs={{0,2},{1,3},{2,0},{3,1},{4,6},{5,7},{6,4},{7,5},{8,10},{9,11},{10,... | collective-permute-start | bytes 2211848 | tf_op jit(solution)/shard_map/ppermute | solution.py:892
  717.1 40.3 %collective-permute-start.49 = (bf16[576,640]{1,0:T(8,128)(2,1)}, bf16[576,640]{1,0:T(8,128)(2,1)}, u32[]{:S(2)}, u32[]{:S(2)}) collective-permute-start(bf16[576,640]{1,0:T(8,128)(2,1)} %get-tuple-element.322), channel_id=1, source_target_pairs={{0,4},{1,5},{2,6},{3,7},{4,0},{5,1},{6,2},{7,3},{8,12},{9,13},{10,... | collective-permute-start | bytes 2211848 | tf_op jit(solution)/shard_map/ppermute | solution.py:892
  729.0 35.2 %collective-permute-start.46 = (bf16[2,576,640]{2,1,0:T(8,128)(2,1)}, bf16[2,576,640]{2,1,0:T(8,128)(2,1)}, u32[]{:S(2)}, u32[]{:S(2)}) collective-permute-start(bf16[2,576,640]{2,1,0:T(8,128)(2,1)} %get-tuple-element.224), channel_id=1, source_target_pairs={{0,16},{8,24},{16,0},{24,8},{1,17},{9,25},{17,1},{25,9},{2,18},{10... | collective-permute-start | bytes 4423688 | tf_op jit(solution)/shard_map/ppermute | solution.py:892
  729.3 34.9 %collective-permute-start.47 = (bf16[2,576,640]{2,1,0:T(8,128)(2,1)}, bf16[2,576,640]{2,1,0:T(8,128)(2,1)}, u32[]{:S(2)}, u32[]{:S(2)}) collective-permute-start(bf16[2,576,640]{2,1,0:T(8,128)(2,1)} %get-tuple-element.225), channel_id=1, source_target_pairs={{0,8},{8,0},{16,24},{24,16},{1,9},{9,1},{17,25},{25,17},{2,10},{10... | collective-permute-start | bytes 4423688 | tf_op jit(solution)/shard_map/ppermute | solution.py:892
  765.7 30.4 %collective-permute-start.50 = (bf16[2,288,640]{2,1,0:T(8,128)(2,1)S(1)}, bf16[2,288,640]{2,1,0:T(8,128)(2,1)S(1)}, u32[]{:S(2)}, u32[]{:S(2)}) collective-permute-start(bf16[2,288,640]{2,1,0:T(8,128)(2,1)S(1)} %fusion.17), channel_id=1, source_target_pairs={{0,8},{8,0},{16,24},{24,16},{1,9},{9,1},{17,25},{25,17},{2,10},{10... | collective-permute-start | bytes 2211848 | tf_op jit(solution)/shard_map/ppermute | solution.py:892
  768.9 27.2 %collective-permute-start.51 = (bf16[2,288,640]{2,1,0:T(8,128)(2,1)S(1)}, bf16[2,288,640]{2,1,0:T(8,128)(2,1)S(1)}, u32[]{:S(2)}, u32[]{:S(2)}) collective-permute-start(bf16[2,288,640]{2,1,0:T(8,128)(2,1)S(1)} %fusion.18), channel_id=1, source_target_pairs={{0,16},{8,24},{16,0},{24,8},{1,17},{9,25},{17,1},{25,9},{2,18},{10... | collective-permute-start | bytes 2211848 | tf_op jit(solution)/shard_map/ppermute | solution.py:892
  770.7 10.7 %collective-permute-start.55 = (bf16[288,384]{1,0:T(8,128)(2,1)S(1)}, bf16[288,384]{1,0:T(8,128)(2,1)S(1)}, u32[]{:S(2)}, u32[]{:S(2)}) collective-permute-start(bf16[288,384]{1,0:T(8,128)(2,1)S(1)} %slice_bitcast_fusion.41), channel_id=1, source_target_pairs={{0,2},{1,3},{2,0},{3,1},{4,6},{5,7},{6,4},{7,5},{8,10},{9,11},{10,... | collective-permute-start | bytes 663560 | tf_op jit(solution)/shard_map/ppermute | solution.py:892
  770.8 14.4 %collective-permute-start.57 = (bf16[288,384]{1,0:T(8,128)(2,1)S(1)}, bf16[288,384]{1,0:T(8,128)(2,1)S(1)}, u32[]{:S(2)}, u32[]{:S(2)}) collective-permute-start(bf16[288,384]{1,0:T(8,128)(2,1)S(1)} %get-tuple-element.236), channel_id=1, source_target_pairs={{0,6},{1,7},{2,4},{3,5},{4,2},{5,3},{6,0},{7,1},{8,14},{9,15},{10,... | collective-permute-start | bytes 663560 | tf_op jit(solution)/shard_map/ppermute | solution.py:892
  773.5 22.5 %collective-permute-start.56 = (bf16[288,384]{1,0:T(8,128)(2,1)S(1)}, bf16[288,384]{1,0:T(8,128)(2,1)S(1)}, u32[]{:S(2)}, u32[]{:S(2)}) collective-permute-start(bf16[288,384]{1,0:T(8,128)(2,1)S(1)} %get-tuple-element.235), channel_id=1, source_target_pairs={{0,4},{1,5},{2,6},{3,7},{4,0},{5,1},{6,2},{7,3},{8,12},{9,13},{10,... | collective-permute-start | bytes 663560 | tf_op jit(solution)/shard_map/ppermute | solution.py:892
  800.6 8.0 collective-permute-start.58
  804.7 24.8 %collective-permute-start.53 = (bf16[288,640]{1,0:T(8,128)(2,1)S(1)}, bf16[288,640]{1,0:T(8,128)(2,1)S(1)}, u32[]{:S(2)}, u32[]{:S(2)}) collective-permute-start(bf16[288,640]{1,0:T(8,128)(2,1)S(1)} %copy-done.49), channel_id=1, source_target_pairs={{0,4},{1,5},{2,6},{3,7},{4,0},{5,1},{6,2},{7,3},{8,12},{9,13},{10,... | collective-permute-start | bytes 1105928 | tf_op jit(solution)/shard_map/ppermute | solution.py:892
  804.7 24.8 %collective-permute-start.54 = (bf16[288,640]{1,0:T(8,128)(2,1)S(1)}, bf16[288,640]{1,0:T(8,128)(2,1)S(1)}, u32[]{:S(2)}, u32[]{:S(2)}) collective-permute-start(bf16[288,640]{1,0:T(8,128)(2,1)S(1)} %copy-done.47), channel_id=1, source_target_pairs={{0,6},{1,7},{2,4},{3,5},{4,2},{5,3},{6,0},{7,1},{8,14},{9,15},{10,... | collective-permute-start | bytes 1105928 | tf_op jit(solution)/shard_map/ppermute | solution.py:892
  807.4 23.2 %collective-permute-start.52 = (bf16[288,640]{1,0:T(8,128)(2,1)S(1)}, bf16[288,640]{1,0:T(8,128)(2,1)S(1)}, u32[]{:S(2)}, u32[]{:S(2)}) collective-permute-start(bf16[288,640]{1,0:T(8,128)(2,1)S(1)} %copy-done.48), channel_id=1, source_target_pairs={{0,2},{1,3},{2,0},{3,1},{4,6},{5,7},{6,4},{7,5},{8,10},{9,11},{10,... | collective-permute-start | bytes 1105928 | tf_op jit(solution)/shard_map/ppermute | solution.py:892
  809.5 25.0 %collective-permute-start.59 = (bf16[512,288]{1,0:T(8,128)(2,1)}, bf16[512,288]{1,0:T(8,128)(2,1)}, u32[]{:S(2)}, u32[]{:S(2)}) collective-permute-start(bf16[512,288]{1,0:T(8,128)(2,1)} %fusion.14), channel_id=1, source_target_pairs={{0,16},{8,24},{16,0},{24,8},{1,17},{9,25},{17,1},{25,9},{2,18},{10... | collective-permute-start | bytes 884744 | tf_op jit(solution)/shard_map/ppermute | solution.py:892
  (78 other events, 948.1 us)
Sparse Core Ops, SparseCore 0:
  27.7 37.3 all-gather.9
  133.4 26.7 reduce-scatter.5
  185.4 59.6 all-gather.11
  248.2 110.5 all-gather.7
  444.5 173.3 reduce-scatter.9
  630.7 54.6 reduce-scatter.7
  734.6 63.7 all-gather.13

commit v5 on v4

--- a/solution.py
+++ b/solution.py
@@ -1321,7 +1321,7 @@
     d_ada = lax.dot_general(
         cond_rows, grad_mod, (((0,), (0,)), ((), ())), precision=highest
     )
-    text_terms = after(text_terms[0], *early.ends).astype(f32)
+    text_terms = after(text_terms[0], *early_first).astype(f32)
     text_terms = text_terms + swap(text_terms.astype(bf16), "gy", 1).astype(f32)
     text_terms = text_terms + swap(text_terms.astype(bf16), "gy", 2).astype(f32)
     text_grad = text_terms.astype(bf16)

time: 855 us -> 867 us (1.014)
  starting transfers between devices: 74.6 us -> 91 us
    ppermute x60, waiting for transfers between devices: 320 us -> 301 us  [swap(): lax.ppermute(values, axis, [(i, i ^ mask) for i in range(lax.axis_size(ax...]
    ppermute x60, starting transfers between devices: 65.4 us -> 81.8 us  [swap(): lax.ppermute(values, axis, [(i, i ^ mask) for i in range(lax.axis_size(ax...]
    reduce_scatter x1, waiting for transfers between devices: 0.01 us -> 14.2 us  [local(): lax.psum_scatter(after(text_terms, late).reshape(nx, -1, kv_width), 'gx',...]
    unnamed x158 -> x136, local copies, waits for them, and re-layouts: 20.2 us -> 21.9 us
  transfers between devices with their start and end apart: 70 -> 70, of which waited for: 34 -> 31; matrix products, arithmetic and copies ran while one was open for 11% -> 11% of each run, Pallas kernels for 26% -> 26%
where the time goes in v5:
time: 867 us; the launch traced here: 858 us
  waiting for transfers between devices  356 us (41%)
  Pallas kernels  244 us (28%)
  starting transfers between devices  91 us (10%)
  other arithmetic  58.4 us (7%)
  local copies, waits for them, and re-layouts  46.2 us (5%)
  blocking collectives  33.3 us (4%)
  between operations  17.7 us (2%)
  matrix products  11.5 us (1%)
    ppermute x60, waiting for transfers between devices, swap(): lax.ppermute(values, axis, [(i, i ^ mask) for i in range(lax.axis_size(ax...  301 us
    pallas_call x10, Pallas kernels, run(): pl.pallas_call(grouped, out_shape=outs, in_specs=flat_specs, out_specs=[v...  176 us
    ppermute x60, starting transfers between devices, swap(): lax.ppermute(values, axis, [(i, i ^ mask) for i in range(lax.axis_size(ax...  81.8 us
    pallas_call x2, Pallas kernels, weight_grads(): pl.pallas_call(functools.partial(weight_kernel, nx, lax.axis_size('gy'),...  31.7 us
    all_to_all x1, blocking collectives, reorder(): lax.all_to_all(values.reshape(devices, values.shape[0] // devices, values...  24.1 us
    unnamed x136, local copies, waits for them, and re-layouts  21.9 us
    pallas_call x1, Pallas kernels, up_grads(): pl.pallas_call(kernel, out_shape=outs, grid_spec=pltpu.PrefetchScalarGrid...  21.6 us
    convert_element_type x12, other arithmetic, total(): return sum((term.astype(f32) for term in terms)).astype(bf16)  20.7 us
  transfers between devices with their start and end apart: 70, of which 31 were waited for; matrix products, arithmetic and copies ran while one was open for 11% of the time, Pallas kernels for 26%

profile of v5, /device:TPU:0, one launch (start us, length us, event | category | flops | bytes accessed | tf_op | source)
XLA Modules:
  0.0 857.6 jit_solution(5516308281359986051)
XLA Ops:
  9.6 3.0 collective-permute-start
  18.4 9.1 %all_to_all.25 = bf16[4,16,1024]{2,1,0:T(8,128)(2,1)} all-to-all(bf16[4,16,1024]{2,1,0:T(8,128)(2,1)S(1)} %copy.214), channel_id=1, replica_groups=mesh['gy'=4,'gx'=8] {'gy'}, dimensions={0} | all-to-all | bytes 262144 | tf_op jit(solution)/shard_map/all_to_all | solution.py:984
  28.3 3.7 collective-permute-start.6
  35.2 35.6 %collective-permute-done.3 = f32[2,4,1296]{2,1,0:T(4,128)S(1)} collective-permute-done((f32[2,4,1296]{2,1,0:T(4,128)S(1)}, f32[2,4,1296]{2,1,0:T(4,128)S(1)}, u32[]{:S(2)}, u32[]{:S(2)}) %collective-permute-start.3) | collective-permute-done | bytes 41504 | tf_op jit(solution)/shard_map/ppermute | solution.py:892
  70.9 9.9 %collective-permute-done.5 = bf16[288,896]{1,0:T(8,128)(2,1)S(1)} collective-permute-done((bf16[288,896]{1,0:T(8,128)(2,1)S(1)}, bf16[288,896]{1,0:T(8,128)(2,1)S(1)}, u32[]{:S(2)}, u32[]{:S(2)}) %collective-permute-start.5) | collective-permute-done | bytes 516128 | tf_op jit(solution)/shard_map/ppermute | solution.py:892
  80.7 5.9 collective-permute-done.7
  92.4 2.5 collective-permute-start.10
  96.7 2.8 fusion.46
  99.5 25.3 %collective-permute-done.11 = bf16[576,640]{1,0:T(8,128)(2,1)} collective-permute-done((bf16[576,640]{1,0:T(8,128)(2,1)}, bf16[576,640]{1,0:T(8,128)(2,1)}, u32[]{:S(2)}, u32[]{:S(2)}) %collective-permute-start.11) | collective-permute-done | bytes 737312 | tf_op jit(solution)/shard_map/ppermute | solution.py:892
  126.7 3.5 pad_maximum_fusion.2.refs_3_.refs_4_.refs_5_.refs_7_
  133.3 4.2 collective-permute-done.14.refs_7_.refs_8_.refs_9_.refs_11_
  139.6 20.6 %reduce-scatter.6.cloned.1.call-done = f32[128,288]{0,1:T(8,128)} async-done(((f32[512,288]{0,1:T(8,128)}), f32[128,288]{0,1:T(8,128)}) %reduce-scatter.6.cloned.1.call-update) | async-done | bytes 147472 | tf_op jit(solution)/shard_map/reduce_scatter | solution.py:1013
  160.2 22.4 %collective-permute-done.12.refs_4_.refs_5_.refs_6_.refs_8_ = bf16[2,2,288,896]{3,2,1,0:T(8,128)(2,1)} collective-permute-done((bf16[2,2,288,896]{3,2,1,0:T(8,128)(2,1)}, bf16[2,2,288,896]{3,2,1,0:T(8,128)(2,1)}, u32[]{:S(2)}, u32[]{:S(2)}) %collective-permute-start.12) | collective-permute-done | bytes 2064416 | tf_op jit(solution)/shard_map/ppermute | solution.py:892
  186.6 4.1 fusion.42
  202.1 9.2 %shard_map.265 = (bf16[256,1152]{1,0:T(8,128)(2,1)}, bf16[256,1152]{1,0:T(8,128)(2,1)}, bf16[256,2304]{1,0:T(8,128)(2,1)}) custom-call(s32[2]{0:T(128)} %pad_add_fusion.refs_0_.me_ref, bf16[256,1152]{1,0:T(8,128)(2,1)} %refs_4_.1, f32[9,1152]{1,0:T(8,128)} %reshape.218.refs_2_.refs_3_.refs_7_.refs_4_.refs_5_, ...), custom_call_target="tpu_custom_call" | custom-call | flops 180000000 | tf_op jit(solution)/shard_map/pallas_call | solution.py:57
  211.3 16.8 %collective-permute-done.20 = bf16[2,576,640]{2,1,0:T(8,128)(2,1)} collective-permute-done((bf16[2,576,640]{2,1,0:T(8,128)(2,1)}, bf16[2,576,640]{2,1,0:T(8,128)(2,1)}, u32[]{:S(2)}, u32[]{:S(2)}) %collective-permute-start.20) | collective-permute-done | bytes 1474592 | tf_op jit(solution)/shard_map/ppermute | solution.py:892
  230.0 4.3 pad_maximum_fusion.refs_4_.refs_8_
  237.1 34.8 %collective-permute-done.21.refs_2_.refs_5_ = bf16[256,2304]{1,0:T(8,128)(2,1)} collective-permute-done((bf16[256,2304]{1,0:T(8,128)(2,1)S(1)}, bf16[256,2304]{1,0:T(8,128)(2,1)}, u32[]{:S(2)}, u32[]{:S(2)}) %collective-permute-start.21) | collective-permute-done | bytes 1179680 | tf_op jit(solution)/shard_map/ppermute | solution.py:892
  277.4 18.7 %shard_map.266 = (bf16[256,1152]{1,0:T(8,128)(2,1)}, f32[16,256]{1,0:T(8,128)}) custom-call(bf16[256,1152]{1,0:T(8,128)(2,1)} %get-tuple-element.155.refs_0_, bf16[256,2304]{1,0:T(8,128)(2,1)} %get-tuple-element.150.refs_1_.refs_4_, bf16[256,2304]{1,0:T(8,128)(2,1)} %collective-permute-done.21.refs_2_.refs_5_, bf16[256,2304]{1,0:T(8,128)(2,1)} %copy-done.18, ...), custom_call_target="tpu_custom_call" | custom-call | flops 360000000 | tf_op jit(solution)/shard_map/pallas_call | solution.py:57
  296.1 17.9 %shard_map.267 = (f32[256,1152]{1,0:T(8,128)}, f32[256,1152]{1,0:T(8,128)}, bf16[256,1152]{1,0:T(8,128)(2,1)}, bf16[256,1152]{1,0:T(8,128)(2,1)}, bf16[256,1152]...) custom-call(s32[2]{0:T(128)} %pad_add_fusion.refs_0_.me_ref, bf16[256,1152]{1,0:T(8,128)(2,1)} %refs_4_.1, ...), custom_call_target="tpu_custom_call" | custom-call | flops 360000000 | tf_op jit(solution)/shard_map/pallas_call | solution.py:57
  316.6 6.6 collective-permute-done.28.refs_9_.refs_13_
  323.2 4.2 collective-permute-done.29.refs_11_.refs_15_
  329.1 20.7 %shard_map.268 = (f32[256,4608]{1,0:T(8,128)}, bf16[256,4608]{1,0:T(8,128)(2,1)}, f32[256,1152]{1,0:T(8,128)}, f32[256,1152]{1,0:T(8,128)}, bf16[256,1152]{1,0:T(8,128)(2,1)}) custom-call(s32[2]{0:T(128)} %pad_add_fusion.refs_0_.me_ref, bf16[256,1152]{1,0:T(8,128)(2,1)} %get-tuple-element.162.refs_1_.refs_0_, ...), custom_call_target="tpu_custom_call" | custom-call | flops 400000000 | tf_op jit(solution)/shard_map/pallas_call | solution.py:57
  354.5 24.1 %all_to_all.26 = bf16[32,8,1152]{2,1,0:T(8,128)(2,1)} all-to-all(bf16[32,8,1152]{2,1,0:T(8,128)(2,1)S(1)} %bitcast.290), channel_id=1, replica_groups=mesh['gy'=4,'gx'=8] {'gy','gx'}, dimensions={0} | all-to-all | bytes 1179648 | tf_op jit(solution)/shard_map/all_to_all | solution.py:897
  378.6 2.6 all-to-all-start.1
  382.2 16.8 %all-to-all-done.1 = bf16[32,8,1152]{2,1,0:T(8,128)(2,1)S(1)} async-done(((bf16[32,8,1152]{2,1,0:T(8,128)(2,1)}), bf16[32,8,1152]{2,1,0:T(8,128)(2,1)S(1)}, u32[]{:S(2)}, u32[]{:S(2)}) %all-to-all-start.1) | async-done | bytes 589856 | tf_op jit(solution)/shard_map/all_to_all | solution.py:897
  399.8 24.0 %shard_map.269 = (bf16[256,4608]{1,0:T(8,128)(2,1)}, bf16[256,1152]{1,0:T(8,128)(2,1)}, bf16[256,1152]{1,0:T(8,128)(2,1)}) custom-call(bf16[256,1152]{1,0:T(8,128)(2,1)} %bitcast.277, bf16[256,1152]{1,0:T(8,128)(2,1)} %bitcast.275, bf16[8,1152,640]{2,1,0:T(8,128)(2,1)} %bitcast.271, f32[256,1]{1,0:T(8,128)} %broadcast_in_dim_reshape.4.refs_3_, f32[8]{0:T(128)} %copy-done.53), custom_call_target="tpu_custom_call" | custom-call | flops 500000000 | tf_op jit(solution)/shard_map/pallas_call | solution.py:57
  423.9 2.6 all-to-all-start.3
  426.6 15.0 %shard_map.278 = bf16[8,1152,640]{2,1,0:T(8,128)(2,1)} custom-call(bf16[256,1152]{1,0:T(8,128)(2,1)} %bitcast.278, bf16[256,1152]{1,0:T(8,128)(2,1)} %bitcast.276, bf16[256,4608]{1,0:T(8,128)(2,1)} %get-tuple-element.238.refs_2_), custom_call_target="tpu_custom_call" | custom-call | flops 260000000 | tf_op jit(solution)/shard_map/pallas_call | solution.py:692
  441.5 2.8 all-to-all-done.3
  445.1 3.1 all-to-all-start.4
  448.7 23.4 %shard_map.271 = (bf16[256,5760]{1,0:T(8,128)(2,1)}, f32[256,1152]{1,0:T(8,128)}, f32[8,1152]{1,0:T(8,128)}) custom-call(s32[2]{0:T(128)} %pad_add_fusion.refs_0_.me_ref, bf16[256,1152]{1,0:T(8,128)(2,1)} %refs_1_.5, bf16[256,1152]{1,0:T(8,128)(2,1)} %bitcast.292, f32[256,1152]{1,0:T(8,128)} %get-tuple-element.177.refs_1_.refs_3_, ...), custom_call_target="tpu_custom_call" | custom-call | flops 440000000 | tf_op jit(solution)/shard_map/pallas_call | solution.py:57
  472.4 3.6 slice_bitcast_fusion.22
  476.0 2.3 collective-permute-done.32.refs_4_
  480.0 21.6 %shard_map.272 = (bf16[2,1152,640]{2,1,0:T(8,128)(2,1)}, bf16[2,1152,640]{2,1,0:T(8,128)(2,1)}, bf16[2,1152,640]{2,1,0:T(8,128)(2,1)}, bf16[2,1152,640]{2,1,0:T(8,128)(2,1)}) custom-call(s32[2]{0:T(128)} %pad_add_fusion.refs_0_.me_ref, bf16[256,1152]{1,0:T(8,128)(2,1)} %get-tuple-element.162.refs_1_.refs_0_, bf16[256,5760]{1,0:T(8,128)(2,1)} %get-tuple-element.183.refs_1_, ...), custom_call_target="tpu_custom_call" | custom-call | flops 320000000 | tf_op jit(solution)/shard_map/pallas_call | solution.py:753
  501.6 19.7 %shard_map.273 = (bf16[256,3456]{1,0:T(8,128)(2,1)}, f32[256,1152]{1,0:T(8,128)}, bf16[256,1152]{1,0:T(8,128)(2,1)}, bf16[8,128,288]{2,1,0:T(8,128)(2,1)}, f32[1,1152]{1,0:T(1,128)}) custom-call(s32[2]{0:T(128)} %pad_add_fusion.refs_0_.me_ref, f32[256,1152]{1,0:T(8,128)} %get-tuple-element.188.refs_1_, f32[256,1152]{1,0:T(8,128)} %get-tuple-element.189.refs_2_, ...), custom_call_target="tpu_custom_call" | custom-call | flops 400000000 | tf_op jit(solution)/shard_map/pallas_call | solution.py:57
  522.6 2.4 collective-permute-start.36
  524.9 2.7 collective-permute-start.37
  527.6 28.3 %shard_map.274 = (bf16[256,1152]{1,0:T(8,128)(2,1)}, bf16[4,256,2304]{2,1,0:T(8,128)(2,1)}) custom-call(bf16[256,1152]{1,0:T(8,128)(2,1)} %get-tuple-element.155.refs_0_, bf16[256,1152]{1,0:T(8,128)(2,1)} %get-tuple-element.192.refs_1_, bf16[256,1152]{1,0:T(8,128)(2,1)} %get-tuple-element.158.refs_2_.refs_1_, f32[16,256]{1,0:T(8,128)} %get-tuple-element.193.refs_3_, ...), custom_call_target="tpu_custom_call" | custom-call | flops 560000000 | tf_op jit(solution)/shard_map/pallas_call | solution.py:57
  555.9 2.5 slice.188
  558.5 54.5 %collective-permute-done.36 = bf16[2,1152,640]{2,1,0:T(8,128)(2,1)} collective-permute-done((bf16[2,1152,640]{2,1,0:T(8,128)(2,1)}, bf16[2,1152,640]{2,1,0:T(8,128)(2,1)}, u32[]{:S(2)}, u32[]{:S(2)}) %collective-permute-start.36) | collective-permute-done | bytes 2949152 | tf_op jit(solution)/shard_map/ppermute | solution.py:892
  614.8 2.3 fusion.2
  617.2 2.7 collective-permute-start.38
  619.9 2.8 fusion.3
  627.8 2.7 shard_map.270
  630.5 14.2 %shard_map.275 = (bf16[2,576,384]{2,1,0:T(8,128)(2,1)}, bf16[2,576,384]{2,1,0:T(8,128)(2,1)}, bf16[2,576,384]{2,1,0:T(8,128)(2,1)}, bf16[2,576,384]{2,1,0:T(8,128)(2,1)}) custom-call(s32[2]{0:T(128)} %pad_add_fusion.refs_0_.me_ref, bf16[256,1152]{1,0:T(8,128)(2,1)} %get-tuple-element.166.refs_0_, bf16[256,1152]{1,0:T(8,128)(2,1)} %get-tuple-element.167.refs_1_, ...), custom_call_target="tpu_custom_call" | custom-call | flops 180000000 | tf_op jit(solution)/shard_map/pallas_call | solution.py:644
  644.7 7.2 collective-permute-done.38
  651.9 4.5 collective-permute-done.39
  656.4 2.5 fusion.1
  661.7 11.0 %shard_map.276 = (bf16[256,3456]{1,0:T(8,128)(2,1)}, bf16[256,1152]{1,0:T(8,128)(2,1)}, f32[2,1152]{1,0:T(2,128)}) custom-call(s32[2]{0:T(128)} %pad_add_fusion.refs_0_.me_ref, bf16[256,1152]{1,0:T(8,128)(2,1)} %get-tuple-element.207.refs_1_, bf16[256,2304]{1,0:T(8,128)(2,1)} %get-tuple-element.319.refs_2_, ...), custom_call_target="tpu_custom_call" | custom-call | flops 220000000 | tf_op jit(solution)/shard_map/pallas_call | solution.py:57
  680.8 2.8 collective-permute-start.49
  685.5 17.6 %shard_map.277 = (bf16[2,576,640]{2,1,0:T(8,128)(2,1)}, bf16[2,576,640]{2,1,0:T(8,128)(2,1)}, bf16[2,576,640]{2,1,0:T(8,128)(2,1)}, bf16[2,576,640]{2,1,0:T(8,128)(2,1)}) custom-call(s32[2]{0:T(128)} %pad_add_fusion.refs_0_.me_ref, bf16[256,1152]{1,0:T(8,128)(2,1)} %get-tuple-element.165.refs_0_, bf16[256,1152]{1,0:T(8,128)(2,1)} %get-tuple-element.158.refs_2_.refs_1_, ...), custom_call_target="tpu_custom_call" | custom-call | flops 180000000 | tf_op jit(solution)/shard_map/pallas_call | solution.py:644
  708.1 25.1 %collective-permute-done.45 = bf16[576,640]{1,0:T(8,128)(2,1)} collective-permute-done((bf16[576,640]{1,0:T(8,128)(2,1)}, bf16[576,640]{1,0:T(8,128)(2,1)}, u32[]{:S(2)}, u32[]{:S(2)}) %collective-permute-start.45) | collective-permute-done | bytes 737312 | tf_op jit(solution)/shard_map/ppermute | solution.py:892
  742.0 18.5 %collective-permute-start.55 = (bf16[288,384]{1,0:T(8,128)(2,1)S(1)}, bf16[288,384]{1,0:T(8,128)(2,1)S(1)}, u32[]{:S(2)}, u32[]{:S(2)}) collective-permute-start(bf16[288,384]{1,0:T(8,128)(2,1)S(1)} %slice_bitcast_fusion.41), channel_id=1, source_target_pairs={{0,2},{1,3},{2,0},{3,1},{4,6},{5,7},{6,4},{7,5},{8,10},{9,11},{10,... | collective-permute-start | bytes 663560 | tf_op jit(solution)/shard_map/ppermute | solution.py:892
  760.6 2.4 collective-permute-start.57
  762.9 6.7 collective-permute-done.46
  778.6 8.6 %collective-permute-done.56 = bf16[288,384]{1,0:T(8,128)(2,1)S(1)} collective-permute-done((bf16[288,384]{1,0:T(8,128)(2,1)S(1)}, bf16[288,384]{1,0:T(8,128)(2,1)S(1)}, u32[]{:S(2)}, u32[]{:S(2)}) %collective-permute-start.56) | collective-permute-done | bytes 221216 | tf_op jit(solution)/shard_map/ppermute | solution.py:892
  789.1 2.5 copy.283
  797.6 14.2 %reduce-scatter.8.cloned.1.call-done = bf16[1,512,288]{2,1,0:T(8,128)(2,1)} async-done(((bf16[8,512,288]{2,1,0:T(8,128)(2,1)}), bf16[1,512,288]{2,1,0:T(8,128)(2,1)}) %reduce-scatter.8.cloned.1.call-update) | async-done | bytes 294928 | tf_op jit(solution)/shard_map/reduce_scatter | solution.py:1225
  813.0 2.5 collective-permute-start.52
  819.2 4.6 collective-permute-done.58
  826.7 3.6 fusion.39
  830.3 13.6 %collective-permute-done.53 = bf16[288,640]{1,0:T(8,128)(2,1)S(1)} collective-permute-done((bf16[288,640]{1,0:T(8,128)(2,1)}, bf16[288,640]{1,0:T(8,128)(2,1)S(1)}, u32[]{:S(2)}, u32[]{:S(2)}) %collective-permute-start.53) | collective-permute-done | bytes 368672 | tf_op jit(solution)/shard_map/ppermute | solution.py:892
  847.8 2.7 fusion.28
  (329 shorter events, 126.6 us)
Async XLA Ops:
  7.2 73.5 %all-gather.10.cloned.1.call-start = ((), (), s32[]{:S(2)}) async-start(), calls=%async_computation.11 | async-start | bytes 1179648 | tf_op jit(solution)/shard_map/all_gather | solution.py:985
  27.5 132.6 %reduce-scatter.6.cloned.1.call-start = ((), (), s32[]{:S(2)}) async-start(), calls=%async_computation.8 | async-start | bytes 737280 | tf_op jit(solution)/shard_map/reduce_scatter | solution.py:1013
  28.3 42.6 %collective-permute-start.6 = (bf16[288,896]{1,0:T(8,128)(2,1)S(1)}, bf16[288,896]{1,0:T(8,128)(2,1)S(1)}, u32[]{:S(2)}, u32[]{:S(2)}) collective-permute-start(bf16[288,896]{1,0:T(8,128)(2,1)S(1)} %fusion.23), channel_id=1, source_target_pairs={{0,6},{1,7},{2,4},{3,5},{4,2},{5,3},{6,0},{7,1},{8,14},{9,15},{10,... | collective-permute-start | bytes 1548296 | tf_op jit(solution)/shard_map/ppermute | solution.py:892
  31.9 48.8 %collective-permute-start.5 = (bf16[288,896]{1,0:T(8,128)(2,1)S(1)}, bf16[288,896]{1,0:T(8,128)(2,1)S(1)}, u32[]{:S(2)}, u32[]{:S(2)}) collective-permute-start(bf16[288,896]{1,0:T(8,128)(2,1)S(1)} %fusion.23), channel_id=1, source_target_pairs={{0,4},{1,5},{2,6},{3,7},{4,0},{5,1},{6,2},{7,3},{8,12},{9,13},{10,... | collective-permute-start | bytes 1548296 | tf_op jit(solution)/shard_map/ppermute | solution.py:892
  31.9 48.8 %collective-permute-start.4 = (bf16[288,896]{1,0:T(8,128)(2,1)S(1)}, bf16[288,896]{1,0:T(8,128)(2,1)S(1)}, u32[]{:S(2)}, u32[]{:S(2)}) collective-permute-start(bf16[288,896]{1,0:T(8,128)(2,1)S(1)} %fusion.23), channel_id=1, source_target_pairs={{0,2},{1,3},{2,0},{3,1},{4,6},{5,7},{6,4},{7,5},{8,10},{9,11},{10,... | collective-permute-start | bytes 1548296 | tf_op jit(solution)/shard_map/ppermute | solution.py:892
  33.9 36.9 %collective-permute-start.3 = (f32[2,4,1296]{2,1,0:T(4,128)S(1)}, f32[2,4,1296]{2,1,0:T(4,128)S(1)}, u32[]{:S(2)}, u32[]{:S(2)}) collective-permute-start(f32[2,4,1296]{2,1,0:T(4,128)S(1)} %maximum_select_fusion.2), channel_id=1, source_target_pairs={{0,2},{1,3},{2,0},{3,1},{4,6},{5,7},{6,4},{7,5},{8,10},{9,11},{10,... | collective-permute-start | bytes 124424 | tf_op jit(solution)/shard_map/ppermute | solution.py:892
  88.5 36.4 %collective-permute-start.8 = (bf16[2,288,896]{2,1,0:T(8,128)(2,1)}, bf16[2,288,896]{2,1,0:T(8,128)(2,1)}, u32[]{:S(2)}, u32[]{:S(2)}) collective-permute-start(bf16[2,288,896]{2,1,0:T(8,128)(2,1)} %get-tuple-element.330), channel_id=1, source_target_pairs={{0,8},{8,0},{16,24},{24,16},{1,9},{9,1},{17,25},{25,17},{2,10},{10... | collective-permute-start | bytes 3096584 | tf_op jit(solution)/shard_map/ppermute | solution.py:892
  90.9 34.0 %collective-permute-start.9 = (bf16[2,288,896]{2,1,0:T(8,128)(2,1)}, bf16[2,288,896]{2,1,0:T(8,128)(2,1)}, u32[]{:S(2)}, u32[]{:S(2)}) collective-permute-start(bf16[2,288,896]{2,1,0:T(8,128)(2,1)} %get-tuple-element.328), channel_id=1, source_target_pairs={{0,16},{8,24},{16,0},{24,8},{1,17},{9,25},{17,1},{25,9},{2,18},{10... | collective-permute-start | bytes 3096584 | tf_op jit(solution)/shard_map/ppermute | solution.py:892
  92.4 32.3 %collective-permute-start.11 = (bf16[576,640]{1,0:T(8,128)(2,1)}, bf16[576,640]{1,0:T(8,128)(2,1)}, u32[]{:S(2)}, u32[]{:S(2)}) collective-permute-start(bf16[576,640]{1,0:T(8,128)(2,1)} %fusion.15), channel_id=1, source_target_pairs={{0,4},{1,5},{2,6},{3,7},{4,0},{5,1},{6,2},{7,3},{8,12},{9,13},{10,... | collective-permute-start | bytes 2211848 | tf_op jit(solution)/shard_map/ppermute | solution.py:892
  92.4 32.4 %collective-permute-start.10 = (bf16[576,640]{1,0:T(8,128)(2,1)}, bf16[576,640]{1,0:T(8,128)(2,1)}, u32[]{:S(2)}, u32[]{:S(2)}) collective-permute-start(bf16[576,640]{1,0:T(8,128)(2,1)} %fusion.15), channel_id=1, source_target_pairs={{0,2},{1,3},{2,0},{3,1},{4,6},{5,7},{6,4},{7,5},{8,10},{9,11},{10,... | collective-permute-start | bytes 2211848 | tf_op jit(solution)/shard_map/ppermute | solution.py:892
  130.2 7.4 collective-permute-start.14
  130.2 7.4 collective-permute-start.15
  130.7 51.9 %collective-permute-start.12 = (bf16[2,2,288,896]{3,2,1,0:T(8,128)(2,1)}, bf16[2,2,288,896]{3,2,1,0:T(8,128)(2,1)}, u32[]{:S(2)}, u32[]{:S(2)}) collective-permute-start(bf16[2,2,288,896]{3,2,1,0:T(8,128)(2,1)} %pad_maximum_fusion.2.refs_3_.refs_4_.refs_5_.refs_7_), channel_id=1, source_target_pairs={{0,16},{8,24},{16,0},{24,8},{1,17},{9,25},{17,1},{25,9},{2,18},{10... | collective-permute-start | bytes 6193160 | tf_op jit(solution)/shard_map/ppermute | solution.py:892
  132.2 51.4 %collective-permute-start.13 = (bf16[2,2,288,896]{3,2,1,0:T(8,128)(2,1)S(1)}, bf16[2,2,288,896]{3,2,1,0:T(8,128)(2,1)}, u32[]{:S(2)}, u32[]{:S(2)}) collective-permute-start(bf16[2,2,288,896]{3,2,1,0:T(8,128)(2,1)S(1)} %pad_maximum_fusion.3.refs_5_.refs_6_.refs_7_.refs_9_), channel_id=1, source_target_pairs={{0,8},{8,0},{16,24},{24,16},{1,9},{9,1},{17,25},{25,17},{2,10},{10... | collective-permute-start | bytes 6193160 | tf_op jit(solution)/shard_map/ppermute | solution.py:892
  133.3 139.9 %all-gather.12.cloned.1.call-start = ((), (), s32[]{:S(2)}) async-start(), calls=%async_computation.12 | async-start | bytes 2433024 | tf_op jit(solution)/shard_map/all_gather | solution.py:1055
  137.6 46.0 %collective-permute-start.16 = (bf16[576,640]{1,0:T(8,128)(2,1)}, bf16[576,640]{1,0:T(8,128)(2,1)S(1)}, u32[]{:S(2)}, u32[]{:S(2)}) collective-permute-start(bf16[576,640]{1,0:T(8,128)(2,1)} %fusion.15), channel_id=1, source_target_pairs={{0,6},{1,7},{2,4},{3,5},{4,2},{5,3},{6,0},{7,1},{8,14},{9,15},{10,... | collective-permute-start | bytes 2211848 | tf_op jit(solution)/shard_map/ppermute | solution.py:892
  185.3 213.8 %all-gather.8.cloned.1.call-start = ((), (), s32[]{:S(2)}) async-start(), calls=%async_computation.9 | async-start | bytes 12165120 | tf_op jit(solution)/shard_map/all_gather | solution.py:1056
  190.7 10.1 %collective-permute-start.17 = (bf16[2,2,288,896]{3,2,1,0:T(8,128)(2,1)}, bf16[2,2,288,896]{3,2,1,0:T(8,128)(2,1)S(1)}, u32[]{:S(2)}, u32[]{:S(2)}) collective-permute-start(bf16[2,2,288,896]{3,2,1,0:T(8,128)(2,1)} %collective-permute-done.12.refs_4_.refs_5_.refs_6_.refs_8_), channel_id=1, source_target_pairs={{0,1},{1,0},{2,3},{3,2},{4,5},{5,4},{6,7},{7,6},{8,9},{9,8},{10,11... | collective-permute-start | bytes 6193160 | tf_op jit(solution)/shard_map/ppermute | solution.py:892
  190.7 10.1 %collective-permute-start.18 = (bf16[2,2,288,896]{3,2,1,0:T(8,128)(2,1)}, bf16[2,2,288,896]{3,2,1,0:T(8,128)(2,1)}, u32[]{:S(2)}, u32[]{:S(2)}) collective-permute-start(bf16[2,2,288,896]{3,2,1,0:T(8,128)(2,1)} %collective-permute-done.13.refs_6_.refs_7_.refs_8_.refs_10_), channel_id=1, source_target_pairs={{0,1},{1,0},{2,3},{3,2},{4,5},{5,4},{6,7},{7,6},{8,9},{9,8},{10,11... | collective-permute-start | bytes 6193160 | tf_op jit(solution)/shard_map/ppermute | solution.py:892
  191.2 36.9 %collective-permute-start.20 = (bf16[2,576,640]{2,1,0:T(8,128)(2,1)}, bf16[2,576,640]{2,1,0:T(8,128)(2,1)}, u32[]{:S(2)}, u32[]{:S(2)}) collective-permute-start(bf16[2,576,640]{2,1,0:T(8,128)(2,1)} %get-tuple-element.324), channel_id=1, source_target_pairs={{0,16},{8,24},{16,0},{24,8},{1,17},{9,25},{17,1},{25,9},{2,18},{10... | collective-permute-start | bytes 4423688 | tf_op jit(solution)/shard_map/ppermute | solution.py:892
  191.8 36.3 %collective-permute-start.19 = (bf16[2,576,640]{2,1,0:T(8,128)(2,1)S(1)}, bf16[2,576,640]{2,1,0:T(8,128)(2,1)}, u32[]{:S(2)}, u32[]{:S(2)}) collective-permute-start(bf16[2,576,640]{2,1,0:T(8,128)(2,1)S(1)} %get-tuple-element.341), channel_id=1, source_target_pairs={{0,8},{8,0},{16,24},{24,16},{1,9},{9,1},{17,25},{25,17},{2,10},{10... | collective-permute-start | bytes 4423688 | tf_op jit(solution)/shard_map/ppermute | solution.py:892
  228.1 8.9 %collective-permute-start.22 = (bf16[256,2304]{1,0:T(8,128)(2,1)}, bf16[256,2304]{1,0:T(8,128)(2,1)S(1)}, u32[]{:S(2)}, u32[]{:S(2)}) collective-permute-start(bf16[256,2304]{1,0:T(8,128)(2,1)} %get-tuple-element.150.refs_1_.refs_4_), channel_id=1, source_target_pairs={{0,1},{1,0},{2,3},{3,2},{4,5},{5,4},{6,7},{7,6},{8,9},{9,8},{10,11... | collective-permute-start | bytes 3538952 | tf_op jit(solution)/shard_map/ppermute | solution.py:892
  234.3 43.0 %collective-permute-start.24 = (bf16[2,2,576,640]{3,2,1,0:T(8,128)(2,1)}, bf16[2,2,576,640]{3,2,1,0:T(8,128)(2,1)}, u32[]{:S(2)}, u32[]{:S(2)}) collective-permute-start(bf16[2,2,576,640]{3,2,1,0:T(8,128)(2,1)} %pad_maximum_fusion.refs_4_.refs_8_), channel_id=1, source_target_pairs={{0,1},{1,0},{2,3},{3,2},{4,5},{5,4},{6,7},{7,6},{8,9},{9,8},{10,11... | collective-permute-start | bytes 8847368 | tf_op jit(solution)/shard_map/ppermute | solution.py:892
  234.8 42.6 %collective-permute-start.25 = (bf16[2,2,576,640]{3,2,1,0:T(8,128)(2,1)S(1)}, bf16[2,2,576,640]{3,2,1,0:T(8,128)(2,1)}, u32[]{:S(2)}, u32[]{:S(2)}) collective-permute-start(bf16[2,2,576,640]{3,2,1,0:T(8,128)(2,1)S(1)} %pad_maximum_fusion.1.refs_6_.refs_10_), channel_id=1, source_target_pairs={{0,1},{1,0},{2,3},{3,2},{4,5},{5,4},{6,7},{7,6},{8,9},{9,8},{10,11... | collective-permute-start | bytes 8847368 | tf_op jit(solution)/shard_map/ppermute | solution.py:892
  234.8 79.2 %collective-permute-start.26 = (bf16[2,2,576,640]{3,2,1,0:T(8,128)(2,1)}, bf16[2,2,576,640]{3,2,1,0:T(8,128)(2,1)}, u32[]{:S(2)}, u32[]{:S(2)}) collective-permute-start(bf16[2,2,576,640]{3,2,1,0:T(8,128)(2,1)} %pad_maximum_fusion.refs_4_.refs_8_), channel_id=1, source_target_pairs={{0,16},{8,24},{16,0},{24,8},{1,17},{9,25},{17,1},{25,9},{2,18},{10... | collective-permute-start | bytes 8847368 | tf_op jit(solution)/shard_map/ppermute | solution.py:892
  235.4 79.3 %collective-permute-start.27 = (bf16[2,2,576,640]{3,2,1,0:T(8,128)(2,1)S(1)}, bf16[2,2,576,640]{3,2,1,0:T(8,128)(2,1)}, u32[]{:S(2)}, u32[]{:S(2)}) collective-permute-start(bf16[2,2,576,640]{3,2,1,0:T(8,128)(2,1)S(1)} %pad_maximum_fusion.1.refs_6_.refs_10_), channel_id=1, source_target_pairs={{0,8},{8,0},{16,24},{24,16},{1,9},{9,1},{17,25},{25,17},{2,10},{10... | collective-permute-start | bytes 8847368 | tf_op jit(solution)/shard_map/ppermute | solution.py:892
  237.1 34.9 %collective-permute-start.21 = (bf16[256,2304]{1,0:T(8,128)(2,1)S(1)}, bf16[256,2304]{1,0:T(8,128)(2,1)}, u32[]{:S(2)}, u32[]{:S(2)}) collective-permute-start(bf16[256,2304]{1,0:T(8,128)(2,1)S(1)} %copy-done.17), channel_id=1, source_target_pairs={{0,2},{1,3},{2,0},{3,1},{4,6},{5,7},{6,4},{7,5},{8,10},{9,11},{10,... | collective-permute-start | bytes 3538952 | tf_op jit(solution)/shard_map/ppermute | solution.py:892
  314.7 8.6 collective-permute-start.28
  315.1 12.3 %collective-permute-start.29 = (bf16[2,2,576,640]{3,2,1,0:T(8,128)(2,1)}, bf16[2,2,576,640]{3,2,1,0:T(8,128)(2,1)S(1)}, u32[]{:S(2)}, u32[]{:S(2)}) collective-permute-start(bf16[2,2,576,640]{3,2,1,0:T(8,128)(2,1)} %collective-permute-done.27.refs_7_.refs_11_), channel_id=1, source_target_pairs={{0,1},{1,0},{2,3},{3,2},{4,5},{5,4},{6,7},{7,6},{8,9},{9,8},{10,11... | collective-permute-start | bytes 8847368 | tf_op jit(solution)/shard_map/ppermute | solution.py:892
  350.7 48.3 %collective-permute-start.30 = (bf16[5,256,1152]{2,1,0:T(8,128)(2,1)}, bf16[5,256,1152]{2,1,0:T(8,128)(2,1)}, u32[]{:S(2)}, u32[]{:S(2)}) collective-permute-start(bf16[5,256,1152]{2,1,0:T(8,128)(2,1)} %bitcast_dynamic-update-slice_fusion), channel_id=1, source_target_pairs={{0,1},{1,0},{2,3},{3,2},{4,5},{5,4},{6,7},{7,6},{8,9},{9,8},{10,11... | collective-permute-start | bytes 8847368 | tf_op jit(solution)/shard_map/ppermute | solution.py:892
  354.3 44.7 %collective-permute-start.31 = (bf16[256,4608]{1,0:T(8,128)(2,1)}, bf16[256,4608]{1,0:T(8,128)(2,1)}, u32[]{:S(2)}, u32[]{:S(2)}) collective-permute-start(bf16[256,4608]{1,0:T(8,128)(2,1)} %get-tuple-element.170.refs_2_), channel_id=1, source_target_pairs={{0,1},{1,0},{2,3},{3,2},{4,5},{5,4},{6,7},{7,6},{8,9},{9,8},{10,11... | collective-permute-start | bytes 7077896 | tf_op jit(solution)/shard_map/ppermute | solution.py:892
  378.6 20.4 %all-to-all-start.1 = ((bf16[32,8,1152]{2,1,0:T(8,128)(2,1)}), bf16[32,8,1152]{2,1,0:T(8,128)(2,1)S(1)}, u32[]{:S(2)}, u32[]{:S(2)}) async-start(bf16[32,8,1152]{2,1,0:T(8,128)(2,1)} %bitcast.31), calls=%async_computation.2 | async-start | bytes 1179648 | tf_op jit(solution)/shard_map/all_to_all | solution.py:897
  423.9 20.4 %all-to-all-start.3 = ((bf16[32,8,1152]{2,1,0:T(8,128)(2,1)}), bf16[32,8,1152]{2,1,0:T(8,128)(2,1)S(1)}, u32[]{:S(2)}, u32[]{:S(2)}) async-start(bf16[32,8,1152]{2,1,0:T(8,128)(2,1)} %bitcast.308), calls=%async_computation.4 | async-start | bytes 1179648 | tf_op jit(solution)/shard_map/all_to_all | solution.py:897
  426.5 257.1 %reduce-scatter.10.cloned.1.call-start = ((), (), s32[]{:S(2)}) async-start(), calls=%async_computation.14 | async-start | bytes 12165120
  445.1 26.9 %all-to-all-start.4 = ((bf16[32,8,1152]{2,1,0:T(8,128)(2,1)}), bf16[32,8,1152]{2,1,0:T(8,128)(2,1)S(1)}, u32[]{:S(2)}, u32[]{:S(2)}) async-start(bf16[32,8,1152]{2,1,0:T(8,128)(2,1)} %bitcast.43), calls=%async_computation.5 | async-start | bytes 1179648 | tf_op jit(solution)/shard_map/all_to_all | solution.py:897
  448.2 340.9 %all-gather.14.cloned.1.call-start = ((), (), s32[]{:S(2)}) async-start(), calls=%async_computation.13 | async-start | bytes 1368576 | tf_op jit(solution)/shard_map/all_gather | solution.py:1312
  521.3 34.7 %collective-permute-start.33 = (bf16[256,3456]{1,0:T(8,128)(2,1)}, bf16[256,3456]{1,0:T(8,128)(2,1)S(1)}, u32[]{:S(2)}, u32[]{:S(2)}) collective-permute-start(bf16[256,3456]{1,0:T(8,128)(2,1)} %get-tuple-element.202.refs_2_.refs_3_), channel_id=1, source_target_pairs={{0,1},{1,0},{2,3},{3,2},{4,5},{5,4},{6,7},{7,6},{8,9},{9,8},{10,11... | collective-permute-start | bytes 5308424 | tf_op jit(solution)/shard_map/ppermute | solution.py:892
  522.6 90.5 %collective-permute-start.36 = (bf16[2,1152,640]{2,1,0:T(8,128)(2,1)}, bf16[2,1152,640]{2,1,0:T(8,128)(2,1)}, u32[]{:S(2)}, u32[]{:S(2)}) collective-permute-start(bf16[2,1152,640]{2,1,0:T(8,128)(2,1)} %get-tuple-element.198), channel_id=1, source_target_pairs={{0,16},{8,24},{16,0},{24,8},{1,17},{9,25},{17,1},{25,9},{2,18},{10... | collective-permute-start | bytes 8847368 | tf_op jit(solution)/shard_map/ppermute | solution.py:892
  524.9 88.1 %collective-permute-start.37 = (bf16[2,1152,640]{2,1,0:T(8,128)(2,1)}, bf16[2,1152,640]{2,1,0:T(8,128)(2,1)S(1)}, u32[]{:S(2)}, u32[]{:S(2)}) collective-permute-start(bf16[2,1152,640]{2,1,0:T(8,128)(2,1)} %get-tuple-element.199), channel_id=1, source_target_pairs={{0,8},{8,0},{16,24},{24,16},{1,9},{9,1},{17,25},{25,17},{2,10},{10... | collective-permute-start | bytes 8847368 | tf_op jit(solution)/shard_map/ppermute | solution.py:892
  558.5 66.0 %collective-permute-start.34 = (bf16[2,256,2304]{2,1,0:T(8,128)(2,1)S(1)}, bf16[2,256,2304]{2,1,0:T(8,128)(2,1)S(1)}, u32[]{:S(2)}, u32[]{:S(2)}) collective-permute-start(bf16[2,256,2304]{2,1,0:T(8,128)(2,1)S(1)} %slice.188), channel_id=1, source_target_pairs={{0,1},{1,0},{2,3},{3,2},{4,5},{5,4},{6,7},{7,6},{8,9},{9,8},{10,11... | collective-permute-start | bytes 7077896 | tf_op jit(solution)/shard_map/ppermute | solution.py:892
  617.2 34.7 %collective-permute-start.38 = (bf16[2,576,640]{2,1,0:T(8,128)(2,1)S(1)}, bf16[2,576,640]{2,1,0:T(8,128)(2,1)S(1)}, u32[]{:S(2)}, u32[]{:S(2)}) collective-permute-start(bf16[2,576,640]{2,1,0:T(8,128)(2,1)S(1)} %fusion.2), channel_id=1, source_target_pairs={{0,8},{8,0},{16,24},{24,16},{1,9},{9,1},{17,25},{25,17},{2,10},{10... | collective-permute-start | bytes 4423688 | tf_op jit(solution)/shard_map/ppermute | solution.py:892
  622.7 33.7 %collective-permute-start.39 = (bf16[2,576,640]{2,1,0:T(8,128)(2,1)}, bf16[2,576,640]{2,1,0:T(8,128)(2,1)S(1)}, u32[]{:S(2)}, u32[]{:S(2)}) collective-permute-start(bf16[2,576,640]{2,1,0:T(8,128)(2,1)} %fusion.3), channel_id=1, source_target_pairs={{0,16},{8,24},{16,0},{24,8},{1,17},{9,25},{17,1},{25,9},{2,18},{10... | collective-permute-start | bytes 4423688 | tf_op jit(solution)/shard_map/ppermute | solution.py:892
  626.6 29.8 %collective-permute-start.35 = (bf16[256,2304]{1,0:T(8,128)(2,1)}, bf16[256,2304]{1,0:T(8,128)(2,1)}, u32[]{:S(2)}, u32[]{:S(2)}) collective-permute-start(bf16[256,2304]{1,0:T(8,128)(2,1)} %get-tuple-element.320), channel_id=1, source_target_pairs={{0,2},{1,3},{2,0},{3,1},{4,6},{5,7},{6,4},{7,5},{8,10},{9,11},{10,... | collective-permute-start | bytes 3538952 | tf_op jit(solution)/shard_map/ppermute | solution.py:892
  674.1 137.7 %reduce-scatter.8.cloned.1.call-start = ((), (), s32[]{:S(2)}) async-start(), calls=%async_computation.10 | async-start | bytes 3538944 | tf_op jit(solution)/shard_map/reduce_scatter | solution.py:1225
  674.2 10.7 %collective-permute-start.40 = (bf16[256,3456]{1,0:T(8,128)(2,1)}, bf16[256,3456]{1,0:T(8,128)(2,1)}, u32[]{:S(2)}, u32[]{:S(2)}) collective-permute-start(bf16[256,3456]{1,0:T(8,128)(2,1)} %get-tuple-element.214.refs_2_), channel_id=1, source_target_pairs={{0,1},{1,0},{2,3},{3,2},{4,5},{5,4},{6,7},{7,6},{8,9},{9,8},{10,11... | collective-permute-start | bytes 5308424 | tf_op jit(solution)/shard_map/ppermute | solution.py:892
  674.3 28.8 %collective-permute-start.41 = (bf16[2,576,384]{2,1,0:T(8,128)(2,1)}, bf16[2,576,384]{2,1,0:T(8,128)(2,1)}, u32[]{:S(2)}, u32[]{:S(2)}) collective-permute-start(bf16[2,576,384]{2,1,0:T(8,128)(2,1)} %get-tuple-element.219), channel_id=1, source_target_pairs={{0,16},{8,24},{16,0},{24,8},{1,17},{9,25},{17,1},{25,9},{2,18},{10... | collective-permute-start | bytes 2654216 | tf_op jit(solution)/shard_map/ppermute | solution.py:892
  675.8 27.3 %collective-permute-start.42 = (bf16[2,576,384]{2,1,0:T(8,128)(2,1)}, bf16[2,576,384]{2,1,0:T(8,128)(2,1)}, u32[]{:S(2)}, u32[]{:S(2)}) collective-permute-start(bf16[2,576,384]{2,1,0:T(8,128)(2,1)} %get-tuple-element.220), channel_id=1, source_target_pairs={{0,8},{8,0},{16,24},{24,16},{1,9},{9,1},{17,25},{25,17},{2,10},{10... | collective-permute-start | bytes 2654216 | tf_op jit(solution)/shard_map/ppermute | solution.py:892
  679.0 56.5 %collective-permute-start.48 = (bf16[576,640]{1,0:T(8,128)(2,1)}, bf16[576,640]{1,0:T(8,128)(2,1)}, u32[]{:S(2)}, u32[]{:S(2)}) collective-permute-start(bf16[576,640]{1,0:T(8,128)(2,1)} %slice_bitcast_fusion.20), channel_id=1, source_target_pairs={{0,2},{1,3},{2,0},{3,1},{4,6},{5,7},{6,4},{7,5},{8,10},{9,11},{10,... | collective-permute-start | bytes 2211848 | tf_op jit(solution)/shard_map/ppermute | solution.py:892
  680.8 54.7 %collective-permute-start.49 = (bf16[576,640]{1,0:T(8,128)(2,1)}, bf16[576,640]{1,0:T(8,128)(2,1)}, u32[]{:S(2)}, u32[]{:S(2)}) collective-permute-start(bf16[576,640]{1,0:T(8,128)(2,1)} %get-tuple-element.322), channel_id=1, source_target_pairs={{0,4},{1,5},{2,6},{3,7},{4,0},{5,1},{6,2},{7,3},{8,12},{9,13},{10,... | collective-permute-start | bytes 2211848 | tf_op jit(solution)/shard_map/ppermute | solution.py:892
  684.9 48.3 %collective-permute-start.45 = (bf16[576,640]{1,0:T(8,128)(2,1)}, bf16[576,640]{1,0:T(8,128)(2,1)}, u32[]{:S(2)}, u32[]{:S(2)}) collective-permute-start(bf16[576,640]{1,0:T(8,128)(2,1)} %get-tuple-element.321), channel_id=1, source_target_pairs={{0,6},{1,7},{2,4},{3,5},{4,2},{5,3},{6,0},{7,1},{8,14},{9,15},{10,... | collective-permute-start | bytes 2211848 | tf_op jit(solution)/shard_map/ppermute | solution.py:892
  704.3 28.9 %collective-permute-start.43 = (bf16[2,288,384]{2,1,0:T(8,128)(2,1)S(1)}, bf16[2,288,384]{2,1,0:T(8,128)(2,1)}, u32[]{:S(2)}, u32[]{:S(2)}) collective-permute-start(bf16[2,288,384]{2,1,0:T(8,128)(2,1)S(1)} %fusion.24), channel_id=1, source_target_pairs={{0,8},{8,0},{16,24},{24,16},{1,9},{9,1},{17,25},{25,17},{2,10},{10... | collective-permute-start | bytes 1327112 | tf_op jit(solution)/shard_map/ppermute | solution.py:892
  706.9 26.2 %collective-permute-start.44 = (bf16[2,288,384]{2,1,0:T(8,128)(2,1)S(1)}, bf16[2,288,384]{2,1,0:T(8,128)(2,1)}, u32[]{:S(2)}, u32[]{:S(2)}) collective-permute-start(bf16[2,288,384]{2,1,0:T(8,128)(2,1)S(1)} %fusion.25), channel_id=1, source_target_pairs={{0,16},{8,24},{16,0},{24,8},{1,17},{9,25},{17,1},{25,9},{2,18},{10... | collective-permute-start | bytes 1327112 | tf_op jit(solution)/shard_map/ppermute | solution.py:892
  733.1 36.4 %collective-permute-start.46 = (bf16[2,576,640]{2,1,0:T(8,128)(2,1)}, bf16[2,576,640]{2,1,0:T(8,128)(2,1)}, u32[]{:S(2)}, u32[]{:S(2)}) collective-permute-start(bf16[2,576,640]{2,1,0:T(8,128)(2,1)} %get-tuple-element.224), channel_id=1, source_target_pairs={{0,16},{8,24},{16,0},{24,8},{1,17},{9,25},{17,1},{25,9},{2,18},{10... | collective-permute-start | bytes 4423688 | tf_op jit(solution)/shard_map/ppermute | solution.py:892
  733.9 36.9 %collective-permute-start.47 = (bf16[2,576,640]{2,1,0:T(8,128)(2,1)}, bf16[2,576,640]{2,1,0:T(8,128)(2,1)}, u32[]{:S(2)}, u32[]{:S(2)}) collective-permute-start(bf16[2,576,640]{2,1,0:T(8,128)(2,1)} %get-tuple-element.225), channel_id=1, source_target_pairs={{0,8},{8,0},{16,24},{24,16},{1,9},{9,1},{17,25},{25,17},{2,10},{10... | collective-permute-start | bytes 4423688 | tf_op jit(solution)/shard_map/ppermute | solution.py:892
  742.0 36.6 %collective-permute-start.55 = (bf16[288,384]{1,0:T(8,128)(2,1)S(1)}, bf16[288,384]{1,0:T(8,128)(2,1)S(1)}, u32[]{:S(2)}, u32[]{:S(2)}) collective-permute-start(bf16[288,384]{1,0:T(8,128)(2,1)S(1)} %slice_bitcast_fusion.41), channel_id=1, source_target_pairs={{0,2},{1,3},{2,0},{3,1},{4,6},{5,7},{6,4},{7,5},{8,10},{9,11},{10,... | collective-permute-start | bytes 663560 | tf_op jit(solution)/shard_map/ppermute | solution.py:892
  760.6 18.0 %collective-permute-start.57 = (bf16[288,384]{1,0:T(8,128)(2,1)S(1)}, bf16[288,384]{1,0:T(8,128)(2,1)S(1)}, u32[]{:S(2)}, u32[]{:S(2)}) collective-permute-start(bf16[288,384]{1,0:T(8,128)(2,1)S(1)} %get-tuple-element.236), channel_id=1, source_target_pairs={{0,6},{1,7},{2,4},{3,5},{4,2},{5,3},{6,0},{7,1},{8,14},{9,15},{10,... | collective-permute-start | bytes 663560 | tf_op jit(solution)/shard_map/ppermute | solution.py:892
  762.9 24.3 %collective-permute-start.56 = (bf16[288,384]{1,0:T(8,128)(2,1)S(1)}, bf16[288,384]{1,0:T(8,128)(2,1)S(1)}, u32[]{:S(2)}, u32[]{:S(2)}) collective-permute-start(bf16[288,384]{1,0:T(8,128)(2,1)S(1)} %get-tuple-element.235), channel_id=1, source_target_pairs={{0,4},{1,5},{2,6},{3,7},{4,0},{5,1},{6,2},{7,3},{8,12},{9,13},{10,... | collective-permute-start | bytes 663560 | tf_op jit(solution)/shard_map/ppermute | solution.py:892
  773.1 18.6 %collective-permute-start.50 = (bf16[2,288,640]{2,1,0:T(8,128)(2,1)}, bf16[2,288,640]{2,1,0:T(8,128)(2,1)S(1)}, u32[]{:S(2)}, u32[]{:S(2)}) collective-permute-start(bf16[2,288,640]{2,1,0:T(8,128)(2,1)} %fusion.17), channel_id=1, source_target_pairs={{0,8},{8,0},{16,24},{24,16},{1,9},{9,1},{17,25},{25,17},{2,10},{10... | collective-permute-start | bytes 2211848 | tf_op jit(solution)/shard_map/ppermute | solution.py:892
  776.6 16.4 %collective-permute-start.51 = (bf16[2,288,640]{2,1,0:T(8,128)(2,1)}, bf16[2,288,640]{2,1,0:T(8,128)(2,1)}, u32[]{:S(2)}, u32[]{:S(2)}) collective-permute-start(bf16[2,288,640]{2,1,0:T(8,128)(2,1)} %fusion.18), channel_id=1, source_target_pairs={{0,16},{8,24},{16,0},{24,8},{1,17},{9,25},{17,1},{25,9},{2,18},{10... | collective-permute-start | bytes 2211848 | tf_op jit(solution)/shard_map/ppermute | solution.py:892
  811.8 12.0 %collective-permute-start.58 = (bf16[512,288]{1,0:T(8,128)(2,1)}, bf16[512,288]{1,0:T(8,128)(2,1)S(1)}, u32[]{:S(2)}, u32[]{:S(2)}) collective-permute-start(bf16[512,288]{1,0:T(8,128)(2,1)} %bitcast.295), channel_id=1, source_target_pairs={{0,8},{8,0},{16,24},{24,16},{1,9},{9,1},{17,25},{25,17},{2,10},{10... | collective-permute-start | bytes 884744 | tf_op jit(solution)/shard_map/ppermute | solution.py:892
  813.0 17.3 %collective-permute-start.52 = (bf16[288,640]{1,0:T(8,128)(2,1)S(1)}, bf16[288,640]{1,0:T(8,128)(2,1)S(1)}, u32[]{:S(2)}, u32[]{:S(2)}) collective-permute-start(bf16[288,640]{1,0:T(8,128)(2,1)S(1)} %slice_bitcast_fusion.37), channel_id=1, source_target_pairs={{0,2},{1,3},{2,0},{3,1},{4,6},{5,7},{6,4},{7,5},{8,10},{9,11},{10,... | collective-permute-start | bytes 1105928 | tf_op jit(solution)/shard_map/ppermute | solution.py:892
  815.5 28.4 %collective-permute-start.53 = (bf16[288,640]{1,0:T(8,128)(2,1)}, bf16[288,640]{1,0:T(8,128)(2,1)S(1)}, u32[]{:S(2)}, u32[]{:S(2)}) collective-permute-start(bf16[288,640]{1,0:T(8,128)(2,1)} %get-tuple-element.332), channel_id=1, source_target_pairs={{0,4},{1,5},{2,6},{3,7},{4,0},{5,1},{6,2},{7,3},{8,12},{9,13},{10,... | collective-permute-start | bytes 1105928 | tf_op jit(solution)/shard_map/ppermute | solution.py:892
  816.5 27.4 %collective-permute-start.54 = (bf16[288,640]{1,0:T(8,128)(2,1)S(1)}, bf16[288,640]{1,0:T(8,128)(2,1)S(1)}, u32[]{:S(2)}, u32[]{:S(2)}) collective-permute-start(bf16[288,640]{1,0:T(8,128)(2,1)S(1)} %get-tuple-element.331), channel_id=1, source_target_pairs={{0,6},{1,7},{2,4},{3,5},{4,2},{5,3},{6,0},{7,1},{8,14},{9,15},{10,... | collective-permute-start | bytes 1105928 | tf_op jit(solution)/shard_map/ppermute | solution.py:892
  825.8 22.1 %collective-permute-start.59 = (bf16[512,288]{1,0:T(8,128)(2,1)}, bf16[512,288]{1,0:T(8,128)(2,1)}, u32[]{:S(2)}, u32[]{:S(2)}) collective-permute-start(bf16[512,288]{1,0:T(8,128)(2,1)} %fusion.14), channel_id=1, source_target_pairs={{0,16},{8,24},{16,0},{24,8},{1,17},{9,25},{17,1},{25,9},{2,18},{10... | collective-permute-start | bytes 884744 | tf_op jit(solution)/shard_map/ppermute | solution.py:892
  (67 other events, 839.2 us)
Sparse Core Ops, SparseCore 0:
  27.7 37.3 all-gather.9
  133.4 26.7 reduce-scatter.5
  185.4 59.6 all-gather.11
  248.3 110.5 all-gather.7
  444.4 173.3 reduce-scatter.9
  674.3 95.8 all-gather.13
  772.5 39.3 reduce-scatter.7
